TPU v7x, 256 devices: a whole 4x4x8 slice. The times are simulated.
256 devices in a mesh: dp: 64 (over y, z_hi, x, core), tensor: 4 (over z_lo).
Axes of the slice: x: 4, y: 4, z: 8 (z_hi: 2, z_lo: 4; z = z_hi * 4 + z_lo), core: 2. Of those that a mesh axis runs over, the one named last changes fastest.
Arguments:
- tokens: bfloat16 [8192, 16384], P('dp', 'tensor'), may hold values from -6 to 6
- norm_gain: float32 [16384], P('tensor'), may hold values from 0.5 to 3, as said below
- query_weight: bfloat16 [16384, 1536], P('dp', 'tensor'), may hold values from -0.046875 to 0.046875
- kv_weight: bfloat16 [16384, 256], P('dp', 'tensor'), may hold values from -0.046875 to 0.046875
- out_weight: bfloat16 [1536, 16384], P('dp', 'tensor'), may hold values from -0.15625 to 0.15625
- lengths: int32 [64], P('dp'), may hold values from 32 to 128, as said below
Outputs:
- mixed: bfloat16 [8192, 16384], P('dp', 'tensor')
Inputs may be any that keep to these rules, and one draw needn't show every extreme that they name: `norm_gain`: gains of the norm, one a feature. `lengths`: valid tokens of each trajectory, counted from its start; some trajectory fills all 128 positions.
All inputs are finite; a program needn't handle non-finite values.
Results may differ from a plain program's by a relative error of at most 0.04.
Values may be sent and summed in bfloat16 or wider, within the bound.
No kernel may reach another device: no remote copies, remote signals or barrier semaphores. Data moves between devices by JAX's collectives and lax.ppermute only.
A program may use at most 128 MiB of HBM per device.

v0:
```python
import math

import jax
import jax.numpy as jnp
from jax import lax
from jax.sharding import PartitionSpec as P


def rotary(values):
    length = values.shape[0]
    width = values.shape[-1]
    position = jnp.arange(length, dtype=jnp.float32)
    freqs = jnp.exp(jnp.arange(width // 2, dtype=jnp.float32) * (-2.0 * math.log(500000.0) / width))
    angle = position[:, None] * freqs[None, :]
    angle = angle.reshape((length,) + (1,) * (values.ndim - 2) + (width // 2,))
    cosine = jnp.cos(angle)
    sine = jnp.sin(angle)
    pairs = values.reshape(values.shape[:-1] + (width // 2, 2))
    former = pairs[..., 0]
    latter = pairs[..., 1]
    turned = jnp.stack([former * cosine - latter * sine, former * sine + latter * cosine], axis=-1)
    return turned.reshape(values.shape)


def attend(query, keys, values, limit):
    length = query.shape[0]
    scale = query.shape[-1] ** (-0.5)
    scores = jnp.einsum("qhd,kd->hqk", query, keys, preferred_element_type=jnp.float32) * scale
    rows_idx = jnp.arange(length, dtype=jnp.int32)
    valid = (rows_idx[None, :] <= rows_idx[:, None]) & (rows_idx[None, :] < limit)
    scores = jnp.where(valid[None], scores, -jnp.inf)
    highest = jnp.max(scores, axis=-1, keepdims=True)
    raised = jnp.exp(scores - highest)
    totals = jnp.sum(raised, axis=-1, keepdims=True)
    weights = (raised / totals).astype(jnp.bfloat16)
    output = jnp.einsum("hqk,kd->qhd", weights, values, preferred_element_type=jnp.float32)
    live = rows_idx < limit
    output = jnp.where(live[:, None, None], output, 0.0).astype(jnp.bfloat16)
    return output.reshape(length, query.shape[1] * query.shape[2])


def body(tokens, norm_gain, query_weight, kv_weight, out_weight, lengths):
    limit = lengths[0]
    whole, gain_whole = (
        lax.all_gather(tokens, "tensor", axis=1, tiled=True),
        lax.all_gather(norm_gain.astype(jnp.bfloat16), "tensor", axis=0, tiled=True).astype(
            norm_gain.dtype
        ),
    )
    widened = whole.astype(jnp.float32)
    meansq = jnp.mean(widened * widened, axis=-1, keepdims=True)
    normed = (widened * lax.rsqrt(meansq + 1e-05) * gain_whole).astype(jnp.bfloat16)
    row_count = normed.shape[0]
    columns = normed
    query_raw = jnp.dot(
        columns,
        lax.all_gather(query_weight, "dp", axis=0, tiled=True),
        preferred_element_type=jnp.float32,
    )
    kv_raw = jnp.dot(
        columns,
        lax.all_gather(kv_weight, "dp", axis=0, tiled=True),
        preferred_element_type=jnp.float32,
    )
    kv_local = kv_raw.astype(jnp.bfloat16)
    kv_rows = lax.all_gather(kv_local, "tensor", axis=1, tiled=True)
    head_size = kv_rows.shape[1] // 2
    heads_here = query_raw.shape[1] // head_size
    query = rotary(query_raw.reshape(row_count, heads_here, head_size)).astype(jnp.bfloat16)
    keys = rotary(kv_rows[:, :head_size].astype(jnp.float32)).astype(jnp.bfloat16)
    values = kv_rows[:, head_size:]
    attended = attend(query, keys, values, limit)
    all_heads = lax.all_gather(attended, "tensor", axis=1, tiled=True)
    columns = all_heads
    terms = jnp.dot(
        columns,
        lax.all_gather(out_weight, "dp", axis=0, tiled=True),
        preferred_element_type=jnp.float32,
    )
    return terms.astype(jnp.bfloat16)


def solution(mesh):
    placed = (
        P("dp", "tensor"),
        P("tensor"),
        P("dp", "tensor"),
        P("dp", "tensor"),
        P("dp", "tensor"),
        P("dp"),
    )
    return jax.shard_map(
        body, mesh=mesh, in_specs=placed, out_specs=P("dp", "tensor"), check_vma=False
    )
```

profile of v0, /device:TPU:24, one launch (start us, length us, event | category | flops | bytes accessed | tf_op | source)
XLA Modules:
  0.0 462.3 jit_solution(7508714411756642357)
XLA Ops:
  6.5 0.0 all-gather.5.cloned.1.call-start
  6.5 0.7 all-gather.5.cloned.1.call-update
  7.3 0.0 all-gather.7.cloned.1.call-start
  7.3 0.7 all-gather.7.cloned.1.call-update
  8.0 0.0 all-gather.9.cloned.1.call-start
  8.1 0.7 all-gather.9.cloned.1.call-update
  8.7 0.0 all-gather.11.cloned.1.call-start
  8.8 0.5 all-gather.11.cloned.1.call-update
  9.3 0.7 convert_element_type.33
  10.0 14.0 %all_gather.22 = bf16[16384]{0:T(1024)(128)(2,1)S(1)} all-gather(bf16[4096]{0:T(1024)(128)(2,1)S(1)} %convert_element_type.33), channel_id=1, replica_groups=mesh['dp'=64,'tensor'=4] {'tensor'}, dimensions={0}, use_global_device_ids=true | all-gather | bytes 40960 | tf_op jit(solution)/shard_map/all_gather | solution.py:46
  24.8 0.1 fusion.20
  24.8 0.2 fusion.24
  25.0 70.8 %all-gather.5.cloned.1.call-done = bf16[128,16384]{1,0:T(8,128)(2,1)} async-done(((bf16[128,4096]{1,0:T(8,128)(2,1)}), bf16[128,16384]{1,0:T(8,128)(2,1)}) %all-gather.5.cloned.1.call-update) | async-done | bytes 4194320 | tf_op jit(solution)/shard_map/all_gather | solution.py:45
  95.8 3.1 fusion.1
  98.9 84.9 %all-gather.7.cloned.1.call-done = bf16[16384,64]{0,1:T(8,128)(2,1)} async-done(((bf16[256,64]{0,1:T(8,128)(2,1)}), bf16[16384,64]{0,1:T(8,128)(2,1)}) %all-gather.7.cloned.1.call-update) | async-done | bytes 2097168 | tf_op jit(solution)/shard_map/all_gather | solution.py:62
  183.8 4.5 fusion.14
  188.3 13.3 %all_gather.24 = bf16[128,256]{0,1:T(8,128)(2,1)S(1)} all-gather(bf16[128,64]{0,1:T(8,128)(2,1)S(1)} %fusion.14), channel_id=1, replica_groups=mesh['dp'=64,'tensor'=4] {'tensor'}, dimensions={1}, use_global_device_ids=true | all-gather | bytes 81920 | tf_op jit(solution)/shard_map/all_gather | solution.py:66
  201.7 0.2 subtract_convert_fusion.1
  201.9 114.3 %all-gather.9.cloned.1.call-done = bf16[16384,384]{1,0:T(8,128)(2,1)} async-done(((bf16[256,384]{1,0:T(8,128)(2,1)}), bf16[16384,384]{1,0:T(8,128)(2,1)}) %all-gather.9.cloned.1.call-update) | async-done | bytes 12582928 | tf_op jit(solution)/shard_map/all_gather | solution.py:57
  316.2 10.9 %fusion.4 = f32[128,384]{0,1:T(8,128)S(1)} fusion(bf16[16384,384]{1,0:T(8,128)(2,1)} %all-gather.9.cloned.1.call-done, bf16[128,16384]{1,0:T(8,128)(2,1)} %all-gather.5.cloned.1.call-done, f32[16384]{0:T(1024)S(1)} %convert_element_type.34, f32[128]{0:T(128)S(1)} %add_rsqrt_fusion), kind=kOutput, calls=%fused_computation.7 | convolution fusion | flops 1619001344 | bytes 17039872 | tf_op jit(solution)/shard_map/dot_general | solution.py:55
  327.1 0.2 fusion.35
  327.3 0.3 fusion.37
  327.6 0.2 fusion.12
  327.8 0.2 fusion.13
  328.0 16.4 %all_gather.26 = bf16[128,1536]{0,1:T(8,128)(2,1)S(1)} all-gather(bf16[128,384]{0,1:T(8,128)(2,1)S(1)} %bitcast.54), channel_id=1, replica_groups=mesh['dp'=64,'tensor'=4] {'tensor'}, dimensions={1}, use_global_device_ids=true | all-gather | bytes 491520 | tf_op jit(solution)/shard_map/all_gather | solution.py:73
  344.4 104.0 %all-gather.11.cloned.1.call-done = bf16[1536,4096]{1,0:T(8,128)(2,1)} async-done(((bf16[24,4096]{1,0:T(8,128)(2,1)}), bf16[1536,4096]{1,0:T(8,128)(2,1)}) %all-gather.11.cloned.1.call-update) | async-done | bytes 12582928 | tf_op jit(solution)/shard_map/all_gather | solution.py:77
  448.4 7.4 %convolution_convert_fusion = bf16[128,4096]{1,0:T(8,128)(2,1)} fusion(bf16[128,1536]{0,1:T(8,128)(2,1)S(1)} %all_gather.26, bf16[1536,4096]{1,0:T(8,128)(2,1)} %all-gather.11.cloned.1.call-done), kind=kOutput, calls=%fused_computation.6 | convolution fusion | flops 1611137024 | bytes 14024704 | tf_op jit(solution)/shard_map/dot_general | solution.py:75
  (7 shorter events, 0.1 us)
Async XLA Ops:
  6.5 89.3 %all-gather.5.cloned.1.call-start = ((), (), s32[]{:S(2)}) async-start(), calls=%async_computation | async-start | bytes 5242880 | tf_op jit(solution)/shard_map/all_gather | solution.py:45
  7.3 176.6 %all-gather.7.cloned.1.call-start = ((), (), s32[]{:S(2)}) async-start(), calls=%async_computation.1 | async-start | bytes 2129920 | tf_op jit(solution)/shard_map/all_gather | solution.py:62
  8.0 308.2 %all-gather.9.cloned.1.call-start = ((), (), s32[]{:S(2)}) async-start(), calls=%async_computation.2 | async-start | bytes 12779520 | tf_op jit(solution)/shard_map/all_gather | solution.py:57
  8.7 439.7 %all-gather.11.cloned.1.call-start = ((), (), s32[]{:S(2)}) async-start(), calls=%async_computation.3 | async-start | bytes 12779520 | tf_op jit(solution)/shard_map/all_gather | solution.py:77
Sparse Core Ops, SparseCore 0:
  9.2 86.6 all-gather.4
  99.2 84.5 all-gather.6
  187.5 128.6 all-gather.8
  319.7 128.6 all-gather.10
where the time goes:
time: 464 us; the launch traced here: 462 us
  waiting for transfers between devices  377 us (81%)
  blocking collectives  43.7 us (9%)
  matrix products  23.5 us (5%)
  between operations  13.9 us (3%)
    all_gather x1, waiting for transfers between devices, body(): lax.all_gather(query_weight, 'dp', axis=0, tiled=True)  114 us
    all_gather x1, waiting for transfers between devices, body(): lax.all_gather(out_weight, 'dp', axis=0, tiled=True)  104 us
    all_gather x1, waiting for transfers between devices, body(): lax.all_gather(kv_weight, 'dp', axis=0, tiled=True)  84.9 us
    all_gather x1, waiting for transfers between devices, body(): lax.all_gather(tokens, 'tensor', axis=1, tiled=True)  70.8 us
    all_gather x1, blocking collectives, body(): all_heads = lax.all_gather(attended, 'tensor', axis=1, tiled=True)  16.4 us
    all_gather x1, blocking collectives, body(): lax.all_gather(norm_gain.astype(jnp.bfloat16), 'tensor', axis=0, tiled=True)  14 us
    all_gather x1, blocking collectives, body(): kv_rows = lax.all_gather(kv_local, 'tensor', axis=1, tiled=True)  13.3 us
    dot_general x1, matrix products, body(): jnp.dot(columns, lax.all_gather(query_weight, 'dp', axis=0, tiled=True),...  10.9 us
  transfers between devices with their start and end apart: 4, of which 4 were waited for; matrix products, arithmetic and copies ran while one was open for 4% of the time, Pallas kernels for 0%

commit v1 on v0

v1 whole, which is shorter than its diff:
```python
import math

import jax
import jax.numpy as jnp
import numpy as np
from jax import lax
from jax.sharding import Mesh
from jax.sharding import PartitionSpec as P

AXES = ("y", "zh", "x", "core", "zl")
SIZES = (4, 2, 4, 2, 4)
D = 16384
HD = 128
ROWS = 128
BF = jnp.bfloat16
F32 = jnp.float32


def flat(*coords):
    index = 0
    for size, coord in zip(SIZES, coords):
        index = index * size + coord
    return index


def every():
    for y in range(4):
        for zh in range(2):
            for x in range(4):
                for c in range(2):
                    for t in range(4):
                        yield y, zh, x, c, t


def swap(value, axis, d):
    n = SIZES[AXES.index(axis)]
    return lax.ppermute(value, axis, [(i, i ^ d) for i in range(n)])


def move(value, where):
    return lax.ppermute(value, AXES, [(flat(*at), flat(*where(*at))) for at in every()])


def tables():
    freqs = np.exp(np.arange(HD // 2, dtype=np.float32) * np.float32(-2.0 * math.log(500000.0) / HD))
    angle = np.arange(ROWS, dtype=np.float32)[:, None] * freqs.astype(np.float32)[None, :]
    cosine = np.repeat(np.cos(angle), 2, axis=1).astype(np.float32)
    sine = np.repeat(np.sin(angle), 2, axis=1).astype(np.float32)
    sine[:, 0::2] *= -1.0
    return cosine, sine


COSINE, SINE = tables()


def rotate(values):
    shape = (ROWS,) + (1,) * (values.ndim - 2) + (HD,)
    even = (jnp.arange(HD) % 2 == 0)
    partner = jnp.where(even, jnp.roll(values, -1, axis=-1), jnp.roll(values, 1, axis=-1))
    return values * COSINE.reshape(shape) + partner * SINE.reshape(shape)


def attend(query, keys, values, limit):
    scale = HD ** (-0.5)
    scores = jnp.einsum("qhd,kd->hqk", query, keys, preferred_element_type=F32) * scale
    at = jnp.arange(ROWS, dtype=jnp.int32)
    valid = (at[None, :] <= at[:, None]) & (at[None, :] < limit)
    scores = jnp.where(valid[None], scores, -jnp.inf)
    raised = jnp.exp(scores - jnp.max(scores, axis=-1, keepdims=True))
    weights = (raised / jnp.sum(raised, axis=-1, keepdims=True)).astype(BF)
    output = jnp.einsum("hqk,kd->qhd", weights, values, preferred_element_type=F32)
    output = jnp.where((at < limit)[:, None, None], output, 0.0).astype(BF)
    return output.reshape(ROWS, query.shape[1] * HD)


def pick(flag, first, second):
    return jnp.where(flag, second, first)


def body(tokens, norm_gain, query_weight, kv_weight, out_weight, lengths):
    y, zh, x, c, t = (lax.axis_index(name) for name in AXES)

    packed = jnp.concatenate(
        [query_weight[:, :128], query_weight[:, 128:256], query_weight[:, 256:]]
        + [kv_weight.T[:, :128], kv_weight.T[:, 128:]],
        axis=0,
    )
    near = move(packed, lambda y, zh, x, c, t: (x ^ y, zh, 2 * c + (t & 1), t >> 1, y))
    far = move(packed, lambda y, zh, x, c, t: (x ^ y, zh ^ 1, 2 * c + (t & 1), t >> 1, y))
    mine = jnp.stack([near, far])
    blocks = [mine] + [swap(mine, "x", d) for d in (1, 2, 3)]

    def heads_of(block):
        return jnp.concatenate([block[:, 0:256], block[:, 256:512], block[:, 512:768]], axis=2)

    def kv_of(block):
        return jnp.concatenate([block[:, 768:832], block[:, 832:896]], axis=2)

    q_w = jnp.stack(
        [jnp.concatenate([heads_of(blocks[2 * cr]), heads_of(blocks[2 * cr + 1])], axis=2) for cr in (0, 1)], axis=1
    ).reshape(1024, 768)
    kv_w = jnp.stack(
        [jnp.concatenate([kv_of(blocks[2 * cr]), kv_of(blocks[2 * cr + 1])], axis=1) for cr in (0, 1)], axis=2
    )
    kv_w = jnp.swapaxes(kv_w, 0, 1).reshape(128, 1024)

    widened = tokens.astype(F32)
    squares = jnp.sum(widened * widened, axis=1)
    gained = (widened * norm_gain[None, :]).astype(BF)
    parts = gained.reshape(ROWS, 16, 256)

    def features(d):
        s = y ^ d ^ t
        picked = [
            lax.dynamic_slice(gained, (0, (((zh ^ a) * 4 + s) * 2 + ((x >> 1) ^ b)) * 256), (ROWS, 256))
            for a in (0, 1)
            for b in (0, 1)
        ]
        return jnp.concatenate(picked, axis=1)

    ring = [features(0)] + [swap(features(d), "y", d) for d in (1, 2, 3)]
    ring = jnp.stack(ring)
    other = swap(ring, "core", 1)
    inputs = jnp.stack([ring, other], axis=1).reshape(1024, 1024)

    note = jnp.stack([squares, jnp.full((ROWS,), lengths[0], jnp.int32).astype(F32)])
    note_other = swap(note, "core", 1)
    both = jnp.stack([squares, note_other[0]])
    total = both
    for d in (1, 2, 3):
        total = total + swap(both, "zl", d)
    scales = lax.rsqrt(total / D + 1e-05)

    q_part = jnp.dot(inputs, q_w, preferred_element_type=F32)
    kv_part = lax.dot_general(inputs, kv_w, (((1,), (1,)), ((), ())), preferred_element_type=F32)
    part = jnp.concatenate([q_part, kv_part], axis=1).reshape(4, 256, 896)
    summed = part[0]
    for d in (1, 2, 3):
        summed = summed + swap(part[d].astype(BF), "y", d).astype(F32)
    summed = summed.reshape(2, ROWS, 896)

    def share(d):
        target = t ^ d
        rows = lax.dynamic_index_in_dim(summed, (target & 1) ^ c, 0, keepdims=False)
        heads = lax.dynamic_slice(rows, (0, (target >> 1) * 384), (ROWS, 384))
        return jnp.concatenate([heads, rows[:, 768:]], axis=1)

    raw = share(0)
    for d in (1, 2, 3):
        raw = raw + swap(share(d).astype(BF), "zl", d).astype(F32)
    mine_here = (t & 1) ^ c
    scale = lax.dynamic_index_in_dim(scales, mine_here, 0, keepdims=False)
    raw = raw * scale[:, None]
    limit = jnp.where(mine_here == 0, lengths[0], note_other[1, 0].astype(jnp.int32))
    kv_half = raw[:, 384:]
    kv_half = pick((x & 1) == 1, kv_half, jnp.roll(kv_half, 64, axis=1)).astype(BF)
    kv_other = swap(kv_half, "core", 1)
    keys = rotate(pick(c == 1, kv_half, kv_other).astype(F32)).astype(BF)
    values = pick(c == 1, kv_other, kv_half)
    query = rotate(raw[:, :384].reshape(ROWS, 3, HD)).astype(BF)
    attended = attend(query, keys, values, limit)

    got = [attended] + [swap(attended, "zl", d) for d in (1, 2, 3)]
    flip_heads = ((t >> 1) ^ (x & 1)) == 1
    flip_rows = mine_here == 1
    by_rows = []
    for a in (0, 1):
        first, second = got[a], got[2 + a]
        by_rows.append(
            jnp.concatenate([pick(flip_heads, first, second), pick(flip_heads, second, first)], axis=1)
        )
    half = jnp.stack([pick(flip_rows, by_rows[0], by_rows[1]), pick(flip_rows, by_rows[1], by_rows[0])])
    other_half = swap(half, "core", 1)[::-1]
    whole = jnp.concatenate([pick(c == 1, half, other_half), pick(c == 1, other_half, half)], axis=2)
    whole = whole.reshape(256, 1536)

    wo = out_weight.reshape(24, 2, 2048)
    here = lax.dynamic_index_in_dim(wo, c, 1, keepdims=False)
    there = swap(lax.dynamic_index_in_dim(wo, 1 - c, 1, keepdims=False), "core", 1)
    pair = jnp.concatenate([pick(c == 1, here, there), pick(c == 1, there, here)], axis=0)

    def gathered(piece, first_axis, last_axis, first_at, exchange):
        width = piece.shape[1]
        if exchange:
            own = move(piece, lambda y, zh, x, c, t: (x, zh, y, c, t))
            away = move(piece, lambda y, zh, x, c, t: (x, zh ^ 1, y, c, t))
        else:
            own = piece
            away = swap(piece, "zh", 1)
        level = jnp.stack([pick(zh == 1, own, away), pick(zh == 1, away, own)])
        ringed = [level] + [swap(level, first_axis, d) for d in (1, 2, 3)]
        low = [(pick((first_at & 1) == 1, ringed[2 * h], ringed[2 * h + 1]),
                pick((first_at & 1) == 1, ringed[2 * h + 1], ringed[2 * h])) for h in (0, 1)]
        high = (first_at >> 1) == 1
        ordered = [pick(high, low[0][0], low[1][0]), pick(high, low[0][1], low[1][1]),
                   pick(high, low[1][0], low[0][0]), pick(high, low[1][1], low[0][1])]
        block = jnp.stack(ordered, axis=1).reshape(384, width)
        return [block] + [swap(block, last_axis, d) for d in (1, 2, 3)]

    a_blocks = gathered(pair[:, :1024], "y", "x", y, True)
    b_blocks = gathered(pair[:, 1024:], "x", "y", x, False)
    outs = []
    for blocks_here, at in ((a_blocks, x), (b_blocks, y)):
        acc = None
        for d in range(4):
            rows = lax.dynamic_slice(whole, (0, (at ^ d) * 384), (256, 384))
            term = jnp.dot(rows, blocks_here[d], preferred_element_type=F32)
            acc = term if acc is None else acc + term
        outs.append(acc.astype(BF))
    out = jnp.concatenate(outs, axis=1)
    kept, sent = out[:ROWS], out[ROWS:]
    came = swap(sent, "core", 1)
    return jnp.concatenate([pick(c == 1, kept, came), pick(c == 1, came, kept)], axis=1)


def solution(mesh):
    fine = Mesh(mesh.devices.reshape(SIZES), AXES)
    rows = ("y", "zh", "x", "core")
    placed = (P(rows, "zl"), P("zl"), P(rows, "zl"), P(rows, "zl"), P(rows, "zl"), P(rows))
    return jax.shard_map(body, mesh=fine, in_specs=placed, out_specs=P(rows, "zl"), check_vma=False)
```

time: 464 us -> 208 us (0.45)
  waiting for transfers between devices: 377 us -> 89.1 us
  starting transfers between devices: 0.12 us -> 77.3 us
  blocking collectives: 43.7 us -> 0 us
  local copies, waits for them, and re-layouts: 0.21 us -> 21.4 us
  matrix products: 23.5 us -> 6.85 us
  between operations: 13.9 us -> 2.34 us
    all_gather x4 -> x0, waiting for transfers between devices: 374 us -> none  [the longest x1 114 us: body(): lax.all_gather(query_weight, 'dp', axis=0, tiled=True)]
    ppermute x0 -> x41, waiting for transfers between devices: none -> 89.1 us  [the longest x37 89.1 us: swap(): return lax.ppermute(value, axis, [(i, i ^ d) for i in range(n)])]
    ppermute x0 -> x41, starting transfers between devices: none -> 77.3 us  [the longest x37 56.3 us: swap(): return lax.ppermute(value, axis, [(i, i ^ d) for i in range(n)])]
    all_gather x3 -> x0, blocking collectives: 43.7 us -> none  [the longest x1 16.4 us: body(): all_heads = lax.all_gather(attended, 'tensor', axis=1, tiled=True)]
    dot_general x5 -> x12, matrix products: 23.2 us -> 6.85 us  [the longest x8 3.57 us: body(): term = jnp.dot(rows, blocks_here[d], preferred_element_type=F32)]
    unnamed x0 -> x28, local copies, waits for them, and re-layouts: none -> 12.5 us
  transfers between devices with their start and end apart: 4 -> 41, of which waited for: 4 -> 15; matrix products, arithmetic and copies ran while one was open for 4% -> 13% of each run, Pallas kernels for 0% -> 0%
where the time goes in v1:
time: 208 us; the launch traced here: 205 us
  waiting for transfers between devices  89.1 us (43%)
  starting transfers between devices  77.3 us (37%)
  local copies, waits for them, and re-layouts  21.4 us (10%)
  other arithmetic  8.25 us (4%)
  matrix products  6.85 us (3%)
  between operations  2.34 us (1%)
    ppermute x37, waiting for transfers between devices, swap(): return lax.ppermute(value, axis, [(i, i ^ d) for i in range(n)])  89.1 us
    ppermute x37, starting transfers between devices, swap(): return lax.ppermute(value, axis, [(i, i ^ d) for i in range(n)])  56.3 us
    ppermute x4, starting transfers between devices, move(): lax.ppermute(value, AXES, [(flat(*at), flat(*where(*at))) for at in every...  20.9 us
    unnamed x28, local copies, waits for them, and re-layouts  12.5 us
  transfers between devices with their start and end apart: 41, of which 15 were waited for; matrix products, arithmetic and copies ran while one was open for 13% of the time, Pallas kernels for 0%

profile of v1, /device:TPU:24, one launch (start us, length us, event | category | flops | bytes accessed | tf_op | source)
XLA Modules:
  0.0 205.2 jit_solution(11262465577471893969)
XLA Ops:
  7.1 6.5 %collective-permute-start.5 = (bf16[896,128]{1,0:T(8,128)(2,1)}, bf16[896,128]{1,0:T(8,128)(2,1)S(1)}, u32[]{:S(2)}, u32[]{:S(2)}) collective-permute-start(bf16[896,128]{1,0:T(8,128)(2,1)} %constant_dynamic-update-slice_fusion), channel_id=1, source_target_pairs={{0,0},{1,8},{2,4},{3,12},{4,16},{5,24},{6,20},{7,28},{8,64},{9,72}... | collective-permute-start | bytes 688136 | tf_op jit(solution)/shard_map/ppermute | solution.py:41
  13.6 2.2 %collective-permute-start.6 = (bf16[896,128]{1,0:T(8,128)(2,1)}, bf16[896,128]{1,0:T(8,128)(2,1)S(1)}, u32[]{:S(2)}, u32[]{:S(2)}) collective-permute-start(bf16[896,128]{1,0:T(8,128)(2,1)} %constant_dynamic-update-slice_fusion), channel_id=1, source_target_pairs={{0,32},{1,40},{2,36},{3,44},{4,48},{5,56},{6,52},{7,60},{8,96},{9,... | collective-permute-start | bytes 688136 | tf_op jit(solution)/shard_map/ppermute | solution.py:41
  18.2 2.4 %collective-permute-start = (f32[2,128]{1,0:T(2,128)S(1)}, f32[2,128]{1,0:T(2,128)S(1)}, u32[]{:S(2)}, u32[]{:S(2)}) collective-permute-start(f32[2,128]{1,0:T(2,128)S(1)} %stack.116), channel_id=1, source_target_pairs={{0,4},{4,0},{1,5},{5,1},{2,6},{6,2},{3,7},{7,3},{8,12},{12,8},{9,1... | collective-permute-start | bytes 3080 | tf_op jit(solution)/shard_map/ppermute | solution.py:37
  22.9 2.2 %collective-permute-start.17 = (f32[2,128]{1,0:T(2,128)S(1)}, f32[2,128]{1,0:T(2,128)S(1)}, u32[]{:S(2)}, u32[]{:S(2)}) collective-permute-start(f32[2,128]{1,0:T(2,128)S(1)} %pad_maximum_fusion.22), channel_id=1, source_target_pairs={{0,2},{1,3},{2,0},{3,1},{4,6},{5,7},{6,4},{7,5},{8,10},{9,11},{10,... | collective-permute-start | bytes 3080 | tf_op jit(solution)/shard_map/ppermute | solution.py:37
  27.4 5.8 %collective-permute-done.16 = f32[2,128]{1,0:T(2,128)S(1)} collective-permute-done((f32[2,128]{1,0:T(2,128)S(1)}, f32[2,128]{1,0:T(2,128)S(1)}, u32[]{:S(2)}, u32[]{:S(2)}) %collective-permute-start.16) | collective-permute-done | bytes 1056 | tf_op jit(solution)/shard_map/ppermute | solution.py:37
  34.9 3.9 %collective-permute-start.3 = (bf16[128,1024]{1,0:T(8,128)(2,1)S(1)}, bf16[128,1024]{1,0:T(8,128)(2,1)S(1)}, u32[]{:S(2)}, u32[]{:S(2)}) collective-permute-start(bf16[128,1024]{1,0:T(8,128)(2,1)S(1)} %pad_maximum_fusion.13), channel_id=1, source_target_pairs={{0,192},{64,128},{128,64},{192,0},{1,193},{65,129},{129,65},{193,1... | collective-permute-start | bytes 786440 | tf_op jit(solution)/shard_map/ppermute | solution.py:37
  39.5 1.8 collective-permute-start.7
  41.3 7.0 %collective-permute-start.8 = (bf16[2,896,128]{2,1,0:T(8,128)(2,1)S(1)}, bf16[2,896,128]{2,1,0:T(8,128)(2,1)S(1)}, u32[]{:S(2)}, u32[]{:S(2)}) collective-permute-start(bf16[2,896,128]{2,1,0:T(8,128)(2,1)S(1)} %pad_maximum_fusion.8), channel_id=1, source_target_pairs={{0,16},{8,24},{16,0},{24,8},{1,17},{9,25},{17,1},{25,9},{2,18},{10... | collective-permute-start | bytes 1376264 | tf_op jit(solution)/shard_map/ppermute | solution.py:37
  48.5 2.7 %collective-permute-start.33 = (bf16[48,1024]{1,0:T(8,128)(2,1)S(1)}, bf16[48,1024]{1,0:T(8,128)(2,1)}, u32[]{:S(2)}, u32[]{:S(2)}) collective-permute-start(bf16[48,1024]{1,0:T(8,128)(2,1)S(1)} %get-tuple-element.64), channel_id=1, source_target_pairs={{0,32},{32,0},{1,33},{33,1},{2,34},{34,2},{3,35},{35,3},{4,36},{36... | collective-permute-start | bytes 294920 | tf_op jit(solution)/shard_map/ppermute | solution.py:37
  53.4 14.5 %collective-permute-done.8 = bf16[2,896,128]{2,1,0:T(8,128)(2,1)S(1)} collective-permute-done((bf16[2,896,128]{2,1,0:T(8,128)(2,1)S(1)}, bf16[2,896,128]{2,1,0:T(8,128)(2,1)S(1)}, u32[]{:S(2)}, u32[]{:S(2)}) %collective-permute-start.8) | collective-permute-done | bytes 458784 | tf_op jit(solution)/shard_map/ppermute | solution.py:37
  67.9 5.6 %collective-permute-done.9 = bf16[2,896,128]{2,1,0:T(8,128)(2,1)} collective-permute-done((bf16[2,896,128]{2,1,0:T(8,128)(2,1)S(1)}, bf16[2,896,128]{2,1,0:T(8,128)(2,1)}, u32[]{:S(2)}, u32[]{:S(2)}) %collective-permute-start.9) | collective-permute-done | bytes 458784 | tf_op jit(solution)/shard_map/ppermute | solution.py:37
  85.4 1.9 fusion.83
  87.8 2.8 %collective-permute-start.10 = (bf16[256,896]{0,1:T(8,128)(2,1)S(1)}, bf16[256,896]{0,1:T(8,128)(2,1)S(1)}, u32[]{:S(2)}, u32[]{:S(2)}) collective-permute-start(bf16[256,896]{0,1:T(8,128)(2,1)S(1)} %get-tuple-element.5), channel_id=1, source_target_pairs={{0,64},{64,0},{128,192},{192,128},{1,65},{65,1},{129,193},{193,129... | collective-permute-start | bytes 1376264 | tf_op jit(solution)/shard_map/ppermute | solution.py:37
  90.6 2.2 %collective-permute-start.11 = (bf16[256,896]{0,1:T(8,128)(2,1)S(1)}, bf16[256,896]{0,1:T(8,128)(2,1)S(1)}, u32[]{:S(2)}, u32[]{:S(2)}) collective-permute-start(bf16[256,896]{0,1:T(8,128)(2,1)S(1)} %get-tuple-element.7), channel_id=1, source_target_pairs={{0,128},{64,192},{128,0},{192,64},{1,129},{65,193},{129,1},{193,65... | collective-permute-start | bytes 1376264 | tf_op jit(solution)/shard_map/ppermute | solution.py:37
  93.4 6.0 %collective-permute-start.25 = (bf16[48,1024]{1,0:T(8,128)(2,1)S(1)}, bf16[48,1024]{1,0:T(8,128)(2,1)S(1)}, u32[]{:S(2)}, u32[]{:S(2)}) collective-permute-start(bf16[48,1024]{1,0:T(8,128)(2,1)S(1)} %copy-done.3), channel_id=1, source_target_pairs={{0,32},{1,33},{2,34},{3,35},{4,36},{5,37},{6,38},{7,39},{8,96},{9,... | collective-permute-start | bytes 294920 | tf_op jit(solution)/shard_map/ppermute | solution.py:41
  99.4 6.2 %collective-permute-start.26 = (bf16[48,1024]{1,0:T(8,128)(2,1)S(1)}, bf16[48,1024]{1,0:T(8,128)(2,1)S(1)}, u32[]{:S(2)}, u32[]{:S(2)}) collective-permute-start(bf16[48,1024]{1,0:T(8,128)(2,1)S(1)} %copy-done.3), channel_id=1, source_target_pairs={{0,0},{1,1},{2,2},{3,3},{4,4},{5,5},{6,6},{7,7},{8,64},{9,65},{10,... | collective-permute-start | bytes 294920 | tf_op jit(solution)/shard_map/ppermute | solution.py:41
  106.5 2.0 collective-permute-start.34
  108.5 7.7 %collective-permute-done.11 = bf16[256,896]{0,1:T(8,128)(2,1)S(1)} collective-permute-done((bf16[256,896]{0,1:T(8,128)(2,1)S(1)}, bf16[256,896]{0,1:T(8,128)(2,1)S(1)}, u32[]{:S(2)}, u32[]{:S(2)}) %collective-permute-start.11) | collective-permute-done | bytes 458784 | tf_op jit(solution)/shard_map/ppermute | solution.py:37
  116.2 3.0 %collective-permute-done.12 = bf16[256,896]{0,1:T(8,128)(2,1)S(1)} collective-permute-done((bf16[256,896]{0,1:T(8,128)(2,1)S(1)}, bf16[256,896]{0,1:T(8,128)(2,1)S(1)}, u32[]{:S(2)}, u32[]{:S(2)}) %collective-permute-start.12) | collective-permute-done | bytes 458784 | tf_op jit(solution)/shard_map/ppermute | solution.py:37
  122.5 3.3 %collective-permute-start.14 = (bf16[128,512]{0,1:T(8,128)(2,1)S(1)}, bf16[128,512]{0,1:T(8,128)(2,1)S(1)}, u32[]{:S(2)}, u32[]{:S(2)}) collective-permute-start(bf16[128,512]{0,1:T(8,128)(2,1)S(1)} %pad_maximum_fusion.19), channel_id=1, source_target_pairs={{0,2},{1,3},{2,0},{3,1},{4,6},{5,7},{6,4},{7,5},{8,10},{9,11},{10,... | collective-permute-start | bytes 393224 | tf_op jit(solution)/shard_map/ppermute | solution.py:37
  127.8 6.8 %collective-permute-done.14 = bf16[128,512]{0,1:T(8,128)(2,1)S(1)} collective-permute-done((bf16[128,512]{0,1:T(8,128)(2,1)S(1)}, bf16[128,512]{0,1:T(8,128)(2,1)S(1)}, u32[]{:S(2)}, u32[]{:S(2)}) %collective-permute-start.14) | collective-permute-done | bytes 131104 | tf_op jit(solution)/shard_map/ppermute | solution.py:37
  134.6 4.2 %collective-permute-start.27 = (bf16[2,48,1024]{2,1,0:T(8,128)(2,1)S(1)}, bf16[2,48,1024]{2,1,0:T(8,128)(2,1)S(1)}, u32[]{:S(2)}, u32[]{:S(2)}) collective-permute-start(bf16[2,48,1024]{2,1,0:T(8,128)(2,1)S(1)} %pad_maximum_fusion.16), channel_id=1, source_target_pairs={{0,192},{64,128},{128,64},{192,0},{1,193},{65,129},{129,65},{193,1... | collective-permute-start | bytes 589832 | tf_op jit(solution)/shard_map/ppermute | solution.py:37
  142.0 3.2 %collective-permute-start.22 = (bf16[128,384]{1,0:T(8,128)(2,1)S(1)}, bf16[128,384]{1,0:T(8,128)(2,1)S(1)}, u32[]{:S(2)}, u32[]{:S(2)}) collective-permute-start(bf16[128,384]{1,0:T(8,128)(2,1)S(1)} %copy.69), channel_id=1, source_target_pairs={{0,2},{1,3},{2,0},{3,1},{4,6},{5,7},{6,4},{7,5},{8,10},{9,11},{10,... | collective-permute-start | bytes 294920 | tf_op jit(solution)/shard_map/ppermute | solution.py:37
  146.7 6.4 %collective-permute-done.22 = bf16[128,384]{1,0:T(8,128)(2,1)S(1)} collective-permute-done((bf16[128,384]{1,0:T(8,128)(2,1)S(1)}, bf16[128,384]{1,0:T(8,128)(2,1)S(1)}, u32[]{:S(2)}, u32[]{:S(2)}) %collective-permute-start.22) | collective-permute-done | bytes 98336 | tf_op jit(solution)/shard_map/ppermute | solution.py:37
  153.1 4.6 %collective-permute-done.21 = bf16[128,384]{1,0:T(8,128)(2,1)S(1)} collective-permute-done((bf16[128,384]{1,0:T(8,128)(2,1)S(1)}, bf16[128,384]{1,0:T(8,128)(2,1)S(1)}, u32[]{:S(2)}, u32[]{:S(2)}) %collective-permute-start.21) | collective-permute-done | bytes 98336 | tf_op jit(solution)/shard_map/ppermute | solution.py:37
  158.7 2.1 %collective-permute-start.39 = (bf16[384,1024]{1,0:T(8,128)(2,1)S(1)}, bf16[384,1024]{1,0:T(8,128)(2,1)S(1)}, u32[]{:S(2)}, u32[]{:S(2)}) collective-permute-start(bf16[384,1024]{1,0:T(8,128)(2,1)S(1)} %bitcast.145), channel_id=1, source_target_pairs={{0,192},{64,128},{128,64},{192,0},{1,193},{65,129},{129,65},{193,1... | collective-permute-start | bytes 2359304 | tf_op jit(solution)/shard_map/ppermute | solution.py:37
  162.7 2.4 %collective-permute-start.32 = (bf16[384,1024]{1,0:T(8,128)(2,1)S(1)}, bf16[384,1024]{1,0:T(8,128)(2,1)S(1)}, u32[]{:S(2)}, u32[]{:S(2)}) collective-permute-start(bf16[384,1024]{1,0:T(8,128)(2,1)S(1)} %bitcast.149), channel_id=1, source_target_pairs={{0,24},{8,16},{16,8},{24,0},{1,25},{9,17},{17,9},{25,1},{2,26},{10... | collective-permute-start | bytes 2359304 | tf_op jit(solution)/shard_map/ppermute | solution.py:37
  165.7 12.9 %collective-permute-done.37 = bf16[384,1024]{1,0:T(8,128)(2,1)S(1)} collective-permute-done((bf16[384,1024]{1,0:T(8,128)(2,1)S(1)}, bf16[384,1024]{1,0:T(8,128)(2,1)S(1)}, u32[]{:S(2)}, u32[]{:S(2)}) %collective-permute-start.37) | collective-permute-done | bytes 786464 | tf_op jit(solution)/shard_map/ppermute | solution.py:37
  178.6 1.8 collective-permute-start.31
  181.3 15.1 %collective-permute-done.39 = bf16[384,1024]{1,0:T(8,128)(2,1)S(1)} collective-permute-done((bf16[384,1024]{1,0:T(8,128)(2,1)S(1)}, bf16[384,1024]{1,0:T(8,128)(2,1)S(1)}, u32[]{:S(2)}, u32[]{:S(2)}) %collective-permute-start.39) | collective-permute-done | bytes 786464 | tf_op jit(solution)/shard_map/ppermute | solution.py:37
  196.8 3.2 %collective-permute-done.32 = bf16[384,1024]{1,0:T(8,128)(2,1)S(1)} collective-permute-done((bf16[384,1024]{1,0:T(8,128)(2,1)S(1)}, bf16[384,1024]{1,0:T(8,128)(2,1)S(1)}, u32[]{:S(2)}, u32[]{:S(2)}) %collective-permute-start.32) | collective-permute-done | bytes 786464 | tf_op jit(solution)/shard_map/ppermute | solution.py:37
  202.0 1.9 collective-permute-done.40
  (176 shorter events, 48.7 us)
Async XLA Ops:
  7.1 32.4 %collective-permute-start.5 = (bf16[896,128]{1,0:T(8,128)(2,1)}, bf16[896,128]{1,0:T(8,128)(2,1)S(1)}, u32[]{:S(2)}, u32[]{:S(2)}) collective-permute-start(bf16[896,128]{1,0:T(8,128)(2,1)} %constant_dynamic-update-slice_fusion), channel_id=1, source_target_pairs={{0,0},{1,8},{2,4},{3,12},{4,16},{5,24},{6,20},{7,28},{8,64},{9,72}... | collective-permute-start | bytes 688136 | tf_op jit(solution)/shard_map/ppermute | solution.py:41
  13.6 25.8 %collective-permute-start.6 = (bf16[896,128]{1,0:T(8,128)(2,1)}, bf16[896,128]{1,0:T(8,128)(2,1)S(1)}, u32[]{:S(2)}, u32[]{:S(2)}) collective-permute-start(bf16[896,128]{1,0:T(8,128)(2,1)} %constant_dynamic-update-slice_fusion), channel_id=1, source_target_pairs={{0,32},{1,40},{2,36},{3,44},{4,48},{5,56},{6,52},{7,60},{8,96},{9,... | collective-permute-start | bytes 688136 | tf_op jit(solution)/shard_map/ppermute | solution.py:41
  21.7 11.4 %collective-permute-start.16 = (f32[2,128]{1,0:T(2,128)S(1)}, f32[2,128]{1,0:T(2,128)S(1)}, u32[]{:S(2)}, u32[]{:S(2)}) collective-permute-start(f32[2,128]{1,0:T(2,128)S(1)} %pad_maximum_fusion.22), channel_id=1, source_target_pairs={{0,1},{1,0},{2,3},{3,2},{4,5},{5,4},{6,7},{7,6},{8,9},{9,8},{10,11... | collective-permute-start | bytes 3080 | tf_op jit(solution)/shard_map/ppermute | solution.py:37
  22.9 11.1 %collective-permute-start.17 = (f32[2,128]{1,0:T(2,128)S(1)}, f32[2,128]{1,0:T(2,128)S(1)}, u32[]{:S(2)}, u32[]{:S(2)}) collective-permute-start(f32[2,128]{1,0:T(2,128)S(1)} %pad_maximum_fusion.22), channel_id=1, source_target_pairs={{0,2},{1,3},{2,0},{3,1},{4,6},{5,7},{6,4},{7,5},{8,10},{9,11},{10,... | collective-permute-start | bytes 3080 | tf_op jit(solution)/shard_map/ppermute | solution.py:37
  33.9 14.5 %collective-permute-start.1 = (bf16[128,1024]{1,0:T(8,128)(2,1)S(1)}, bf16[128,1024]{1,0:T(8,128)(2,1)S(1)}, u32[]{:S(2)}, u32[]{:S(2)}) collective-permute-start(bf16[128,1024]{1,0:T(8,128)(2,1)S(1)} %pad_maximum_fusion.11), channel_id=1, source_target_pairs={{0,64},{64,0},{128,192},{192,128},{1,65},{65,1},{129,193},{193,129... | collective-permute-start | bytes 786440 | tf_op jit(solution)/shard_map/ppermute | solution.py:37
  34.0 17.3 %collective-permute-start.2 = (bf16[128,1024]{1,0:T(8,128)(2,1)S(1)}, bf16[128,1024]{1,0:T(8,128)(2,1)S(1)}, u32[]{:S(2)}, u32[]{:S(2)}) collective-permute-start(bf16[128,1024]{1,0:T(8,128)(2,1)S(1)} %pad_maximum_fusion.12), channel_id=1, source_target_pairs={{0,128},{64,192},{128,0},{192,64},{1,129},{65,193},{129,1},{193,65... | collective-permute-start | bytes 786440 | tf_op jit(solution)/shard_map/ppermute | solution.py:37
  34.9 18.0 %collective-permute-start.3 = (bf16[128,1024]{1,0:T(8,128)(2,1)S(1)}, bf16[128,1024]{1,0:T(8,128)(2,1)S(1)}, u32[]{:S(2)}, u32[]{:S(2)}) collective-permute-start(bf16[128,1024]{1,0:T(8,128)(2,1)S(1)} %pad_maximum_fusion.13), channel_id=1, source_target_pairs={{0,192},{64,128},{128,64},{192,0},{1,193},{65,129},{129,65},{193,1... | collective-permute-start | bytes 786440 | tf_op jit(solution)/shard_map/ppermute | solution.py:37
  39.5 13.8 %collective-permute-start.7 = (bf16[2,896,128]{2,1,0:T(8,128)(2,1)S(1)}, bf16[2,896,128]{2,1,0:T(8,128)(2,1)S(1)}, u32[]{:S(2)}, u32[]{:S(2)}) collective-permute-start(bf16[2,896,128]{2,1,0:T(8,128)(2,1)S(1)} %pad_maximum_fusion.8), channel_id=1, source_target_pairs={{0,8},{8,0},{16,24},{24,16},{1,9},{9,1},{17,25},{25,17},{2,10},{10... | collective-permute-start | bytes 1376264 | tf_op jit(solution)/shard_map/ppermute | solution.py:37
  41.3 26.5 %collective-permute-start.8 = (bf16[2,896,128]{2,1,0:T(8,128)(2,1)S(1)}, bf16[2,896,128]{2,1,0:T(8,128)(2,1)S(1)}, u32[]{:S(2)}, u32[]{:S(2)}) collective-permute-start(bf16[2,896,128]{2,1,0:T(8,128)(2,1)S(1)} %pad_maximum_fusion.8), channel_id=1, source_target_pairs={{0,16},{8,24},{16,0},{24,8},{1,17},{9,25},{17,1},{25,9},{2,18},{10... | collective-permute-start | bytes 1376264 | tf_op jit(solution)/shard_map/ppermute | solution.py:37
  48.5 50.9 %collective-permute-start.33 = (bf16[48,1024]{1,0:T(8,128)(2,1)S(1)}, bf16[48,1024]{1,0:T(8,128)(2,1)}, u32[]{:S(2)}, u32[]{:S(2)}) collective-permute-start(bf16[48,1024]{1,0:T(8,128)(2,1)S(1)} %get-tuple-element.64), channel_id=1, source_target_pairs={{0,32},{32,0},{1,33},{33,1},{2,34},{34,2},{3,35},{35,3},{4,36},{36... | collective-permute-start | bytes 294920 | tf_op jit(solution)/shard_map/ppermute | solution.py:37
  51.2 22.3 %collective-permute-start.9 = (bf16[2,896,128]{2,1,0:T(8,128)(2,1)S(1)}, bf16[2,896,128]{2,1,0:T(8,128)(2,1)}, u32[]{:S(2)}, u32[]{:S(2)}) collective-permute-start(bf16[2,896,128]{2,1,0:T(8,128)(2,1)S(1)} %pad_maximum_fusion.8), channel_id=1, source_target_pairs={{0,24},{8,16},{16,8},{24,0},{1,25},{9,17},{17,9},{25,1},{2,26},{10... | collective-permute-start | bytes 1376264 | tf_op jit(solution)/shard_map/ppermute | solution.py:37
  53.1 30.1 %collective-permute-start.4 = (bf16[4,128,1024]{2,1,0:T(8,128)(2,1)S(1)}, bf16[4,128,1024]{2,1,0:T(8,128)(2,1)}, u32[]{:S(2)}, u32[]{:S(2)}) collective-permute-start(bf16[4,128,1024]{2,1,0:T(8,128)(2,1)S(1)} %get-tuple-element.13), channel_id=1, source_target_pairs={{0,4},{4,0},{1,5},{5,1},{2,6},{6,2},{3,7},{7,3},{8,12},{12,8},{9,1... | collective-permute-start | bytes 3145736 | tf_op jit(solution)/shard_map/ppermute | solution.py:37
  87.8 18.7 %collective-permute-start.10 = (bf16[256,896]{0,1:T(8,128)(2,1)S(1)}, bf16[256,896]{0,1:T(8,128)(2,1)S(1)}, u32[]{:S(2)}, u32[]{:S(2)}) collective-permute-start(bf16[256,896]{0,1:T(8,128)(2,1)S(1)} %get-tuple-element.5), channel_id=1, source_target_pairs={{0,64},{64,0},{128,192},{192,128},{1,65},{65,1},{129,193},{193,129... | collective-permute-start | bytes 1376264 | tf_op jit(solution)/shard_map/ppermute | solution.py:37
  90.6 25.6 %collective-permute-start.11 = (bf16[256,896]{0,1:T(8,128)(2,1)S(1)}, bf16[256,896]{0,1:T(8,128)(2,1)S(1)}, u32[]{:S(2)}, u32[]{:S(2)}) collective-permute-start(bf16[256,896]{0,1:T(8,128)(2,1)S(1)} %get-tuple-element.7), channel_id=1, source_target_pairs={{0,128},{64,192},{128,0},{192,64},{1,129},{65,193},{129,1},{193,65... | collective-permute-start | bytes 1376264 | tf_op jit(solution)/shard_map/ppermute | solution.py:37
  92.8 26.4 %collective-permute-start.12 = (bf16[256,896]{0,1:T(8,128)(2,1)S(1)}, bf16[256,896]{0,1:T(8,128)(2,1)S(1)}, u32[]{:S(2)}, u32[]{:S(2)}) collective-permute-start(bf16[256,896]{0,1:T(8,128)(2,1)S(1)} %get-tuple-element.6), channel_id=1, source_target_pairs={{0,192},{64,128},{128,64},{192,0},{1,193},{65,129},{129,65},{193,1... | collective-permute-start | bytes 1376264 | tf_op jit(solution)/shard_map/ppermute | solution.py:37
  93.4 29.1 %collective-permute-start.25 = (bf16[48,1024]{1,0:T(8,128)(2,1)S(1)}, bf16[48,1024]{1,0:T(8,128)(2,1)S(1)}, u32[]{:S(2)}, u32[]{:S(2)}) collective-permute-start(bf16[48,1024]{1,0:T(8,128)(2,1)S(1)} %copy-done.3), channel_id=1, source_target_pairs={{0,32},{1,33},{2,34},{3,35},{4,36},{5,37},{6,38},{7,39},{8,96},{9,... | collective-permute-start | bytes 294920 | tf_op jit(solution)/shard_map/ppermute | solution.py:41
  99.4 26.5 %collective-permute-start.26 = (bf16[48,1024]{1,0:T(8,128)(2,1)S(1)}, bf16[48,1024]{1,0:T(8,128)(2,1)S(1)}, u32[]{:S(2)}, u32[]{:S(2)}) collective-permute-start(bf16[48,1024]{1,0:T(8,128)(2,1)S(1)} %copy-done.3), channel_id=1, source_target_pairs={{0,0},{1,1},{2,2},{3,3},{4,4},{5,5},{6,6},{7,7},{8,64},{9,65},{10,... | collective-permute-start | bytes 294920 | tf_op jit(solution)/shard_map/ppermute | solution.py:41
  106.5 35.4 %collective-permute-start.34 = (bf16[2,48,1024]{2,1,0:T(8,128)(2,1)S(1)}, bf16[2,48,1024]{2,1,0:T(8,128)(2,1)S(1)}, u32[]{:S(2)}, u32[]{:S(2)}) collective-permute-start(bf16[2,48,1024]{2,1,0:T(8,128)(2,1)S(1)} %pad_maximum_fusion.17), channel_id=1, source_target_pairs={{0,24},{8,16},{16,8},{24,0},{1,25},{9,17},{17,9},{25,1},{2,26},{10... | collective-permute-start | bytes 589832 | tf_op jit(solution)/shard_map/ppermute | solution.py:37
  116.2 25.9 %collective-permute-start.35 = (bf16[2,48,1024]{2,1,0:T(8,128)(2,1)S(1)}, bf16[2,48,1024]{2,1,0:T(8,128)(2,1)S(1)}, u32[]{:S(2)}, u32[]{:S(2)}) collective-permute-start(bf16[2,48,1024]{2,1,0:T(8,128)(2,1)S(1)} %pad_maximum_fusion.17), channel_id=1, source_target_pairs={{0,16},{8,24},{16,0},{24,8},{1,17},{9,25},{17,1},{25,9},{2,18},{10... | collective-permute-start | bytes 589832 | tf_op jit(solution)/shard_map/ppermute | solution.py:37
  122.5 12.1 %collective-permute-start.14 = (bf16[128,512]{0,1:T(8,128)(2,1)S(1)}, bf16[128,512]{0,1:T(8,128)(2,1)S(1)}, u32[]{:S(2)}, u32[]{:S(2)}) collective-permute-start(bf16[128,512]{0,1:T(8,128)(2,1)S(1)} %pad_maximum_fusion.19), channel_id=1, source_target_pairs={{0,2},{1,3},{2,0},{3,1},{4,6},{5,7},{6,4},{7,5},{8,10},{9,11},{10,... | collective-permute-start | bytes 393224 | tf_op jit(solution)/shard_map/ppermute | solution.py:37
  125.8 12.9 %collective-permute-start.15 = (bf16[128,512]{0,1:T(8,128)(2,1)S(1)}, bf16[128,512]{0,1:T(8,128)(2,1)S(1)}, u32[]{:S(2)}, u32[]{:S(2)}) collective-permute-start(bf16[128,512]{0,1:T(8,128)(2,1)S(1)} %pad_maximum_fusion.20), channel_id=1, source_target_pairs={{0,3},{1,2},{2,1},{3,0},{4,7},{5,6},{6,5},{7,4},{8,11},{9,10},{10,... | collective-permute-start | bytes 393224 | tf_op jit(solution)/shard_map/ppermute | solution.py:37
  127.7 17.6 %collective-permute-start.36 = (bf16[2,48,1024]{2,1,0:T(8,128)(2,1)S(1)}, bf16[2,48,1024]{2,1,0:T(8,128)(2,1)S(1)}, u32[]{:S(2)}, u32[]{:S(2)}) collective-permute-start(bf16[2,48,1024]{2,1,0:T(8,128)(2,1)S(1)} %pad_maximum_fusion.17), channel_id=1, source_target_pairs={{0,8},{8,0},{16,24},{24,16},{1,9},{9,1},{17,25},{25,17},{2,10},{10... | collective-permute-start | bytes 589832 | tf_op jit(solution)/shard_map/ppermute | solution.py:37
  134.6 24.1 %collective-permute-start.27 = (bf16[2,48,1024]{2,1,0:T(8,128)(2,1)S(1)}, bf16[2,48,1024]{2,1,0:T(8,128)(2,1)S(1)}, u32[]{:S(2)}, u32[]{:S(2)}) collective-permute-start(bf16[2,48,1024]{2,1,0:T(8,128)(2,1)S(1)} %pad_maximum_fusion.16), channel_id=1, source_target_pairs={{0,192},{64,128},{128,64},{192,0},{1,193},{65,129},{129,65},{193,1... | collective-permute-start | bytes 589832 | tf_op jit(solution)/shard_map/ppermute | solution.py:37
  140.2 20.6 %collective-permute-start.28 = (bf16[2,48,1024]{2,1,0:T(8,128)(2,1)S(1)}, bf16[2,48,1024]{2,1,0:T(8,128)(2,1)S(1)}, u32[]{:S(2)}, u32[]{:S(2)}) collective-permute-start(bf16[2,48,1024]{2,1,0:T(8,128)(2,1)S(1)} %pad_maximum_fusion.16), channel_id=1, source_target_pairs={{0,128},{64,192},{128,0},{192,64},{1,129},{65,193},{129,1},{193,65... | collective-permute-start | bytes 589832 | tf_op jit(solution)/shard_map/ppermute | solution.py:37
  141.9 20.5 %collective-permute-start.29 = (bf16[2,48,1024]{2,1,0:T(8,128)(2,1)S(1)}, bf16[2,48,1024]{2,1,0:T(8,128)(2,1)S(1)}, u32[]{:S(2)}, u32[]{:S(2)}) collective-permute-start(bf16[2,48,1024]{2,1,0:T(8,128)(2,1)S(1)} %pad_maximum_fusion.16), channel_id=1, source_target_pairs={{0,64},{64,0},{128,192},{192,128},{1,65},{65,1},{129,193},{193,129... | collective-permute-start | bytes 589832 | tf_op jit(solution)/shard_map/ppermute | solution.py:37
  142.0 11.1 %collective-permute-start.22 = (bf16[128,384]{1,0:T(8,128)(2,1)S(1)}, bf16[128,384]{1,0:T(8,128)(2,1)S(1)}, u32[]{:S(2)}, u32[]{:S(2)}) collective-permute-start(bf16[128,384]{1,0:T(8,128)(2,1)S(1)} %copy.69), channel_id=1, source_target_pairs={{0,2},{1,3},{2,0},{3,1},{4,6},{5,7},{6,4},{7,5},{8,10},{9,11},{10,... | collective-permute-start | bytes 294920 | tf_op jit(solution)/shard_map/ppermute | solution.py:37
  158.2 20.4 %collective-permute-start.37 = (bf16[384,1024]{1,0:T(8,128)(2,1)S(1)}, bf16[384,1024]{1,0:T(8,128)(2,1)S(1)}, u32[]{:S(2)}, u32[]{:S(2)}) collective-permute-start(bf16[384,1024]{1,0:T(8,128)(2,1)S(1)} %bitcast.144), channel_id=1, source_target_pairs={{0,64},{64,0},{128,192},{192,128},{1,65},{65,1},{129,193},{193,129... | collective-permute-start | bytes 2359304 | tf_op jit(solution)/shard_map/ppermute | solution.py:37
  158.7 37.7 %collective-permute-start.39 = (bf16[384,1024]{1,0:T(8,128)(2,1)S(1)}, bf16[384,1024]{1,0:T(8,128)(2,1)S(1)}, u32[]{:S(2)}, u32[]{:S(2)}) collective-permute-start(bf16[384,1024]{1,0:T(8,128)(2,1)S(1)} %bitcast.145), channel_id=1, source_target_pairs={{0,192},{64,128},{128,64},{192,0},{1,193},{65,129},{129,65},{193,1... | collective-permute-start | bytes 2359304 | tf_op jit(solution)/shard_map/ppermute | solution.py:37
  160.8 40.1 %collective-permute-start.38 = (bf16[384,1024]{1,0:T(8,128)(2,1)S(1)}, bf16[384,1024]{1,0:T(8,128)(2,1)S(1)}, u32[]{:S(2)}, u32[]{:S(2)}) collective-permute-start(bf16[384,1024]{1,0:T(8,128)(2,1)S(1)} %bitcast.146), channel_id=1, source_target_pairs={{0,128},{64,192},{128,0},{192,64},{1,129},{65,193},{129,1},{193,65... | collective-permute-start | bytes 2359304 | tf_op jit(solution)/shard_map/ppermute | solution.py:37
  162.6 37.8 %collective-permute-start.30 = (bf16[384,1024]{1,0:T(8,128)(2,1)S(1)}, bf16[384,1024]{1,0:T(8,128)(2,1)S(1)}, u32[]{:S(2)}, u32[]{:S(2)}) collective-permute-start(bf16[384,1024]{1,0:T(8,128)(2,1)S(1)} %bitcast.148), channel_id=1, source_target_pairs={{0,8},{8,0},{16,24},{24,16},{1,9},{9,1},{17,25},{25,17},{2,10},{10... | collective-permute-start | bytes 2359304 | tf_op jit(solution)/shard_map/ppermute | solution.py:37
  162.7 37.2 %collective-permute-start.32 = (bf16[384,1024]{1,0:T(8,128)(2,1)S(1)}, bf16[384,1024]{1,0:T(8,128)(2,1)S(1)}, u32[]{:S(2)}, u32[]{:S(2)}) collective-permute-start(bf16[384,1024]{1,0:T(8,128)(2,1)S(1)} %bitcast.149), channel_id=1, source_target_pairs={{0,24},{8,16},{16,8},{24,0},{1,25},{9,17},{17,9},{25,1},{2,26},{10... | collective-permute-start | bytes 2359304 | tf_op jit(solution)/shard_map/ppermute | solution.py:37
  178.6 22.8 %collective-permute-start.31 = (bf16[384,1024]{1,0:T(8,128)(2,1)S(1)}, bf16[384,1024]{1,0:T(8,128)(2,1)S(1)}, u32[]{:S(2)}, u32[]{:S(2)}) collective-permute-start(bf16[384,1024]{1,0:T(8,128)(2,1)S(1)} %bitcast.150), channel_id=1, source_target_pairs={{0,16},{8,24},{16,0},{24,8},{1,17},{9,25},{17,1},{25,9},{2,18},{10... | collective-permute-start | bytes 2359304 | tf_op jit(solution)/shard_map/ppermute | solution.py:37
  (17 other events, 150.0 us)

commit v2 on v1

v2 whole, which is shorter than its diff:
```python
import math

import jax
import jax.numpy as jnp
import numpy as np
from jax import lax
from jax.experimental import pallas as pl
from jax.experimental.pallas import tpu as pltpu
from jax.sharding import Mesh
from jax.sharding import PartitionSpec as P

AXES = ("y", "zh", "x", "core", "zl")
SIZES = (4, 2, 4, 2, 4)
D = 16384
HD = 128
ROWS = 128
BF = jnp.bfloat16
F32 = jnp.float32


def flat(*coords):
    index = 0
    for size, coord in zip(SIZES, coords):
        index = index * size + coord
    return index


def every():
    for y in range(4):
        for zh in range(2):
            for x in range(4):
                for c in range(2):
                    for t in range(4):
                        yield y, zh, x, c, t


def swap(value, axis, d):
    n = SIZES[AXES.index(axis)]
    return lax.ppermute(value, axis, [(i, i ^ d) for i in range(n)])


def move(value, where):
    return lax.ppermute(value, AXES, [(flat(*at), flat(*where(*at))) for at in every()])


def tables():
    freqs = np.exp(np.arange(HD // 2, dtype=np.float32) * np.float32(-2.0 * math.log(500000.0) / HD))
    angle = np.arange(ROWS, dtype=np.float32)[:, None] * freqs.astype(np.float32)[None, :]
    cosine = np.repeat(np.cos(angle), 2, axis=1).astype(np.float32)
    sine = np.repeat(np.sin(angle), 2, axis=1).astype(np.float32)
    sine[:, 0::2] *= -1.0
    return cosine, sine


COSINE, SINE = tables()


def rotate(values, cosine, sine):
    shape = (values.shape[0],) + (1,) * (values.ndim - 2) + (HD,)
    even = jnp.arange(HD) % 2 == 0
    partner = jnp.where(even, jnp.roll(values, -1, axis=-1), jnp.roll(values, 1, axis=-1))
    return values * cosine.reshape(shape) + partner * sine.reshape(shape)


def pick(flag, first, second):
    return jnp.where(flag, second, first)


def by_index(parts, at):
    odd = (at & 1) == 1
    high = (at >> 1) == 1
    a, b = pick(odd, parts[0], parts[1]), pick(odd, parts[1], parts[0])
    c, d = pick(odd, parts[2], parts[3]), pick(odd, parts[3], parts[2])
    return [pick(high, a, c), pick(high, b, d), pick(high, c, a), pick(high, d, b)]


def whole(shape):
    return pl.BlockSpec(memory_space=pltpu.VMEM)


def pack_kernel(q_ref, kv_ref, out_ref):
    for h in range(3):
        out_ref[256 * h : 256 * h + 256, :] = q_ref[:, 128 * h : 128 * h + 128]
    for h in range(2):
        out_ref[768 + 64 * h : 832 + 64 * h, :] = kv_ref[:, 128 * h : 128 * h + 128]


def pack(query_weight, kv_turned):
    return pl.pallas_call(
        pack_kernel,
        out_shape=jax.ShapeDtypeStruct((896, 128), BF),
        in_specs=[whole(0)] * 2,
        out_specs=whole(0),
        compiler_params=pltpu.CompilerParams(vmem_limit_bytes=32 * 2**20),
        cost_estimate=pl.CostEstimate(flops=0, bytes_accessed=460000, transcendentals=0),
    )(query_weight, kv_turned)


def project_kernel(x_ref, a0, b0, a1, b1, out_ref, own_ref):
    q_columns = []
    kv_rows = []
    for pair in ((a0, b0), (a1, b1)):
        for h in range(3):
            q_columns.append(
                jnp.concatenate([ref[a, 256 * h : 256 * h + 256, :] for ref in pair for a in (0, 1)], axis=0)
            )
        kv_rows.append(
            jnp.concatenate(
                [ref[a, 768 + 64 * h : 832 + 64 * h, :] for ref in pair for a in (0, 1) for h in (0, 1)], axis=1
            )
        )
    inputs = x_ref[...]
    q = jnp.dot(inputs, jnp.concatenate(q_columns, axis=1), preferred_element_type=F32)
    kv = lax.dot_general(
        inputs, jnp.concatenate(kv_rows, axis=0), (((1,), (1,)), ((), ())), preferred_element_type=F32
    )
    own_ref[:, :768] = q[:ROWS]
    own_ref[:, 768:] = kv[:ROWS]
    for e in (1, 2, 3):
        out_ref[e - 1, :, :768] = q[ROWS * e : ROWS * e + ROWS].astype(BF)
        out_ref[e - 1, :, 768:] = kv[ROWS * e : ROWS * e + ROWS].astype(BF)


def project(inputs, first, second):
    return pl.pallas_call(
        project_kernel,
        out_shape=(jax.ShapeDtypeStruct((3, ROWS, 896), BF), jax.ShapeDtypeStruct((ROWS, 896), F32)),
        in_specs=[whole(0)] * 5,
        out_specs=(whole(0),) * 2,
        compiler_params=pltpu.CompilerParams(vmem_limit_bytes=32 * 2**20),
        cost_estimate=pl.CostEstimate(flops=2 * 512 * 1024 * 896, bytes_accessed=4000000, transcendentals=0),
    )(inputs, *first, *second)


def attend(query, keys, values, limit, first):
    scores = jnp.einsum("qhd,kd->hqk", query, keys, preferred_element_type=F32) * HD ** (-0.5)
    keys_at = jnp.arange(ROWS, dtype=jnp.int32)
    rows_at = first + jnp.arange(32, dtype=jnp.int32)
    valid = (keys_at[None, :] <= rows_at[:, None]) & (keys_at[None, :] < limit)
    scores = jnp.where(valid[None], scores, -jnp.inf)
    raised = jnp.exp(scores - jnp.max(scores, axis=-1, keepdims=True))
    weights = (raised / jnp.sum(raised, axis=-1, keepdims=True)).astype(BF)
    output = jnp.einsum("hqk,kd->qhd", weights, values, preferred_element_type=F32)
    return jnp.where((rows_at < limit)[:, None, None], output, 0.0).astype(BF)


def body(tokens, norm_gain, query_weight, kv_weight, out_weight, lengths):
    y, zh, x, c, t = (lax.axis_index(name) for name in AXES)

    packed = pack(query_weight, kv_weight.T)
    near = move(packed, lambda y, zh, x, c, t: (x ^ y, zh, t, c, y))
    far = move(packed, lambda y, zh, x, c, t: (x ^ y, zh ^ 1, t, c, y))
    mine = jnp.stack([near, far])
    blocks = [mine] + [swap(mine, "x", d) for d in (1, 2, 3)]
    pairs = [(block, swap(block, "core", 1)) for block in blocks]

    wo_near = move(out_weight, lambda y, zh, x, c, t: (y, c, 2 * zh + (x >> 1), x & 1, t))
    wo_far = move(out_weight, lambda y, zh, x, c, t: (y, 1 - c, 2 * zh + (x >> 1), x & 1, t))
    wo_piece = jnp.concatenate([pick(zh == 1, wo_near, wo_far), pick(zh == 1, wo_far, wo_near)], axis=0)
    wo = lax.all_gather(wo_piece, ("y", "x", "core"), axis=0, tiled=True)

    widened = tokens.astype(F32)
    squares = jnp.sum(widened * widened, axis=1)
    gained = (widened * norm_gain[None, :]).astype(BF)

    def features(d):
        s = y ^ d ^ t
        picked = [
            lax.dynamic_slice(gained, (0, (((zh ^ a) * 4 + s) * 2 + (c ^ b)) * 256), (ROWS, 256))
            for b in (0, 1)
            for a in (0, 1)
        ]
        return jnp.concatenate(picked, axis=1)

    inputs = jnp.concatenate([features(0)] + [swap(features(d), "y", d) for d in (1, 2, 3)], axis=0)

    squares, _ = lax.optimization_barrier((squares, inputs))
    total = squares
    for d in (1, 2, 3):
        total = total + swap(squares, "zl", d)
    scales = lax.rsqrt(total / D + 1e-05)

    q_sums, kv_sums = [], []
    for first, second in ((0, 1), (2, 3)):
        sent, summed = project(inputs, pairs[first], pairs[second])
        for d in (1, 2, 3):
            summed = summed + swap(sent[d - 1], "y", d).astype(F32)
        q_sums.append(summed[:, :768])
        kv_sums.append(summed[:, 768:])
    q_sum = jnp.concatenate(q_sums, axis=1)
    kv_sum = jnp.concatenate(kv_sums, axis=1)

    kv_short = kv_sum.astype(BF)
    kv_flat = jnp.concatenate([kv_short[32 * r : 32 * r + 32] for r in range(4)], axis=1)

    def rows_for(d):
        return lax.dynamic_slice(q_sum, ((t ^ d) * 32, 0), (32, 1536))

    q_raw, kv_raw = rows_for(0), kv_sum
    for d in (1, 2, 3):
        came = swap(jnp.concatenate([rows_for(d).astype(BF), kv_flat], axis=1), "zl", d).astype(F32)
        q_raw = q_raw + came[:, :1536]
        kv_raw = kv_raw + jnp.concatenate([came[:, 1536 + 256 * r : 1792 + 256 * r] for r in range(4)], axis=0)

    limit = lengths[0]
    kv = (kv_raw * scales[:, None]).astype(BF)
    kv = by_index([kv[:, 64 * d : 64 * d + 64] for d in range(4)], x)
    keys = rotate(jnp.concatenate(kv[:2], axis=1).astype(F32), COSINE, SINE).astype(BF)
    values = jnp.concatenate(kv[2:], axis=1)
    mine_rows = [lax.dynamic_slice(table, (t * 32, 0), (32, HD)) for table in (COSINE, SINE)]
    scale_here = lax.dynamic_slice(scales, (t * 32,), (32,))
    query = rotate((q_raw * scale_here[:, None]).reshape(32, 12, HD), *mine_rows).astype(BF)
    attended = attend(query, keys, values, limit, t * 32).reshape(32, 1536)
    attended = jnp.concatenate(by_index([attended[:, 384 * d : 384 * d + 384] for d in range(4)], x), axis=1)

    got = [attended] + [swap(attended, "zl", d) for d in (1, 2, 3)]
    all_rows = jnp.concatenate(by_index(got, t), axis=0)
    return jnp.dot(all_rows, wo, preferred_element_type=F32).astype(BF)


def solution(mesh):
    fine = Mesh(mesh.devices.reshape(SIZES), AXES)
    rows = ("y", "zh", "x", "core")
    placed = (P(rows, "zl"), P("zl"), P(rows, "zl"), P(rows, "zl"), P(rows, "zl"), P(rows))
    return jax.shard_map(body, mesh=fine, in_specs=placed, out_specs=P(rows, "zl"), check_vma=False)
```

time: 208 us -> 183 us (0.88)
  the two profiles are of different devices: /device:TPU:24 before, /device:TPU:1 now
where the time goes in v2:
time: 183 us; the launch traced here: 182 us
  starting transfers between devices  78.3 us (43%)
  waiting for transfers between devices  67 us (37%)
  between operations  14.6 us (8%)
  matrix products  8.43 us (5%)
  other arithmetic  8.05 us (4%)
  local copies, waits for them, and re-layouts  3.14 us (2%)
  Pallas kernels  2.55 us (1%)
    ppermute x25, waiting for transfers between devices, swap(): return lax.ppermute(value, axis, [(i, i ^ d) for i in range(n)])  64 us
    ppermute x25, starting transfers between devices, swap(): return lax.ppermute(value, axis, [(i, i ^ d) for i in range(n)])  56.2 us
    ppermute x4, starting transfers between devices, move(): lax.ppermute(value, AXES, [(flat(*at), flat(*where(*at))) for at in every...  22.1 us
    dot_general x1, matrix products, body(): return jnp.dot(all_rows, wo, preferred_element_type=F32).astype(BF)  7.35 us
  transfers between devices with their start and end apart: 30, of which 12 were waited for; matrix products, arithmetic and copies ran while one was open for 6% of the time, Pallas kernels for 1%

profile of v2, /device:TPU:1, one launch (start us, length us, event | category | flops | bytes accessed | tf_op | source)
XLA Modules:
  0.0 182.1 jit_solution(12174559180971110387)
XLA Ops:
  6.5 3.3 %collective-permute-start.27 = (bf16[24,4096]{1,0:T(8,128)(2,1)}, bf16[24,4096]{1,0:T(8,128)(2,1)S(1)}, u32[]{:S(2)}, u32[]{:S(2)}) collective-permute-start(bf16[24,4096]{1,0:T(8,128)(2,1)} %param.14), channel_id=1, source_target_pairs={{0,32},{1,33},{2,34},{3,35},{4,0},{5,1},{6,2},{7,3},{8,36},{9,37},... | collective-permute-start | bytes 589832 | tf_op jit(solution)/shard_map/ppermute | solution.py:43
  9.9 10.0 %collective-permute-start.28 = (bf16[24,4096]{1,0:T(8,128)(2,1)}, bf16[24,4096]{1,0:T(8,128)(2,1)S(1)}, u32[]{:S(2)}, u32[]{:S(2)}) collective-permute-start(bf16[24,4096]{1,0:T(8,128)(2,1)} %param.14), channel_id=1, source_target_pairs={{0,0},{1,1},{2,2},{3,3},{4,32},{5,33},{6,34},{7,35},{8,4},{9,5},{1... | collective-permute-start | bytes 589832 | tf_op jit(solution)/shard_map/ppermute | solution.py:43
  19.9 3.0 %collective-permute-done.28 = bf16[24,4096]{1,0:T(8,128)(2,1)S(1)} collective-permute-done((bf16[24,4096]{1,0:T(8,128)(2,1)}, bf16[24,4096]{1,0:T(8,128)(2,1)S(1)}, u32[]{:S(2)}, u32[]{:S(2)}) %collective-permute-start.28) | collective-permute-done | bytes 196640 | tf_op jit(solution)/shard_map/ppermute | solution.py:43
  25.2 8.1 %collective-permute-start.4 = (bf16[896,128]{1,0:T(8,128)(2,1)S(1)}, bf16[896,128]{1,0:T(8,128)(2,1)S(1)}, u32[]{:S(2)}, u32[]{:S(2)}) collective-permute-start(bf16[896,128]{1,0:T(8,128)(2,1)S(1)} %shard_map.100), channel_id=1, source_target_pairs={{0,32},{1,40},{2,48},{3,56},{4,36},{5,44},{6,52},{7,60},{8,96},{9,... | collective-permute-start | bytes 688136 | tf_op jit(solution)/shard_map/ppermute | solution.py:43
  34.5 5.9 %collective-permute-start = (bf16[128,1024]{1,0:T(8,128)(2,1)S(1)}, bf16[128,1024]{1,0:T(8,128)(2,1)}, u32[]{:S(2)}, u32[]{:S(2)}) collective-permute-start(bf16[128,1024]{1,0:T(8,128)(2,1)S(1)} %pad_maximum_fusion.3), channel_id=1, source_target_pairs={{0,64},{64,0},{128,192},{192,128},{1,65},{65,1},{129,193},{193,129... | collective-permute-start | bytes 786440 | tf_op jit(solution)/shard_map/ppermute | solution.py:39
  40.6 18.9 %collective-permute-start.11 = (bf16[2,896,128]{2,1,0:T(8,128)(2,1)S(1)}, bf16[2,896,128]{2,1,0:T(8,128)(2,1)S(1)}, u32[]{:S(2)}, u32[]{:S(2)}) collective-permute-start(bf16[2,896,128]{2,1,0:T(8,128)(2,1)S(1)} %pad_maximum_fusion.1.a0), channel_id=1, source_target_pairs={{0,16},{8,24},{16,0},{24,8},{1,17},{9,25},{17,1},{25,9},{2,18},{10... | collective-permute-start | bytes 1376264 | tf_op jit(solution)/shard_map/ppermute | solution.py:39
  60.0 1.3 constant_dynamic-slice_fusion
  63.3 6.0 %collective-permute-start.2 = (bf16[128,1024]{1,0:T(8,128)(2,1)S(1)}, bf16[128,1024]{1,0:T(8,128)(2,1)}, u32[]{:S(2)}, u32[]{:S(2)}) collective-permute-start(bf16[128,1024]{1,0:T(8,128)(2,1)S(1)} %pad_maximum_fusion.5), channel_id=1, source_target_pairs={{0,192},{64,128},{128,64},{192,0},{1,193},{65,129},{129,65},{193,1... | collective-permute-start | bytes 786440 | tf_op jit(solution)/shard_map/ppermute | solution.py:39
  69.3 2.5 %collective-permute-done.11.a0 = bf16[2,896,128]{2,1,0:T(8,128)(2,1)S(1)} collective-permute-done((bf16[2,896,128]{2,1,0:T(8,128)(2,1)S(1)}, bf16[2,896,128]{2,1,0:T(8,128)(2,1)S(1)}, u32[]{:S(2)}, u32[]{:S(2)}) %collective-permute-start.11) | collective-permute-done | bytes 458784 | tf_op jit(solution)/shard_map/ppermute | solution.py:39
  71.8 2.7 %collective-permute-start.12 = (bf16[2,896,128]{2,1,0:T(8,128)(2,1)S(1)}, bf16[2,896,128]{2,1,0:T(8,128)(2,1)S(1)}, u32[]{:S(2)}, u32[]{:S(2)}) collective-permute-start(bf16[2,896,128]{2,1,0:T(8,128)(2,1)S(1)} %collective-permute-done.11.a0), channel_id=1, source_target_pairs={{0,4},{4,0},{1,5},{5,1},{2,6},{6,2},{3,7},{7,3},{8,12},{12,8},{9,1... | collective-permute-start | bytes 1376264 | tf_op jit(solution)/shard_map/ppermute | solution.py:39
  74.5 7.7 %collective-permute-done.13.a1 = bf16[2,896,128]{2,1,0:T(8,128)(2,1)S(1)} collective-permute-done((bf16[2,896,128]{2,1,0:T(8,128)(2,1)S(1)}, bf16[2,896,128]{2,1,0:T(8,128)(2,1)S(1)}, u32[]{:S(2)}, u32[]{:S(2)}) %collective-permute-start.13) | collective-permute-done | bytes 458784 | tf_op jit(solution)/shard_map/ppermute | solution.py:39
  84.0 1.4 fusion.47
  87.3 1.3 shard_map.102
  88.6 4.7 %collective-permute-start.15 = (bf16[128,896]{1,0:T(8,128)(2,1)S(1)}, bf16[128,896]{1,0:T(8,128)(2,1)S(1)}, u32[]{:S(2)}, u32[]{:S(2)}) collective-permute-start(bf16[128,896]{1,0:T(8,128)(2,1)S(1)} %get-tuple-element.36), channel_id=1, source_target_pairs={{0,64},{64,0},{128,192},{192,128},{1,65},{65,1},{129,193},{193,129... | collective-permute-start | bytes 688136 | tf_op jit(solution)/shard_map/ppermute | solution.py:39
  93.3 1.6 collective-permute-start.16
  95.8 1.3 shard_map.101
  97.2 7.0 %collective-permute-done.15 = bf16[128,896]{1,0:T(8,128)(2,1)S(1)} collective-permute-done((bf16[128,896]{1,0:T(8,128)(2,1)S(1)}, bf16[128,896]{1,0:T(8,128)(2,1)S(1)}, u32[]{:S(2)}, u32[]{:S(2)}) %collective-permute-start.15) | collective-permute-done | bytes 229408 | tf_op jit(solution)/shard_map/ppermute | solution.py:39
  104.2 1.7 collective-permute-start.10
  105.9 9.4 %collective-permute-done.16 = bf16[128,896]{1,0:T(8,128)(2,1)S(1)} collective-permute-done((bf16[128,896]{1,0:T(8,128)(2,1)S(1)}, bf16[128,896]{1,0:T(8,128)(2,1)S(1)}, u32[]{:S(2)}, u32[]{:S(2)}) %collective-permute-start.16) | collective-permute-done | bytes 229408 | tf_op jit(solution)/shard_map/ppermute | solution.py:39
  115.4 2.1 %collective-permute-start.9 = (bf16[128,896]{1,0:T(8,128)(2,1)S(1)}, bf16[128,896]{1,0:T(8,128)(2,1)S(1)}, u32[]{:S(2)}, u32[]{:S(2)}) collective-permute-start(bf16[128,896]{1,0:T(8,128)(2,1)S(1)} %get-tuple-element.41), channel_id=1, source_target_pairs={{0,128},{64,192},{128,0},{192,64},{1,129},{65,193},{129,1},{193,65... | collective-permute-start | bytes 688136 | tf_op jit(solution)/shard_map/ppermute | solution.py:39
  117.7 5.2 %collective-permute-done.10 = bf16[128,896]{1,0:T(8,128)(2,1)S(1)} collective-permute-done((bf16[128,896]{1,0:T(8,128)(2,1)S(1)}, bf16[128,896]{1,0:T(8,128)(2,1)S(1)}, u32[]{:S(2)}, u32[]{:S(2)}) %collective-permute-start.10) | collective-permute-done | bytes 229408 | tf_op jit(solution)/shard_map/ppermute | solution.py:39
  122.9 2.1 %collective-permute-start.23 = (f32[128]{0:T(128)S(1)}, f32[128]{0:T(128)S(1)}, u32[]{:S(2)}, u32[]{:S(2)}) collective-permute-start(f32[128]{0:T(128)S(1)} %copy-done.8), channel_id=1, source_target_pairs={{0,3},{1,2},{2,1},{3,0},{4,7},{5,6},{6,5},{7,4},{8,11},{9,10},{10,... | collective-permute-start | bytes 1544 | tf_op jit(solution)/shard_map/ppermute | solution.py:39
  125.0 2.3 %collective-permute-done.8 = bf16[128,896]{1,0:T(8,128)(2,1)S(1)} collective-permute-done((bf16[128,896]{1,0:T(8,128)(2,1)S(1)}, bf16[128,896]{1,0:T(8,128)(2,1)S(1)}, u32[]{:S(2)}, u32[]{:S(2)}) %collective-permute-start.8) | collective-permute-done | bytes 229408 | tf_op jit(solution)/shard_map/ppermute | solution.py:39
  127.3 9.8 %collective-permute-done.9 = bf16[128,896]{1,0:T(8,128)(2,1)S(1)} collective-permute-done((bf16[128,896]{1,0:T(8,128)(2,1)S(1)}, bf16[128,896]{1,0:T(8,128)(2,1)S(1)}, u32[]{:S(2)}, u32[]{:S(2)}) %collective-permute-start.9) | collective-permute-done | bytes 229408 | tf_op jit(solution)/shard_map/ppermute | solution.py:39
  137.4 3.4 %collective-permute-start.20 = (bf16[32,2560]{1,0:T(8,128)(2,1)S(1)}, bf16[32,2560]{1,0:T(8,128)(2,1)S(1)}, u32[]{:S(2)}, u32[]{:S(2)}) collective-permute-start(bf16[32,2560]{1,0:T(8,128)(2,1)S(1)} %constant_dynamic-update-slice_fusion.8), channel_id=1, source_target_pairs={{0,3},{1,2},{2,1},{3,0},{4,7},{5,6},{6,5},{7,4},{8,11},{9,10},{10,... | collective-permute-start | bytes 491528 | tf_op jit(solution)/shard_map/ppermute | solution.py:39
  141.3 2.9 %collective-permute-done.20 = bf16[32,2560]{1,0:T(8,128)(2,1)S(1)} collective-permute-done((bf16[32,2560]{1,0:T(8,128)(2,1)S(1)}, bf16[32,2560]{1,0:T(8,128)(2,1)S(1)}, u32[]{:S(2)}, u32[]{:S(2)}) %collective-permute-start.20) | collective-permute-done | bytes 163872 | tf_op jit(solution)/shard_map/ppermute | solution.py:39
  144.3 10.3 %collective-permute-done.19 = bf16[32,2560]{1,0:T(8,128)(2,1)S(1)} collective-permute-done((bf16[32,2560]{1,0:T(8,128)(2,1)S(1)}, bf16[32,2560]{1,0:T(8,128)(2,1)S(1)}, u32[]{:S(2)}, u32[]{:S(2)}) %collective-permute-start.19) | collective-permute-done | bytes 163872 | tf_op jit(solution)/shard_map/ppermute | solution.py:39
  157.3 1.7 collective-permute-start.24
  159.0 1.9 %collective-permute-start.26 = (bf16[32,1536]{1,0:T(8,128)(2,1)S(1)}, bf16[32,1536]{1,0:T(8,128)(2,1)S(1)}, u32[]{:S(2)}, u32[]{:S(2)}) collective-permute-start(bf16[32,1536]{1,0:T(8,128)(2,1)S(1)} %pad_maximum_fusion.7), channel_id=1, source_target_pairs={{0,1},{1,0},{2,3},{3,2},{4,5},{5,4},{6,7},{7,6},{8,9},{9,8},{10,11... | collective-permute-start | bytes 294920 | tf_op jit(solution)/shard_map/ppermute | solution.py:39
  160.9 1.8 %collective-permute-done.24 = bf16[32,1536]{1,0:T(8,128)(2,1)S(1)} collective-permute-done((bf16[32,1536]{1,0:T(8,128)(2,1)S(1)}, bf16[32,1536]{1,0:T(8,128)(2,1)S(1)}, u32[]{:S(2)}, u32[]{:S(2)}) %collective-permute-start.24) | collective-permute-done | bytes 98336 | tf_op jit(solution)/shard_map/ppermute | solution.py:39
  162.8 5.0 %collective-permute-done.25 = bf16[32,1536]{1,0:T(8,128)(2,1)S(1)} collective-permute-done((bf16[32,1536]{1,0:T(8,128)(2,1)S(1)}, bf16[32,1536]{1,0:T(8,128)(2,1)S(1)}, u32[]{:S(2)}, u32[]{:S(2)}) %collective-permute-start.25) | collective-permute-done | bytes 98336 | tf_op jit(solution)/shard_map/ppermute | solution.py:39
  167.9 7.4 %convolution_convert_fusion = bf16[128,4096]{1,0:T(8,128)(2,1)} fusion(bf16[1536,4096]{1,0:T(8,128)(2,1)} %all-gather.2.cloned.1.call-done, bf16[32,1536]{1,0:T(8,128)(2,1)S(1)} %broadcast_select_fusion.6, bf16[32,1536]{1,0:T(8,128)(2,1)S(1)} %get-tuple-element.44, bf16[32,1536]{1,0:T(8,128)(2,1)S(1)} %get-tuple-element.43, ...), kind=kOutput, calls=%fused_computation.1 | convolution fusion | flops 1612709888 | bytes 14024704 | tf_op jit(solution)/shard_map/dot_general | solution.py:218
  (115 shorter events, 13.8 us)
Async XLA Ops:
  6.5 26.8 %copy-start.2 = (bf16[128,4096]{1,0:T(8,128)(2,1)S(1)}, bf16[128,4096]{1,0:T(8,128)(2,1)}, u32[]{:S(2)}) copy-start(bf16[128,4096]{1,0:T(8,128)(2,1)} %param.10) | copy-start | bytes 3145732
  6.5 26.8 %copy-start.6 = (f32[4096]{0:T(1024)S(1)}, f32[4096]{0:T(1024)}, u32[]{:S(2)}) copy-start(f32[4096]{0:T(1024)} %param.11) | copy-start | bytes 49156
  6.5 161.4 %all-gather.2.cloned.1.call-start = ((), (), s32[]{:S(2)}) async-start(), calls=%async_computation | async-start | bytes 12976128 | tf_op jit(solution)/shard_map/all_gather | solution.py:160
  6.5 13.3 %collective-permute-start.27 = (bf16[24,4096]{1,0:T(8,128)(2,1)}, bf16[24,4096]{1,0:T(8,128)(2,1)S(1)}, u32[]{:S(2)}, u32[]{:S(2)}) collective-permute-start(bf16[24,4096]{1,0:T(8,128)(2,1)} %param.14), channel_id=1, source_target_pairs={{0,32},{1,33},{2,34},{3,35},{4,0},{5,1},{6,2},{7,3},{8,36},{9,37},... | collective-permute-start | bytes 589832 | tf_op jit(solution)/shard_map/ppermute | solution.py:43
  9.9 13.0 %collective-permute-start.28 = (bf16[24,4096]{1,0:T(8,128)(2,1)}, bf16[24,4096]{1,0:T(8,128)(2,1)S(1)}, u32[]{:S(2)}, u32[]{:S(2)}) collective-permute-start(bf16[24,4096]{1,0:T(8,128)(2,1)} %param.14), channel_id=1, source_target_pairs={{0,0},{1,1},{2,2},{3,3},{4,32},{5,33},{6,34},{7,35},{8,4},{9,5},{1... | collective-permute-start | bytes 589832 | tf_op jit(solution)/shard_map/ppermute | solution.py:43
  24.5 16.0 %collective-permute-start.3 = (bf16[896,128]{1,0:T(8,128)(2,1)S(1)}, bf16[896,128]{1,0:T(8,128)(2,1)S(1)}, u32[]{:S(2)}, u32[]{:S(2)}) collective-permute-start(bf16[896,128]{1,0:T(8,128)(2,1)S(1)} %shard_map.100), channel_id=1, source_target_pairs={{0,0},{1,8},{2,16},{3,24},{4,4},{5,12},{6,20},{7,28},{8,64},{9,72}... | collective-permute-start | bytes 688136 | tf_op jit(solution)/shard_map/ppermute | solution.py:43
  25.2 15.4 %collective-permute-start.4 = (bf16[896,128]{1,0:T(8,128)(2,1)S(1)}, bf16[896,128]{1,0:T(8,128)(2,1)S(1)}, u32[]{:S(2)}, u32[]{:S(2)}) collective-permute-start(bf16[896,128]{1,0:T(8,128)(2,1)S(1)} %shard_map.100), channel_id=1, source_target_pairs={{0,32},{1,40},{2,48},{3,56},{4,36},{5,44},{6,52},{7,60},{8,96},{9,... | collective-permute-start | bytes 688136 | tf_op jit(solution)/shard_map/ppermute | solution.py:43
  34.5 28.8 %collective-permute-start = (bf16[128,1024]{1,0:T(8,128)(2,1)S(1)}, bf16[128,1024]{1,0:T(8,128)(2,1)}, u32[]{:S(2)}, u32[]{:S(2)}) collective-permute-start(bf16[128,1024]{1,0:T(8,128)(2,1)S(1)} %pad_maximum_fusion.3), channel_id=1, source_target_pairs={{0,64},{64,0},{128,192},{192,128},{1,65},{65,1},{129,193},{193,129... | collective-permute-start | bytes 786440 | tf_op jit(solution)/shard_map/ppermute | solution.py:39
  40.4 44.9 %collective-permute-start.1 = (bf16[128,1024]{1,0:T(8,128)(2,1)S(1)}, bf16[128,1024]{1,0:T(8,128)(2,1)}, u32[]{:S(2)}, u32[]{:S(2)}) collective-permute-start(bf16[128,1024]{1,0:T(8,128)(2,1)S(1)} %pad_maximum_fusion.4), channel_id=1, source_target_pairs={{0,128},{64,192},{128,0},{192,64},{1,129},{65,193},{129,1},{193,65... | collective-permute-start | bytes 786440 | tf_op jit(solution)/shard_map/ppermute | solution.py:39
  40.6 31.2 %collective-permute-start.11 = (bf16[2,896,128]{2,1,0:T(8,128)(2,1)S(1)}, bf16[2,896,128]{2,1,0:T(8,128)(2,1)S(1)}, u32[]{:S(2)}, u32[]{:S(2)}) collective-permute-start(bf16[2,896,128]{2,1,0:T(8,128)(2,1)S(1)} %pad_maximum_fusion.1.a0), channel_id=1, source_target_pairs={{0,16},{8,24},{16,0},{24,8},{1,17},{9,25},{17,1},{25,9},{2,18},{10... | collective-permute-start | bytes 1376264 | tf_op jit(solution)/shard_map/ppermute | solution.py:39
  59.5 22.7 %collective-permute-start.13 = (bf16[2,896,128]{2,1,0:T(8,128)(2,1)S(1)}, bf16[2,896,128]{2,1,0:T(8,128)(2,1)S(1)}, u32[]{:S(2)}, u32[]{:S(2)}) collective-permute-start(bf16[2,896,128]{2,1,0:T(8,128)(2,1)S(1)} %pad_maximum_fusion.1.a0), channel_id=1, source_target_pairs={{0,24},{8,16},{16,8},{24,0},{1,25},{9,17},{17,9},{25,1},{2,26},{10... | collective-permute-start | bytes 1376264 | tf_op jit(solution)/shard_map/ppermute | solution.py:39
  62.6 22.8 %collective-permute-start.6 = (bf16[2,896,128]{2,1,0:T(8,128)(2,1)S(1)}, bf16[2,896,128]{2,1,0:T(8,128)(2,1)S(1)}, u32[]{:S(2)}, u32[]{:S(2)}) collective-permute-start(bf16[2,896,128]{2,1,0:T(8,128)(2,1)S(1)} %pad_maximum_fusion.1.a0), channel_id=1, source_target_pairs={{0,8},{8,0},{16,24},{24,16},{1,9},{9,1},{17,25},{25,17},{2,10},{10... | collective-permute-start | bytes 1376264 | tf_op jit(solution)/shard_map/ppermute | solution.py:39
  63.3 22.5 %collective-permute-start.2 = (bf16[128,1024]{1,0:T(8,128)(2,1)S(1)}, bf16[128,1024]{1,0:T(8,128)(2,1)}, u32[]{:S(2)}, u32[]{:S(2)}) collective-permute-start(bf16[128,1024]{1,0:T(8,128)(2,1)S(1)} %pad_maximum_fusion.5), channel_id=1, source_target_pairs={{0,192},{64,128},{128,64},{192,0},{1,193},{65,129},{129,65},{193,1... | collective-permute-start | bytes 786440 | tf_op jit(solution)/shard_map/ppermute | solution.py:39
  71.8 15.3 %collective-permute-start.12 = (bf16[2,896,128]{2,1,0:T(8,128)(2,1)S(1)}, bf16[2,896,128]{2,1,0:T(8,128)(2,1)S(1)}, u32[]{:S(2)}, u32[]{:S(2)}) collective-permute-start(bf16[2,896,128]{2,1,0:T(8,128)(2,1)S(1)} %collective-permute-done.11.a0), channel_id=1, source_target_pairs={{0,4},{4,0},{1,5},{5,1},{2,6},{6,2},{3,7},{7,3},{8,12},{12,8},{9,1... | collective-permute-start | bytes 1376264 | tf_op jit(solution)/shard_map/ppermute | solution.py:39
  82.2 5.0 %collective-permute-start.14 = (bf16[2,896,128]{2,1,0:T(8,128)(2,1)S(1)}, bf16[2,896,128]{2,1,0:T(8,128)(2,1)S(1)}, u32[]{:S(2)}, u32[]{:S(2)}) collective-permute-start(bf16[2,896,128]{2,1,0:T(8,128)(2,1)S(1)} %collective-permute-done.13.a1), channel_id=1, source_target_pairs={{0,4},{4,0},{1,5},{5,1},{2,6},{6,2},{3,7},{7,3},{8,12},{12,8},{9,1... | collective-permute-start | bytes 1376264 | tf_op jit(solution)/shard_map/ppermute | solution.py:39
  85.3 8.0 %collective-permute-start.5 = (bf16[2,896,128]{2,1,0:T(8,128)(2,1)S(1)}, bf16[2,896,128]{2,1,0:T(8,128)(2,1)S(1)}, u32[]{:S(2)}, u32[]{:S(2)}) collective-permute-start(bf16[2,896,128]{2,1,0:T(8,128)(2,1)S(1)} %pad_maximum_fusion.1.a0), channel_id=1, source_target_pairs={{0,4},{4,0},{1,5},{5,1},{2,6},{6,2},{3,7},{7,3},{8,12},{12,8},{9,1... | collective-permute-start | bytes 1376264 | tf_op jit(solution)/shard_map/ppermute | solution.py:39
  85.3 9.5 %collective-permute-start.7 = (bf16[2,896,128]{2,1,0:T(8,128)(2,1)S(1)}, bf16[2,896,128]{2,1,0:T(8,128)(2,1)S(1)}, u32[]{:S(2)}, u32[]{:S(2)}) collective-permute-start(bf16[2,896,128]{2,1,0:T(8,128)(2,1)S(1)} %collective-permute-done.6.a1), channel_id=1, source_target_pairs={{0,4},{4,0},{1,5},{5,1},{2,6},{6,2},{3,7},{7,3},{8,12},{12,8},{9,1... | collective-permute-start | bytes 1376264 | tf_op jit(solution)/shard_map/ppermute | solution.py:39
  87.0 53.8 %collective-permute-start.21 = (f32[128]{0:T(128)S(1)}, f32[128]{0:T(128)S(1)}, u32[]{:S(2)}, u32[]{:S(2)}) collective-permute-start(f32[128]{0:T(128)S(1)} %copy-done.8), channel_id=1, source_target_pairs={{0,1},{1,0},{2,3},{3,2},{4,5},{5,4},{6,7},{7,6},{8,9},{9,8},{10,11... | collective-permute-start | bytes 1544 | tf_op jit(solution)/shard_map/ppermute | solution.py:39
  87.2 54.1 %collective-permute-start.22 = (f32[128]{0:T(128)S(1)}, f32[128]{0:T(128)S(1)}, u32[]{:S(2)}, u32[]{:S(2)}) collective-permute-start(f32[128]{0:T(128)S(1)} %copy-done.8), channel_id=1, source_target_pairs={{0,2},{1,3},{2,0},{3,1},{4,6},{5,7},{6,4},{7,5},{8,10},{9,11},{10,... | collective-permute-start | bytes 1544 | tf_op jit(solution)/shard_map/ppermute | solution.py:39
  88.6 15.6 %collective-permute-start.15 = (bf16[128,896]{1,0:T(8,128)(2,1)S(1)}, bf16[128,896]{1,0:T(8,128)(2,1)S(1)}, u32[]{:S(2)}, u32[]{:S(2)}) collective-permute-start(bf16[128,896]{1,0:T(8,128)(2,1)S(1)} %get-tuple-element.36), channel_id=1, source_target_pairs={{0,64},{64,0},{128,192},{192,128},{1,65},{65,1},{129,193},{193,129... | collective-permute-start | bytes 688136 | tf_op jit(solution)/shard_map/ppermute | solution.py:39
  93.3 22.1 %collective-permute-start.16 = (bf16[128,896]{1,0:T(8,128)(2,1)S(1)}, bf16[128,896]{1,0:T(8,128)(2,1)S(1)}, u32[]{:S(2)}, u32[]{:S(2)}) collective-permute-start(bf16[128,896]{1,0:T(8,128)(2,1)S(1)} %get-tuple-element.38), channel_id=1, source_target_pairs={{0,128},{64,192},{128,0},{192,64},{1,129},{65,193},{129,1},{193,65... | collective-permute-start | bytes 688136 | tf_op jit(solution)/shard_map/ppermute | solution.py:39
  94.9 20.5 %collective-permute-start.17 = (bf16[128,896]{1,0:T(8,128)(2,1)S(1)}, bf16[128,896]{1,0:T(8,128)(2,1)S(1)}, u32[]{:S(2)}, u32[]{:S(2)}) collective-permute-start(bf16[128,896]{1,0:T(8,128)(2,1)S(1)} %get-tuple-element.37), channel_id=1, source_target_pairs={{0,192},{64,128},{128,64},{192,0},{1,193},{65,129},{129,65},{193,1... | collective-permute-start | bytes 688136 | tf_op jit(solution)/shard_map/ppermute | solution.py:39
  104.2 18.7 %collective-permute-start.10 = (bf16[128,896]{1,0:T(8,128)(2,1)S(1)}, bf16[128,896]{1,0:T(8,128)(2,1)S(1)}, u32[]{:S(2)}, u32[]{:S(2)}) collective-permute-start(bf16[128,896]{1,0:T(8,128)(2,1)S(1)} %get-tuple-element.40), channel_id=1, source_target_pairs={{0,192},{64,128},{128,64},{192,0},{1,193},{65,129},{129,65},{193,1... | collective-permute-start | bytes 688136 | tf_op jit(solution)/shard_map/ppermute | solution.py:39
  115.4 12.0 %collective-permute-start.8 = (bf16[128,896]{1,0:T(8,128)(2,1)S(1)}, bf16[128,896]{1,0:T(8,128)(2,1)S(1)}, u32[]{:S(2)}, u32[]{:S(2)}) collective-permute-start(bf16[128,896]{1,0:T(8,128)(2,1)S(1)} %get-tuple-element.39), channel_id=1, source_target_pairs={{0,64},{64,0},{128,192},{192,128},{1,65},{65,1},{129,193},{193,129... | collective-permute-start | bytes 688136 | tf_op jit(solution)/shard_map/ppermute | solution.py:39
  115.4 21.7 %collective-permute-start.9 = (bf16[128,896]{1,0:T(8,128)(2,1)S(1)}, bf16[128,896]{1,0:T(8,128)(2,1)S(1)}, u32[]{:S(2)}, u32[]{:S(2)}) collective-permute-start(bf16[128,896]{1,0:T(8,128)(2,1)S(1)} %get-tuple-element.41), channel_id=1, source_target_pairs={{0,128},{64,192},{128,0},{192,64},{1,129},{65,193},{129,1},{193,65... | collective-permute-start | bytes 688136 | tf_op jit(solution)/shard_map/ppermute | solution.py:39
  122.9 18.3 %collective-permute-start.23 = (f32[128]{0:T(128)S(1)}, f32[128]{0:T(128)S(1)}, u32[]{:S(2)}, u32[]{:S(2)}) collective-permute-start(f32[128]{0:T(128)S(1)} %copy-done.8), channel_id=1, source_target_pairs={{0,3},{1,2},{2,1},{3,0},{4,7},{5,6},{6,5},{7,4},{8,11},{9,10},{10,... | collective-permute-start | bytes 1544 | tf_op jit(solution)/shard_map/ppermute | solution.py:39
  137.4 6.8 %collective-permute-start.20 = (bf16[32,2560]{1,0:T(8,128)(2,1)S(1)}, bf16[32,2560]{1,0:T(8,128)(2,1)S(1)}, u32[]{:S(2)}, u32[]{:S(2)}) collective-permute-start(bf16[32,2560]{1,0:T(8,128)(2,1)S(1)} %constant_dynamic-update-slice_fusion.8), channel_id=1, source_target_pairs={{0,3},{1,2},{2,1},{3,0},{4,7},{5,6},{6,5},{7,4},{8,11},{9,10},{10,... | collective-permute-start | bytes 491528 | tf_op jit(solution)/shard_map/ppermute | solution.py:39
  140.8 13.7 %collective-permute-start.19 = (bf16[32,2560]{1,0:T(8,128)(2,1)S(1)}, bf16[32,2560]{1,0:T(8,128)(2,1)S(1)}, u32[]{:S(2)}, u32[]{:S(2)}) collective-permute-start(bf16[32,2560]{1,0:T(8,128)(2,1)S(1)} %get-tuple-element.78), channel_id=1, source_target_pairs={{0,2},{1,3},{2,0},{3,1},{4,6},{5,7},{6,4},{7,5},{8,10},{9,11},{10,... | collective-permute-start | bytes 491528 | tf_op jit(solution)/shard_map/ppermute | solution.py:39
  140.8 13.7 %collective-permute-start.18 = (bf16[32,2560]{1,0:T(8,128)(2,1)S(1)}, bf16[32,2560]{1,0:T(8,128)(2,1)S(1)}, u32[]{:S(2)}, u32[]{:S(2)}) collective-permute-start(bf16[32,2560]{1,0:T(8,128)(2,1)S(1)} %get-tuple-element.75), channel_id=1, source_target_pairs={{0,1},{1,0},{2,3},{3,2},{4,5},{5,4},{6,7},{7,6},{8,9},{9,8},{10,11... | collective-permute-start | bytes 491528 | tf_op jit(solution)/shard_map/ppermute | solution.py:39
  157.3 5.5 %collective-permute-start.24 = (bf16[32,1536]{1,0:T(8,128)(2,1)S(1)}, bf16[32,1536]{1,0:T(8,128)(2,1)S(1)}, u32[]{:S(2)}, u32[]{:S(2)}) collective-permute-start(bf16[32,1536]{1,0:T(8,128)(2,1)S(1)} %pad_maximum_fusion.7), channel_id=1, source_target_pairs={{0,3},{1,2},{2,1},{3,0},{4,7},{5,6},{6,5},{7,4},{8,11},{9,10},{10,... | collective-permute-start | bytes 294920 | tf_op jit(solution)/shard_map/ppermute | solution.py:39
  159.0 8.7 %collective-permute-start.25 = (bf16[32,1536]{1,0:T(8,128)(2,1)S(1)}, bf16[32,1536]{1,0:T(8,128)(2,1)S(1)}, u32[]{:S(2)}, u32[]{:S(2)}) collective-permute-start(bf16[32,1536]{1,0:T(8,128)(2,1)S(1)} %pad_maximum_fusion.7), channel_id=1, source_target_pairs={{0,2},{1,3},{2,0},{3,1},{4,6},{5,7},{6,4},{7,5},{8,10},{9,11},{10,... | collective-permute-start | bytes 294920 | tf_op jit(solution)/shard_map/ppermute | solution.py:39
  159.0 8.7 %collective-permute-start.26 = (bf16[32,1536]{1,0:T(8,128)(2,1)S(1)}, bf16[32,1536]{1,0:T(8,128)(2,1)S(1)}, u32[]{:S(2)}, u32[]{:S(2)}) collective-permute-start(bf16[32,1536]{1,0:T(8,128)(2,1)S(1)} %pad_maximum_fusion.7), channel_id=1, source_target_pairs={{0,1},{1,0},{2,3},{3,2},{4,5},{5,4},{6,7},{7,6},{8,9},{9,8},{10,11... | collective-permute-start | bytes 294920 | tf_op jit(solution)/shard_map/ppermute | solution.py:39
  (9 other events, 26.3 us)
Sparse Core Ops, SparseCore 0:
  23.8 114.2 all-gather.1

commit v3 on v2

--- a/solution.py
+++ b/solution.py
@@ -53,6 +53,15 @@
 
 
 COSINE, SINE = tables()
+
+
+def order_of(zh):
+    order = np.arange(384).reshape(2, 8, 24)
+    order = np.stack([order[zh], order[1 - zh]], axis=1).reshape(384)
+    return np.eye(384, dtype=np.float32)[:, order].astype(jnp.bfloat16)
+
+
+ORDER = (order_of(0), order_of(1))
 
 
 def rotate(values, cosine, sine):
@@ -117,8 +126,11 @@
     own_ref[:, :768] = q[:ROWS]
     own_ref[:, 768:] = kv[:ROWS]
     for e in (1, 2, 3):
-        out_ref[e - 1, :, :768] = q[ROWS * e : ROWS * e + ROWS].astype(BF)
-        out_ref[e - 1, :, 768:] = kv[ROWS * e : ROWS * e + ROWS].astype(BF)
+        at = ROWS * e
+        for half in (0, 1):
+            to = half ^ (e & 1)
+            out_ref[e - 1, :, 384 * to : 384 * to + 384] = q[at : at + ROWS, 384 * half : 384 * half + 384].astype(BF)
+            out_ref[e - 1, :, 768 + 64 * to : 832 + 64 * to] = kv[at : at + ROWS, 64 * half : 64 * half + 64].astype(BF)
 
 
 def project(inputs, first, second):
@@ -148,16 +160,15 @@
     y, zh, x, c, t = (lax.axis_index(name) for name in AXES)
 
     packed = pack(query_weight, kv_weight.T)
-    near = move(packed, lambda y, zh, x, c, t: (x ^ y, zh, t, c, y))
-    far = move(packed, lambda y, zh, x, c, t: (x ^ y, zh ^ 1, t, c, y))
+    near = move(packed, lambda y, zh, x, c, t: (x ^ y, zh, t ^ x, c, y))
+    far = move(packed, lambda y, zh, x, c, t: (x ^ y, zh ^ 1, t ^ x, c, y))
+    wo_other, near, far = lax.optimization_barrier((swap(out_weight, "zh", 1), near, far))
+    wo_piece = jnp.concatenate([out_weight, wo_other], axis=0)
+    wo = lax.all_gather(wo_piece, ("y", "x", "core"), axis=0, tiled=True)
+
     mine = jnp.stack([near, far])
     blocks = [mine] + [swap(mine, "x", d) for d in (1, 2, 3)]
     pairs = [(block, swap(block, "core", 1)) for block in blocks]
-
-    wo_near = move(out_weight, lambda y, zh, x, c, t: (y, c, 2 * zh + (x >> 1), x & 1, t))
-    wo_far = move(out_weight, lambda y, zh, x, c, t: (y, 1 - c, 2 * zh + (x >> 1), x & 1, t))
-    wo_piece = jnp.concatenate([pick(zh == 1, wo_near, wo_far), pick(zh == 1, wo_far, wo_near)], axis=0)
-    wo = lax.all_gather(wo_piece, ("y", "x", "core"), axis=0, tiled=True)
 
     widened = tokens.astype(F32)
     squares = jnp.sum(widened * widened, axis=1)
@@ -174,44 +185,47 @@
 
     inputs = jnp.concatenate([features(0)] + [swap(features(d), "y", d) for d in (1, 2, 3)], axis=0)
 
-    squares, _ = lax.optimization_barrier((squares, inputs))
-    total = squares
-    for d in (1, 2, 3):
-        total = total + swap(squares, "zl", d)
-    scales = lax.rsqrt(total / D + 1e-05)
-
-    q_sums, kv_sums = [], []
-    for first, second in ((0, 1), (2, 3)):
-        sent, summed = project(inputs, pairs[first], pairs[second])
-        for d in (1, 2, 3):
-            summed = summed + swap(sent[d - 1], "y", d).astype(F32)
-        q_sums.append(summed[:, :768])
-        kv_sums.append(summed[:, 768:])
-    q_sum = jnp.concatenate(q_sums, axis=1)
-    kv_sum = jnp.concatenate(kv_sums, axis=1)
+    sent_a, own_a = project(inputs, pairs[0], pairs[1])
+    sent_b, own_b = project(inputs, pairs[2], pairs[3])
+    got_a = [swap(sent_a[d - 1], "y", d) for d in (1, 2, 3)]
+    got_b = [swap(sent_b[d - 1], "y", d) for d in (1, 2, 3)]
+    summed = [
+        own + sum(part.astype(F32) for part in parts)
+        for own, parts in ((own_a, (got_a[0], got_b[1], got_b[2])), (own_b, (got_b[0], got_a[1], got_a[2])))
+    ]
+    base = x ^ y ^ t
+    q_sum = jnp.concatenate(by_index([half[:, at : at + 384] for half in summed for at in (0, 384)], base), axis=1)
+    kv_sum = jnp.concatenate(by_index([half[:, at : at + 64] for half in summed for at in (768, 832)], base), axis=1)
 
     kv_short = kv_sum.astype(BF)
-    kv_flat = jnp.concatenate([kv_short[32 * r : 32 * r + 32] for r in range(4)], axis=1)
+    high = lax.reduce_precision(squares, 8, 7)
+    middle = lax.reduce_precision(squares - high, 8, 7)
+    low = squares - high - middle
+    note = jnp.pad(jnp.stack([high, middle, low]), ((0, 29), (0, 0))).astype(BF)
+    shared = jnp.concatenate([kv_short[32 * r : 32 * r + 32] for r in range(4)] + [note], axis=1)
 
     def rows_for(d):
         return lax.dynamic_slice(q_sum, ((t ^ d) * 32, 0), (32, 1536))
 
-    q_raw, kv_raw = rows_for(0), kv_sum
+    q_raw, kv_raw, total = rows_for(0), kv_sum, squares
     for d in (1, 2, 3):
-        came = swap(jnp.concatenate([rows_for(d).astype(BF), kv_flat], axis=1), "zl", d).astype(F32)
+        came = swap(jnp.concatenate([rows_for(d).astype(BF), shared], axis=1), "zl", d).astype(F32)
         q_raw = q_raw + came[:, :1536]
         kv_raw = kv_raw + jnp.concatenate([came[:, 1536 + 256 * r : 1792 + 256 * r] for r in range(4)], axis=0)
+        total = total + ((came[2, 2560:] + came[1, 2560:]) + came[0, 2560:])
+    scales = lax.rsqrt(total / D + 1e-05)
 
     limit = lengths[0]
     kv = (kv_raw * scales[:, None]).astype(BF)
-    kv = by_index([kv[:, 64 * d : 64 * d + 64] for d in range(4)], x)
-    keys = rotate(jnp.concatenate(kv[:2], axis=1).astype(F32), COSINE, SINE).astype(BF)
-    values = jnp.concatenate(kv[2:], axis=1)
+    keys = rotate(kv[:, :HD].astype(F32), COSINE, SINE).astype(BF)
+    values = kv[:, HD:]
     mine_rows = [lax.dynamic_slice(table, (t * 32, 0), (32, HD)) for table in (COSINE, SINE)]
     scale_here = lax.dynamic_slice(scales, (t * 32,), (32,))
     query = rotate((q_raw * scale_here[:, None]).reshape(32, 12, HD), *mine_rows).astype(BF)
     attended = attend(query, keys, values, limit, t * 32).reshape(32, 1536)
-    attended = jnp.concatenate(by_index([attended[:, 384 * d : 384 * d + 384] for d in range(4)], x), axis=1)
+    stacked = jnp.concatenate([attended[:, 384 * d : 384 * d + 384] for d in range(4)], axis=0)
+    stacked = jnp.dot(stacked, pick(zh == 1, ORDER[0], ORDER[1]), preferred_element_type=F32).astype(BF)
+    attended = jnp.concatenate([stacked[32 * d : 32 * d + 32] for d in range(4)], axis=1)
 
     got = [attended] + [swap(attended, "zl", d) for d in (1, 2, 3)]
     all_rows = jnp.concatenate(by_index(got, t), axis=0)

time: 183 us -> 176 us (0.962)
  the two profiles are of different devices: /device:TPU:1 before, /device:TPU:24 now
where the time goes in v3:
time: 176 us
  waiting for transfers between devices  99 us (56%)
  starting transfers between devices  38.6 us (22%)
  between operations  14.7 us (8%)
  matrix products  8.6 us (5%)
  other arithmetic  7.94 us (5%)
  local copies, waits for them, and re-layouts  4.12 us (2%)
  Pallas kernels  2.68 us (2%)
    ppermute x23, waiting for transfers between devices, swap(): return lax.ppermute(value, axis, [(i, i ^ d) for i in range(n)])  77.3 us
    ppermute x23, starting transfers between devices, swap(): return lax.ppermute(value, axis, [(i, i ^ d) for i in range(n)])  27.8 us
    ppermute x2, waiting for transfers between devices, move(): lax.ppermute(value, AXES, [(flat(*at), flat(*where(*at))) for at in every...  21.6 us
    ppermute x2, starting transfers between devices, move(): lax.ppermute(value, AXES, [(flat(*at), flat(*where(*at))) for at in every...  10.7 us
    dot_general x1, matrix products, body(): return jnp.dot(all_rows, wo, preferred_element_type=F32).astype(BF)  7.35 us
  transfers between devices with their start and end apart: 26, of which 12 were waited for; matrix products, arithmetic and copies ran while one was open for 6% of the time, Pallas kernels for 2%

profile of v3, /device:TPU:24, one launch (start us, length us, event | category | flops | bytes accessed | tf_op | source)
XLA Modules:
  0.0 175.6 jit_solution(9587213440276815214)
XLA Ops:
  8.3 6.7 %collective-permute-start.4 = (bf16[896,128]{1,0:T(8,128)(2,1)S(1)}, bf16[896,128]{1,0:T(8,128)(2,1)S(1)}, u32[]{:S(2)}, u32[]{:S(2)}) collective-permute-start(bf16[896,128]{1,0:T(8,128)(2,1)S(1)} %shard_map.118), channel_id=1, source_target_pairs={{0,0},{1,8},{2,16},{3,24},{4,4},{5,12},{6,20},{7,28},{8,72},{9,64}... | collective-permute-start | bytes 688136 | tf_op jit(solution)/shard_map/ppermute | solution.py:43
  14.9 4.1 %collective-permute-start.5 = (bf16[896,128]{1,0:T(8,128)(2,1)S(1)}, bf16[896,128]{1,0:T(8,128)(2,1)S(1)}, u32[]{:S(2)}, u32[]{:S(2)}) collective-permute-start(bf16[896,128]{1,0:T(8,128)(2,1)S(1)} %shard_map.118), channel_id=1, source_target_pairs={{0,32},{1,40},{2,48},{3,56},{4,36},{5,44},{6,52},{7,60},{8,104},{9... | collective-permute-start | bytes 688136 | tf_op jit(solution)/shard_map/ppermute | solution.py:43
  19.0 1.4 collective-permute-start.3
  20.4 8.8 %collective-permute-done.3 = bf16[24,4096]{1,0:T(8,128)(2,1)S(1)} collective-permute-done((bf16[24,4096]{1,0:T(8,128)(2,1)}, bf16[24,4096]{1,0:T(8,128)(2,1)S(1)}, u32[]{:S(2)}, u32[]{:S(2)}) %collective-permute-start.3) | collective-permute-done | bytes 196640 | tf_op jit(solution)/shard_map/ppermute | solution.py:39
  29.3 21.6 %collective-permute-done.5 = bf16[896,128]{1,0:T(8,128)(2,1)S(1)} collective-permute-done((bf16[896,128]{1,0:T(8,128)(2,1)S(1)}, bf16[896,128]{1,0:T(8,128)(2,1)S(1)}, u32[]{:S(2)}, u32[]{:S(2)}) %collective-permute-start.5) | collective-permute-done | bytes 229408 | tf_op jit(solution)/shard_map/ppermute | solution.py:43
  50.9 1.7 pad_maximum_fusion.3
  52.7 1.7 fusion.2
  54.7 1.5 collective-permute-start
  57.1 2.6 %collective-permute-start.8 = (bf16[2,896,128]{2,1,0:T(8,128)(2,1)S(1)}, bf16[2,896,128]{2,1,0:T(8,128)(2,1)S(1)}, u32[]{:S(2)}, u32[]{:S(2)}) collective-permute-start(bf16[2,896,128]{2,1,0:T(8,128)(2,1)S(1)} %pad_maximum_fusion.2.a0), channel_id=1, source_target_pairs={{0,24},{8,16},{16,8},{24,0},{1,25},{9,17},{17,9},{25,1},{2,26},{10... | collective-permute-start | bytes 1376264 | tf_op jit(solution)/shard_map/ppermute | solution.py:39
  60.3 3.7 %collective-permute-done = bf16[128,1024]{1,0:T(8,128)(2,1)S(1)} collective-permute-done((bf16[128,1024]{1,0:T(8,128)(2,1)S(1)}, bf16[128,1024]{1,0:T(8,128)(2,1)S(1)}, u32[]{:S(2)}, u32[]{:S(2)}) %collective-permute-start) | collective-permute-done | bytes 262176 | tf_op jit(solution)/shard_map/ppermute | solution.py:39
  64.0 1.0 collective-permute-start.2
  65.0 3.3 %collective-permute-done.1 = bf16[128,1024]{1,0:T(8,128)(2,1)} collective-permute-done((bf16[128,1024]{1,0:T(8,128)(2,1)S(1)}, bf16[128,1024]{1,0:T(8,128)(2,1)}, u32[]{:S(2)}, u32[]{:S(2)}) %collective-permute-start.1) | collective-permute-done | bytes 262176 | tf_op jit(solution)/shard_map/ppermute | solution.py:39
  70.6 1.3 constant_dynamic-slice_fusion
  71.9 1.8 %collective-permute-done.6.a0 = bf16[2,896,128]{2,1,0:T(8,128)(2,1)S(1)} collective-permute-done((bf16[2,896,128]{2,1,0:T(8,128)(2,1)S(1)}, bf16[2,896,128]{2,1,0:T(8,128)(2,1)S(1)}, u32[]{:S(2)}, u32[]{:S(2)}) %collective-permute-start.6) | collective-permute-done | bytes 458784 | tf_op jit(solution)/shard_map/ppermute | solution.py:39
  73.7 12.0 %collective-permute-done.8.a1 = bf16[2,896,128]{2,1,0:T(8,128)(2,1)S(1)} collective-permute-done((bf16[2,896,128]{2,1,0:T(8,128)(2,1)S(1)}, bf16[2,896,128]{2,1,0:T(8,128)(2,1)S(1)}, u32[]{:S(2)}, u32[]{:S(2)}) %collective-permute-start.8) | collective-permute-done | bytes 458784 | tf_op jit(solution)/shard_map/ppermute | solution.py:39
  85.8 1.2 pad_maximum_fusion.x_ref
  87.0 1.3 shard_map.120
  88.7 1.3 shard_map.119
  90.1 3.7 %collective-permute-start.17 = (bf16[128,896]{1,0:T(8,128)(2,1)S(1)}, bf16[128,896]{1,0:T(8,128)(2,1)S(1)}, u32[]{:S(2)}, u32[]{:S(2)}) collective-permute-start(bf16[128,896]{1,0:T(8,128)(2,1)S(1)} %get-tuple-element.51), channel_id=1, source_target_pairs={{0,128},{64,192},{128,0},{192,64},{1,129},{65,193},{129,1},{193,65... | collective-permute-start | bytes 688136 | tf_op jit(solution)/shard_map/ppermute | solution.py:39
  94.7 2.0 %collective-permute-start.14 = (bf16[128,896]{1,0:T(8,128)(2,1)S(1)}, bf16[128,896]{1,0:T(8,128)(2,1)S(1)}, u32[]{:S(2)}, u32[]{:S(2)}) collective-permute-start(bf16[128,896]{1,0:T(8,128)(2,1)S(1)} %get-tuple-element.50), channel_id=1, source_target_pairs={{0,128},{64,192},{128,0},{192,64},{1,129},{65,193},{129,1},{193,65... | collective-permute-start | bytes 688136 | tf_op jit(solution)/shard_map/ppermute | solution.py:39
  97.4 1.0 collective-permute-start.10
  98.4 8.3 %collective-permute-done.17 = bf16[128,896]{1,0:T(8,128)(2,1)S(1)} collective-permute-done((bf16[128,896]{1,0:T(8,128)(2,1)S(1)}, bf16[128,896]{1,0:T(8,128)(2,1)S(1)}, u32[]{:S(2)}, u32[]{:S(2)}) %collective-permute-start.17) | collective-permute-done | bytes 229408 | tf_op jit(solution)/shard_map/ppermute | solution.py:39
  106.8 10.9 %collective-permute-done.18 = bf16[128,896]{1,0:T(8,128)(2,1)S(1)} collective-permute-done((bf16[128,896]{1,0:T(8,128)(2,1)S(1)}, bf16[128,896]{1,0:T(8,128)(2,1)S(1)}, u32[]{:S(2)}, u32[]{:S(2)}) %collective-permute-start.18) | collective-permute-done | bytes 229408 | tf_op jit(solution)/shard_map/ppermute | solution.py:39
  117.8 9.0 %collective-permute-done.15 = bf16[128,896]{1,0:T(8,128)(2,1)S(1)} collective-permute-done((bf16[128,896]{1,0:T(8,128)(2,1)S(1)}, bf16[128,896]{1,0:T(8,128)(2,1)S(1)}, u32[]{:S(2)}, u32[]{:S(2)}) %collective-permute-start.15) | collective-permute-done | bytes 229408 | tf_op jit(solution)/shard_map/ppermute | solution.py:39
  127.5 1.6 collective-permute-start.19
  129.1 4.8 %collective-permute-start.20 = (bf16[32,2688]{1,0:T(8,128)(2,1)S(1)}, bf16[32,2688]{1,0:T(8,128)(2,1)S(1)}, u32[]{:S(2)}, u32[]{:S(2)}) collective-permute-start(bf16[32,2688]{1,0:T(8,128)(2,1)S(1)} %get-tuple-element.91), channel_id=1, source_target_pairs={{0,2},{1,3},{2,0},{3,1},{4,6},{5,7},{6,4},{7,5},{8,10},{9,11},{10,... | collective-permute-start | bytes 516104 | tf_op jit(solution)/shard_map/ppermute | solution.py:39
  134.0 12.5 %collective-permute-done.20 = bf16[32,2688]{1,0:T(8,128)(2,1)S(1)} collective-permute-done((bf16[32,2688]{1,0:T(8,128)(2,1)S(1)}, bf16[32,2688]{1,0:T(8,128)(2,1)S(1)}, u32[]{:S(2)}, u32[]{:S(2)}) %collective-permute-start.20) | collective-permute-done | bytes 172064 | tf_op jit(solution)/shard_map/ppermute | solution.py:39
  149.5 2.5 %collective-permute-start.22 = (bf16[32,1536]{1,0:T(8,128)(2,1)S(1)}, bf16[32,1536]{1,0:T(8,128)(2,1)S(1)}, u32[]{:S(2)}, u32[]{:S(2)}) collective-permute-start(bf16[32,1536]{1,0:T(8,128)(2,1)S(1)} %pad_maximum_fusion.8), channel_id=1, source_target_pairs={{0,3},{1,2},{2,1},{3,0},{4,7},{5,6},{6,5},{7,4},{8,11},{9,10},{10,... | collective-permute-start | bytes 294920 | tf_op jit(solution)/shard_map/ppermute | solution.py:39
  152.0 2.2 %collective-permute-start.23 = (bf16[32,1536]{1,0:T(8,128)(2,1)S(1)}, bf16[32,1536]{1,0:T(8,128)(2,1)S(1)}, u32[]{:S(2)}, u32[]{:S(2)}) collective-permute-start(bf16[32,1536]{1,0:T(8,128)(2,1)S(1)} %pad_maximum_fusion.8), channel_id=1, source_target_pairs={{0,2},{1,3},{2,0},{3,1},{4,6},{5,7},{6,4},{7,5},{8,10},{9,11},{10,... | collective-permute-start | bytes 294920 | tf_op jit(solution)/shard_map/ppermute | solution.py:39
  154.3 1.8 %collective-permute-done.22 = bf16[32,1536]{1,0:T(8,128)(2,1)S(1)} collective-permute-done((bf16[32,1536]{1,0:T(8,128)(2,1)S(1)}, bf16[32,1536]{1,0:T(8,128)(2,1)S(1)}, u32[]{:S(2)}, u32[]{:S(2)}) %collective-permute-start.22) | collective-permute-done | bytes 98336 | tf_op jit(solution)/shard_map/ppermute | solution.py:39
  156.1 5.0 %collective-permute-done.23 = bf16[32,1536]{1,0:T(8,128)(2,1)S(1)} collective-permute-done((bf16[32,1536]{1,0:T(8,128)(2,1)S(1)}, bf16[32,1536]{1,0:T(8,128)(2,1)S(1)}, u32[]{:S(2)}, u32[]{:S(2)}) %collective-permute-start.23) | collective-permute-done | bytes 98336 | tf_op jit(solution)/shard_map/ppermute | solution.py:39
  161.4 7.4 %convolution_convert_fusion = bf16[128,4096]{1,0:T(8,128)(2,1)} fusion(bf16[1536,4096]{1,0:T(8,128)(2,1)} %all-gather.2.cloned.1.call-done, bf16[32,1536]{1,0:T(8,128)(2,1)S(1)} %broadcast_select_fusion.8, bf16[32,1536]{1,0:T(8,128)(2,1)S(1)} %get-tuple-element.56, bf16[32,1536]{1,0:T(8,128)(2,1)S(1)} %get-tuple-element.55, ...), kind=kOutput, calls=%fused_computation.1 | convolution fusion | flops 1612709888 | bytes 14024704 | tf_op jit(solution)/shard_map/dot_general | solution.py:232
  (112 shorter events, 11.2 us)
Async XLA Ops:
  6.5 154.8 %all-gather.2.cloned.1.call-start = ((), (), s32[]{:S(2)}) async-start(), calls=%async_computation | async-start | bytes 12976128 | tf_op jit(solution)/shard_map/all_gather | solution.py:167
  8.2 44.5 %copy-start.2 = (bf16[128,4096]{1,0:T(8,128)(2,1)S(1)}, bf16[128,4096]{1,0:T(8,128)(2,1)}, u32[]{:S(2)}) copy-start(bf16[128,4096]{1,0:T(8,128)(2,1)} %param.12) | copy-start | bytes 3145732
  8.3 21.0 %collective-permute-start.4 = (bf16[896,128]{1,0:T(8,128)(2,1)S(1)}, bf16[896,128]{1,0:T(8,128)(2,1)S(1)}, u32[]{:S(2)}, u32[]{:S(2)}) collective-permute-start(bf16[896,128]{1,0:T(8,128)(2,1)S(1)} %shard_map.118), channel_id=1, source_target_pairs={{0,0},{1,8},{2,16},{3,24},{4,4},{5,12},{6,20},{7,28},{8,72},{9,64}... | collective-permute-start | bytes 688136 | tf_op jit(solution)/shard_map/ppermute | solution.py:43
  14.9 35.9 %collective-permute-start.5 = (bf16[896,128]{1,0:T(8,128)(2,1)S(1)}, bf16[896,128]{1,0:T(8,128)(2,1)S(1)}, u32[]{:S(2)}, u32[]{:S(2)}) collective-permute-start(bf16[896,128]{1,0:T(8,128)(2,1)S(1)} %shard_map.118), channel_id=1, source_target_pairs={{0,32},{1,40},{2,48},{3,56},{4,36},{5,44},{6,52},{7,60},{8,104},{9... | collective-permute-start | bytes 688136 | tf_op jit(solution)/shard_map/ppermute | solution.py:43
  19.0 10.3 %collective-permute-start.3 = (bf16[24,4096]{1,0:T(8,128)(2,1)}, bf16[24,4096]{1,0:T(8,128)(2,1)S(1)}, u32[]{:S(2)}, u32[]{:S(2)}) collective-permute-start(bf16[24,4096]{1,0:T(8,128)(2,1)} %param.16), channel_id=1, source_target_pairs={{0,32},{32,0},{1,33},{33,1},{2,34},{34,2},{3,35},{35,3},{4,36},{36... | collective-permute-start | bytes 589832 | tf_op jit(solution)/shard_map/ppermute | solution.py:39
  54.4 16.2 %copy-start.4 = (f32[128,128]{1,0:T(8,128)S(1)}, f32[128,128]{1,0:T(8,128)}, u32[]{:S(2)}) copy-start(f32[128,128]{1,0:T(8,128)} %constant.76.clone) | copy-start | bytes 196612
  54.6 13.7 %collective-permute-start.12 = (bf16[2,896,128]{2,1,0:T(8,128)(2,1)S(1)}, bf16[2,896,128]{2,1,0:T(8,128)(2,1)S(1)}, u32[]{:S(2)}, u32[]{:S(2)}) collective-permute-start(bf16[2,896,128]{2,1,0:T(8,128)(2,1)S(1)} %pad_maximum_fusion.2.a0), channel_id=1, source_target_pairs={{0,8},{8,0},{16,24},{24,16},{1,9},{9,1},{17,25},{25,17},{2,10},{10... | collective-permute-start | bytes 1376264 | tf_op jit(solution)/shard_map/ppermute | solution.py:39
  54.7 9.3 %collective-permute-start = (bf16[128,1024]{1,0:T(8,128)(2,1)S(1)}, bf16[128,1024]{1,0:T(8,128)(2,1)S(1)}, u32[]{:S(2)}, u32[]{:S(2)}) collective-permute-start(bf16[128,1024]{1,0:T(8,128)(2,1)S(1)} %pad_maximum_fusion.4), channel_id=1, source_target_pairs={{0,64},{64,0},{128,192},{192,128},{1,65},{65,1},{129,193},{193,129... | collective-permute-start | bytes 786440 | tf_op jit(solution)/shard_map/ppermute | solution.py:39
  56.2 12.1 %collective-permute-start.1 = (bf16[128,1024]{1,0:T(8,128)(2,1)S(1)}, bf16[128,1024]{1,0:T(8,128)(2,1)}, u32[]{:S(2)}, u32[]{:S(2)}) collective-permute-start(bf16[128,1024]{1,0:T(8,128)(2,1)S(1)} %pad_maximum_fusion.5), channel_id=1, source_target_pairs={{0,128},{64,192},{128,0},{192,64},{1,129},{65,193},{129,1},{193,65... | collective-permute-start | bytes 786440 | tf_op jit(solution)/shard_map/ppermute | solution.py:39
  56.3 17.4 %collective-permute-start.6 = (bf16[2,896,128]{2,1,0:T(8,128)(2,1)S(1)}, bf16[2,896,128]{2,1,0:T(8,128)(2,1)S(1)}, u32[]{:S(2)}, u32[]{:S(2)}) collective-permute-start(bf16[2,896,128]{2,1,0:T(8,128)(2,1)S(1)} %pad_maximum_fusion.2.a0), channel_id=1, source_target_pairs={{0,16},{8,24},{16,0},{24,8},{1,17},{9,25},{17,1},{25,9},{2,18},{10... | collective-permute-start | bytes 1376264 | tf_op jit(solution)/shard_map/ppermute | solution.py:39
  57.1 28.7 %collective-permute-start.8 = (bf16[2,896,128]{2,1,0:T(8,128)(2,1)S(1)}, bf16[2,896,128]{2,1,0:T(8,128)(2,1)S(1)}, u32[]{:S(2)}, u32[]{:S(2)}) collective-permute-start(bf16[2,896,128]{2,1,0:T(8,128)(2,1)S(1)} %pad_maximum_fusion.2.a0), channel_id=1, source_target_pairs={{0,24},{8,16},{16,8},{24,0},{1,25},{9,17},{17,9},{25,1},{2,26},{10... | collective-permute-start | bytes 1376264 | tf_op jit(solution)/shard_map/ppermute | solution.py:39
  64.0 4.3 %copy-start.3 = (bf16[128,1024]{1,0:T(8,128)(2,1)}, bf16[128,1024]{1,0:T(8,128)(2,1)S(1)}, u32[]{:S(2)}) copy-start(bf16[128,1024]{1,0:T(8,128)(2,1)S(1)} %collective-permute-done) | copy-start | bytes 786436
  64.0 21.7 %collective-permute-start.2 = (bf16[128,1024]{1,0:T(8,128)(2,1)S(1)}, bf16[128,1024]{1,0:T(8,128)(2,1)}, u32[]{:S(2)}, u32[]{:S(2)}) collective-permute-start(bf16[128,1024]{1,0:T(8,128)(2,1)S(1)} %pad_maximum_fusion.6), channel_id=1, source_target_pairs={{0,192},{64,128},{128,64},{192,0},{1,193},{65,129},{129,65},{193,1... | collective-permute-start | bytes 786440 | tf_op jit(solution)/shard_map/ppermute | solution.py:39
  68.3 18.7 %collective-permute-start.11 = (bf16[2,896,128]{2,1,0:T(8,128)(2,1)S(1)}, bf16[2,896,128]{2,1,0:T(8,128)(2,1)S(1)}, u32[]{:S(2)}, u32[]{:S(2)}) collective-permute-start(bf16[2,896,128]{2,1,0:T(8,128)(2,1)S(1)} %pad_maximum_fusion.2.a0), channel_id=1, source_target_pairs={{0,4},{4,0},{1,5},{5,1},{2,6},{6,2},{3,7},{7,3},{8,12},{12,8},{9,1... | collective-permute-start | bytes 1376264 | tf_op jit(solution)/shard_map/ppermute | solution.py:39
  68.3 18.7 %collective-permute-start.13 = (bf16[2,896,128]{2,1,0:T(8,128)(2,1)S(1)}, bf16[2,896,128]{2,1,0:T(8,128)(2,1)S(1)}, u32[]{:S(2)}, u32[]{:S(2)}) collective-permute-start(bf16[2,896,128]{2,1,0:T(8,128)(2,1)S(1)} %collective-permute-done.12.a1), channel_id=1, source_target_pairs={{0,4},{4,0},{1,5},{5,1},{2,6},{6,2},{3,7},{7,3},{8,12},{12,8},{9,1... | collective-permute-start | bytes 1376264 | tf_op jit(solution)/shard_map/ppermute | solution.py:39
  73.7 15.0 %collective-permute-start.7 = (bf16[2,896,128]{2,1,0:T(8,128)(2,1)S(1)}, bf16[2,896,128]{2,1,0:T(8,128)(2,1)S(1)}, u32[]{:S(2)}, u32[]{:S(2)}) collective-permute-start(bf16[2,896,128]{2,1,0:T(8,128)(2,1)S(1)} %collective-permute-done.6.a0), channel_id=1, source_target_pairs={{0,4},{4,0},{1,5},{5,1},{2,6},{6,2},{3,7},{7,3},{8,12},{12,8},{9,1... | collective-permute-start | bytes 1376264 | tf_op jit(solution)/shard_map/ppermute | solution.py:39
  85.8 3.0 %collective-permute-start.9 = (bf16[2,896,128]{2,1,0:T(8,128)(2,1)S(1)}, bf16[2,896,128]{2,1,0:T(8,128)(2,1)S(1)}, u32[]{:S(2)}, u32[]{:S(2)}) collective-permute-start(bf16[2,896,128]{2,1,0:T(8,128)(2,1)S(1)} %collective-permute-done.8.a1), channel_id=1, source_target_pairs={{0,4},{4,0},{1,5},{5,1},{2,6},{6,2},{3,7},{7,3},{8,12},{12,8},{9,1... | collective-permute-start | bytes 1376264 | tf_op jit(solution)/shard_map/ppermute | solution.py:39
  88.4 6.3 %copy-start.7 = (f32[128]{0:T(128)S(1)}, f32[128]{0:T(128)}, u32[]{:S(2)}) copy-start(f32[128]{0:T(128)} %get-tuple-element.19) | copy-start | bytes 1540
  88.4 9.0 %collective-permute-start.16 = (bf16[128,896]{1,0:T(8,128)(2,1)S(1)}, bf16[128,896]{1,0:T(8,128)(2,1)S(1)}, u32[]{:S(2)}, u32[]{:S(2)}) collective-permute-start(bf16[128,896]{1,0:T(8,128)(2,1)S(1)} %get-tuple-element.48), channel_id=1, source_target_pairs={{0,64},{64,0},{128,192},{192,128},{1,65},{65,1},{129,193},{193,129... | collective-permute-start | bytes 688136 | tf_op jit(solution)/shard_map/ppermute | solution.py:39
  90.1 16.7 %collective-permute-start.17 = (bf16[128,896]{1,0:T(8,128)(2,1)S(1)}, bf16[128,896]{1,0:T(8,128)(2,1)S(1)}, u32[]{:S(2)}, u32[]{:S(2)}) collective-permute-start(bf16[128,896]{1,0:T(8,128)(2,1)S(1)} %get-tuple-element.51), channel_id=1, source_target_pairs={{0,128},{64,192},{128,0},{192,64},{1,129},{65,193},{129,1},{193,65... | collective-permute-start | bytes 688136 | tf_op jit(solution)/shard_map/ppermute | solution.py:39
  93.8 23.9 %collective-permute-start.18 = (bf16[128,896]{1,0:T(8,128)(2,1)S(1)}, bf16[128,896]{1,0:T(8,128)(2,1)S(1)}, u32[]{:S(2)}, u32[]{:S(2)}) collective-permute-start(bf16[128,896]{1,0:T(8,128)(2,1)S(1)} %get-tuple-element.52), channel_id=1, source_target_pairs={{0,192},{64,128},{128,64},{192,0},{1,193},{65,129},{129,65},{193,1... | collective-permute-start | bytes 688136 | tf_op jit(solution)/shard_map/ppermute | solution.py:39
  94.7 23.1 %collective-permute-start.14 = (bf16[128,896]{1,0:T(8,128)(2,1)S(1)}, bf16[128,896]{1,0:T(8,128)(2,1)S(1)}, u32[]{:S(2)}, u32[]{:S(2)}) collective-permute-start(bf16[128,896]{1,0:T(8,128)(2,1)S(1)} %get-tuple-element.50), channel_id=1, source_target_pairs={{0,128},{64,192},{128,0},{192,64},{1,129},{65,193},{129,1},{193,65... | collective-permute-start | bytes 688136 | tf_op jit(solution)/shard_map/ppermute | solution.py:39
  96.6 30.2 %collective-permute-start.15 = (bf16[128,896]{1,0:T(8,128)(2,1)S(1)}, bf16[128,896]{1,0:T(8,128)(2,1)S(1)}, u32[]{:S(2)}, u32[]{:S(2)}) collective-permute-start(bf16[128,896]{1,0:T(8,128)(2,1)S(1)} %get-tuple-element.49), channel_id=1, source_target_pairs={{0,192},{64,128},{128,64},{192,0},{1,193},{65,129},{129,65},{193,1... | collective-permute-start | bytes 688136 | tf_op jit(solution)/shard_map/ppermute | solution.py:39
  97.4 29.5 %collective-permute-start.10 = (bf16[128,896]{1,0:T(8,128)(2,1)S(1)}, bf16[128,896]{1,0:T(8,128)(2,1)S(1)}, u32[]{:S(2)}, u32[]{:S(2)}) collective-permute-start(bf16[128,896]{1,0:T(8,128)(2,1)S(1)} %get-tuple-element.53), channel_id=1, source_target_pairs={{0,64},{64,0},{128,192},{192,128},{1,65},{65,1},{129,193},{193,129... | collective-permute-start | bytes 688136 | tf_op jit(solution)/shard_map/ppermute | solution.py:39
  127.2 6.7 %copy-start.9 = (s32[32]{0:T(128)S(1)}, s32[32]{0:T(128)}, u32[]{:S(2)}) copy-start(s32[32]{0:T(128)} %iota_add_fusion) | copy-start | bytes 388
  127.2 6.7 %copy-start.10 = (pred[128]{0:T(512)(128)(4,1)S(1)}, pred[128]{0:T(512)(128)(4,1)}, u32[]{:S(2)}) copy-start(pred[128]{0:T(512)(128)(4,1)} %iota_compare_fusion.2) | copy-start | bytes 388
  127.5 6.5 %collective-permute-start.19 = (bf16[32,2688]{1,0:T(8,128)(2,1)S(1)}, bf16[32,2688]{1,0:T(8,128)(2,1)S(1)}, u32[]{:S(2)}, u32[]{:S(2)}) collective-permute-start(bf16[32,2688]{1,0:T(8,128)(2,1)S(1)} %get-tuple-element.90), channel_id=1, source_target_pairs={{0,1},{1,0},{2,3},{3,2},{4,5},{5,4},{6,7},{7,6},{8,9},{9,8},{10,11... | collective-permute-start | bytes 516104 | tf_op jit(solution)/shard_map/ppermute | solution.py:39
  129.1 17.4 %collective-permute-start.20 = (bf16[32,2688]{1,0:T(8,128)(2,1)S(1)}, bf16[32,2688]{1,0:T(8,128)(2,1)S(1)}, u32[]{:S(2)}, u32[]{:S(2)}) collective-permute-start(bf16[32,2688]{1,0:T(8,128)(2,1)S(1)} %get-tuple-element.91), channel_id=1, source_target_pairs={{0,2},{1,3},{2,0},{3,1},{4,6},{5,7},{6,4},{7,5},{8,10},{9,11},{10,... | collective-permute-start | bytes 516104 | tf_op jit(solution)/shard_map/ppermute | solution.py:39
  133.9 12.6 %collective-permute-start.21 = (bf16[32,2688]{1,0:T(8,128)(2,1)S(1)}, bf16[32,2688]{1,0:T(8,128)(2,1)S(1)}, u32[]{:S(2)}, u32[]{:S(2)}) collective-permute-start(bf16[32,2688]{1,0:T(8,128)(2,1)S(1)} %get-tuple-element.92), channel_id=1, source_target_pairs={{0,3},{1,2},{2,1},{3,0},{4,7},{5,6},{6,5},{7,4},{8,11},{9,10},{10,... | collective-permute-start | bytes 516104 | tf_op jit(solution)/shard_map/ppermute | solution.py:39
  149.5 6.7 %collective-permute-start.22 = (bf16[32,1536]{1,0:T(8,128)(2,1)S(1)}, bf16[32,1536]{1,0:T(8,128)(2,1)S(1)}, u32[]{:S(2)}, u32[]{:S(2)}) collective-permute-start(bf16[32,1536]{1,0:T(8,128)(2,1)S(1)} %pad_maximum_fusion.8), channel_id=1, source_target_pairs={{0,3},{1,2},{2,1},{3,0},{4,7},{5,6},{6,5},{7,4},{8,11},{9,10},{10,... | collective-permute-start | bytes 294920 | tf_op jit(solution)/shard_map/ppermute | solution.py:39
  152.0 9.2 %collective-permute-start.23 = (bf16[32,1536]{1,0:T(8,128)(2,1)S(1)}, bf16[32,1536]{1,0:T(8,128)(2,1)S(1)}, u32[]{:S(2)}, u32[]{:S(2)}) collective-permute-start(bf16[32,1536]{1,0:T(8,128)(2,1)S(1)} %pad_maximum_fusion.8), channel_id=1, source_target_pairs={{0,2},{1,3},{2,0},{3,1},{4,6},{5,7},{6,4},{7,5},{8,10},{9,11},{10,... | collective-permute-start | bytes 294920 | tf_op jit(solution)/shard_map/ppermute | solution.py:39
  154.2 7.0 %collective-permute-start.24 = (bf16[32,1536]{1,0:T(8,128)(2,1)S(1)}, bf16[32,1536]{1,0:T(8,128)(2,1)S(1)}, u32[]{:S(2)}, u32[]{:S(2)}) collective-permute-start(bf16[32,1536]{1,0:T(8,128)(2,1)S(1)} %pad_maximum_fusion.8), channel_id=1, source_target_pairs={{0,1},{1,0},{2,3},{3,2},{4,5},{5,4},{6,7},{7,6},{8,9},{9,8},{10,11... | collective-permute-start | bytes 294920 | tf_op jit(solution)/shard_map/ppermute | solution.py:39
  (7 other events, 7.3 us)
Sparse Core Ops, SparseCore 0:
  52.7 91.6 all-gather.1

commit v4 on v3

--- a/solution.py
+++ b/solution.py
@@ -105,43 +105,37 @@
     )(query_weight, kv_turned)
 
 
-def project_kernel(x_ref, a0, b0, a1, b1, out_ref, own_ref):
-    q_columns = []
-    kv_rows = []
-    for pair in ((a0, b0), (a1, b1)):
-        for h in range(3):
-            q_columns.append(
-                jnp.concatenate([ref[a, 256 * h : 256 * h + 256, :] for ref in pair for a in (0, 1)], axis=0)
-            )
-        kv_rows.append(
-            jnp.concatenate(
-                [ref[a, 768 + 64 * h : 832 + 64 * h, :] for ref in pair for a in (0, 1) for h in (0, 1)], axis=1
-            )
-        )
+def project_kernel(x_ref, here_ref, there_ref, out_ref, own_ref):
     inputs = x_ref[...]
-    q = jnp.dot(inputs, jnp.concatenate(q_columns, axis=1), preferred_element_type=F32)
+    for slot, ref in enumerate((here_ref, there_ref)):
+        heads = [
+            jnp.concatenate([ref[d, 256 * h : 256 * h + 256, :] for d in range(4)], axis=0) for h in range(3)
+        ]
+        q = jnp.dot(inputs, jnp.concatenate(heads, axis=1), preferred_element_type=F32)
+        own_ref[:, 384 * slot : 384 * slot + 384] = q[:ROWS]
+        for e in (1, 2, 3):
+            out_ref[e - 1, :, 384 * slot : 384 * slot + 384] = q[ROWS * e : ROWS * e + ROWS].astype(BF)
+    kv_rows = [
+        jnp.concatenate([ref[d, 768 + 64 * h : 832 + 64 * h, :] for d in range(4) for h in (0, 1)], axis=1)
+        for ref in (here_ref, there_ref)
+    ]
     kv = lax.dot_general(
         inputs, jnp.concatenate(kv_rows, axis=0), (((1,), (1,)), ((), ())), preferred_element_type=F32
     )
-    own_ref[:, :768] = q[:ROWS]
     own_ref[:, 768:] = kv[:ROWS]
     for e in (1, 2, 3):
-        at = ROWS * e
-        for half in (0, 1):
-            to = half ^ (e & 1)
-            out_ref[e - 1, :, 384 * to : 384 * to + 384] = q[at : at + ROWS, 384 * half : 384 * half + 384].astype(BF)
-            out_ref[e - 1, :, 768 + 64 * to : 832 + 64 * to] = kv[at : at + ROWS, 64 * half : 64 * half + 64].astype(BF)
-
-
-def project(inputs, first, second):
+        out_ref[e - 1, :, 768:] = kv[ROWS * e : ROWS * e + ROWS].astype(BF)
+
+
+def project(inputs, here, there):
     return pl.pallas_call(
         project_kernel,
         out_shape=(jax.ShapeDtypeStruct((3, ROWS, 896), BF), jax.ShapeDtypeStruct((ROWS, 896), F32)),
-        in_specs=[whole(0)] * 5,
+        in_specs=[whole(0)] * 3,
         out_specs=(whole(0),) * 2,
         compiler_params=pltpu.CompilerParams(vmem_limit_bytes=32 * 2**20),
         cost_estimate=pl.CostEstimate(flops=2 * 512 * 1024 * 896, bytes_accessed=4000000, transcendentals=0),
-    )(inputs, *first, *second)
+    )(inputs, here, there)
 
 
 def attend(query, keys, values, limit, first):
@@ -160,42 +154,41 @@
     y, zh, x, c, t = (lax.axis_index(name) for name in AXES)
 
     packed = pack(query_weight, kv_weight.T)
-    near = move(packed, lambda y, zh, x, c, t: (x ^ y, zh, t ^ x, c, y))
-    far = move(packed, lambda y, zh, x, c, t: (x ^ y, zh ^ 1, t ^ x, c, y))
-    wo_other, near, far = lax.optimization_barrier((swap(out_weight, "zh", 1), near, far))
-    wo_piece = jnp.concatenate([out_weight, wo_other], axis=0)
-    wo = lax.all_gather(wo_piece, ("y", "x", "core"), axis=0, tiled=True)
-
-    mine = jnp.stack([near, far])
-    blocks = [mine] + [swap(mine, "x", d) for d in (1, 2, 3)]
-    pairs = [(block, swap(block, "core", 1)) for block in blocks]
+    first = move(packed, lambda y, zh, x, c, t: ((2 * zh + c) ^ y, t & 1, x, t >> 1, y))
+    wo_other = swap(out_weight, "zh", 1)
 
     widened = tokens.astype(F32)
     squares = jnp.sum(widened * widened, axis=1)
     gained = (widened * norm_gain[None, :]).astype(BF)
 
-    def features(d):
-        s = y ^ d ^ t
+    def features(e):
+        s = y ^ e ^ t
         picked = [
-            lax.dynamic_slice(gained, (0, (((zh ^ a) * 4 + s) * 2 + (c ^ b)) * 256), (ROWS, 256))
-            for b in (0, 1)
-            for a in (0, 1)
+            lax.dynamic_slice(gained, (0, (((s >> 1) * 4 + (x ^ d)) * 2 + (s & 1)) * 256), (ROWS, 256))
+            for d in range(4)
         ]
         return jnp.concatenate(picked, axis=1)
 
-    inputs = jnp.concatenate([features(0)] + [swap(features(d), "y", d) for d in (1, 2, 3)], axis=0)
-
-    sent_a, own_a = project(inputs, pairs[0], pairs[1])
-    sent_b, own_b = project(inputs, pairs[2], pairs[3])
-    got_a = [swap(sent_a[d - 1], "y", d) for d in (1, 2, 3)]
-    got_b = [swap(sent_b[d - 1], "y", d) for d in (1, 2, 3)]
-    summed = [
-        own + sum(part.astype(F32) for part in parts)
-        for own, parts in ((own_a, (got_a[0], got_b[1], got_b[2])), (own_b, (got_b[0], got_a[1], got_a[2])))
-    ]
-    base = x ^ y ^ t
-    q_sum = jnp.concatenate(by_index([half[:, at : at + 384] for half in summed for at in (0, 384)], base), axis=1)
-    kv_sum = jnp.concatenate(by_index([half[:, at : at + 64] for half in summed for at in (768, 832)], base), axis=1)
+    ring = [swap(features(e), "y", e) for e in (1, 2, 3)]
+    first, wo_other, packed, *ring = lax.optimization_barrier((first, wo_other, packed, *ring))
+    second = move(packed, lambda y, zh, x, c, t: ((2 * zh + c) ^ y, 1 - (t & 1), x, t >> 1, y))
+    inputs = jnp.concatenate([features(0)] + ring, axis=0)
+
+    wo_piece = jnp.concatenate([out_weight, wo_other], axis=0)
+    wo = lax.all_gather(wo_piece, ("y", "x", "core"), axis=0, tiled=True)
+
+    summed = []
+    for block in (first, second):
+        here = jnp.stack([block] + [swap(block, "x", d) for d in (1, 2, 3)])
+        sent, total = project(inputs, here, swap(here, "core", 1))
+        for e in (1, 2, 3):
+            total = total + swap(sent[e - 1], "y", e).astype(F32)
+        summed.append(total)
+    base = 2 * c + zh
+    q_slots = [half[:, at : at + 384] for at in (0, 384) for half in summed]
+    kv_slots = [half[:, at : at + 64] for at in (768, 832) for half in summed]
+    q_sum = jnp.concatenate(by_index(q_slots, base), axis=1)
+    kv_sum = jnp.concatenate(by_index(kv_slots, base), axis=1)
 
     kv_short = kv_sum.astype(BF)
     high = lax.reduce_precision(squares, 8, 7)

time: 176 us -> 171 us (0.972)
  waiting for transfers between devices: 99 us -> 77.4 us
  starting transfers between devices: 38.6 us -> 60 us
  local copies, waits for them, and re-layouts: 4.12 us -> 1.08 us
  other arithmetic: 7.94 us -> 5.37 us
    ppermute x2, waiting for transfers between devices: 21.6 us -> 4.15 us  [move(): lax.ppermute(value, AXES, [(flat(*at), flat(*where(*at))) for at in every...]
    ppermute x23 -> x24, starting transfers between devices: 27.8 us -> 41.9 us  [swap(): return lax.ppermute(value, axis, [(i, i ^ d) for i in range(n)])]
    ppermute x2, starting transfers between devices: 10.7 us -> 18.1 us  [move(): lax.ppermute(value, AXES, [(flat(*at), flat(*where(*at))) for at in every...]
    ppermute x23 -> x24, waiting for transfers between devices: 77.3 us -> 73.3 us  [swap(): return lax.ppermute(value, axis, [(i, i ^ d) for i in range(n)])]
    unnamed x36 -> x24, local copies, waits for them, and re-layouts: 1.91 us -> 0.12 us
  transfers between devices with their start and end apart: 26 -> 27, of which waited for: 12 -> 14; matrix products, arithmetic and copies ran while one was open for 6% -> 3% of each run, Pallas kernels for 2% -> 2%
where the time goes in v4:
time: 171 us; the launch traced here: 170 us
  waiting for transfers between devices  77.4 us (45%)
  starting transfers between devices  60 us (35%)
  between operations  14.6 us (9%)
  matrix products  8.59 us (5%)
  other arithmetic  5.37 us (3%)
  Pallas kernels  3.08 us (2%)
    ppermute x24, waiting for transfers between devices, swap(): return lax.ppermute(value, axis, [(i, i ^ d) for i in range(n)])  73.3 us
    ppermute x24, starting transfers between devices, swap(): return lax.ppermute(value, axis, [(i, i ^ d) for i in range(n)])  41.9 us
    ppermute x2, starting transfers between devices, move(): lax.ppermute(value, AXES, [(flat(*at), flat(*where(*at))) for at in every...  18.1 us
    dot_general x1, matrix products, body(): return jnp.dot(all_rows, wo, preferred_element_type=F32).astype(BF)  7.35 us
    ppermute x2, waiting for transfers between devices, move(): lax.ppermute(value, AXES, [(flat(*at), flat(*where(*at))) for at in every...  4.15 us
  transfers between devices with their start and end apart: 27, of which 14 were waited for; matrix products, arithmetic and copies ran while one was open for 3% of the time, Pallas kernels for 2%

profile of v4, /device:TPU:24, one launch (start us, length us, event | category | flops | bytes accessed | tf_op | source)
XLA Modules:
  0.0 170.2 jit_solution(13398455325984211264)
XLA Ops:
  6.5 1.6 fusion.2
  8.4 2.0 %collective-permute-start.4 = (bf16[128,1024]{1,0:T(8,128)(2,1)S(1)}, bf16[128,1024]{1,0:T(8,128)(2,1)S(1)}, u32[]{:S(2)}, u32[]{:S(2)}) collective-permute-start(bf16[128,1024]{1,0:T(8,128)(2,1)S(1)} %pad_maximum_fusion.7), channel_id=1, source_target_pairs={{0,192},{64,128},{128,64},{192,0},{1,193},{65,129},{129,65},{193,1... | collective-permute-start | bytes 786440 | tf_op jit(solution)/shard_map/ppermute | solution.py:39
  11.5 1.4 collective-permute-start.2
  12.9 6.5 %collective-permute-start = (bf16[896,128]{1,0:T(8,128)(2,1)S(1)}, bf16[896,128]{1,0:T(8,128)(2,1)S(1)}, u32[]{:S(2)}, u32[]{:S(2)}) collective-permute-start(bf16[896,128]{1,0:T(8,128)(2,1)S(1)} %shard_map.118), channel_id=1, source_target_pairs={{0,0},{1,32},{2,4},{3,36},{4,64},{5,96},{6,68},{7,100},{8,8},{9,40... | collective-permute-start | bytes 688136 | tf_op jit(solution)/shard_map/ppermute | solution.py:43
  19.4 3.4 %collective-permute-start.1 = (bf16[24,4096]{1,0:T(8,128)(2,1)S(1)}, bf16[24,4096]{1,0:T(8,128)(2,1)S(1)}, u32[]{:S(2)}, u32[]{:S(2)}) collective-permute-start(bf16[24,4096]{1,0:T(8,128)(2,1)S(1)} %copy-done.2), channel_id=1, source_target_pairs={{0,32},{32,0},{1,33},{33,1},{2,34},{34,2},{3,35},{35,3},{4,36},{36... | collective-permute-start | bytes 589832 | tf_op jit(solution)/shard_map/ppermute | solution.py:39
  22.9 7.9 %collective-permute-done.1 = bf16[24,4096]{1,0:T(8,128)(2,1)S(1)} collective-permute-done((bf16[24,4096]{1,0:T(8,128)(2,1)S(1)}, bf16[24,4096]{1,0:T(8,128)(2,1)S(1)}, u32[]{:S(2)}, u32[]{:S(2)}) %collective-permute-start.1) | collective-permute-done | bytes 196640 | tf_op jit(solution)/shard_map/ppermute | solution.py:39
  31.6 11.5 %collective-permute-start.5 = (bf16[896,128]{1,0:T(8,128)(2,1)S(1)}, bf16[896,128]{1,0:T(8,128)(2,1)S(1)}, u32[]{:S(2)}, u32[]{:S(2)}) collective-permute-start(bf16[896,128]{1,0:T(8,128)(2,1)S(1)} %shard_map.118), channel_id=1, source_target_pairs={{0,32},{1,0},{2,36},{3,4},{4,96},{5,64},{6,100},{7,68},{8,40},{9,8... | collective-permute-start | bytes 688136 | tf_op jit(solution)/shard_map/ppermute | solution.py:43
  43.1 1.6 collective-permute-start.13
  44.7 2.7 %collective-permute-start.14 = (bf16[896,128]{1,0:T(8,128)(2,1)S(1)}, bf16[896,128]{1,0:T(8,128)(2,1)S(1)}, u32[]{:S(2)}, u32[]{:S(2)}) collective-permute-start(bf16[896,128]{1,0:T(8,128)(2,1)S(1)} %collective-permute-done), channel_id=1, source_target_pairs={{0,16},{8,24},{16,0},{24,8},{1,17},{9,25},{17,1},{25,9},{2,18},{10... | collective-permute-start | bytes 688136 | tf_op jit(solution)/shard_map/ppermute | solution.py:39
  47.9 4.1 %collective-permute-done.5 = bf16[896,128]{1,0:T(8,128)(2,1)S(1)} collective-permute-done((bf16[896,128]{1,0:T(8,128)(2,1)S(1)}, bf16[896,128]{1,0:T(8,128)(2,1)S(1)}, u32[]{:S(2)}, u32[]{:S(2)}) %collective-permute-start.5) | collective-permute-done | bytes 229408 | tf_op jit(solution)/shard_map/ppermute | solution.py:43
  52.1 1.5 collective-permute-start.6
  53.6 2.7 %collective-permute-start.7 = (bf16[896,128]{1,0:T(8,128)(2,1)S(1)}, bf16[896,128]{1,0:T(8,128)(2,1)}, u32[]{:S(2)}, u32[]{:S(2)}) collective-permute-start(bf16[896,128]{1,0:T(8,128)(2,1)S(1)} %collective-permute-done.5), channel_id=1, source_target_pairs={{0,16},{8,24},{16,0},{24,8},{1,17},{9,25},{17,1},{25,9},{2,18},{10... | collective-permute-start | bytes 688136 | tf_op jit(solution)/shard_map/ppermute | solution.py:39
  56.8 2.0 %collective-permute-done.14 = bf16[896,128]{1,0:T(8,128)(2,1)S(1)} collective-permute-done((bf16[896,128]{1,0:T(8,128)(2,1)S(1)}, bf16[896,128]{1,0:T(8,128)(2,1)S(1)}, u32[]{:S(2)}, u32[]{:S(2)}) %collective-permute-start.14) | collective-permute-done | bytes 229408 | tf_op jit(solution)/shard_map/ppermute | solution.py:39
  58.8 6.4 %collective-permute-done.15 = bf16[896,128]{1,0:T(8,128)(2,1)S(1)} collective-permute-done((bf16[896,128]{1,0:T(8,128)(2,1)S(1)}, bf16[896,128]{1,0:T(8,128)(2,1)S(1)}, u32[]{:S(2)}, u32[]{:S(2)}) %collective-permute-start.15) | collective-permute-done | bytes 229408 | tf_op jit(solution)/shard_map/ppermute | solution.py:39
  66.2 8.5 %collective-permute-done.7 = bf16[896,128]{1,0:T(8,128)(2,1)} collective-permute-done((bf16[896,128]{1,0:T(8,128)(2,1)S(1)}, bf16[896,128]{1,0:T(8,128)(2,1)}, u32[]{:S(2)}, u32[]{:S(2)}) %collective-permute-start.7) | collective-permute-done | bytes 229408 | tf_op jit(solution)/shard_map/ppermute | solution.py:39
  74.6 2.6 %collective-permute-done.8 = bf16[896,128]{1,0:T(8,128)(2,1)} collective-permute-done((bf16[896,128]{1,0:T(8,128)(2,1)S(1)}, bf16[896,128]{1,0:T(8,128)(2,1)}, u32[]{:S(2)}, u32[]{:S(2)}) %collective-permute-start.8) | collective-permute-done | bytes 229408 | tf_op jit(solution)/shard_map/ppermute | solution.py:39
  78.6 1.5 shard_map.120
  80.5 3.6 %collective-permute-start.18 = (bf16[128,896]{1,0:T(8,128)(2,1)S(1)}, bf16[128,896]{1,0:T(8,128)(2,1)S(1)}, u32[]{:S(2)}, u32[]{:S(2)}) collective-permute-start(bf16[128,896]{1,0:T(8,128)(2,1)S(1)} %get-tuple-element.56), channel_id=1, source_target_pairs={{0,128},{64,192},{128,0},{192,64},{1,129},{65,193},{129,1},{193,65... | collective-permute-start | bytes 688136 | tf_op jit(solution)/shard_map/ppermute | solution.py:39
  85.1 1.5 shard_map.119
  87.1 3.4 %collective-permute-start.11 = (bf16[128,896]{1,0:T(8,128)(2,1)S(1)}, bf16[128,896]{1,0:T(8,128)(2,1)S(1)}, u32[]{:S(2)}, u32[]{:S(2)}) collective-permute-start(bf16[128,896]{1,0:T(8,128)(2,1)S(1)} %get-tuple-element.59), channel_id=1, source_target_pairs={{0,128},{64,192},{128,0},{192,64},{1,129},{65,193},{129,1},{193,65... | collective-permute-start | bytes 688136 | tf_op jit(solution)/shard_map/ppermute | solution.py:39
  90.5 4.3 %collective-permute-start.12 = (bf16[128,896]{1,0:T(8,128)(2,1)S(1)}, bf16[128,896]{1,0:T(8,128)(2,1)S(1)}, u32[]{:S(2)}, u32[]{:S(2)}) collective-permute-start(bf16[128,896]{1,0:T(8,128)(2,1)S(1)} %get-tuple-element.58), channel_id=1, source_target_pairs={{0,192},{64,128},{128,64},{192,0},{1,193},{65,129},{129,65},{193,1... | collective-permute-start | bytes 688136 | tf_op jit(solution)/shard_map/ppermute | solution.py:39
  94.9 8.1 %collective-permute-done.18 = bf16[128,896]{1,0:T(8,128)(2,1)S(1)} collective-permute-done((bf16[128,896]{1,0:T(8,128)(2,1)S(1)}, bf16[128,896]{1,0:T(8,128)(2,1)S(1)}, u32[]{:S(2)}, u32[]{:S(2)}) %collective-permute-start.18) | collective-permute-done | bytes 229408 | tf_op jit(solution)/shard_map/ppermute | solution.py:39
  103.7 6.2 %collective-permute-done.10 = bf16[128,896]{1,0:T(8,128)(2,1)S(1)} collective-permute-done((bf16[128,896]{1,0:T(8,128)(2,1)S(1)}, bf16[128,896]{1,0:T(8,128)(2,1)S(1)}, u32[]{:S(2)}, u32[]{:S(2)}) %collective-permute-start.10) | collective-permute-done | bytes 229408 | tf_op jit(solution)/shard_map/ppermute | solution.py:39
  109.9 12.5 %collective-permute-done.11 = bf16[128,896]{1,0:T(8,128)(2,1)S(1)} collective-permute-done((bf16[128,896]{1,0:T(8,128)(2,1)S(1)}, bf16[128,896]{1,0:T(8,128)(2,1)S(1)}, u32[]{:S(2)}, u32[]{:S(2)}) %collective-permute-start.11) | collective-permute-done | bytes 229408 | tf_op jit(solution)/shard_map/ppermute | solution.py:39
  123.0 3.7 %collective-permute-start.20 = (bf16[32,2688]{1,0:T(8,128)(2,1)S(1)}, bf16[32,2688]{1,0:T(8,128)(2,1)S(1)}, u32[]{:S(2)}, u32[]{:S(2)}) collective-permute-start(bf16[32,2688]{1,0:T(8,128)(2,1)S(1)} %get-tuple-element.96), channel_id=1, source_target_pairs={{0,1},{1,0},{2,3},{3,2},{4,5},{5,4},{6,7},{7,6},{8,9},{9,8},{10,11... | collective-permute-start | bytes 516104 | tf_op jit(solution)/shard_map/ppermute | solution.py:39
  126.7 2.5 %collective-permute-start.22 = (bf16[32,2688]{1,0:T(8,128)(2,1)S(1)}, bf16[32,2688]{1,0:T(8,128)(2,1)S(1)}, u32[]{:S(2)}, u32[]{:S(2)}) collective-permute-start(bf16[32,2688]{1,0:T(8,128)(2,1)S(1)} %get-tuple-element.98), channel_id=1, source_target_pairs={{0,3},{1,2},{2,1},{3,0},{4,7},{5,6},{6,5},{7,4},{8,11},{9,10},{10,... | collective-permute-start | bytes 516104 | tf_op jit(solution)/shard_map/ppermute | solution.py:39
  129.2 2.3 %collective-permute-done.20 = bf16[32,2688]{1,0:T(8,128)(2,1)S(1)} collective-permute-done((bf16[32,2688]{1,0:T(8,128)(2,1)S(1)}, bf16[32,2688]{1,0:T(8,128)(2,1)S(1)}, u32[]{:S(2)}, u32[]{:S(2)}) %collective-permute-start.20) | collective-permute-done | bytes 172064 | tf_op jit(solution)/shard_map/ppermute | solution.py:39
  131.5 8.7 %collective-permute-done.21 = bf16[32,2688]{1,0:T(8,128)(2,1)S(1)} collective-permute-done((bf16[32,2688]{1,0:T(8,128)(2,1)S(1)}, bf16[32,2688]{1,0:T(8,128)(2,1)S(1)}, u32[]{:S(2)}, u32[]{:S(2)}) %collective-permute-start.21) | collective-permute-done | bytes 172064 | tf_op jit(solution)/shard_map/ppermute | solution.py:39
  144.1 4.2 %collective-permute-start.24 = (bf16[32,1536]{1,0:T(8,128)(2,1)S(1)}, bf16[32,1536]{1,0:T(8,128)(2,1)S(1)}, u32[]{:S(2)}, u32[]{:S(2)}) collective-permute-start(bf16[32,1536]{1,0:T(8,128)(2,1)S(1)} %pad_maximum_fusion.9), channel_id=1, source_target_pairs={{0,2},{1,3},{2,0},{3,1},{4,6},{5,7},{6,4},{7,5},{8,10},{9,11},{10,... | collective-permute-start | bytes 294920 | tf_op jit(solution)/shard_map/ppermute | solution.py:39
  148.3 1.3 collective-permute-done.23
  149.6 6.2 %collective-permute-done.24 = bf16[32,1536]{1,0:T(8,128)(2,1)S(1)} collective-permute-done((bf16[32,1536]{1,0:T(8,128)(2,1)S(1)}, bf16[32,1536]{1,0:T(8,128)(2,1)S(1)}, u32[]{:S(2)}, u32[]{:S(2)}) %collective-permute-start.24) | collective-permute-done | bytes 98336 | tf_op jit(solution)/shard_map/ppermute | solution.py:39
  156.0 7.4 %convolution_convert_fusion = bf16[128,4096]{1,0:T(8,128)(2,1)} fusion(bf16[1536,4096]{1,0:T(8,128)(2,1)} %all-gather.2.cloned.1.call-done, bf16[32,1536]{1,0:T(8,128)(2,1)S(1)} %broadcast_select_fusion.8, bf16[32,1536]{1,0:T(8,128)(2,1)S(1)} %get-tuple-element.62, bf16[32,1536]{1,0:T(8,128)(2,1)S(1)} %get-tuple-element.61, ...), kind=kOutput, calls=%fused_computation.1 | convolution fusion | flops 1612709888 | bytes 14024704 | tf_op jit(solution)/shard_map/dot_general | solution.py:225
  (103 shorter events, 11.6 us)
Async XLA Ops:
  6.5 149.5 %all-gather.2.cloned.1.call-start = ((), (), s32[]{:S(2)}) async-start(), calls=%async_computation | async-start | bytes 12976128 | tf_op jit(solution)/shard_map/all_gather | solution.py:178
  8.2 4.7 %copy-start = (bf16[256,384]{1,0:T(8,128)(2,1)S(1)}, bf16[256,384]{1,0:T(8,128)(2,1)}, u32[]{:S(2)}) copy-start(bf16[256,384]{1,0:T(8,128)(2,1)} %q_ref.1) | copy-start | bytes 589828
  8.2 4.7 %copy-start.1 = (bf16[256,64]{0,1:T(8,128)(2,1)S(1)}, bf16[256,64]{0,1:T(8,128)(2,1)}, u32[]{:S(2)}) copy-start(bf16[256,64]{0,1:T(8,128)(2,1)} %param.15) | copy-start | bytes 98308
  8.2 11.2 %copy-start.2 = (bf16[24,4096]{1,0:T(8,128)(2,1)S(1)}, bf16[24,4096]{1,0:T(8,128)(2,1)}, u32[]{:S(2)}) copy-start(bf16[24,4096]{1,0:T(8,128)(2,1)} %param.16) | copy-start | bytes 589828
  8.4 22.3 %collective-permute-start.4 = (bf16[128,1024]{1,0:T(8,128)(2,1)S(1)}, bf16[128,1024]{1,0:T(8,128)(2,1)S(1)}, u32[]{:S(2)}, u32[]{:S(2)}) collective-permute-start(bf16[128,1024]{1,0:T(8,128)(2,1)S(1)} %pad_maximum_fusion.7), channel_id=1, source_target_pairs={{0,192},{64,128},{128,64},{192,0},{1,193},{65,129},{129,65},{193,1... | collective-permute-start | bytes 786440 | tf_op jit(solution)/shard_map/ppermute | solution.py:39
  10.5 20.2 %collective-permute-start.3 = (bf16[128,1024]{1,0:T(8,128)(2,1)S(1)}, bf16[128,1024]{1,0:T(8,128)(2,1)S(1)}, u32[]{:S(2)}, u32[]{:S(2)}) collective-permute-start(bf16[128,1024]{1,0:T(8,128)(2,1)S(1)} %pad_maximum_fusion.6), channel_id=1, source_target_pairs={{0,128},{64,192},{128,0},{192,64},{1,129},{65,193},{129,1},{193,65... | collective-permute-start | bytes 786440 | tf_op jit(solution)/shard_map/ppermute | solution.py:39
  11.5 19.3 %collective-permute-start.2 = (bf16[128,1024]{1,0:T(8,128)(2,1)S(1)}, bf16[128,1024]{1,0:T(8,128)(2,1)S(1)}, u32[]{:S(2)}, u32[]{:S(2)}) collective-permute-start(bf16[128,1024]{1,0:T(8,128)(2,1)S(1)} %pad_maximum_fusion.5), channel_id=1, source_target_pairs={{0,64},{64,0},{128,192},{192,128},{1,65},{65,1},{129,193},{193,129... | collective-permute-start | bytes 786440 | tf_op jit(solution)/shard_map/ppermute | solution.py:39
  12.9 17.9 %collective-permute-start = (bf16[896,128]{1,0:T(8,128)(2,1)S(1)}, bf16[896,128]{1,0:T(8,128)(2,1)S(1)}, u32[]{:S(2)}, u32[]{:S(2)}) collective-permute-start(bf16[896,128]{1,0:T(8,128)(2,1)S(1)} %shard_map.118), channel_id=1, source_target_pairs={{0,0},{1,32},{2,4},{3,36},{4,64},{5,96},{6,68},{7,100},{8,8},{9,40... | collective-permute-start | bytes 688136 | tf_op jit(solution)/shard_map/ppermute | solution.py:43
  19.4 11.3 %collective-permute-start.1 = (bf16[24,4096]{1,0:T(8,128)(2,1)S(1)}, bf16[24,4096]{1,0:T(8,128)(2,1)S(1)}, u32[]{:S(2)}, u32[]{:S(2)}) collective-permute-start(bf16[24,4096]{1,0:T(8,128)(2,1)S(1)} %copy-done.2), channel_id=1, source_target_pairs={{0,32},{32,0},{1,33},{33,1},{2,34},{34,2},{3,35},{35,3},{4,36},{36... | collective-permute-start | bytes 589832 | tf_op jit(solution)/shard_map/ppermute | solution.py:39
  31.5 46.9 %copy-start.3 = (f32[128,128]{1,0:T(8,128)S(1)}, f32[128,128]{1,0:T(8,128)}, u32[]{:S(2)}) copy-start(f32[128,128]{1,0:T(8,128)} %constant.76.clone) | copy-start | bytes 196612
  31.5 46.9 %copy-start.4 = (f32[128,128]{1,0:T(8,128)S(1)}, f32[128,128]{1,0:T(8,128)}, u32[]{:S(2)}) copy-start(f32[128,128]{1,0:T(8,128)} %constant.77.clone) | copy-start | bytes 196612
  31.6 20.5 %collective-permute-start.5 = (bf16[896,128]{1,0:T(8,128)(2,1)S(1)}, bf16[896,128]{1,0:T(8,128)(2,1)S(1)}, u32[]{:S(2)}, u32[]{:S(2)}) collective-permute-start(bf16[896,128]{1,0:T(8,128)(2,1)S(1)} %shard_map.118), channel_id=1, source_target_pairs={{0,32},{1,0},{2,36},{3,4},{4,96},{5,64},{6,100},{7,68},{8,40},{9,8... | collective-permute-start | bytes 688136 | tf_op jit(solution)/shard_map/ppermute | solution.py:43
  43.1 13.2 %collective-permute-start.13 = (bf16[896,128]{1,0:T(8,128)(2,1)S(1)}, bf16[896,128]{1,0:T(8,128)(2,1)S(1)}, u32[]{:S(2)}, u32[]{:S(2)}) collective-permute-start(bf16[896,128]{1,0:T(8,128)(2,1)S(1)} %collective-permute-done), channel_id=1, source_target_pairs={{0,8},{8,0},{16,24},{24,16},{1,9},{9,1},{17,25},{25,17},{2,10},{10... | collective-permute-start | bytes 688136 | tf_op jit(solution)/shard_map/ppermute | solution.py:39
  44.7 14.1 %collective-permute-start.14 = (bf16[896,128]{1,0:T(8,128)(2,1)S(1)}, bf16[896,128]{1,0:T(8,128)(2,1)S(1)}, u32[]{:S(2)}, u32[]{:S(2)}) collective-permute-start(bf16[896,128]{1,0:T(8,128)(2,1)S(1)} %collective-permute-done), channel_id=1, source_target_pairs={{0,16},{8,24},{16,0},{24,8},{1,17},{9,25},{17,1},{25,9},{2,18},{10... | collective-permute-start | bytes 688136 | tf_op jit(solution)/shard_map/ppermute | solution.py:39
  47.4 17.8 %collective-permute-start.15 = (bf16[896,128]{1,0:T(8,128)(2,1)S(1)}, bf16[896,128]{1,0:T(8,128)(2,1)S(1)}, u32[]{:S(2)}, u32[]{:S(2)}) collective-permute-start(bf16[896,128]{1,0:T(8,128)(2,1)S(1)} %collective-permute-done), channel_id=1, source_target_pairs={{0,24},{8,16},{16,8},{24,0},{1,25},{9,17},{17,9},{25,1},{2,26},{10... | collective-permute-start | bytes 688136 | tf_op jit(solution)/shard_map/ppermute | solution.py:39
  52.1 14.1 %collective-permute-start.6 = (bf16[896,128]{1,0:T(8,128)(2,1)S(1)}, bf16[896,128]{1,0:T(8,128)(2,1)S(1)}, u32[]{:S(2)}, u32[]{:S(2)}) collective-permute-start(bf16[896,128]{1,0:T(8,128)(2,1)S(1)} %collective-permute-done.5), channel_id=1, source_target_pairs={{0,8},{8,0},{16,24},{24,16},{1,9},{9,1},{17,25},{25,17},{2,10},{10... | collective-permute-start | bytes 688136 | tf_op jit(solution)/shard_map/ppermute | solution.py:39
  53.6 21.1 %collective-permute-start.7 = (bf16[896,128]{1,0:T(8,128)(2,1)S(1)}, bf16[896,128]{1,0:T(8,128)(2,1)}, u32[]{:S(2)}, u32[]{:S(2)}) collective-permute-start(bf16[896,128]{1,0:T(8,128)(2,1)S(1)} %collective-permute-done.5), channel_id=1, source_target_pairs={{0,16},{8,24},{16,0},{24,8},{1,17},{9,25},{17,1},{25,9},{2,18},{10... | collective-permute-start | bytes 688136 | tf_op jit(solution)/shard_map/ppermute | solution.py:39
  56.3 20.9 %collective-permute-start.8 = (bf16[896,128]{1,0:T(8,128)(2,1)S(1)}, bf16[896,128]{1,0:T(8,128)(2,1)}, u32[]{:S(2)}, u32[]{:S(2)}) collective-permute-start(bf16[896,128]{1,0:T(8,128)(2,1)S(1)} %collective-permute-done.5), channel_id=1, source_target_pairs={{0,24},{8,16},{16,8},{24,0},{1,25},{9,17},{17,9},{25,1},{2,26},{10... | collective-permute-start | bytes 688136 | tf_op jit(solution)/shard_map/ppermute | solution.py:39
  65.3 13.3 %collective-permute-start.16 = (bf16[4,896,128]{2,1,0:T(8,128)(2,1)S(1)}, bf16[4,896,128]{2,1,0:T(8,128)(2,1)S(1)}, u32[]{:S(2)}, u32[]{:S(2)}) collective-permute-start(bf16[4,896,128]{2,1,0:T(8,128)(2,1)S(1)} %pad_maximum_fusion.2.here_ref), channel_id=1, source_target_pairs={{0,4},{4,0},{1,5},{5,1},{2,6},{6,2},{3,7},{7,3},{8,12},{12,8},{9,1... | collective-permute-start | bytes 2752520 | tf_op jit(solution)/shard_map/ppermute | solution.py:39
  78.4 6.7 %collective-permute-start.9 = (bf16[4,896,128]{2,1,0:T(8,128)(2,1)S(1)}, bf16[4,896,128]{2,1,0:T(8,128)(2,1)S(1)}, u32[]{:S(2)}, u32[]{:S(2)}) collective-permute-start(bf16[4,896,128]{2,1,0:T(8,128)(2,1)S(1)} %pad_maximum_fusion.1.here_ref), channel_id=1, source_target_pairs={{0,4},{4,0},{1,5},{5,1},{2,6},{6,2},{3,7},{7,3},{8,12},{12,8},{9,1... | collective-permute-start | bytes 2752520 | tf_op jit(solution)/shard_map/ppermute | solution.py:39
  80.2 10.3 %collective-permute-start.17 = (bf16[128,896]{1,0:T(8,128)(2,1)S(1)}, bf16[128,896]{1,0:T(8,128)(2,1)S(1)}, u32[]{:S(2)}, u32[]{:S(2)}) collective-permute-start(bf16[128,896]{1,0:T(8,128)(2,1)S(1)} %get-tuple-element.54), channel_id=1, source_target_pairs={{0,64},{64,0},{128,192},{192,128},{1,65},{65,1},{129,193},{193,129... | collective-permute-start | bytes 688136 | tf_op jit(solution)/shard_map/ppermute | solution.py:39
  80.5 22.5 %collective-permute-start.18 = (bf16[128,896]{1,0:T(8,128)(2,1)S(1)}, bf16[128,896]{1,0:T(8,128)(2,1)S(1)}, u32[]{:S(2)}, u32[]{:S(2)}) collective-permute-start(bf16[128,896]{1,0:T(8,128)(2,1)S(1)} %get-tuple-element.56), channel_id=1, source_target_pairs={{0,128},{64,192},{128,0},{192,64},{1,129},{65,193},{129,1},{193,65... | collective-permute-start | bytes 688136 | tf_op jit(solution)/shard_map/ppermute | solution.py:39
  84.1 19.4 %collective-permute-start.19 = (bf16[128,896]{1,0:T(8,128)(2,1)S(1)}, bf16[128,896]{1,0:T(8,128)(2,1)S(1)}, u32[]{:S(2)}, u32[]{:S(2)}) collective-permute-start(bf16[128,896]{1,0:T(8,128)(2,1)S(1)} %get-tuple-element.55), channel_id=1, source_target_pairs={{0,192},{64,128},{128,64},{192,0},{1,193},{65,129},{129,65},{193,1... | collective-permute-start | bytes 688136 | tf_op jit(solution)/shard_map/ppermute | solution.py:39
  86.7 23.2 %collective-permute-start.10 = (bf16[128,896]{1,0:T(8,128)(2,1)S(1)}, bf16[128,896]{1,0:T(8,128)(2,1)S(1)}, u32[]{:S(2)}, u32[]{:S(2)}) collective-permute-start(bf16[128,896]{1,0:T(8,128)(2,1)S(1)} %get-tuple-element.57), channel_id=1, source_target_pairs={{0,64},{64,0},{128,192},{192,128},{1,65},{65,1},{129,193},{193,129... | collective-permute-start | bytes 688136 | tf_op jit(solution)/shard_map/ppermute | solution.py:39
  87.1 35.2 %collective-permute-start.11 = (bf16[128,896]{1,0:T(8,128)(2,1)S(1)}, bf16[128,896]{1,0:T(8,128)(2,1)S(1)}, u32[]{:S(2)}, u32[]{:S(2)}) collective-permute-start(bf16[128,896]{1,0:T(8,128)(2,1)S(1)} %get-tuple-element.59), channel_id=1, source_target_pairs={{0,128},{64,192},{128,0},{192,64},{1,129},{65,193},{129,1},{193,65... | collective-permute-start | bytes 688136 | tf_op jit(solution)/shard_map/ppermute | solution.py:39
  90.5 31.8 %collective-permute-start.12 = (bf16[128,896]{1,0:T(8,128)(2,1)S(1)}, bf16[128,896]{1,0:T(8,128)(2,1)S(1)}, u32[]{:S(2)}, u32[]{:S(2)}) collective-permute-start(bf16[128,896]{1,0:T(8,128)(2,1)S(1)} %get-tuple-element.58), channel_id=1, source_target_pairs={{0,192},{64,128},{128,64},{192,0},{1,193},{65,129},{129,65},{193,1... | collective-permute-start | bytes 688136 | tf_op jit(solution)/shard_map/ppermute | solution.py:39
  123.0 8.5 %collective-permute-start.20 = (bf16[32,2688]{1,0:T(8,128)(2,1)S(1)}, bf16[32,2688]{1,0:T(8,128)(2,1)S(1)}, u32[]{:S(2)}, u32[]{:S(2)}) collective-permute-start(bf16[32,2688]{1,0:T(8,128)(2,1)S(1)} %get-tuple-element.96), channel_id=1, source_target_pairs={{0,1},{1,0},{2,3},{3,2},{4,5},{5,4},{6,7},{7,6},{8,9},{9,8},{10,11... | collective-permute-start | bytes 516104 | tf_op jit(solution)/shard_map/ppermute | solution.py:39
  126.7 13.5 %collective-permute-start.21 = (bf16[32,2688]{1,0:T(8,128)(2,1)S(1)}, bf16[32,2688]{1,0:T(8,128)(2,1)S(1)}, u32[]{:S(2)}, u32[]{:S(2)}) collective-permute-start(bf16[32,2688]{1,0:T(8,128)(2,1)S(1)} %get-tuple-element.97), channel_id=1, source_target_pairs={{0,2},{1,3},{2,0},{3,1},{4,6},{5,7},{6,4},{7,5},{8,10},{9,11},{10,... | collective-permute-start | bytes 516104 | tf_op jit(solution)/shard_map/ppermute | solution.py:39
  126.7 13.5 %collective-permute-start.22 = (bf16[32,2688]{1,0:T(8,128)(2,1)S(1)}, bf16[32,2688]{1,0:T(8,128)(2,1)S(1)}, u32[]{:S(2)}, u32[]{:S(2)}) collective-permute-start(bf16[32,2688]{1,0:T(8,128)(2,1)S(1)} %get-tuple-element.98), channel_id=1, source_target_pairs={{0,3},{1,2},{2,1},{3,0},{4,7},{5,6},{6,5},{7,4},{8,11},{9,10},{10,... | collective-permute-start | bytes 516104 | tf_op jit(solution)/shard_map/ppermute | solution.py:39
  143.0 6.6 %collective-permute-start.23 = (bf16[32,1536]{1,0:T(8,128)(2,1)S(1)}, bf16[32,1536]{1,0:T(8,128)(2,1)S(1)}, u32[]{:S(2)}, u32[]{:S(2)}) collective-permute-start(bf16[32,1536]{1,0:T(8,128)(2,1)S(1)} %pad_maximum_fusion.9), channel_id=1, source_target_pairs={{0,3},{1,2},{2,1},{3,0},{4,7},{5,6},{6,5},{7,4},{8,11},{9,10},{10,... | collective-permute-start | bytes 294920 | tf_op jit(solution)/shard_map/ppermute | solution.py:39
  144.1 11.8 %collective-permute-start.24 = (bf16[32,1536]{1,0:T(8,128)(2,1)S(1)}, bf16[32,1536]{1,0:T(8,128)(2,1)S(1)}, u32[]{:S(2)}, u32[]{:S(2)}) collective-permute-start(bf16[32,1536]{1,0:T(8,128)(2,1)S(1)} %pad_maximum_fusion.9), channel_id=1, source_target_pairs={{0,2},{1,3},{2,0},{3,1},{4,6},{5,7},{6,4},{7,5},{8,10},{9,11},{10,... | collective-permute-start | bytes 294920 | tf_op jit(solution)/shard_map/ppermute | solution.py:39
  148.3 7.5 %collective-permute-start.25 = (bf16[32,1536]{1,0:T(8,128)(2,1)S(1)}, bf16[32,1536]{1,0:T(8,128)(2,1)S(1)}, u32[]{:S(2)}, u32[]{:S(2)}) collective-permute-start(bf16[32,1536]{1,0:T(8,128)(2,1)S(1)} %pad_maximum_fusion.9), channel_id=1, source_target_pairs={{0,1},{1,0},{2,3},{3,2},{4,5},{5,4},{6,7},{7,6},{8,9},{9,8},{10,11... | collective-permute-start | bytes 294920 | tf_op jit(solution)/shard_map/ppermute | solution.py:39
  (2 other events, 3.1 us)
Sparse Core Ops, SparseCore 0:
  31.7 101.6 all-gather.1

commit v5 on v4

--- a/solution.py
+++ b/solution.py
@@ -138,6 +138,26 @@
     )(inputs, here, there)
 
 
+def mix_kernel(x_ref, w_ref, out_ref):
+    out_ref[...] = jnp.dot(x_ref[...], w_ref[...], preferred_element_type=F32).astype(BF)
+
+
+def mix(attended, weight):
+    columns = weight.shape[1]
+    return pl.pallas_call(
+        mix_kernel,
+        out_shape=jax.ShapeDtypeStruct((ROWS, columns), BF),
+        grid=(columns // 512,),
+        in_specs=[
+            pl.BlockSpec((ROWS, 1536), lambda i: (0, 0)),
+            pl.BlockSpec((1536, 512), lambda i: (0, i)),
+        ],
+        out_specs=pl.BlockSpec((ROWS, 512), lambda i: (0, i)),
+        compiler_params=pltpu.CompilerParams(vmem_limit_bytes=32 * 2**20),
+        cost_estimate=pl.CostEstimate(flops=2 * ROWS * 1536 * columns, bytes_accessed=14000000, transcendentals=0),
+    )(attended, weight)
+
+
 def attend(query, keys, values, limit, first):
     scores = jnp.einsum("qhd,kd->hqk", query, keys, preferred_element_type=F32) * HD ** (-0.5)
     keys_at = jnp.arange(ROWS, dtype=jnp.int32)
@@ -155,7 +175,6 @@
 
     packed = pack(query_weight, kv_weight.T)
     first = move(packed, lambda y, zh, x, c, t: ((2 * zh + c) ^ y, t & 1, x, t >> 1, y))
-    wo_other = swap(out_weight, "zh", 1)
 
     widened = tokens.astype(F32)
     squares = jnp.sum(widened * widened, axis=1)
@@ -170,16 +189,19 @@
         return jnp.concatenate(picked, axis=1)
 
     ring = [swap(features(e), "y", e) for e in (1, 2, 3)]
-    first, wo_other, packed, *ring = lax.optimization_barrier((first, wo_other, packed, *ring))
+    first, packed, out_weight, *ring = lax.optimization_barrier((first, packed, out_weight, *ring))
     second = move(packed, lambda y, zh, x, c, t: ((2 * zh + c) ^ y, 1 - (t & 1), x, t >> 1, y))
     inputs = jnp.concatenate([features(0)] + ring, axis=0)
 
+    wo_other = swap(out_weight, "zh", 1)
+    first_blocks = [first] + [swap(first, "x", d) for d in (1, 2, 3)]
+    wo_other, second, *first_blocks = lax.optimization_barrier((wo_other, second, *first_blocks))
     wo_piece = jnp.concatenate([out_weight, wo_other], axis=0)
     wo = lax.all_gather(wo_piece, ("y", "x", "core"), axis=0, tiled=True)
 
     summed = []
-    for block in (first, second):
-        here = jnp.stack([block] + [swap(block, "x", d) for d in (1, 2, 3)])
+    for blocks in (first_blocks, [second] + [swap(second, "x", d) for d in (1, 2, 3)]):
+        here = jnp.stack(blocks)
         sent, total = project(inputs, here, swap(here, "core", 1))
         for e in (1, 2, 3):
             total = total + swap(sent[e - 1], "y", e).astype(F32)
@@ -222,7 +244,7 @@
 
     got = [attended] + [swap(attended, "zl", d) for d in (1, 2, 3)]
     all_rows = jnp.concatenate(by_index(got, t), axis=0)
-    return jnp.dot(all_rows, wo, preferred_element_type=F32).astype(BF)
+    return mix(all_rows, wo)
 
 
 def solution(mesh):

time: 171 us -> 162 us (0.947)
  matrix products: 8.59 us -> 1.25 us
  waiting for transfers between devices: 77.4 us -> 71.3 us
  Pallas kernels: 3.08 us -> 8.27 us
  local copies, waits for them, and re-layouts: 1.08 us -> 5.65 us
  starting transfers between devices: 60 us -> 55.7 us
    ppermute x24, waiting for transfers between devices: 73.3 us -> 61.2 us  [swap(): return lax.ppermute(value, axis, [(i, i ^ d) for i in range(n)])]
    dot_general x1 -> x0, matrix products: 7.35 us -> none  [body(): return jnp.dot(all_rows, wo, preferred_element_type=F32).astype(BF)]
    ppermute x2, waiting for transfers between devices: 4.15 us -> 10.1 us  [move(): lax.ppermute(value, AXES, [(flat(*at), flat(*where(*at))) for at in every...]
    pallas_call x0 -> x1, Pallas kernels: none -> 5.19 us  [mix(): pl.pallas_call(mix_kernel, out_shape=jax.ShapeDtypeStruct((ROWS, columns)...]
    unnamed x24 -> x26, local copies, waits for them, and re-layouts: 0.12 us -> 4.69 us
    ppermute x24, starting transfers between devices: 41.9 us -> 37.5 us  [swap(): return lax.ppermute(value, axis, [(i, i ^ d) for i in range(n)])]
  transfers between devices with their start and end apart: 27 -> 27, of which waited for: 14 -> 16; matrix products, arithmetic and copies ran while one was open for 3% -> 3% of each run, Pallas kernels for 2% -> 2%
where the time goes in v5:
time: 162 us
  waiting for transfers between devices  71.3 us (44%)
  starting transfers between devices  55.7 us (34%)
  between operations  14.7 us (9%)
  Pallas kernels  8.27 us (5%)
  local copies, waits for them, and re-layouts  5.65 us (3%)
  other arithmetic  5.4 us (3%)
    ppermute x24, waiting for transfers between devices, swap(): return lax.ppermute(value, axis, [(i, i ^ d) for i in range(n)])  61.2 us
    ppermute x24, starting transfers between devices, swap(): return lax.ppermute(value, axis, [(i, i ^ d) for i in range(n)])  37.5 us
    ppermute x2, starting transfers between devices, move(): lax.ppermute(value, AXES, [(flat(*at), flat(*where(*at))) for at in every...  18.2 us
    ppermute x2, waiting for transfers between devices, move(): lax.ppermute(value, AXES, [(flat(*at), flat(*where(*at))) for at in every...  10.1 us
    pallas_call x1, Pallas kernels, mix(): pl.pallas_call(mix_kernel, out_shape=jax.ShapeDtypeStruct((ROWS, columns)...  5.19 us
    unnamed x26, local copies, waits for them, and re-layouts  4.69 us
  transfers between devices with their start and end apart: 27, of which 16 were waited for; matrix products, arithmetic and copies ran while one was open for 3% of the time, Pallas kernels for 2%

profile of v5, /device:TPU:24, one launch (start us, length us, event | category | flops | bytes accessed | tf_op | source)
XLA Modules:
  0.0 162.2 jit_solution(10691496920850533119)
XLA Ops:
  6.5 1.6 fusion.2
  8.4 2.0 %collective-permute-start.3 = (bf16[128,1024]{1,0:T(8,128)(2,1)S(1)}, bf16[128,1024]{1,0:T(8,128)(2,1)S(1)}, u32[]{:S(2)}, u32[]{:S(2)}) collective-permute-start(bf16[128,1024]{1,0:T(8,128)(2,1)S(1)} %pad_maximum_fusion.8), channel_id=1, source_target_pairs={{0,192},{64,128},{128,64},{192,0},{1,193},{65,129},{129,65},{193,1... | collective-permute-start | bytes 786440 | tf_op jit(solution)/shard_map/ppermute | solution.py:39
  11.5 1.4 collective-permute-start.1
  12.9 6.5 %collective-permute-start = (bf16[896,128]{1,0:T(8,128)(2,1)S(1)}, bf16[896,128]{1,0:T(8,128)(2,1)S(1)}, u32[]{:S(2)}, u32[]{:S(2)}) collective-permute-start(bf16[896,128]{1,0:T(8,128)(2,1)S(1)} %shard_map.118), channel_id=1, source_target_pairs={{0,0},{1,32},{2,4},{3,36},{4,64},{5,96},{6,68},{7,100},{8,8},{9,40... | collective-permute-start | bytes 688136 | tf_op jit(solution)/shard_map/ppermute | solution.py:43
  19.4 8.7 %collective-permute-done = bf16[896,128]{1,0:T(8,128)(2,1)S(1)} collective-permute-done((bf16[896,128]{1,0:T(8,128)(2,1)S(1)}, bf16[896,128]{1,0:T(8,128)(2,1)S(1)}, u32[]{:S(2)}, u32[]{:S(2)}) %collective-permute-start) | collective-permute-done | bytes 229408 | tf_op jit(solution)/shard_map/ppermute | solution.py:43
  28.3 11.7 %collective-permute-start.5 = (bf16[896,128]{1,0:T(8,128)(2,1)S(1)}, bf16[896,128]{1,0:T(8,128)(2,1)S(1)}, u32[]{:S(2)}, u32[]{:S(2)}) collective-permute-start(bf16[896,128]{1,0:T(8,128)(2,1)S(1)} %shard_map.118), channel_id=1, source_target_pairs={{0,32},{1,0},{2,36},{3,4},{4,96},{5,64},{6,100},{7,68},{8,40},{9,8... | collective-permute-start | bytes 688136 | tf_op jit(solution)/shard_map/ppermute | solution.py:43
  40.0 1.6 collective-permute-start.6
  41.6 2.7 %collective-permute-start.7 = (bf16[896,128]{1,0:T(8,128)(2,1)S(1)}, bf16[896,128]{1,0:T(8,128)(2,1)S(1)}, u32[]{:S(2)}, u32[]{:S(2)}) collective-permute-start(bf16[896,128]{1,0:T(8,128)(2,1)S(1)} %collective-permute-done), channel_id=1, source_target_pairs={{0,16},{8,24},{16,0},{24,8},{1,17},{9,25},{17,1},{25,9},{2,18},{10... | collective-permute-start | bytes 688136 | tf_op jit(solution)/shard_map/ppermute | solution.py:39
  44.8 10.6 %collective-permute-done.4 = bf16[24,4096]{1,0:T(8,128)(2,1)S(1)} collective-permute-done((bf16[24,4096]{1,0:T(8,128)(2,1)S(1)}, bf16[24,4096]{1,0:T(8,128)(2,1)S(1)}, u32[]{:S(2)}, u32[]{:S(2)}) %collective-permute-start.4) | collective-permute-done | bytes 196640 | tf_op jit(solution)/shard_map/ppermute | solution.py:39
  55.4 1.4 collective-permute-done.5
  57.8 1.5 collective-permute-start.9
  59.3 2.7 %collective-permute-start.10 = (bf16[896,128]{1,0:T(8,128)(2,1)S(1)}, bf16[896,128]{1,0:T(8,128)(2,1)}, u32[]{:S(2)}, u32[]{:S(2)}) collective-permute-start(bf16[896,128]{1,0:T(8,128)(2,1)S(1)} %collective-permute-done.5), channel_id=1, source_target_pairs={{0,16},{8,24},{16,0},{24,8},{1,17},{9,25},{17,1},{25,9},{2,18},{10... | collective-permute-start | bytes 688136 | tf_op jit(solution)/shard_map/ppermute | solution.py:39
  63.5 2.9 %collective-permute-done.9 = bf16[896,128]{1,0:T(8,128)(2,1)S(1)} collective-permute-done((bf16[896,128]{1,0:T(8,128)(2,1)S(1)}, bf16[896,128]{1,0:T(8,128)(2,1)S(1)}, u32[]{:S(2)}, u32[]{:S(2)}) %collective-permute-start.9) | collective-permute-done | bytes 229408 | tf_op jit(solution)/shard_map/ppermute | solution.py:39
  66.3 6.3 %collective-permute-done.10 = bf16[896,128]{1,0:T(8,128)(2,1)} collective-permute-done((bf16[896,128]{1,0:T(8,128)(2,1)S(1)}, bf16[896,128]{1,0:T(8,128)(2,1)}, u32[]{:S(2)}, u32[]{:S(2)}) %collective-permute-start.10) | collective-permute-done | bytes 229408 | tf_op jit(solution)/shard_map/ppermute | solution.py:39
  72.6 3.1 %collective-permute-done.11 = bf16[896,128]{1,0:T(8,128)(2,1)} collective-permute-done((bf16[896,128]{1,0:T(8,128)(2,1)S(1)}, bf16[896,128]{1,0:T(8,128)(2,1)}, u32[]{:S(2)}, u32[]{:S(2)}) %collective-permute-start.11) | collective-permute-done | bytes 229408 | tf_op jit(solution)/shard_map/ppermute | solution.py:39
  77.2 1.5 shard_map.120
  78.8 6.8 %collective-permute-start.17 = (bf16[128,896]{1,0:T(8,128)(2,1)S(1)}, bf16[128,896]{1,0:T(8,128)(2,1)S(1)}, u32[]{:S(2)}, u32[]{:S(2)}) collective-permute-start(bf16[128,896]{1,0:T(8,128)(2,1)S(1)} %get-tuple-element.66), channel_id=1, source_target_pairs={{0,64},{64,0},{128,192},{192,128},{1,65},{65,1},{129,193},{193,129... | collective-permute-start | bytes 688136 | tf_op jit(solution)/shard_map/ppermute | solution.py:39
  85.6 2.4 %collective-permute-start.18 = (bf16[128,896]{1,0:T(8,128)(2,1)S(1)}, bf16[128,896]{1,0:T(8,128)(2,1)S(1)}, u32[]{:S(2)}, u32[]{:S(2)}) collective-permute-start(bf16[128,896]{1,0:T(8,128)(2,1)S(1)} %get-tuple-element.68), channel_id=1, source_target_pairs={{0,128},{64,192},{128,0},{192,64},{1,129},{65,193},{129,1},{193,65... | collective-permute-start | bytes 688136 | tf_op jit(solution)/shard_map/ppermute | solution.py:39
  88.3 1.5 shard_map.119
  90.7 3.6 %collective-permute-start.14 = (bf16[128,896]{1,0:T(8,128)(2,1)S(1)}, bf16[128,896]{1,0:T(8,128)(2,1)S(1)}, u32[]{:S(2)}, u32[]{:S(2)}) collective-permute-start(bf16[128,896]{1,0:T(8,128)(2,1)S(1)} %get-tuple-element.71), channel_id=1, source_target_pairs={{0,128},{64,192},{128,0},{192,64},{1,129},{65,193},{129,1},{193,65... | collective-permute-start | bytes 688136 | tf_op jit(solution)/shard_map/ppermute | solution.py:39
  94.9 4.4 %collective-permute-done.18 = bf16[128,896]{1,0:T(8,128)(2,1)S(1)} collective-permute-done((bf16[128,896]{1,0:T(8,128)(2,1)S(1)}, bf16[128,896]{1,0:T(8,128)(2,1)S(1)}, u32[]{:S(2)}, u32[]{:S(2)}) %collective-permute-start.18) | collective-permute-done | bytes 229408 | tf_op jit(solution)/shard_map/ppermute | solution.py:39
  99.3 3.3 %collective-permute-done.19 = bf16[128,896]{1,0:T(8,128)(2,1)S(1)} collective-permute-done((bf16[128,896]{1,0:T(8,128)(2,1)S(1)}, bf16[128,896]{1,0:T(8,128)(2,1)S(1)}, u32[]{:S(2)}, u32[]{:S(2)}) %collective-permute-start.19) | collective-permute-done | bytes 229408 | tf_op jit(solution)/shard_map/ppermute | solution.py:39
  102.6 11.1 %collective-permute-done.14 = bf16[128,896]{1,0:T(8,128)(2,1)S(1)} collective-permute-done((bf16[128,896]{1,0:T(8,128)(2,1)S(1)}, bf16[128,896]{1,0:T(8,128)(2,1)S(1)}, u32[]{:S(2)}, u32[]{:S(2)}) %collective-permute-start.14) | collective-permute-done | bytes 229408 | tf_op jit(solution)/shard_map/ppermute | solution.py:39
  113.7 2.1 %collective-permute-done.15 = bf16[128,896]{1,0:T(8,128)(2,1)S(1)} collective-permute-done((bf16[128,896]{1,0:T(8,128)(2,1)S(1)}, bf16[128,896]{1,0:T(8,128)(2,1)S(1)}, u32[]{:S(2)}, u32[]{:S(2)}) %collective-permute-start.15) | collective-permute-done | bytes 229408 | tf_op jit(solution)/shard_map/ppermute | solution.py:39
  117.6 3.3 %collective-permute-start.22 = (bf16[32,2688]{1,0:T(8,128)(2,1)S(1)}, bf16[32,2688]{1,0:T(8,128)(2,1)S(1)}, u32[]{:S(2)}, u32[]{:S(2)}) collective-permute-start(bf16[32,2688]{1,0:T(8,128)(2,1)S(1)} %get-tuple-element.110), channel_id=1, source_target_pairs={{0,3},{1,2},{2,1},{3,0},{4,7},{5,6},{6,5},{7,4},{8,11},{9,10},{10,... | collective-permute-start | bytes 516104 | tf_op jit(solution)/shard_map/ppermute | solution.py:39
  122.2 8.9 %collective-permute-done.21 = bf16[32,2688]{1,0:T(8,128)(2,1)S(1)} collective-permute-done((bf16[32,2688]{1,0:T(8,128)(2,1)S(1)}, bf16[32,2688]{1,0:T(8,128)(2,1)S(1)}, u32[]{:S(2)}, u32[]{:S(2)}) %collective-permute-start.21) | collective-permute-done | bytes 172064 | tf_op jit(solution)/shard_map/ppermute | solution.py:39
  134.0 1.9 %collective-permute-start.23 = (bf16[32,1536]{1,0:T(8,128)(2,1)S(1)}, bf16[32,1536]{1,0:T(8,128)(2,1)S(1)}, u32[]{:S(2)}, u32[]{:S(2)}) collective-permute-start(bf16[32,1536]{1,0:T(8,128)(2,1)S(1)} %pad_maximum_fusion.10), channel_id=1, source_target_pairs={{0,3},{1,2},{2,1},{3,0},{4,7},{5,6},{6,5},{7,4},{8,11},{9,10},{10,... | collective-permute-start | bytes 294920 | tf_op jit(solution)/shard_map/ppermute | solution.py:39
  135.9 2.0 %collective-permute-start.24 = (bf16[32,1536]{1,0:T(8,128)(2,1)S(1)}, bf16[32,1536]{1,0:T(8,128)(2,1)S(1)}, u32[]{:S(2)}, u32[]{:S(2)}) collective-permute-start(bf16[32,1536]{1,0:T(8,128)(2,1)S(1)} %pad_maximum_fusion.10), channel_id=1, source_target_pairs={{0,2},{1,3},{2,0},{3,1},{4,6},{5,7},{6,4},{7,5},{8,10},{9,11},{10,... | collective-permute-start | bytes 294920 | tf_op jit(solution)/shard_map/ppermute | solution.py:39
  138.5 2.2 %collective-permute-done.23 = bf16[32,1536]{1,0:T(8,128)(2,1)S(1)} collective-permute-done((bf16[32,1536]{1,0:T(8,128)(2,1)S(1)}, bf16[32,1536]{1,0:T(8,128)(2,1)S(1)}, u32[]{:S(2)}, u32[]{:S(2)}) %collective-permute-start.23) | collective-permute-done | bytes 98336 | tf_op jit(solution)/shard_map/ppermute | solution.py:39
  140.7 4.7 %collective-permute-done.24 = bf16[32,1536]{1,0:T(8,128)(2,1)S(1)} collective-permute-done((bf16[32,1536]{1,0:T(8,128)(2,1)S(1)}, bf16[32,1536]{1,0:T(8,128)(2,1)S(1)}, u32[]{:S(2)}, u32[]{:S(2)}) %collective-permute-start.24) | collective-permute-done | bytes 98336 | tf_op jit(solution)/shard_map/ppermute | solution.py:39
  145.6 4.6 %copy-done = bf16[1536,4096]{1,0:T(8,128)(2,1)S(1)} copy-done((bf16[1536,4096]{1,0:T(8,128)(2,1)S(1)}, bf16[1536,4096]{1,0:T(8,128)(2,1)}, u32[]{:S(2)}) %copy-start) | copy-done | bytes 12582936
  150.2 5.2 %shard_map.121 = bf16[128,4096]{1,0:T(8,128)(2,1)} custom-call(bf16[128,1536]{1,0:T(8,128)(2,1)S(1)} %pad_maximum_fusion.4.x_ref, bf16[1536,4096]{1,0:T(8,128)(2,1)S(1)} %copy-done), custom_call_target="tpu_custom_call" | custom-call | flops 1610612736 | bytes 14000000 | tf_op jit(solution)/shard_map/pallas_call | solution.py:147
  (106 shorter events, 13.3 us)
Async XLA Ops:
  6.5 139.1 %all-gather.2.cloned.1.call-start = ((), (), s32[]{:S(2)}) async-start(), calls=%async_computation | async-start | bytes 12976128 | tf_op jit(solution)/shard_map/all_gather | solution.py:200
  8.2 4.7 %copy-start.1 = (bf16[256,384]{1,0:T(8,128)(2,1)S(1)}, bf16[256,384]{1,0:T(8,128)(2,1)}, u32[]{:S(2)}) copy-start(bf16[256,384]{1,0:T(8,128)(2,1)} %q_ref.1) | copy-start | bytes 589828
  8.2 4.7 %copy-start.2 = (bf16[256,64]{0,1:T(8,128)(2,1)S(1)}, bf16[256,64]{0,1:T(8,128)(2,1)}, u32[]{:S(2)}) copy-start(bf16[256,64]{0,1:T(8,128)(2,1)} %param.15) | copy-start | bytes 98308
  8.2 36.6 %copy-start.3 = (bf16[24,4096]{1,0:T(8,128)(2,1)S(1)}, bf16[24,4096]{1,0:T(8,128)(2,1)}, u32[]{:S(2)}) copy-start(bf16[24,4096]{1,0:T(8,128)(2,1)} %param.16) | copy-start | bytes 589828
  8.4 19.9 %collective-permute-start.3 = (bf16[128,1024]{1,0:T(8,128)(2,1)S(1)}, bf16[128,1024]{1,0:T(8,128)(2,1)S(1)}, u32[]{:S(2)}, u32[]{:S(2)}) collective-permute-start(bf16[128,1024]{1,0:T(8,128)(2,1)S(1)} %pad_maximum_fusion.8), channel_id=1, source_target_pairs={{0,192},{64,128},{128,64},{192,0},{1,193},{65,129},{129,65},{193,1... | collective-permute-start | bytes 786440 | tf_op jit(solution)/shard_map/ppermute | solution.py:39
  10.5 17.8 %collective-permute-start.2 = (bf16[128,1024]{1,0:T(8,128)(2,1)S(1)}, bf16[128,1024]{1,0:T(8,128)(2,1)S(1)}, u32[]{:S(2)}, u32[]{:S(2)}) collective-permute-start(bf16[128,1024]{1,0:T(8,128)(2,1)S(1)} %pad_maximum_fusion.7), channel_id=1, source_target_pairs={{0,128},{64,192},{128,0},{192,64},{1,129},{65,193},{129,1},{193,65... | collective-permute-start | bytes 786440 | tf_op jit(solution)/shard_map/ppermute | solution.py:39
  11.5 16.8 %collective-permute-start.1 = (bf16[128,1024]{1,0:T(8,128)(2,1)S(1)}, bf16[128,1024]{1,0:T(8,128)(2,1)S(1)}, u32[]{:S(2)}, u32[]{:S(2)}) collective-permute-start(bf16[128,1024]{1,0:T(8,128)(2,1)S(1)} %pad_maximum_fusion.6), channel_id=1, source_target_pairs={{0,64},{64,0},{128,192},{192,128},{1,65},{65,1},{129,193},{193,129... | collective-permute-start | bytes 786440 | tf_op jit(solution)/shard_map/ppermute | solution.py:39
  12.9 15.2 %collective-permute-start = (bf16[896,128]{1,0:T(8,128)(2,1)S(1)}, bf16[896,128]{1,0:T(8,128)(2,1)S(1)}, u32[]{:S(2)}, u32[]{:S(2)}) collective-permute-start(bf16[896,128]{1,0:T(8,128)(2,1)S(1)} %shard_map.118), channel_id=1, source_target_pairs={{0,0},{1,32},{2,4},{3,36},{4,64},{5,96},{6,68},{7,100},{8,8},{9,40... | collective-permute-start | bytes 688136 | tf_op jit(solution)/shard_map/ppermute | solution.py:43
  28.3 28.6 %collective-permute-start.5 = (bf16[896,128]{1,0:T(8,128)(2,1)S(1)}, bf16[896,128]{1,0:T(8,128)(2,1)S(1)}, u32[]{:S(2)}, u32[]{:S(2)}) collective-permute-start(bf16[896,128]{1,0:T(8,128)(2,1)S(1)} %shard_map.118), channel_id=1, source_target_pairs={{0,32},{1,0},{2,36},{3,4},{4,96},{5,64},{6,100},{7,68},{8,40},{9,8... | collective-permute-start | bytes 688136 | tf_op jit(solution)/shard_map/ppermute | solution.py:43
  40.0 16.9 %collective-permute-start.6 = (bf16[896,128]{1,0:T(8,128)(2,1)S(1)}, bf16[896,128]{1,0:T(8,128)(2,1)S(1)}, u32[]{:S(2)}, u32[]{:S(2)}) collective-permute-start(bf16[896,128]{1,0:T(8,128)(2,1)S(1)} %collective-permute-done), channel_id=1, source_target_pairs={{0,8},{8,0},{16,24},{24,16},{1,9},{9,1},{17,25},{25,17},{2,10},{10... | collective-permute-start | bytes 688136 | tf_op jit(solution)/shard_map/ppermute | solution.py:39
  41.6 15.3 %collective-permute-start.7 = (bf16[896,128]{1,0:T(8,128)(2,1)S(1)}, bf16[896,128]{1,0:T(8,128)(2,1)S(1)}, u32[]{:S(2)}, u32[]{:S(2)}) collective-permute-start(bf16[896,128]{1,0:T(8,128)(2,1)S(1)} %collective-permute-done), channel_id=1, source_target_pairs={{0,16},{8,24},{16,0},{24,8},{1,17},{9,25},{17,1},{25,9},{2,18},{10... | collective-permute-start | bytes 688136 | tf_op jit(solution)/shard_map/ppermute | solution.py:39
  44.3 12.6 %collective-permute-start.8 = (bf16[896,128]{1,0:T(8,128)(2,1)S(1)}, bf16[896,128]{1,0:T(8,128)(2,1)S(1)}, u32[]{:S(2)}, u32[]{:S(2)}) collective-permute-start(bf16[896,128]{1,0:T(8,128)(2,1)S(1)} %collective-permute-done), channel_id=1, source_target_pairs={{0,24},{8,16},{16,8},{24,0},{1,25},{9,17},{17,9},{25,1},{2,26},{10... | collective-permute-start | bytes 688136 | tf_op jit(solution)/shard_map/ppermute | solution.py:39
  44.8 10.6 %collective-permute-start.4 = (bf16[24,4096]{1,0:T(8,128)(2,1)S(1)}, bf16[24,4096]{1,0:T(8,128)(2,1)S(1)}, u32[]{:S(2)}, u32[]{:S(2)}) collective-permute-start(bf16[24,4096]{1,0:T(8,128)(2,1)S(1)} %copy-done.3), channel_id=1, source_target_pairs={{0,32},{32,0},{1,33},{33,1},{2,34},{34,2},{3,35},{35,3},{4,36},{36... | collective-permute-start | bytes 589832 | tf_op jit(solution)/shard_map/ppermute | solution.py:39
  57.7 19.3 %copy-start.4 = (f32[128,128]{1,0:T(8,128)S(1)}, f32[128,128]{1,0:T(8,128)}, u32[]{:S(2)}) copy-start(f32[128,128]{1,0:T(8,128)} %constant.76.clone) | copy-start | bytes 196612
  57.7 19.3 %copy-start.5 = (f32[128,128]{1,0:T(8,128)S(1)}, f32[128,128]{1,0:T(8,128)}, u32[]{:S(2)}) copy-start(f32[128,128]{1,0:T(8,128)} %constant.77.clone) | copy-start | bytes 196612
  57.8 8.6 %collective-permute-start.9 = (bf16[896,128]{1,0:T(8,128)(2,1)S(1)}, bf16[896,128]{1,0:T(8,128)(2,1)S(1)}, u32[]{:S(2)}, u32[]{:S(2)}) collective-permute-start(bf16[896,128]{1,0:T(8,128)(2,1)S(1)} %collective-permute-done.5), channel_id=1, source_target_pairs={{0,8},{8,0},{16,24},{24,16},{1,9},{9,1},{17,25},{25,17},{2,10},{10... | collective-permute-start | bytes 688136 | tf_op jit(solution)/shard_map/ppermute | solution.py:39
  59.3 13.4 %collective-permute-start.10 = (bf16[896,128]{1,0:T(8,128)(2,1)S(1)}, bf16[896,128]{1,0:T(8,128)(2,1)}, u32[]{:S(2)}, u32[]{:S(2)}) collective-permute-start(bf16[896,128]{1,0:T(8,128)(2,1)S(1)} %collective-permute-done.5), channel_id=1, source_target_pairs={{0,16},{8,24},{16,0},{24,8},{1,17},{9,25},{17,1},{25,9},{2,18},{10... | collective-permute-start | bytes 688136 | tf_op jit(solution)/shard_map/ppermute | solution.py:39
  62.0 13.8 %collective-permute-start.11 = (bf16[896,128]{1,0:T(8,128)(2,1)S(1)}, bf16[896,128]{1,0:T(8,128)(2,1)}, u32[]{:S(2)}, u32[]{:S(2)}) collective-permute-start(bf16[896,128]{1,0:T(8,128)(2,1)S(1)} %collective-permute-done.5), channel_id=1, source_target_pairs={{0,24},{8,16},{16,8},{24,0},{1,25},{9,17},{17,9},{25,1},{2,26},{10... | collective-permute-start | bytes 688136 | tf_op jit(solution)/shard_map/ppermute | solution.py:39
  62.7 14.5 %collective-permute-start.16 = (bf16[4,896,128]{2,1,0:T(8,128)(2,1)S(1)}, bf16[4,896,128]{2,1,0:T(8,128)(2,1)S(1)}, u32[]{:S(2)}, u32[]{:S(2)}) collective-permute-start(bf16[4,896,128]{2,1,0:T(8,128)(2,1)S(1)} %pad_maximum_fusion.2.here_ref), channel_id=1, source_target_pairs={{0,4},{4,0},{1,5},{5,1},{2,6},{6,2},{3,7},{7,3},{8,12},{12,8},{9,1... | collective-permute-start | bytes 2752520 | tf_op jit(solution)/shard_map/ppermute | solution.py:39
  76.9 11.4 %collective-permute-start.12 = (bf16[4,896,128]{2,1,0:T(8,128)(2,1)S(1)}, bf16[4,896,128]{2,1,0:T(8,128)(2,1)S(1)}, u32[]{:S(2)}, u32[]{:S(2)}) collective-permute-start(bf16[4,896,128]{2,1,0:T(8,128)(2,1)S(1)} %pad_maximum_fusion.1.here_ref), channel_id=1, source_target_pairs={{0,4},{4,0},{1,5},{5,1},{2,6},{6,2},{3,7},{7,3},{8,12},{12,8},{9,1... | collective-permute-start | bytes 2752520 | tf_op jit(solution)/shard_map/ppermute | solution.py:39
  78.8 15.5 %collective-permute-start.17 = (bf16[128,896]{1,0:T(8,128)(2,1)S(1)}, bf16[128,896]{1,0:T(8,128)(2,1)S(1)}, u32[]{:S(2)}, u32[]{:S(2)}) collective-permute-start(bf16[128,896]{1,0:T(8,128)(2,1)S(1)} %get-tuple-element.66), channel_id=1, source_target_pairs={{0,64},{64,0},{128,192},{192,128},{1,65},{65,1},{129,193},{193,129... | collective-permute-start | bytes 688136 | tf_op jit(solution)/shard_map/ppermute | solution.py:39
  85.6 13.7 %collective-permute-start.18 = (bf16[128,896]{1,0:T(8,128)(2,1)S(1)}, bf16[128,896]{1,0:T(8,128)(2,1)S(1)}, u32[]{:S(2)}, u32[]{:S(2)}) collective-permute-start(bf16[128,896]{1,0:T(8,128)(2,1)S(1)} %get-tuple-element.68), channel_id=1, source_target_pairs={{0,128},{64,192},{128,0},{192,64},{1,129},{65,193},{129,1},{193,65... | collective-permute-start | bytes 688136 | tf_op jit(solution)/shard_map/ppermute | solution.py:39
  87.9 14.6 %collective-permute-start.19 = (bf16[128,896]{1,0:T(8,128)(2,1)S(1)}, bf16[128,896]{1,0:T(8,128)(2,1)S(1)}, u32[]{:S(2)}, u32[]{:S(2)}) collective-permute-start(bf16[128,896]{1,0:T(8,128)(2,1)S(1)} %get-tuple-element.67), channel_id=1, source_target_pairs={{0,192},{64,128},{128,64},{192,0},{1,193},{65,129},{129,65},{193,1... | collective-permute-start | bytes 688136 | tf_op jit(solution)/shard_map/ppermute | solution.py:39
  89.9 12.7 %collective-permute-start.13 = (bf16[128,896]{1,0:T(8,128)(2,1)S(1)}, bf16[128,896]{1,0:T(8,128)(2,1)S(1)}, u32[]{:S(2)}, u32[]{:S(2)}) collective-permute-start(bf16[128,896]{1,0:T(8,128)(2,1)S(1)} %get-tuple-element.69), channel_id=1, source_target_pairs={{0,64},{64,0},{128,192},{192,128},{1,65},{65,1},{129,193},{193,129... | collective-permute-start | bytes 688136 | tf_op jit(solution)/shard_map/ppermute | solution.py:39
  90.7 23.0 %collective-permute-start.14 = (bf16[128,896]{1,0:T(8,128)(2,1)S(1)}, bf16[128,896]{1,0:T(8,128)(2,1)S(1)}, u32[]{:S(2)}, u32[]{:S(2)}) collective-permute-start(bf16[128,896]{1,0:T(8,128)(2,1)S(1)} %get-tuple-element.71), channel_id=1, source_target_pairs={{0,128},{64,192},{128,0},{192,64},{1,129},{65,193},{129,1},{193,65... | collective-permute-start | bytes 688136 | tf_op jit(solution)/shard_map/ppermute | solution.py:39
  94.3 21.4 %collective-permute-start.15 = (bf16[128,896]{1,0:T(8,128)(2,1)S(1)}, bf16[128,896]{1,0:T(8,128)(2,1)S(1)}, u32[]{:S(2)}, u32[]{:S(2)}) collective-permute-start(bf16[128,896]{1,0:T(8,128)(2,1)S(1)} %get-tuple-element.70), channel_id=1, source_target_pairs={{0,192},{64,128},{128,64},{192,0},{1,193},{65,129},{129,65},{193,1... | collective-permute-start | bytes 688136 | tf_op jit(solution)/shard_map/ppermute | solution.py:39
  116.4 5.8 %collective-permute-start.20 = (bf16[32,2688]{1,0:T(8,128)(2,1)S(1)}, bf16[32,2688]{1,0:T(8,128)(2,1)S(1)}, u32[]{:S(2)}, u32[]{:S(2)}) collective-permute-start(bf16[32,2688]{1,0:T(8,128)(2,1)S(1)} %get-tuple-element.108), channel_id=1, source_target_pairs={{0,1},{1,0},{2,3},{3,2},{4,5},{5,4},{6,7},{7,6},{8,9},{9,8},{10,11... | collective-permute-start | bytes 516104 | tf_op jit(solution)/shard_map/ppermute | solution.py:39
  116.5 14.7 %collective-permute-start.21 = (bf16[32,2688]{1,0:T(8,128)(2,1)S(1)}, bf16[32,2688]{1,0:T(8,128)(2,1)S(1)}, u32[]{:S(2)}, u32[]{:S(2)}) collective-permute-start(bf16[32,2688]{1,0:T(8,128)(2,1)S(1)} %get-tuple-element.109), channel_id=1, source_target_pairs={{0,2},{1,3},{2,0},{3,1},{4,6},{5,7},{6,4},{7,5},{8,10},{9,11},{10,... | collective-permute-start | bytes 516104 | tf_op jit(solution)/shard_map/ppermute | solution.py:39
  117.6 13.6 %collective-permute-start.22 = (bf16[32,2688]{1,0:T(8,128)(2,1)S(1)}, bf16[32,2688]{1,0:T(8,128)(2,1)S(1)}, u32[]{:S(2)}, u32[]{:S(2)}) collective-permute-start(bf16[32,2688]{1,0:T(8,128)(2,1)S(1)} %get-tuple-element.110), channel_id=1, source_target_pairs={{0,3},{1,2},{2,1},{3,0},{4,7},{5,6},{6,5},{7,4},{8,11},{9,10},{10,... | collective-permute-start | bytes 516104 | tf_op jit(solution)/shard_map/ppermute | solution.py:39
  134.0 6.7 %collective-permute-start.23 = (bf16[32,1536]{1,0:T(8,128)(2,1)S(1)}, bf16[32,1536]{1,0:T(8,128)(2,1)S(1)}, u32[]{:S(2)}, u32[]{:S(2)}) collective-permute-start(bf16[32,1536]{1,0:T(8,128)(2,1)S(1)} %pad_maximum_fusion.10), channel_id=1, source_target_pairs={{0,3},{1,2},{2,1},{3,0},{4,7},{5,6},{6,5},{7,4},{8,11},{9,10},{10,... | collective-permute-start | bytes 294920 | tf_op jit(solution)/shard_map/ppermute | solution.py:39
  135.9 9.5 %collective-permute-start.24 = (bf16[32,1536]{1,0:T(8,128)(2,1)S(1)}, bf16[32,1536]{1,0:T(8,128)(2,1)S(1)}, u32[]{:S(2)}, u32[]{:S(2)}) collective-permute-start(bf16[32,1536]{1,0:T(8,128)(2,1)S(1)} %pad_maximum_fusion.10), channel_id=1, source_target_pairs={{0,2},{1,3},{2,0},{3,1},{4,6},{5,7},{6,4},{7,5},{8,10},{9,11},{10,... | collective-permute-start | bytes 294920 | tf_op jit(solution)/shard_map/ppermute | solution.py:39
  137.9 7.5 %collective-permute-start.25 = (bf16[32,1536]{1,0:T(8,128)(2,1)S(1)}, bf16[32,1536]{1,0:T(8,128)(2,1)S(1)}, u32[]{:S(2)}, u32[]{:S(2)}) collective-permute-start(bf16[32,1536]{1,0:T(8,128)(2,1)S(1)} %pad_maximum_fusion.10), channel_id=1, source_target_pairs={{0,1},{1,0},{2,3},{3,2},{4,5},{5,4},{6,7},{7,6},{8,9},{9,8},{10,11... | collective-permute-start | bytes 294920 | tf_op jit(solution)/shard_map/ppermute | solution.py:39
  (3 other events, 7.7 us)
Sparse Core Ops, SparseCore 0:
  57.9 80.5 all-gather.1

commit v6 on v5

--- a/solution.py
+++ b/solution.py
@@ -53,15 +53,6 @@
 
 
 COSINE, SINE = tables()
-
-
-def order_of(zh):
-    order = np.arange(384).reshape(2, 8, 24)
-    order = np.stack([order[zh], order[1 - zh]], axis=1).reshape(384)
-    return np.eye(384, dtype=np.float32)[:, order].astype(jnp.bfloat16)
-
-
-ORDER = (order_of(0), order_of(1))
 
 
 def rotate(values, cosine, sine):
@@ -138,24 +129,26 @@
     )(inputs, here, there)
 
 
-def mix_kernel(x_ref, w_ref, out_ref):
-    out_ref[...] = jnp.dot(x_ref[...], w_ref[...], preferred_element_type=F32).astype(BF)
-
-
-def mix(attended, weight):
-    columns = weight.shape[1]
+def mix_kernel(x_ref, near_ref, far_ref, out_ref):
+    out = jnp.dot(x_ref[:, :768], near_ref[...], preferred_element_type=F32)
+    out_ref[...] = (out + jnp.dot(x_ref[:, 768:], far_ref[...], preferred_element_type=F32)).astype(BF)
+
+
+def mix(attended, near, far):
+    columns = near.shape[1]
     return pl.pallas_call(
         mix_kernel,
         out_shape=jax.ShapeDtypeStruct((ROWS, columns), BF),
         grid=(columns // 512,),
         in_specs=[
             pl.BlockSpec((ROWS, 1536), lambda i: (0, 0)),
-            pl.BlockSpec((1536, 512), lambda i: (0, i)),
+            pl.BlockSpec((768, 512), lambda i: (0, i)),
+            pl.BlockSpec((768, 512), lambda i: (0, i)),
         ],
         out_specs=pl.BlockSpec((ROWS, 512), lambda i: (0, i)),
-        compiler_params=pltpu.CompilerParams(vmem_limit_bytes=32 * 2**20),
+        compiler_params=pltpu.CompilerParams(vmem_limit_bytes=58 * 2**20),
         cost_estimate=pl.CostEstimate(flops=2 * ROWS * 1536 * columns, bytes_accessed=14000000, transcendentals=0),
-    )(attended, weight)
+    )(attended, near, far)
 
 
 def attend(query, keys, values, limit, first):
@@ -189,23 +182,30 @@
         return jnp.concatenate(picked, axis=1)
 
     ring = [swap(features(e), "y", e) for e in (1, 2, 3)]
-    first, packed, out_weight, *ring = lax.optimization_barrier((first, packed, out_weight, *ring))
+    first, packed, *ring = lax.optimization_barrier((first, packed, *ring))
     second = move(packed, lambda y, zh, x, c, t: ((2 * zh + c) ^ y, 1 - (t & 1), x, t >> 1, y))
     inputs = jnp.concatenate([features(0)] + ring, axis=0)
 
-    wo_other = swap(out_weight, "zh", 1)
-    first_blocks = [first] + [swap(first, "x", d) for d in (1, 2, 3)]
-    wo_other, second, *first_blocks = lax.optimization_barrier((wo_other, second, *first_blocks))
-    wo_piece = jnp.concatenate([out_weight, wo_other], axis=0)
-    wo = lax.all_gather(wo_piece, ("y", "x", "core"), axis=0, tiled=True)
-
-    summed = []
-    for blocks in (first_blocks, [second] + [swap(second, "x", d) for d in (1, 2, 3)]):
-        here = jnp.stack(blocks)
-        sent, total = project(inputs, here, swap(here, "core", 1))
+    wo_near = lax.all_gather(out_weight, ("y", "x", "core"), axis=0, tiled=True)
+
+    def along(block):
+        return jnp.stack([block] + [swap(block, "x", d) for d in (1, 2, 3)])
+
+    def reduced(here, there):
+        sent, total = project(inputs, here, there)
         for e in (1, 2, 3):
             total = total + swap(sent[e - 1], "y", e).astype(F32)
-        summed.append(total)
+        return total
+
+    here = along(first)
+    here, second, out_weight = lax.optimization_barrier((here, second, out_weight))
+    total = reduced(here, swap(here, "core", 1))
+    here = along(second)
+    there = swap(here, "core", 1)
+    wo_other = swap(out_weight, "zh", 1)
+    total, there, wo_other = lax.optimization_barrier((total, there, wo_other))
+    wo_far = lax.all_gather(wo_other, ("y", "x", "core"), axis=0, tiled=True)
+    summed = [total, reduced(here, there)]
     base = 2 * c + zh
     q_slots = [half[:, at : at + 384] for at in (0, 384) for half in summed]
     kv_slots = [half[:, at : at + 64] for at in (768, 832) for half in summed]
@@ -238,13 +238,13 @@
     scale_here = lax.dynamic_slice(scales, (t * 32,), (32,))
     query = rotate((q_raw * scale_here[:, None]).reshape(32, 12, HD), *mine_rows).astype(BF)
     attended = attend(query, keys, values, limit, t * 32).reshape(32, 1536)
-    stacked = jnp.concatenate([attended[:, 384 * d : 384 * d + 384] for d in range(4)], axis=0)
-    stacked = jnp.dot(stacked, pick(zh == 1, ORDER[0], ORDER[1]), preferred_element_type=F32).astype(BF)
-    attended = jnp.concatenate([stacked[32 * d : 32 * d + 32] for d in range(4)], axis=1)
+    lows = jnp.concatenate([attended[:, 384 * d : 384 * d + 192] for d in range(4)], axis=1)
+    highs = jnp.concatenate([attended[:, 384 * d + 192 : 384 * d + 384] for d in range(4)], axis=1)
+    attended = jnp.concatenate([pick(zh == 1, lows, highs), pick(zh == 1, highs, lows)], axis=1)
 
     got = [attended] + [swap(attended, "zl", d) for d in (1, 2, 3)]
     all_rows = jnp.concatenate(by_index(got, t), axis=0)
-    return mix(all_rows, wo)
+    return mix(all_rows, wo_near, wo_far)
 
 
 def solution(mesh):

time: 162 us -> 171 us (1.056); the launches traced: 162 us -> 169 us
  starting transfers between devices: 55.7 us -> 62.2 us
  Pallas kernels: 8.27 us -> 12 us
  local copies, waits for them, and re-layouts: 5.65 us -> 2.04 us
    ppermute x24, waiting for transfers between devices: 61.2 us -> 54.6 us  [swap(): return lax.ppermute(value, axis, [(i, i ^ d) for i in range(n)])]
    ppermute x2, waiting for transfers between devices: 10.1 us -> 16.6 us  [move(): lax.ppermute(value, AXES, [(flat(*at), flat(*where(*at))) for at in every...]
    unnamed x26 -> x22, local copies, waits for them, and re-layouts: 4.69 us -> 0.28 us
    ppermute x24, starting transfers between devices: 37.5 us -> 41.8 us  [swap(): return lax.ppermute(value, axis, [(i, i ^ d) for i in range(n)])]
    pallas_call x1, Pallas kernels: 5.19 us -> 8.9 us  [mix(): pl.pallas_call(mix_kernel, out_shape=jax.ShapeDtypeStruct((ROWS, columns)...]
    ppermute x2, starting transfers between devices: 18.2 us -> 20.4 us  [move(): lax.ppermute(value, AXES, [(flat(*at), flat(*where(*at))) for at in every...]
  transfers between devices with their start and end apart: 27 -> 28, of which waited for: 16 -> 13; matrix products, arithmetic and copies ran while one was open for 3% -> 5% of each run, Pallas kernels for 2% -> 2%
where the time goes in v6:
time: 171 us; the launch traced here: 169 us
  waiting for transfers between devices  71.9 us (42%)
  starting transfers between devices  62.2 us (36%)
  between operations  14.7 us (9%)
  Pallas kernels  12 us (7%)
  other arithmetic  5.17 us (3%)
  local copies, waits for them, and re-layouts  2.04 us (1%)
    ppermute x24, waiting for transfers between devices, swap(): return lax.ppermute(value, axis, [(i, i ^ d) for i in range(n)])  54.6 us
    ppermute x24, starting transfers between devices, swap(): return lax.ppermute(value, axis, [(i, i ^ d) for i in range(n)])  41.8 us
    ppermute x2, starting transfers between devices, move(): lax.ppermute(value, AXES, [(flat(*at), flat(*where(*at))) for at in every...  20.4 us
    ppermute x2, waiting for transfers between devices, move(): lax.ppermute(value, AXES, [(flat(*at), flat(*where(*at))) for at in every...  16.6 us
    pallas_call x1, Pallas kernels, mix(): pl.pallas_call(mix_kernel, out_shape=jax.ShapeDtypeStruct((ROWS, columns)...  8.9 us
  transfers between devices with their start and end apart: 28, of which 13 were waited for; matrix products, arithmetic and copies ran while one was open for 5% of the time, Pallas kernels for 2%

profile of v6, /device:TPU:24, one launch (start us, length us, event | category | flops | bytes accessed | tf_op | source)
XLA Modules:
  0.0 169.1 jit_solution(8652000250765950664)
XLA Ops:
  7.4 1.6 fusion.2
  9.3 2.0 %collective-permute-start.3 = (bf16[128,1024]{1,0:T(8,128)(2,1)S(1)}, bf16[128,1024]{1,0:T(8,128)(2,1)S(1)}, u32[]{:S(2)}, u32[]{:S(2)}) collective-permute-start(bf16[128,1024]{1,0:T(8,128)(2,1)S(1)} %pad_maximum_fusion.7), channel_id=1, source_target_pairs={{0,192},{64,128},{128,64},{192,0},{1,193},{65,129},{129,65},{193,1... | collective-permute-start | bytes 786440 | tf_op jit(solution)/shard_map/ppermute | solution.py:39
  12.4 1.4 collective-permute-start.1
  13.8 6.5 %collective-permute-start = (bf16[896,128]{1,0:T(8,128)(2,1)S(1)}, bf16[896,128]{1,0:T(8,128)(2,1)S(1)}, u32[]{:S(2)}, u32[]{:S(2)}) collective-permute-start(bf16[896,128]{1,0:T(8,128)(2,1)S(1)} %shard_map.100), channel_id=1, source_target_pairs={{0,0},{1,32},{2,4},{3,36},{4,64},{5,96},{6,68},{7,100},{8,8},{9,40... | collective-permute-start | bytes 688136 | tf_op jit(solution)/shard_map/ppermute | solution.py:43
  20.3 8.7 %collective-permute-done = bf16[896,128]{1,0:T(8,128)(2,1)S(1)} collective-permute-done((bf16[896,128]{1,0:T(8,128)(2,1)S(1)}, bf16[896,128]{1,0:T(8,128)(2,1)S(1)}, u32[]{:S(2)}, u32[]{:S(2)}) %collective-permute-start) | collective-permute-done | bytes 229408 | tf_op jit(solution)/shard_map/ppermute | solution.py:43
  29.0 1.3 collective-permute-done.3
  30.3 1.5 collective-permute-start.4
  31.8 2.7 %collective-permute-start.5 = (bf16[896,128]{1,0:T(8,128)(2,1)S(1)}, bf16[896,128]{1,0:T(8,128)(2,1)S(1)}, u32[]{:S(2)}, u32[]{:S(2)}) collective-permute-start(bf16[896,128]{1,0:T(8,128)(2,1)S(1)} %collective-permute-done), channel_id=1, source_target_pairs={{0,16},{8,24},{16,0},{24,8},{1,17},{9,25},{17,1},{25,9},{2,18},{10... | collective-permute-start | bytes 688136 | tf_op jit(solution)/shard_map/ppermute | solution.py:39
  35.0 13.9 %collective-permute-start.7 = (bf16[896,128]{1,0:T(8,128)(2,1)S(1)}, bf16[896,128]{1,0:T(8,128)(2,1)S(1)}, u32[]{:S(2)}, u32[]{:S(2)}) collective-permute-start(bf16[896,128]{1,0:T(8,128)(2,1)S(1)} %shard_map.100), channel_id=1, source_target_pairs={{0,32},{1,0},{2,36},{3,4},{4,96},{5,64},{6,100},{7,68},{8,40},{9,8... | collective-permute-start | bytes 688136 | tf_op jit(solution)/shard_map/ppermute | solution.py:43
  49.0 8.0 %collective-permute-done.7 = bf16[896,128]{1,0:T(8,128)(2,1)S(1)} collective-permute-done((bf16[896,128]{1,0:T(8,128)(2,1)S(1)}, bf16[896,128]{1,0:T(8,128)(2,1)S(1)}, u32[]{:S(2)}, u32[]{:S(2)}) %collective-permute-start.7) | collective-permute-done | bytes 229408 | tf_op jit(solution)/shard_map/ppermute | solution.py:43
  57.3 3.9 %collective-permute-start.9 = (bf16[896,128]{1,0:T(8,128)(2,1)S(1)}, bf16[896,128]{1,0:T(8,128)(2,1)S(1)}, u32[]{:S(2)}, u32[]{:S(2)}) collective-permute-start(bf16[896,128]{1,0:T(8,128)(2,1)S(1)} %collective-permute-done.7), channel_id=1, source_target_pairs={{0,16},{8,24},{16,0},{24,8},{1,17},{9,25},{17,1},{25,9},{2,18},{10... | collective-permute-start | bytes 688136 | tf_op jit(solution)/shard_map/ppermute | solution.py:39
  61.7 8.2 %collective-permute-done.8 = bf16[896,128]{1,0:T(8,128)(2,1)S(1)} collective-permute-done((bf16[896,128]{1,0:T(8,128)(2,1)S(1)}, bf16[896,128]{1,0:T(8,128)(2,1)S(1)}, u32[]{:S(2)}, u32[]{:S(2)}) %collective-permute-start.8) | collective-permute-done | bytes 229408 | tf_op jit(solution)/shard_map/ppermute | solution.py:39
  69.8 8.5 %collective-permute-done.9 = bf16[896,128]{1,0:T(8,128)(2,1)S(1)} collective-permute-done((bf16[896,128]{1,0:T(8,128)(2,1)S(1)}, bf16[896,128]{1,0:T(8,128)(2,1)S(1)}, u32[]{:S(2)}, u32[]{:S(2)}) %collective-permute-start.9) | collective-permute-done | bytes 229408 | tf_op jit(solution)/shard_map/ppermute | solution.py:39
  78.7 1.5 shard_map.101
  81.2 1.9 %collective-permute-start.13 = (bf16[128,896]{1,0:T(8,128)(2,1)S(1)}, bf16[128,896]{1,0:T(8,128)(2,1)S(1)}, u32[]{:S(2)}, u32[]{:S(2)}) collective-permute-start(bf16[128,896]{1,0:T(8,128)(2,1)S(1)} %get-tuple-element.69), channel_id=1, source_target_pairs={{0,128},{64,192},{128,0},{192,64},{1,129},{65,193},{129,1},{193,65... | collective-permute-start | bytes 688136 | tf_op jit(solution)/shard_map/ppermute | solution.py:39
  83.0 2.0 %collective-permute-start.14 = (bf16[128,896]{1,0:T(8,128)(2,1)S(1)}, bf16[128,896]{1,0:T(8,128)(2,1)S(1)}, u32[]{:S(2)}, u32[]{:S(2)}) collective-permute-start(bf16[128,896]{1,0:T(8,128)(2,1)S(1)} %get-tuple-element.68), channel_id=1, source_target_pairs={{0,192},{64,128},{128,64},{192,0},{1,193},{65,129},{129,65},{193,1... | collective-permute-start | bytes 688136 | tf_op jit(solution)/shard_map/ppermute | solution.py:39
  85.1 4.2 %collective-permute-start.16 = (bf16[24,4096]{1,0:T(8,128)(2,1)S(1)}, bf16[24,4096]{1,0:T(8,128)(2,1)}, u32[]{:S(2)}, u32[]{:S(2)}) collective-permute-start(bf16[24,4096]{1,0:T(8,128)(2,1)S(1)} %copy-done.3), channel_id=1, source_target_pairs={{0,32},{32,0},{1,33},{33,1},{2,34},{34,2},{3,35},{35,3},{4,36},{36... | collective-permute-start | bytes 589832 | tf_op jit(solution)/shard_map/ppermute | solution.py:39
  89.3 4.8 %collective-permute-done.13 = bf16[128,896]{1,0:T(8,128)(2,1)S(1)} collective-permute-done((bf16[128,896]{1,0:T(8,128)(2,1)S(1)}, bf16[128,896]{1,0:T(8,128)(2,1)S(1)}, u32[]{:S(2)}, u32[]{:S(2)}) %collective-permute-start.13) | collective-permute-done | bytes 229408 | tf_op jit(solution)/shard_map/ppermute | solution.py:39
  94.0 2.6 %collective-permute-done.14 = bf16[128,896]{1,0:T(8,128)(2,1)S(1)} collective-permute-done((bf16[128,896]{1,0:T(8,128)(2,1)S(1)}, bf16[128,896]{1,0:T(8,128)(2,1)S(1)}, u32[]{:S(2)}, u32[]{:S(2)}) %collective-permute-start.14) | collective-permute-done | bytes 229408 | tf_op jit(solution)/shard_map/ppermute | solution.py:39
  98.9 1.5 shard_map.102
  101.8 3.4 %collective-permute-start.18 = (bf16[128,896]{1,0:T(8,128)(2,1)S(1)}, bf16[128,896]{1,0:T(8,128)(2,1)S(1)}, u32[]{:S(2)}, u32[]{:S(2)}) collective-permute-start(bf16[128,896]{1,0:T(8,128)(2,1)S(1)} %get-tuple-element.66), channel_id=1, source_target_pairs={{0,128},{64,192},{128,0},{192,64},{1,129},{65,193},{129,1},{193,65... | collective-permute-start | bytes 688136 | tf_op jit(solution)/shard_map/ppermute | solution.py:39
  105.3 3.8 %collective-permute-done.17 = bf16[128,896]{1,0:T(8,128)(2,1)S(1)} collective-permute-done((bf16[128,896]{1,0:T(8,128)(2,1)S(1)}, bf16[128,896]{1,0:T(8,128)(2,1)S(1)}, u32[]{:S(2)}, u32[]{:S(2)}) %collective-permute-start.17) | collective-permute-done | bytes 229408 | tf_op jit(solution)/shard_map/ppermute | solution.py:39
  109.2 5.3 %collective-permute-done.18 = bf16[128,896]{1,0:T(8,128)(2,1)S(1)} collective-permute-done((bf16[128,896]{1,0:T(8,128)(2,1)S(1)}, bf16[128,896]{1,0:T(8,128)(2,1)S(1)}, u32[]{:S(2)}, u32[]{:S(2)}) %collective-permute-start.18) | collective-permute-done | bytes 229408 | tf_op jit(solution)/shard_map/ppermute | solution.py:39
  114.5 2.7 %collective-permute-done.19 = bf16[128,896]{1,0:T(8,128)(2,1)S(1)} collective-permute-done((bf16[128,896]{1,0:T(8,128)(2,1)S(1)}, bf16[128,896]{1,0:T(8,128)(2,1)S(1)}, u32[]{:S(2)}, u32[]{:S(2)}) %collective-permute-start.19) | collective-permute-done | bytes 229408 | tf_op jit(solution)/shard_map/ppermute | solution.py:39
  117.9 1.8 %collective-permute-start.20 = (bf16[32,2688]{1,0:T(8,128)(2,1)S(1)}, bf16[32,2688]{1,0:T(8,128)(2,1)S(1)}, u32[]{:S(2)}, u32[]{:S(2)}) collective-permute-start(bf16[32,2688]{1,0:T(8,128)(2,1)S(1)} %get-tuple-element.109), channel_id=1, source_target_pairs={{0,1},{1,0},{2,3},{3,2},{4,5},{5,4},{6,7},{7,6},{8,9},{9,8},{10,11... | collective-permute-start | bytes 516104 | tf_op jit(solution)/shard_map/ppermute | solution.py:39
  119.7 7.8 %collective-permute-start.21 = (bf16[32,2688]{1,0:T(8,128)(2,1)S(1)}, bf16[32,2688]{1,0:T(8,128)(2,1)S(1)}, u32[]{:S(2)}, u32[]{:S(2)}) collective-permute-start(bf16[32,2688]{1,0:T(8,128)(2,1)S(1)} %get-tuple-element.110), channel_id=1, source_target_pairs={{0,2},{1,3},{2,0},{3,1},{4,6},{5,7},{6,4},{7,5},{8,10},{9,11},{10,... | collective-permute-start | bytes 516104 | tf_op jit(solution)/shard_map/ppermute | solution.py:39
  127.6 11.1 %collective-permute-done.21 = bf16[32,2688]{1,0:T(8,128)(2,1)S(1)} collective-permute-done((bf16[32,2688]{1,0:T(8,128)(2,1)S(1)}, bf16[32,2688]{1,0:T(8,128)(2,1)S(1)}, u32[]{:S(2)}, u32[]{:S(2)}) %collective-permute-start.21) | collective-permute-done | bytes 172064 | tf_op jit(solution)/shard_map/ppermute | solution.py:39
  141.6 2.0 %collective-permute-start.23 = (bf16[32,1536]{1,0:T(8,128)(2,1)S(1)}, bf16[32,1536]{1,0:T(8,128)(2,1)S(1)}, u32[]{:S(2)}, u32[]{:S(2)}) collective-permute-start(bf16[32,1536]{1,0:T(8,128)(2,1)S(1)} %pad_maximum_fusion.9), channel_id=1, source_target_pairs={{0,3},{1,2},{2,1},{3,0},{4,7},{5,6},{6,5},{7,4},{8,11},{9,10},{10,... | collective-permute-start | bytes 294920 | tf_op jit(solution)/shard_map/ppermute | solution.py:39
  143.6 2.0 %collective-permute-start.24 = (bf16[32,1536]{1,0:T(8,128)(2,1)S(1)}, bf16[32,1536]{1,0:T(8,128)(2,1)S(1)}, u32[]{:S(2)}, u32[]{:S(2)}) collective-permute-start(bf16[32,1536]{1,0:T(8,128)(2,1)S(1)} %pad_maximum_fusion.9), channel_id=1, source_target_pairs={{0,2},{1,3},{2,0},{3,1},{4,6},{5,7},{6,4},{7,5},{8,10},{9,11},{10,... | collective-permute-start | bytes 294920 | tf_op jit(solution)/shard_map/ppermute | solution.py:39
  146.1 2.8 %collective-permute-done.23 = bf16[32,1536]{1,0:T(8,128)(2,1)S(1)} collective-permute-done((bf16[32,1536]{1,0:T(8,128)(2,1)S(1)}, bf16[32,1536]{1,0:T(8,128)(2,1)S(1)}, u32[]{:S(2)}, u32[]{:S(2)}) %collective-permute-start.23) | collective-permute-done | bytes 98336 | tf_op jit(solution)/shard_map/ppermute | solution.py:39
  148.9 3.5 %collective-permute-done.24 = bf16[32,1536]{1,0:T(8,128)(2,1)S(1)} collective-permute-done((bf16[32,1536]{1,0:T(8,128)(2,1)S(1)}, bf16[32,1536]{1,0:T(8,128)(2,1)S(1)}, u32[]{:S(2)}, u32[]{:S(2)}) %collective-permute-start.24) | collective-permute-done | bytes 98336 | tf_op jit(solution)/shard_map/ppermute | solution.py:39
  153.3 8.9 %shard_map.103 = bf16[128,4096]{1,0:T(8,128)(2,1)} custom-call(bf16[128,1536]{1,0:T(8,128)(2,1)} %pad_maximum_fusion.4.x_ref, bf16[768,4096]{1,0:T(8,128)(2,1)} %all-gather.3.cloned.1.call-done.near_ref, bf16[768,4096]{1,0:T(8,128)(2,1)} %all-gather.5.cloned.1.call-done.far_ref), custom_call_target="tpu_custom_call" | custom-call | flops 1610612736 | bytes 14000000 | tf_op jit(solution)/shard_map/pallas_call | solution.py:139
  (102 shorter events, 12.6 us)
Async XLA Ops:
  6.5 146.8 %all-gather.3.cloned.1.call-start = ((), (), s32[]{:S(2)}) async-start(), calls=%async_computation | async-start | bytes 6488064 | tf_op jit(solution)/shard_map/all_gather | solution.py:189
  7.3 146.1 %all-gather.5.cloned.1.call-start = ((), (), s32[]{:S(2)}) async-start(), calls=%async_computation.1 | async-start | bytes 6488064 | tf_op jit(solution)/shard_map/all_gather | solution.py:207
  9.1 4.7 %copy-start = (bf16[256,384]{1,0:T(8,128)(2,1)S(1)}, bf16[256,384]{1,0:T(8,128)(2,1)}, u32[]{:S(2)}) copy-start(bf16[256,384]{1,0:T(8,128)(2,1)} %q_ref.1) | copy-start | bytes 589828
  9.1 4.7 %copy-start.1 = (bf16[256,64]{0,1:T(8,128)(2,1)S(1)}, bf16[256,64]{0,1:T(8,128)(2,1)}, u32[]{:S(2)}) copy-start(bf16[256,64]{0,1:T(8,128)(2,1)} %param.13) | copy-start | bytes 98308
  9.3 20.9 %collective-permute-start.3 = (bf16[128,1024]{1,0:T(8,128)(2,1)S(1)}, bf16[128,1024]{1,0:T(8,128)(2,1)S(1)}, u32[]{:S(2)}, u32[]{:S(2)}) collective-permute-start(bf16[128,1024]{1,0:T(8,128)(2,1)S(1)} %pad_maximum_fusion.7), channel_id=1, source_target_pairs={{0,192},{64,128},{128,64},{192,0},{1,193},{65,129},{129,65},{193,1... | collective-permute-start | bytes 786440 | tf_op jit(solution)/shard_map/ppermute | solution.py:39
  11.4 18.9 %collective-permute-start.2 = (bf16[128,1024]{1,0:T(8,128)(2,1)S(1)}, bf16[128,1024]{1,0:T(8,128)(2,1)S(1)}, u32[]{:S(2)}, u32[]{:S(2)}) collective-permute-start(bf16[128,1024]{1,0:T(8,128)(2,1)S(1)} %pad_maximum_fusion.6), channel_id=1, source_target_pairs={{0,128},{64,192},{128,0},{192,64},{1,129},{65,193},{129,1},{193,65... | collective-permute-start | bytes 786440 | tf_op jit(solution)/shard_map/ppermute | solution.py:39
  12.4 17.9 %collective-permute-start.1 = (bf16[128,1024]{1,0:T(8,128)(2,1)S(1)}, bf16[128,1024]{1,0:T(8,128)(2,1)S(1)}, u32[]{:S(2)}, u32[]{:S(2)}) collective-permute-start(bf16[128,1024]{1,0:T(8,128)(2,1)S(1)} %pad_maximum_fusion.5), channel_id=1, source_target_pairs={{0,64},{64,0},{128,192},{192,128},{1,65},{65,1},{129,193},{193,129... | collective-permute-start | bytes 786440 | tf_op jit(solution)/shard_map/ppermute | solution.py:39
  13.8 15.2 %collective-permute-start = (bf16[896,128]{1,0:T(8,128)(2,1)S(1)}, bf16[896,128]{1,0:T(8,128)(2,1)S(1)}, u32[]{:S(2)}, u32[]{:S(2)}) collective-permute-start(bf16[896,128]{1,0:T(8,128)(2,1)S(1)} %shard_map.100), channel_id=1, source_target_pairs={{0,0},{1,32},{2,4},{3,36},{4,64},{5,96},{6,68},{7,100},{8,8},{9,40... | collective-permute-start | bytes 688136 | tf_op jit(solution)/shard_map/ppermute | solution.py:43
  30.3 18.6 %collective-permute-start.4 = (bf16[896,128]{1,0:T(8,128)(2,1)S(1)}, bf16[896,128]{1,0:T(8,128)(2,1)S(1)}, u32[]{:S(2)}, u32[]{:S(2)}) collective-permute-start(bf16[896,128]{1,0:T(8,128)(2,1)S(1)} %collective-permute-done), channel_id=1, source_target_pairs={{0,8},{8,0},{16,24},{24,16},{1,9},{9,1},{17,25},{25,17},{2,10},{10... | collective-permute-start | bytes 688136 | tf_op jit(solution)/shard_map/ppermute | solution.py:39
  31.8 17.1 %collective-permute-start.5 = (bf16[896,128]{1,0:T(8,128)(2,1)S(1)}, bf16[896,128]{1,0:T(8,128)(2,1)S(1)}, u32[]{:S(2)}, u32[]{:S(2)}) collective-permute-start(bf16[896,128]{1,0:T(8,128)(2,1)S(1)} %collective-permute-done), channel_id=1, source_target_pairs={{0,16},{8,24},{16,0},{24,8},{1,17},{9,25},{17,1},{25,9},{2,18},{10... | collective-permute-start | bytes 688136 | tf_op jit(solution)/shard_map/ppermute | solution.py:39
  34.5 14.4 %collective-permute-start.6 = (bf16[896,128]{1,0:T(8,128)(2,1)S(1)}, bf16[896,128]{1,0:T(8,128)(2,1)S(1)}, u32[]{:S(2)}, u32[]{:S(2)}) collective-permute-start(bf16[896,128]{1,0:T(8,128)(2,1)S(1)} %collective-permute-done), channel_id=1, source_target_pairs={{0,24},{8,16},{16,8},{24,0},{1,25},{9,17},{17,9},{25,1},{2,26},{10... | collective-permute-start | bytes 688136 | tf_op jit(solution)/shard_map/ppermute | solution.py:39
  35.0 22.0 %collective-permute-start.7 = (bf16[896,128]{1,0:T(8,128)(2,1)S(1)}, bf16[896,128]{1,0:T(8,128)(2,1)S(1)}, u32[]{:S(2)}, u32[]{:S(2)}) collective-permute-start(bf16[896,128]{1,0:T(8,128)(2,1)S(1)} %shard_map.100), channel_id=1, source_target_pairs={{0,32},{1,0},{2,36},{3,4},{4,96},{5,64},{6,100},{7,68},{8,40},{9,8... | collective-permute-start | bytes 688136 | tf_op jit(solution)/shard_map/ppermute | solution.py:43
  57.0 21.7 %collective-permute-start.11 = (bf16[4,896,128]{2,1,0:T(8,128)(2,1)S(1)}, bf16[4,896,128]{2,1,0:T(8,128)(2,1)S(1)}, u32[]{:S(2)}, u32[]{:S(2)}) collective-permute-start(bf16[4,896,128]{2,1,0:T(8,128)(2,1)S(1)} %pad_maximum_fusion.1.here_ref), channel_id=1, source_target_pairs={{0,4},{4,0},{1,5},{5,1},{2,6},{6,2},{3,7},{7,3},{8,12},{12,8},{9,1... | collective-permute-start | bytes 2752520 | tf_op jit(solution)/shard_map/ppermute | solution.py:39
  57.0 12.9 %collective-permute-start.8 = (bf16[896,128]{1,0:T(8,128)(2,1)S(1)}, bf16[896,128]{1,0:T(8,128)(2,1)S(1)}, u32[]{:S(2)}, u32[]{:S(2)}) collective-permute-start(bf16[896,128]{1,0:T(8,128)(2,1)S(1)} %collective-permute-done.7), channel_id=1, source_target_pairs={{0,8},{8,0},{16,24},{24,16},{1,9},{9,1},{17,25},{25,17},{2,10},{10... | collective-permute-start | bytes 688136 | tf_op jit(solution)/shard_map/ppermute | solution.py:39
  57.3 21.1 %collective-permute-start.9 = (bf16[896,128]{1,0:T(8,128)(2,1)S(1)}, bf16[896,128]{1,0:T(8,128)(2,1)S(1)}, u32[]{:S(2)}, u32[]{:S(2)}) collective-permute-start(bf16[896,128]{1,0:T(8,128)(2,1)S(1)} %collective-permute-done.7), channel_id=1, source_target_pairs={{0,16},{8,24},{16,0},{24,8},{1,17},{9,25},{17,1},{25,9},{2,18},{10... | collective-permute-start | bytes 688136 | tf_op jit(solution)/shard_map/ppermute | solution.py:39
  61.2 17.1 %collective-permute-start.10 = (bf16[896,128]{1,0:T(8,128)(2,1)S(1)}, bf16[896,128]{1,0:T(8,128)(2,1)S(1)}, u32[]{:S(2)}, u32[]{:S(2)}) collective-permute-start(bf16[896,128]{1,0:T(8,128)(2,1)S(1)} %collective-permute-done.7), channel_id=1, source_target_pairs={{0,24},{8,16},{16,8},{24,0},{1,25},{9,17},{17,9},{25,1},{2,26},{10... | collective-permute-start | bytes 688136 | tf_op jit(solution)/shard_map/ppermute | solution.py:39
  78.5 19.0 %collective-permute-start.15 = (bf16[4,896,128]{2,1,0:T(8,128)(2,1)S(1)}, bf16[4,896,128]{2,1,0:T(8,128)(2,1)S(1)}, u32[]{:S(2)}, u32[]{:S(2)}) collective-permute-start(bf16[4,896,128]{2,1,0:T(8,128)(2,1)S(1)} %pad_maximum_fusion.2.here_ref), channel_id=1, source_target_pairs={{0,4},{4,0},{1,5},{5,1},{2,6},{6,2},{3,7},{7,3},{8,12},{12,8},{9,1... | collective-permute-start | bytes 2752520 | tf_op jit(solution)/shard_map/ppermute | solution.py:39
  78.6 6.4 %copy-start.3 = (bf16[24,4096]{1,0:T(8,128)(2,1)S(1)}, bf16[24,4096]{1,0:T(8,128)(2,1)}, u32[]{:S(2)}) copy-start(bf16[24,4096]{1,0:T(8,128)(2,1)} %param.14) | copy-start | bytes 589828
  80.3 9.0 %collective-permute-start.12 = (bf16[128,896]{1,0:T(8,128)(2,1)S(1)}, bf16[128,896]{1,0:T(8,128)(2,1)S(1)}, u32[]{:S(2)}, u32[]{:S(2)}) collective-permute-start(bf16[128,896]{1,0:T(8,128)(2,1)S(1)} %get-tuple-element.67), channel_id=1, source_target_pairs={{0,64},{64,0},{128,192},{192,128},{1,65},{65,1},{129,193},{193,129... | collective-permute-start | bytes 688136 | tf_op jit(solution)/shard_map/ppermute | solution.py:39
  81.2 12.9 %collective-permute-start.13 = (bf16[128,896]{1,0:T(8,128)(2,1)S(1)}, bf16[128,896]{1,0:T(8,128)(2,1)S(1)}, u32[]{:S(2)}, u32[]{:S(2)}) collective-permute-start(bf16[128,896]{1,0:T(8,128)(2,1)S(1)} %get-tuple-element.69), channel_id=1, source_target_pairs={{0,128},{64,192},{128,0},{192,64},{1,129},{65,193},{129,1},{193,65... | collective-permute-start | bytes 688136 | tf_op jit(solution)/shard_map/ppermute | solution.py:39
  83.0 13.6 %collective-permute-start.14 = (bf16[128,896]{1,0:T(8,128)(2,1)S(1)}, bf16[128,896]{1,0:T(8,128)(2,1)S(1)}, u32[]{:S(2)}, u32[]{:S(2)}) collective-permute-start(bf16[128,896]{1,0:T(8,128)(2,1)S(1)} %get-tuple-element.68), channel_id=1, source_target_pairs={{0,192},{64,128},{128,64},{192,0},{1,193},{65,129},{129,65},{193,1... | collective-permute-start | bytes 688136 | tf_op jit(solution)/shard_map/ppermute | solution.py:39
  85.1 12.4 %collective-permute-start.16 = (bf16[24,4096]{1,0:T(8,128)(2,1)S(1)}, bf16[24,4096]{1,0:T(8,128)(2,1)}, u32[]{:S(2)}, u32[]{:S(2)}) collective-permute-start(bf16[24,4096]{1,0:T(8,128)(2,1)S(1)} %copy-done.3), channel_id=1, source_target_pairs={{0,32},{32,0},{1,33},{33,1},{2,34},{34,2},{3,35},{35,3},{4,36},{36... | collective-permute-start | bytes 589832 | tf_op jit(solution)/shard_map/ppermute | solution.py:39
  100.5 16.9 %copy-start.2 = (f32[128,896]{1,0:T(8,128)S(1)}, f32[128,896]{1,0:T(8,128)}, u32[]{:S(2)}) copy-start(f32[128,896]{1,0:T(8,128)} %convert_add_fusion.1) | copy-start | bytes 1376260
  100.5 8.6 %collective-permute-start.17 = (bf16[128,896]{1,0:T(8,128)(2,1)S(1)}, bf16[128,896]{1,0:T(8,128)(2,1)S(1)}, u32[]{:S(2)}, u32[]{:S(2)}) collective-permute-start(bf16[128,896]{1,0:T(8,128)(2,1)S(1)} %get-tuple-element.64), channel_id=1, source_target_pairs={{0,64},{64,0},{128,192},{192,128},{1,65},{65,1},{129,193},{193,129... | collective-permute-start | bytes 688136 | tf_op jit(solution)/shard_map/ppermute | solution.py:39
  101.8 12.7 %collective-permute-start.18 = (bf16[128,896]{1,0:T(8,128)(2,1)S(1)}, bf16[128,896]{1,0:T(8,128)(2,1)S(1)}, u32[]{:S(2)}, u32[]{:S(2)}) collective-permute-start(bf16[128,896]{1,0:T(8,128)(2,1)S(1)} %get-tuple-element.66), channel_id=1, source_target_pairs={{0,128},{64,192},{128,0},{192,64},{1,129},{65,193},{129,1},{193,65... | collective-permute-start | bytes 688136 | tf_op jit(solution)/shard_map/ppermute | solution.py:39
  105.2 12.1 %collective-permute-start.19 = (bf16[128,896]{1,0:T(8,128)(2,1)S(1)}, bf16[128,896]{1,0:T(8,128)(2,1)S(1)}, u32[]{:S(2)}, u32[]{:S(2)}) collective-permute-start(bf16[128,896]{1,0:T(8,128)(2,1)S(1)} %get-tuple-element.65), channel_id=1, source_target_pairs={{0,192},{64,128},{128,64},{192,0},{1,193},{65,129},{129,65},{193,1... | collective-permute-start | bytes 688136 | tf_op jit(solution)/shard_map/ppermute | solution.py:39
  117.9 9.7 %collective-permute-start.20 = (bf16[32,2688]{1,0:T(8,128)(2,1)S(1)}, bf16[32,2688]{1,0:T(8,128)(2,1)S(1)}, u32[]{:S(2)}, u32[]{:S(2)}) collective-permute-start(bf16[32,2688]{1,0:T(8,128)(2,1)S(1)} %get-tuple-element.109), channel_id=1, source_target_pairs={{0,1},{1,0},{2,3},{3,2},{4,5},{5,4},{6,7},{7,6},{8,9},{9,8},{10,11... | collective-permute-start | bytes 516104 | tf_op jit(solution)/shard_map/ppermute | solution.py:39
  119.7 19.0 %collective-permute-start.21 = (bf16[32,2688]{1,0:T(8,128)(2,1)S(1)}, bf16[32,2688]{1,0:T(8,128)(2,1)S(1)}, u32[]{:S(2)}, u32[]{:S(2)}) collective-permute-start(bf16[32,2688]{1,0:T(8,128)(2,1)S(1)} %get-tuple-element.110), channel_id=1, source_target_pairs={{0,2},{1,3},{2,0},{3,1},{4,6},{5,7},{6,4},{7,5},{8,10},{9,11},{10,... | collective-permute-start | bytes 516104 | tf_op jit(solution)/shard_map/ppermute | solution.py:39
  127.5 11.2 %collective-permute-start.22 = (bf16[32,2688]{1,0:T(8,128)(2,1)S(1)}, bf16[32,2688]{1,0:T(8,128)(2,1)S(1)}, u32[]{:S(2)}, u32[]{:S(2)}) collective-permute-start(bf16[32,2688]{1,0:T(8,128)(2,1)S(1)} %get-tuple-element.111), channel_id=1, source_target_pairs={{0,3},{1,2},{2,1},{3,0},{4,7},{5,6},{6,5},{7,4},{8,11},{9,10},{10,... | collective-permute-start | bytes 516104 | tf_op jit(solution)/shard_map/ppermute | solution.py:39
  141.6 7.3 %collective-permute-start.23 = (bf16[32,1536]{1,0:T(8,128)(2,1)S(1)}, bf16[32,1536]{1,0:T(8,128)(2,1)S(1)}, u32[]{:S(2)}, u32[]{:S(2)}) collective-permute-start(bf16[32,1536]{1,0:T(8,128)(2,1)S(1)} %pad_maximum_fusion.9), channel_id=1, source_target_pairs={{0,3},{1,2},{2,1},{3,0},{4,7},{5,6},{6,5},{7,4},{8,11},{9,10},{10,... | collective-permute-start | bytes 294920 | tf_op jit(solution)/shard_map/ppermute | solution.py:39
  143.6 8.8 %collective-permute-start.24 = (bf16[32,1536]{1,0:T(8,128)(2,1)S(1)}, bf16[32,1536]{1,0:T(8,128)(2,1)S(1)}, u32[]{:S(2)}, u32[]{:S(2)}) collective-permute-start(bf16[32,1536]{1,0:T(8,128)(2,1)S(1)} %pad_maximum_fusion.9), channel_id=1, source_target_pairs={{0,2},{1,3},{2,0},{3,1},{4,6},{5,7},{6,4},{7,5},{8,10},{9,11},{10,... | collective-permute-start | bytes 294920 | tf_op jit(solution)/shard_map/ppermute | solution.py:39
  145.6 6.8 %collective-permute-start.25 = (bf16[32,1536]{1,0:T(8,128)(2,1)S(1)}, bf16[32,1536]{1,0:T(8,128)(2,1)S(1)}, u32[]{:S(2)}, u32[]{:S(2)}) collective-permute-start(bf16[32,1536]{1,0:T(8,128)(2,1)S(1)} %pad_maximum_fusion.9), channel_id=1, source_target_pairs={{0,1},{1,0},{2,3},{3,2},{4,5},{5,4},{6,7},{7,6},{8,9},{9,8},{10,11... | collective-permute-start | bytes 294920 | tf_op jit(solution)/shard_map/ppermute | solution.py:39
  (2 other events, 1.7 us)
Sparse Core Ops, SparseCore 0:
  9.9 66.0 all-gather.2
  97.6 55.3 all-gather.4

commit v7 on v4

--- a/solution.py
+++ b/solution.py
@@ -154,41 +154,60 @@
     y, zh, x, c, t = (lax.axis_index(name) for name in AXES)
 
     packed = pack(query_weight, kv_weight.T)
-    first = move(packed, lambda y, zh, x, c, t: ((2 * zh + c) ^ y, t & 1, x, t >> 1, y))
     wo_other = swap(out_weight, "zh", 1)
+    first = move(packed, lambda y, zh, x, c, t: ((2 * zh + c) ^ y, t >> 1, x, t & 1, y))
+    second = move(packed, lambda y, zh, x, c, t: ((2 * zh + c) ^ y, 1 - (t >> 1), x, t & 1, y))
 
     widened = tokens.astype(F32)
     squares = jnp.sum(widened * widened, axis=1)
     gained = (widened * norm_gain[None, :]).astype(BF)
 
-    def features(e):
-        s = y ^ e ^ t
+    def features(pairs_at):
         picked = [
-            lax.dynamic_slice(gained, (0, (((s >> 1) * 4 + (x ^ d)) * 2 + (s & 1)) * 256), (ROWS, 256))
-            for d in range(4)
+            lax.dynamic_slice(gained, (0, (((s >> 1) * 4 + at) * 2 + (s & 1)) * 256), (ROWS, 256))
+            for s, at in pairs_at
         ]
         return jnp.concatenate(picked, axis=1)
 
-    ring = [swap(features(e), "y", e) for e in (1, 2, 3)]
-    first, wo_other, packed, *ring = lax.optimization_barrier((first, wo_other, packed, *ring))
-    second = move(packed, lambda y, zh, x, c, t: ((2 * zh + c) ^ y, 1 - (t & 1), x, t >> 1, y))
-    inputs = jnp.concatenate([features(0)] + ring, axis=0)
+    def features_a(e):
+        return features([(y ^ e ^ t, x ^ d) for d in range(4)])
+
+    def features_b(e):
+        return features([(y ^ d ^ t, x ^ e) for d in range(4)])
+
+    ring_a = [swap(features_a(e), "y", e) for e in (1, 2, 3)]
+    ring_b = [swap(features_b(e), "x", e) for e in (1, 2, 3)]
+    ring_a[0], wo_other = lax.optimization_barrier((ring_a[0], wo_other))
+    first, second, *rings = lax.optimization_barrier((first, second, *ring_a, *ring_b))
+    inputs_a = jnp.concatenate([features_a(0)] + rings[:3], axis=0)
+    inputs_b = jnp.concatenate([features_b(0)] + rings[3:], axis=0)
 
     wo_piece = jnp.concatenate([out_weight, wo_other], axis=0)
     wo = lax.all_gather(wo_piece, ("y", "x", "core"), axis=0, tiled=True)
 
-    summed = []
-    for block in (first, second):
-        here = jnp.stack([block] + [swap(block, "x", d) for d in (1, 2, 3)])
-        sent, total = project(inputs, here, swap(here, "core", 1))
-        for e in (1, 2, 3):
-            total = total + swap(sent[e - 1], "y", e).astype(F32)
-        summed.append(total)
-    base = 2 * c + zh
-    q_slots = [half[:, at : at + 384] for at in (0, 384) for half in summed]
-    kv_slots = [half[:, at : at + 64] for at in (768, 832) for half in summed]
-    q_sum = jnp.concatenate(by_index(q_slots, base), axis=1)
-    kv_sum = jnp.concatenate(by_index(kv_slots, base), axis=1)
+    block_a = pick(zh == 1, first, second)
+    block_b = pick(zh == 1, second, first)
+    came_a = [swap(block_a, "x", d) for d in (1, 2, 3)]
+    came_b = [swap(block_b, "y", d) for d in (1, 2, 3)]
+    here_a = jnp.stack([block_a] + came_a)
+    here_b = jnp.stack([block_b] + came_b)
+    sent_a, total_a = project(inputs_a, here_a, swap(here_a, "core", 1))
+    sent_b, total_b = project(inputs_b, here_b, swap(here_b, "core", 1))
+    got_a = [swap(sent_a[e - 1], "y", e) for e in (1, 2, 3)]
+    got_b = [swap(sent_b[e - 1], "x", e) for e in (1, 2, 3)]
+    summed = [
+        total + sum(part.astype(F32) for part in parts) for total, parts in ((total_a, got_a), (total_b, got_b))
+    ]
+
+    def ordered(width, at):
+        columns = []
+        for half in summed:
+            here, there = half[:, at : at + width], half[:, at + width : at + 2 * width]
+            columns += [pick(c == 1, here, there), pick(c == 1, there, here)]
+        return jnp.concatenate(columns, axis=1)
+
+    q_sum = ordered(384, 0)
+    kv_sum = ordered(64, 768)
 
     kv_short = kv_sum.astype(BF)
     high = lax.reduce_precision(squares, 8, 7)

time: 171 us -> 175 us (1.023); the launches traced: 170 us -> 172 us
  waiting for transfers between devices: 77.4 us -> 73.5 us
  other arithmetic: 5.37 us -> 7.19 us
    ppermute x24 -> x27, waiting for transfers between devices: 73.3 us -> 62.7 us  [swap(): return lax.ppermute(value, axis, [(i, i ^ d) for i in range(n)])]
    ppermute x24 -> x27, starting transfers between devices: 41.9 us -> 49.1 us  [swap(): return lax.ppermute(value, axis, [(i, i ^ d) for i in range(n)])]
    ppermute x2, waiting for transfers between devices: 4.15 us -> 10.7 us  [move(): lax.ppermute(value, AXES, [(flat(*at), flat(*where(*at))) for at in every...]
    ppermute x2, starting transfers between devices: 18.1 us -> 11.7 us  [move(): lax.ppermute(value, AXES, [(flat(*at), flat(*where(*at))) for at in every...]
    concatenate x2, other arithmetic: 0.15 us -> 2.82 us  [the longest x1 2.75 us: body(): inputs_a = jnp.concatenate([features_a(0)] + rings[:3], axis=0)]
  transfers between devices with their start and end apart: 27 -> 30, of which waited for: 14 -> 17; matrix products, arithmetic and copies ran while one was open for 3% -> 4% of each run, Pallas kernels for 2% -> 3%
where the time goes in v7:
time: 175 us; the launch traced here: 172 us
  waiting for transfers between devices  73.5 us (42%)
  starting transfers between devices  60.9 us (35%)
  between operations  14.7 us (8%)
  matrix products  8.6 us (5%)
  other arithmetic  7.19 us (4%)
  Pallas kernels  4.39 us (3%)
  local copies, waits for them, and re-layouts  2.72 us (2%)
    ppermute x27, waiting for transfers between devices, swap(): return lax.ppermute(value, axis, [(i, i ^ d) for i in range(n)])  62.7 us
    ppermute x27, starting transfers between devices, swap(): return lax.ppermute(value, axis, [(i, i ^ d) for i in range(n)])  49.1 us
    ppermute x2, starting transfers between devices, move(): lax.ppermute(value, AXES, [(flat(*at), flat(*where(*at))) for at in every...  11.7 us
    ppermute x2, waiting for transfers between devices, move(): lax.ppermute(value, AXES, [(flat(*at), flat(*where(*at))) for at in every...  10.7 us
    dot_general x1, matrix products, body(): return jnp.dot(all_rows, wo, preferred_element_type=F32).astype(BF)  7.35 us
    pallas_call x2, Pallas kernels, project(): pl.pallas_call(project_kernel, out_shape=(jax.ShapeDtypeStruct((3, ROWS,...  4.35 us
  transfers between devices with their start and end apart: 30, of which 17 were waited for; matrix products, arithmetic and copies ran while one was open for 4% of the time, Pallas kernels for 3%

profile of v7, /device:TPU:24, one launch (start us, length us, event | category | flops | bytes accessed | tf_op | source)
XLA Modules:
  0.0 172.0 jit_solution(5766970350232342594)
XLA Ops:
  9.4 7.2 %collective-permute-start.3 = (bf16[24,4096]{1,0:T(8,128)(2,1)S(1)}, bf16[24,4096]{1,0:T(8,128)(2,1)S(1)}, u32[]{:S(2)}, u32[]{:S(2)}) collective-permute-start(bf16[24,4096]{1,0:T(8,128)(2,1)S(1)} %copy-done.6), channel_id=1, source_target_pairs={{0,32},{32,0},{1,33},{33,1},{2,34},{34,2},{3,35},{35,3},{4,36},{36... | collective-permute-start | bytes 589832 | tf_op jit(solution)/shard_map/ppermute | solution.py:39
  16.6 4.7 %collective-permute-done.3 = bf16[24,4096]{1,0:T(8,128)(2,1)S(1)} collective-permute-done((bf16[24,4096]{1,0:T(8,128)(2,1)S(1)}, bf16[24,4096]{1,0:T(8,128)(2,1)S(1)}, u32[]{:S(2)}, u32[]{:S(2)}) %collective-permute-start.3) | collective-permute-done | bytes 196640 | tf_op jit(solution)/shard_map/ppermute | solution.py:39
  22.2 6.9 %collective-permute-start = (bf16[896,128]{1,0:T(8,128)(2,1)S(1)}, bf16[896,128]{1,0:T(8,128)(2,1)S(1)}, u32[]{:S(2)}, u32[]{:S(2)}) collective-permute-start(bf16[896,128]{1,0:T(8,128)(2,1)S(1)} %shard_map.118), channel_id=1, source_target_pairs={{0,0},{1,4},{2,32},{3,36},{4,64},{5,68},{6,96},{7,100},{8,8},{9,12... | collective-permute-start | bytes 688136 | tf_op jit(solution)/shard_map/ppermute | solution.py:43
  29.1 4.8 %collective-permute-start.1 = (bf16[896,128]{1,0:T(8,128)(2,1)S(1)}, bf16[896,128]{1,0:T(8,128)(2,1)S(1)}, u32[]{:S(2)}, u32[]{:S(2)}) collective-permute-start(bf16[896,128]{1,0:T(8,128)(2,1)S(1)} %shard_map.118), channel_id=1, source_target_pairs={{0,32},{1,36},{2,0},{3,4},{4,96},{5,100},{6,64},{7,68},{8,40},{9,4... | collective-permute-start | bytes 688136 | tf_op jit(solution)/shard_map/ppermute | solution.py:43
  34.0 2.3 %collective-permute-start.5 = (bf16[128,1024]{1,0:T(8,128)(2,1)S(1)}, bf16[128,1024]{1,0:T(8,128)(2,1)S(1)}, u32[]{:S(2)}, u32[]{:S(2)}) collective-permute-start(bf16[128,1024]{1,0:T(8,128)(2,1)S(1)} %get-tuple-element.113), channel_id=1, source_target_pairs={{0,192},{64,128},{128,64},{192,0},{1,193},{65,129},{129,65},{193,1... | collective-permute-start | bytes 786440 | tf_op jit(solution)/shard_map/ppermute | solution.py:39
  37.8 2.6 %collective-permute-start.4 = (bf16[128,1024]{1,0:T(8,128)(2,1)S(1)}, bf16[128,1024]{1,0:T(8,128)(2,1)S(1)}, u32[]{:S(2)}, u32[]{:S(2)}) collective-permute-start(bf16[128,1024]{1,0:T(8,128)(2,1)S(1)} %get-tuple-element.111), channel_id=1, source_target_pairs={{0,128},{64,192},{128,0},{192,64},{1,129},{65,193},{129,1},{193,65... | collective-permute-start | bytes 786440 | tf_op jit(solution)/shard_map/ppermute | solution.py:39
  40.4 2.7 %collective-permute-start.7 = (bf16[128,1024]{1,0:T(8,128)(2,1)S(1)}, bf16[128,1024]{1,0:T(8,128)(2,1)S(1)}, u32[]{:S(2)}, u32[]{:S(2)}) collective-permute-start(bf16[128,1024]{1,0:T(8,128)(2,1)S(1)} %get-tuple-element.110), channel_id=1, source_target_pairs={{0,16},{8,24},{16,0},{24,8},{1,17},{9,25},{17,1},{25,9},{2,18},{10... | collective-permute-start | bytes 786440 | tf_op jit(solution)/shard_map/ppermute | solution.py:39
  43.1 10.7 %collective-permute-done.1 = bf16[896,128]{1,0:T(8,128)(2,1)S(1)} collective-permute-done((bf16[896,128]{1,0:T(8,128)(2,1)S(1)}, bf16[896,128]{1,0:T(8,128)(2,1)S(1)}, u32[]{:S(2)}, u32[]{:S(2)}) %collective-permute-start.1) | collective-permute-done | bytes 229408 | tf_op jit(solution)/shard_map/ppermute | solution.py:43
  53.8 2.8 %collective-permute-start.8 = (bf16[128,1024]{1,0:T(8,128)(2,1)S(1)}, bf16[128,1024]{1,0:T(8,128)(2,1)}, u32[]{:S(2)}, u32[]{:S(2)}) collective-permute-start(bf16[128,1024]{1,0:T(8,128)(2,1)S(1)} %get-tuple-element.108), channel_id=1, source_target_pairs={{0,24},{8,16},{16,8},{24,0},{1,25},{9,17},{17,9},{25,1},{2,26},{10... | collective-permute-start | bytes 786440 | tf_op jit(solution)/shard_map/ppermute | solution.py:39
  56.6 2.6 %collective-permute-done.5 = bf16[128,1024]{1,0:T(8,128)(2,1)S(1)} collective-permute-done((bf16[128,1024]{1,0:T(8,128)(2,1)S(1)}, bf16[128,1024]{1,0:T(8,128)(2,1)S(1)}, u32[]{:S(2)}, u32[]{:S(2)}) %collective-permute-start.5) | collective-permute-done | bytes 262176 | tf_op jit(solution)/shard_map/ppermute | solution.py:39
  60.0 7.1 %collective-permute-done.8 = bf16[128,1024]{1,0:T(8,128)(2,1)} collective-permute-done((bf16[128,1024]{1,0:T(8,128)(2,1)S(1)}, bf16[128,1024]{1,0:T(8,128)(2,1)}, u32[]{:S(2)}, u32[]{:S(2)}) %collective-permute-start.8) | collective-permute-done | bytes 262176 | tf_op jit(solution)/shard_map/ppermute | solution.py:39
  67.5 2.8 %collective-permute-start.10 = (bf16[896,128]{1,0:T(8,128)(2,1)S(1)}, bf16[896,128]{1,0:T(8,128)(2,1)S(1)}, u32[]{:S(2)}, u32[]{:S(2)}) collective-permute-start(bf16[896,128]{1,0:T(8,128)(2,1)S(1)} %get-tuple-element.66), channel_id=1, source_target_pairs={{0,16},{8,24},{16,0},{24,8},{1,17},{9,25},{17,1},{25,9},{2,18},{10... | collective-permute-start | bytes 688136 | tf_op jit(solution)/shard_map/ppermute | solution.py:39
  70.3 1.7 collective-permute-start.11
  72.8 2.9 %collective-permute-done.9 = bf16[896,128]{1,0:T(8,128)(2,1)S(1)} collective-permute-done((bf16[896,128]{1,0:T(8,128)(2,1)S(1)}, bf16[896,128]{1,0:T(8,128)(2,1)S(1)}, u32[]{:S(2)}, u32[]{:S(2)}) %collective-permute-start.9) | collective-permute-done | bytes 229408 | tf_op jit(solution)/shard_map/ppermute | solution.py:39
  75.7 1.7 collective-permute-start.18
  77.4 4.8 %collective-permute-done.10 = bf16[896,128]{1,0:T(8,128)(2,1)S(1)} collective-permute-done((bf16[896,128]{1,0:T(8,128)(2,1)S(1)}, bf16[896,128]{1,0:T(8,128)(2,1)S(1)}, u32[]{:S(2)}, u32[]{:S(2)}) %collective-permute-start.10) | collective-permute-done | bytes 229408 | tf_op jit(solution)/shard_map/ppermute | solution.py:39
  82.2 4.8 %collective-permute-done.11 = bf16[896,128]{1,0:T(8,128)(2,1)S(1)} collective-permute-done((bf16[896,128]{1,0:T(8,128)(2,1)S(1)}, bf16[896,128]{1,0:T(8,128)(2,1)S(1)}, u32[]{:S(2)}, u32[]{:S(2)}) %collective-permute-start.11) | collective-permute-done | bytes 229408 | tf_op jit(solution)/shard_map/ppermute | solution.py:39
  89.3 2.2 %collective-permute-done.18 = bf16[896,128]{1,0:T(8,128)(2,1)S(1)} collective-permute-done((bf16[896,128]{1,0:T(8,128)(2,1)S(1)}, bf16[896,128]{1,0:T(8,128)(2,1)S(1)}, u32[]{:S(2)}, u32[]{:S(2)}) %collective-permute-start.18) | collective-permute-done | bytes 229408 | tf_op jit(solution)/shard_map/ppermute | solution.py:39
  91.8 2.8 %fusion.13 = (bf16[512,1024]{1,0:T(8,128)(2,1)S(1)}, bf16[512,1024]{1,0:T(8,128)(2,1)S(1)}) fusion(bf16[128,256]{1,0:T(8,128)(2,1)S(1)} %get-tuple-element.50, bf16[128,1024]{1,0:T(8,128)(2,1)} %copy-done.2, bf16[128,1024]{1,0:T(8,128)(2,1)} %copy-done.4, bf16[128,1024]{1,0:T(8,128)(2,1)S(1)} %collective-permute-done.2, ...), kind=kLoop, calls=%fused_computation.21 | loop fusion | flops 14155776 | bytes 4128768 | tf_op jit(solution)/shard_map/concatenate | solution.py:182
  94.6 2.8 %shard_map.119 = (bf16[3,128,896]{2,1,0:T(8,128)(2,1)S(1)}, f32[128,896]{1,0:T(8,128)S(1)}) custom-call(bf16[512,1024]{1,0:T(8,128)(2,1)S(1)} %get-tuple-element.106.x_ref, bf16[4,896,128]{2,1,0:T(8,128)(2,1)S(1)} %pad_maximum_fusion.2.here_ref, bf16[4,896,128]{2,1,0:T(8,128)(2,1)} %collective-permute-done.12.there_ref), custom_call_target="tpu_custom_call" | custom-call | flops 939524096 | bytes 4000000 | tf_op jit(solution)/shard_map/pallas_call | solution.py:131
  98.6 4.5 %collective-permute-start.14 = (bf16[128,896]{1,0:T(8,128)(2,1)S(1)}, bf16[128,896]{1,0:T(8,128)(2,1)S(1)}, u32[]{:S(2)}, u32[]{:S(2)}) collective-permute-start(bf16[128,896]{1,0:T(8,128)(2,1)S(1)} %get-tuple-element.56), channel_id=1, source_target_pairs={{0,128},{64,192},{128,0},{192,64},{1,129},{65,193},{129,1},{193,65... | collective-permute-start | bytes 688136 | tf_op jit(solution)/shard_map/ppermute | solution.py:39
  104.8 2.1 %collective-permute-start.21 = (bf16[128,896]{1,0:T(8,128)(2,1)S(1)}, bf16[128,896]{1,0:T(8,128)(2,1)S(1)}, u32[]{:S(2)}, u32[]{:S(2)}) collective-permute-start(bf16[128,896]{1,0:T(8,128)(2,1)S(1)} %get-tuple-element.59), channel_id=1, source_target_pairs={{0,16},{8,24},{16,0},{24,8},{1,17},{9,25},{17,1},{25,9},{2,18},{10... | collective-permute-start | bytes 688136 | tf_op jit(solution)/shard_map/ppermute | solution.py:39
  106.9 4.2 %collective-permute-done.13 = bf16[128,896]{1,0:T(8,128)(2,1)S(1)} collective-permute-done((bf16[128,896]{1,0:T(8,128)(2,1)S(1)}, bf16[128,896]{1,0:T(8,128)(2,1)S(1)}, u32[]{:S(2)}, u32[]{:S(2)}) %collective-permute-start.13) | collective-permute-done | bytes 229408 | tf_op jit(solution)/shard_map/ppermute | solution.py:39
  112.1 5.6 %collective-permute-done.14 = bf16[128,896]{1,0:T(8,128)(2,1)S(1)} collective-permute-done((bf16[128,896]{1,0:T(8,128)(2,1)S(1)}, bf16[128,896]{1,0:T(8,128)(2,1)S(1)}, u32[]{:S(2)}, u32[]{:S(2)}) %collective-permute-start.14) | collective-permute-done | bytes 229408 | tf_op jit(solution)/shard_map/ppermute | solution.py:39
  117.7 3.1 %collective-permute-done.15 = bf16[128,896]{1,0:T(8,128)(2,1)S(1)} collective-permute-done((bf16[128,896]{1,0:T(8,128)(2,1)S(1)}, bf16[128,896]{1,0:T(8,128)(2,1)S(1)}, u32[]{:S(2)}, u32[]{:S(2)}) %collective-permute-start.15) | collective-permute-done | bytes 229408 | tf_op jit(solution)/shard_map/ppermute | solution.py:39
  122.8 6.3 %collective-permute-start.24 = (bf16[32,2688]{1,0:T(8,128)(2,1)S(1)}, bf16[32,2688]{1,0:T(8,128)(2,1)S(1)}, u32[]{:S(2)}, u32[]{:S(2)}) collective-permute-start(bf16[32,2688]{1,0:T(8,128)(2,1)S(1)} %get-tuple-element.115), channel_id=1, source_target_pairs={{0,2},{1,3},{2,0},{3,1},{4,6},{5,7},{6,4},{7,5},{8,10},{9,11},{10,... | collective-permute-start | bytes 516104 | tf_op jit(solution)/shard_map/ppermute | solution.py:39
  130.6 5.2 %collective-permute-done.24 = bf16[32,2688]{1,0:T(8,128)(2,1)S(1)} collective-permute-done((bf16[32,2688]{1,0:T(8,128)(2,1)S(1)}, bf16[32,2688]{1,0:T(8,128)(2,1)S(1)}, u32[]{:S(2)}, u32[]{:S(2)}) %collective-permute-start.24) | collective-permute-done | bytes 172064 | tf_op jit(solution)/shard_map/ppermute | solution.py:39
  135.8 6.0 %collective-permute-done.25 = bf16[32,2688]{1,0:T(8,128)(2,1)S(1)} collective-permute-done((bf16[32,2688]{1,0:T(8,128)(2,1)S(1)}, bf16[32,2688]{1,0:T(8,128)(2,1)S(1)}, u32[]{:S(2)}, u32[]{:S(2)}) %collective-permute-start.25) | collective-permute-done | bytes 172064 | tf_op jit(solution)/shard_map/ppermute | solution.py:39
  144.7 2.6 %collective-permute-start.26 = (bf16[32,1536]{1,0:T(8,128)(2,1)S(1)}, bf16[32,1536]{1,0:T(8,128)(2,1)S(1)}, u32[]{:S(2)}, u32[]{:S(2)}) collective-permute-start(bf16[32,1536]{1,0:T(8,128)(2,1)S(1)} %pad_maximum_fusion.13), channel_id=1, source_target_pairs={{0,3},{1,2},{2,1},{3,0},{4,7},{5,6},{6,5},{7,4},{8,11},{9,10},{10,... | collective-permute-start | bytes 294920 | tf_op jit(solution)/shard_map/ppermute | solution.py:39
  147.3 2.8 %collective-permute-start.27 = (bf16[32,1536]{1,0:T(8,128)(2,1)S(1)}, bf16[32,1536]{1,0:T(8,128)(2,1)S(1)}, u32[]{:S(2)}, u32[]{:S(2)}) collective-permute-start(bf16[32,1536]{1,0:T(8,128)(2,1)S(1)} %pad_maximum_fusion.13), channel_id=1, source_target_pairs={{0,2},{1,3},{2,0},{3,1},{4,6},{5,7},{6,4},{7,5},{8,10},{9,11},{10,... | collective-permute-start | bytes 294920 | tf_op jit(solution)/shard_map/ppermute | solution.py:39
  151.3 6.3 %collective-permute-done.27 = bf16[32,1536]{1,0:T(8,128)(2,1)S(1)} collective-permute-done((bf16[32,1536]{1,0:T(8,128)(2,1)S(1)}, bf16[32,1536]{1,0:T(8,128)(2,1)S(1)}, u32[]{:S(2)}, u32[]{:S(2)}) %collective-permute-start.27) | collective-permute-done | bytes 98336 | tf_op jit(solution)/shard_map/ppermute | solution.py:39
  157.8 7.4 %convolution_convert_fusion = bf16[128,4096]{1,0:T(8,128)(2,1)} fusion(bf16[1536,4096]{1,0:T(8,128)(2,1)} %all-gather.2.cloned.1.call-done, bf16[32,1536]{1,0:T(8,128)(2,1)S(1)} %broadcast_select_fusion.6, bf16[32,1536]{1,0:T(8,128)(2,1)S(1)} %get-tuple-element.72, bf16[32,1536]{1,0:T(8,128)(2,1)S(1)} %get-tuple-element.71, ...), kind=kOutput, calls=%fused_computation.1 | convolution fusion | flops 1612709888 | bytes 14024704 | tf_op jit(solution)/shard_map/dot_general | solution.py:244
  (119 shorter events, 20.2 us)
Async XLA Ops:
  6.5 151.2 %all-gather.2.cloned.1.call-start = ((), (), s32[]{:S(2)}) async-start(), calls=%async_computation | async-start | bytes 12976128 | tf_op jit(solution)/shard_map/all_gather | solution.py:186
  8.5 12.8 %collective-permute-start.2 = (bf16[128,1024]{1,0:T(8,128)(2,1)S(1)}, bf16[128,1024]{1,0:T(8,128)(2,1)S(1)}, u32[]{:S(2)}, u32[]{:S(2)}) collective-permute-start(bf16[128,1024]{1,0:T(8,128)(2,1)S(1)} %get-tuple-element.109), channel_id=1, source_target_pairs={{0,64},{64,0},{128,192},{192,128},{1,65},{65,1},{129,193},{193,129... | collective-permute-start | bytes 786440 | tf_op jit(solution)/shard_map/ppermute | solution.py:39
  9.4 11.9 %collective-permute-start.3 = (bf16[24,4096]{1,0:T(8,128)(2,1)S(1)}, bf16[24,4096]{1,0:T(8,128)(2,1)S(1)}, u32[]{:S(2)}, u32[]{:S(2)}) collective-permute-start(bf16[24,4096]{1,0:T(8,128)(2,1)S(1)} %copy-done.6), channel_id=1, source_target_pairs={{0,32},{32,0},{1,33},{33,1},{2,34},{34,2},{3,35},{35,3},{4,36},{36... | collective-permute-start | bytes 589832 | tf_op jit(solution)/shard_map/ppermute | solution.py:39
  22.2 18.2 %collective-permute-start = (bf16[896,128]{1,0:T(8,128)(2,1)S(1)}, bf16[896,128]{1,0:T(8,128)(2,1)S(1)}, u32[]{:S(2)}, u32[]{:S(2)}) collective-permute-start(bf16[896,128]{1,0:T(8,128)(2,1)S(1)} %shard_map.118), channel_id=1, source_target_pairs={{0,0},{1,4},{2,32},{3,36},{4,64},{5,68},{6,96},{7,100},{8,8},{9,12... | collective-permute-start | bytes 688136 | tf_op jit(solution)/shard_map/ppermute | solution.py:43
  29.1 24.7 %collective-permute-start.1 = (bf16[896,128]{1,0:T(8,128)(2,1)S(1)}, bf16[896,128]{1,0:T(8,128)(2,1)S(1)}, u32[]{:S(2)}, u32[]{:S(2)}) collective-permute-start(bf16[896,128]{1,0:T(8,128)(2,1)S(1)} %shard_map.118), channel_id=1, source_target_pairs={{0,32},{1,36},{2,0},{3,4},{4,96},{5,100},{6,64},{7,68},{8,40},{9,4... | collective-permute-start | bytes 688136 | tf_op jit(solution)/shard_map/ppermute | solution.py:43
  34.0 25.2 %collective-permute-start.5 = (bf16[128,1024]{1,0:T(8,128)(2,1)S(1)}, bf16[128,1024]{1,0:T(8,128)(2,1)S(1)}, u32[]{:S(2)}, u32[]{:S(2)}) collective-permute-start(bf16[128,1024]{1,0:T(8,128)(2,1)S(1)} %get-tuple-element.113), channel_id=1, source_target_pairs={{0,192},{64,128},{128,64},{192,0},{1,193},{65,129},{129,65},{193,1... | collective-permute-start | bytes 786440 | tf_op jit(solution)/shard_map/ppermute | solution.py:39
  36.3 22.9 %collective-permute-start.6 = (bf16[128,1024]{1,0:T(8,128)(2,1)S(1)}, bf16[128,1024]{1,0:T(8,128)(2,1)S(1)}, u32[]{:S(2)}, u32[]{:S(2)}) collective-permute-start(bf16[128,1024]{1,0:T(8,128)(2,1)S(1)} %get-tuple-element.112), channel_id=1, source_target_pairs={{0,8},{8,0},{16,24},{24,16},{1,9},{9,1},{17,25},{25,17},{2,10},{10... | collective-permute-start | bytes 786440 | tf_op jit(solution)/shard_map/ppermute | solution.py:39
  37.8 21.5 %collective-permute-start.4 = (bf16[128,1024]{1,0:T(8,128)(2,1)S(1)}, bf16[128,1024]{1,0:T(8,128)(2,1)S(1)}, u32[]{:S(2)}, u32[]{:S(2)}) collective-permute-start(bf16[128,1024]{1,0:T(8,128)(2,1)S(1)} %get-tuple-element.111), channel_id=1, source_target_pairs={{0,128},{64,192},{128,0},{192,64},{1,129},{65,193},{129,1},{193,65... | collective-permute-start | bytes 786440 | tf_op jit(solution)/shard_map/ppermute | solution.py:39
  40.4 18.8 %collective-permute-start.7 = (bf16[128,1024]{1,0:T(8,128)(2,1)S(1)}, bf16[128,1024]{1,0:T(8,128)(2,1)S(1)}, u32[]{:S(2)}, u32[]{:S(2)}) collective-permute-start(bf16[128,1024]{1,0:T(8,128)(2,1)S(1)} %get-tuple-element.110), channel_id=1, source_target_pairs={{0,16},{8,24},{16,0},{24,8},{1,17},{9,25},{17,1},{25,9},{2,18},{10... | collective-permute-start | bytes 786440 | tf_op jit(solution)/shard_map/ppermute | solution.py:39
  53.8 13.3 %collective-permute-start.8 = (bf16[128,1024]{1,0:T(8,128)(2,1)S(1)}, bf16[128,1024]{1,0:T(8,128)(2,1)}, u32[]{:S(2)}, u32[]{:S(2)}) collective-permute-start(bf16[128,1024]{1,0:T(8,128)(2,1)S(1)} %get-tuple-element.108), channel_id=1, source_target_pairs={{0,24},{8,16},{16,8},{24,0},{1,25},{9,17},{17,9},{25,1},{2,26},{10... | collective-permute-start | bytes 786440 | tf_op jit(solution)/shard_map/ppermute | solution.py:39
  59.2 27.9 %copy-start.2 = (bf16[128,1024]{1,0:T(8,128)(2,1)}, bf16[128,1024]{1,0:T(8,128)(2,1)S(1)}, u32[]{:S(2)}) copy-start(bf16[128,1024]{1,0:T(8,128)(2,1)S(1)} %collective-permute-done.5) | copy-start | bytes 786436
  59.2 27.9 %copy-start.3 = (bf16[128,1024]{1,0:T(8,128)(2,1)}, bf16[128,1024]{1,0:T(8,128)(2,1)S(1)}, u32[]{:S(2)}) copy-start(bf16[128,1024]{1,0:T(8,128)(2,1)S(1)} %collective-permute-done.6) | copy-start | bytes 786436
  67.2 8.6 %collective-permute-start.9 = (bf16[896,128]{1,0:T(8,128)(2,1)S(1)}, bf16[896,128]{1,0:T(8,128)(2,1)S(1)}, u32[]{:S(2)}, u32[]{:S(2)}) collective-permute-start(bf16[896,128]{1,0:T(8,128)(2,1)S(1)} %get-tuple-element.66), channel_id=1, source_target_pairs={{0,8},{8,0},{16,24},{24,16},{1,9},{9,1},{17,25},{25,17},{2,10},{10... | collective-permute-start | bytes 688136 | tf_op jit(solution)/shard_map/ppermute | solution.py:39
  67.5 14.7 %collective-permute-start.10 = (bf16[896,128]{1,0:T(8,128)(2,1)S(1)}, bf16[896,128]{1,0:T(8,128)(2,1)S(1)}, u32[]{:S(2)}, u32[]{:S(2)}) collective-permute-start(bf16[896,128]{1,0:T(8,128)(2,1)S(1)} %get-tuple-element.66), channel_id=1, source_target_pairs={{0,16},{8,24},{16,0},{24,8},{1,17},{9,25},{17,1},{25,9},{2,18},{10... | collective-permute-start | bytes 688136 | tf_op jit(solution)/shard_map/ppermute | solution.py:39
  70.3 16.8 %collective-permute-start.11 = (bf16[896,128]{1,0:T(8,128)(2,1)S(1)}, bf16[896,128]{1,0:T(8,128)(2,1)S(1)}, u32[]{:S(2)}, u32[]{:S(2)}) collective-permute-start(bf16[896,128]{1,0:T(8,128)(2,1)S(1)} %get-tuple-element.66), channel_id=1, source_target_pairs={{0,24},{8,16},{16,8},{24,0},{1,25},{9,17},{17,9},{25,1},{2,26},{10... | collective-permute-start | bytes 688136 | tf_op jit(solution)/shard_map/ppermute | solution.py:39
  72.6 15.5 %collective-permute-start.16 = (bf16[896,128]{1,0:T(8,128)(2,1)S(1)}, bf16[896,128]{1,0:T(8,128)(2,1)S(1)}, u32[]{:S(2)}, u32[]{:S(2)}) collective-permute-start(bf16[896,128]{1,0:T(8,128)(2,1)S(1)} %get-tuple-element.67), channel_id=1, source_target_pairs={{0,64},{64,0},{128,192},{192,128},{1,65},{65,1},{129,193},{193,129... | collective-permute-start | bytes 688136 | tf_op jit(solution)/shard_map/ppermute | solution.py:39
  72.7 16.6 %collective-permute-start.17 = (bf16[896,128]{1,0:T(8,128)(2,1)S(1)}, bf16[896,128]{1,0:T(8,128)(2,1)S(1)}, u32[]{:S(2)}, u32[]{:S(2)}) collective-permute-start(bf16[896,128]{1,0:T(8,128)(2,1)S(1)} %get-tuple-element.67), channel_id=1, source_target_pairs={{0,128},{64,192},{128,0},{192,64},{1,129},{65,193},{129,1},{193,65... | collective-permute-start | bytes 688136 | tf_op jit(solution)/shard_map/ppermute | solution.py:39
  75.7 15.8 %collective-permute-start.18 = (bf16[896,128]{1,0:T(8,128)(2,1)S(1)}, bf16[896,128]{1,0:T(8,128)(2,1)S(1)}, u32[]{:S(2)}, u32[]{:S(2)}) collective-permute-start(bf16[896,128]{1,0:T(8,128)(2,1)S(1)} %get-tuple-element.67), channel_id=1, source_target_pairs={{0,192},{64,128},{128,64},{192,0},{1,193},{65,129},{129,65},{193,1... | collective-permute-start | bytes 688136 | tf_op jit(solution)/shard_map/ppermute | solution.py:39
  87.2 7.3 %collective-permute-start.12 = (bf16[4,896,128]{2,1,0:T(8,128)(2,1)S(1)}, bf16[4,896,128]{2,1,0:T(8,128)(2,1)}, u32[]{:S(2)}, u32[]{:S(2)}) collective-permute-start(bf16[4,896,128]{2,1,0:T(8,128)(2,1)S(1)} %pad_maximum_fusion.2.here_ref), channel_id=1, source_target_pairs={{0,4},{4,0},{1,5},{5,1},{2,6},{6,2},{3,7},{7,3},{8,12},{12,8},{9,1... | collective-permute-start | bytes 2752520 | tf_op jit(solution)/shard_map/ppermute | solution.py:39
  91.7 11.4 %collective-permute-start.19 = (bf16[4,896,128]{2,1,0:T(8,128)(2,1)S(1)}, bf16[4,896,128]{2,1,0:T(8,128)(2,1)S(1)}, u32[]{:S(2)}, u32[]{:S(2)}) collective-permute-start(bf16[4,896,128]{2,1,0:T(8,128)(2,1)S(1)} %pad_maximum_fusion.3.here_ref), channel_id=1, source_target_pairs={{0,4},{4,0},{1,5},{5,1},{2,6},{6,2},{3,7},{7,3},{8,12},{12,8},{9,1... | collective-permute-start | bytes 2752520 | tf_op jit(solution)/shard_map/ppermute | solution.py:39
  97.5 13.6 %collective-permute-start.13 = (bf16[128,896]{1,0:T(8,128)(2,1)S(1)}, bf16[128,896]{1,0:T(8,128)(2,1)S(1)}, u32[]{:S(2)}, u32[]{:S(2)}) collective-permute-start(bf16[128,896]{1,0:T(8,128)(2,1)S(1)} %get-tuple-element.54), channel_id=1, source_target_pairs={{0,64},{64,0},{128,192},{192,128},{1,65},{65,1},{129,193},{193,129... | collective-permute-start | bytes 688136 | tf_op jit(solution)/shard_map/ppermute | solution.py:39
  98.6 19.1 %collective-permute-start.14 = (bf16[128,896]{1,0:T(8,128)(2,1)S(1)}, bf16[128,896]{1,0:T(8,128)(2,1)S(1)}, u32[]{:S(2)}, u32[]{:S(2)}) collective-permute-start(bf16[128,896]{1,0:T(8,128)(2,1)S(1)} %get-tuple-element.56), channel_id=1, source_target_pairs={{0,128},{64,192},{128,0},{192,64},{1,129},{65,193},{129,1},{193,65... | collective-permute-start | bytes 688136 | tf_op jit(solution)/shard_map/ppermute | solution.py:39
  103.1 17.8 %collective-permute-start.15 = (bf16[128,896]{1,0:T(8,128)(2,1)S(1)}, bf16[128,896]{1,0:T(8,128)(2,1)S(1)}, u32[]{:S(2)}, u32[]{:S(2)}) collective-permute-start(bf16[128,896]{1,0:T(8,128)(2,1)S(1)} %get-tuple-element.55), channel_id=1, source_target_pairs={{0,192},{64,128},{128,64},{192,0},{1,193},{65,129},{129,65},{193,1... | collective-permute-start | bytes 688136 | tf_op jit(solution)/shard_map/ppermute | solution.py:39
  104.7 16.3 %collective-permute-start.20 = (bf16[128,896]{1,0:T(8,128)(2,1)S(1)}, bf16[128,896]{1,0:T(8,128)(2,1)S(1)}, u32[]{:S(2)}, u32[]{:S(2)}) collective-permute-start(bf16[128,896]{1,0:T(8,128)(2,1)S(1)} %get-tuple-element.57), channel_id=1, source_target_pairs={{0,8},{8,0},{16,24},{24,16},{1,9},{9,1},{17,25},{25,17},{2,10},{10... | collective-permute-start | bytes 688136 | tf_op jit(solution)/shard_map/ppermute | solution.py:39
  104.8 16.3 %collective-permute-start.21 = (bf16[128,896]{1,0:T(8,128)(2,1)S(1)}, bf16[128,896]{1,0:T(8,128)(2,1)S(1)}, u32[]{:S(2)}, u32[]{:S(2)}) collective-permute-start(bf16[128,896]{1,0:T(8,128)(2,1)S(1)} %get-tuple-element.59), channel_id=1, source_target_pairs={{0,16},{8,24},{16,0},{24,8},{1,17},{9,25},{17,1},{25,9},{2,18},{10... | collective-permute-start | bytes 688136 | tf_op jit(solution)/shard_map/ppermute | solution.py:39
  111.1 11.0 %collective-permute-start.22 = (bf16[128,896]{1,0:T(8,128)(2,1)S(1)}, bf16[128,896]{1,0:T(8,128)(2,1)S(1)}, u32[]{:S(2)}, u32[]{:S(2)}) collective-permute-start(bf16[128,896]{1,0:T(8,128)(2,1)S(1)} %get-tuple-element.58), channel_id=1, source_target_pairs={{0,24},{8,16},{16,8},{24,0},{1,25},{9,17},{17,9},{25,1},{2,26},{10... | collective-permute-start | bytes 688136 | tf_op jit(solution)/shard_map/ppermute | solution.py:39
  122.7 7.9 %collective-permute-start.23 = (bf16[32,2688]{1,0:T(8,128)(2,1)S(1)}, bf16[32,2688]{1,0:T(8,128)(2,1)S(1)}, u32[]{:S(2)}, u32[]{:S(2)}) collective-permute-start(bf16[32,2688]{1,0:T(8,128)(2,1)S(1)} %get-tuple-element.114), channel_id=1, source_target_pairs={{0,1},{1,0},{2,3},{3,2},{4,5},{5,4},{6,7},{7,6},{8,9},{9,8},{10,11... | collective-permute-start | bytes 516104 | tf_op jit(solution)/shard_map/ppermute | solution.py:39
  122.8 13.0 %collective-permute-start.24 = (bf16[32,2688]{1,0:T(8,128)(2,1)S(1)}, bf16[32,2688]{1,0:T(8,128)(2,1)S(1)}, u32[]{:S(2)}, u32[]{:S(2)}) collective-permute-start(bf16[32,2688]{1,0:T(8,128)(2,1)S(1)} %get-tuple-element.115), channel_id=1, source_target_pairs={{0,2},{1,3},{2,0},{3,1},{4,6},{5,7},{6,4},{7,5},{8,10},{9,11},{10,... | collective-permute-start | bytes 516104 | tf_op jit(solution)/shard_map/ppermute | solution.py:39
  129.1 12.7 %collective-permute-start.25 = (bf16[32,2688]{1,0:T(8,128)(2,1)S(1)}, bf16[32,2688]{1,0:T(8,128)(2,1)S(1)}, u32[]{:S(2)}, u32[]{:S(2)}) collective-permute-start(bf16[32,2688]{1,0:T(8,128)(2,1)S(1)} %get-tuple-element.116), channel_id=1, source_target_pairs={{0,3},{1,2},{2,1},{3,0},{4,7},{5,6},{6,5},{7,4},{8,11},{9,10},{10,... | collective-permute-start | bytes 516104 | tf_op jit(solution)/shard_map/ppermute | solution.py:39
  144.7 6.5 %collective-permute-start.26 = (bf16[32,1536]{1,0:T(8,128)(2,1)S(1)}, bf16[32,1536]{1,0:T(8,128)(2,1)S(1)}, u32[]{:S(2)}, u32[]{:S(2)}) collective-permute-start(bf16[32,1536]{1,0:T(8,128)(2,1)S(1)} %pad_maximum_fusion.13), channel_id=1, source_target_pairs={{0,3},{1,2},{2,1},{3,0},{4,7},{5,6},{6,5},{7,4},{8,11},{9,10},{10,... | collective-permute-start | bytes 294920 | tf_op jit(solution)/shard_map/ppermute | solution.py:39
  147.3 10.2 %collective-permute-start.27 = (bf16[32,1536]{1,0:T(8,128)(2,1)S(1)}, bf16[32,1536]{1,0:T(8,128)(2,1)S(1)}, u32[]{:S(2)}, u32[]{:S(2)}) collective-permute-start(bf16[32,1536]{1,0:T(8,128)(2,1)S(1)} %pad_maximum_fusion.13), channel_id=1, source_target_pairs={{0,2},{1,3},{2,0},{3,1},{4,6},{5,7},{6,4},{7,5},{8,10},{9,11},{10,... | collective-permute-start | bytes 294920 | tf_op jit(solution)/shard_map/ppermute | solution.py:39
  150.1 7.5 %collective-permute-start.28 = (bf16[32,1536]{1,0:T(8,128)(2,1)S(1)}, bf16[32,1536]{1,0:T(8,128)(2,1)S(1)}, u32[]{:S(2)}, u32[]{:S(2)}) collective-permute-start(bf16[32,1536]{1,0:T(8,128)(2,1)S(1)} %pad_maximum_fusion.13), channel_id=1, source_target_pairs={{0,1},{1,0},{2,3},{3,2},{4,5},{5,4},{6,7},{7,6},{8,9},{9,8},{10,11... | collective-permute-start | bytes 294920 | tf_op jit(solution)/shard_map/ppermute | solution.py:39
  (9 other events, 62.7 us)
Sparse Core Ops, SparseCore 0:
  22.2 99.3 all-gather.1

commit v8 on v4

--- a/solution.py
+++ b/solution.py
@@ -41,6 +41,15 @@
 
 def move(value, where):
     return lax.ppermute(value, AXES, [(flat(*at), flat(*where(*at))) for at in every()])
+
+
+def along(value, e, first, second):
+    def target(*at):
+        at = list(at)
+        at[AXES.index((first, second)[at[3]])] ^= e
+        return at
+
+    return move(value, target)
 
 
 def tables():
@@ -105,19 +114,20 @@
     )(query_weight, kv_turned)
 
 
-def project_kernel(x_ref, here_ref, there_ref, out_ref, own_ref):
+def project_kernel(x_ref, *refs):
+    blocks, (out_ref, own_ref) = refs[:4], refs[4:]
     inputs = x_ref[...]
-    for slot, ref in enumerate((here_ref, there_ref)):
+    for slot in (0, 1):
         heads = [
-            jnp.concatenate([ref[d, 256 * h : 256 * h + 256, :] for d in range(4)], axis=0) for h in range(3)
+            jnp.concatenate([ref[slot, 256 * h : 256 * h + 256, :] for ref in blocks], axis=0) for h in range(3)
         ]
         q = jnp.dot(inputs, jnp.concatenate(heads, axis=1), preferred_element_type=F32)
         own_ref[:, 384 * slot : 384 * slot + 384] = q[:ROWS]
         for e in (1, 2, 3):
             out_ref[e - 1, :, 384 * slot : 384 * slot + 384] = q[ROWS * e : ROWS * e + ROWS].astype(BF)
     kv_rows = [
-        jnp.concatenate([ref[d, 768 + 64 * h : 832 + 64 * h, :] for d in range(4) for h in (0, 1)], axis=1)
-        for ref in (here_ref, there_ref)
+        jnp.concatenate([ref[slot, 768 + 64 * h : 832 + 64 * h, :] for ref in blocks for h in (0, 1)], axis=1)
+        for slot in (0, 1)
     ]
     kv = lax.dot_general(
         inputs, jnp.concatenate(kv_rows, axis=0), (((1,), (1,)), ((), ())), preferred_element_type=F32
@@ -127,15 +137,15 @@
         out_ref[e - 1, :, 768:] = kv[ROWS * e : ROWS * e + ROWS].astype(BF)
 
 
-def project(inputs, here, there):
+def project(inputs, blocks):
     return pl.pallas_call(
         project_kernel,
         out_shape=(jax.ShapeDtypeStruct((3, ROWS, 896), BF), jax.ShapeDtypeStruct((ROWS, 896), F32)),
-        in_specs=[whole(0)] * 3,
+        in_specs=[whole(0)] * 5,
         out_specs=(whole(0),) * 2,
         compiler_params=pltpu.CompilerParams(vmem_limit_bytes=32 * 2**20),
         cost_estimate=pl.CostEstimate(flops=2 * 512 * 1024 * 896, bytes_accessed=4000000, transcendentals=0),
-    )(inputs, here, there)
+    )(inputs, *blocks)
 
 
 def attend(query, keys, values, limit, first):
@@ -162,28 +172,34 @@
     gained = (widened * norm_gain[None, :]).astype(BF)
 
     def features(e):
-        s = y ^ e ^ t
-        picked = [
-            lax.dynamic_slice(gained, (0, (((s >> 1) * 4 + (x ^ d)) * 2 + (s & 1)) * 256), (ROWS, 256))
-            for d in range(4)
-        ]
+        picked = []
+        for d in range(4):
+            s = y ^ t ^ jnp.where(c == 0, e, d)
+            at = x ^ jnp.where(c == 0, d, e)
+            picked.append(lax.dynamic_slice(gained, (0, (((s >> 1) * 4 + at) * 2 + (s & 1)) * 256), (ROWS, 256)))
         return jnp.concatenate(picked, axis=1)
 
-    ring = [swap(features(e), "y", e) for e in (1, 2, 3)]
-    first, wo_other, packed, *ring = lax.optimization_barrier((first, wo_other, packed, *ring))
+    ring = [along(features(e), e, "y", "x") for e in (1, 2, 3)]
+    first, packed, wo_other, *ring = lax.optimization_barrier((first, packed, wo_other, *ring))
     second = move(packed, lambda y, zh, x, c, t: ((2 * zh + c) ^ y, 1 - (t & 1), x, t >> 1, y))
     inputs = jnp.concatenate([features(0)] + ring, axis=0)
 
     wo_piece = jnp.concatenate([out_weight, wo_other], axis=0)
     wo = lax.all_gather(wo_piece, ("y", "x", "core"), axis=0, tiled=True)
 
-    summed = []
-    for block in (first, second):
-        here = jnp.stack([block] + [swap(block, "x", d) for d in (1, 2, 3)])
-        sent, total = project(inputs, here, swap(here, "core", 1))
+    def gathered(block):
+        pair = jnp.stack([block, swap(block, "core", 1)])
+        return [pair] + [along(pair, d, "x", "y") for d in (1, 2, 3)]
+
+    def reduced(blocks):
+        sent, total = project(inputs, blocks)
         for e in (1, 2, 3):
-            total = total + swap(sent[e - 1], "y", e).astype(F32)
-        summed.append(total)
+            total = total + along(sent[e - 1], e, "y", "x").astype(F32)
+        return total
+
+    second, *blocks = lax.optimization_barrier((second, *gathered(first)))
+    total, *blocks = lax.optimization_barrier((reduced(blocks), *gathered(second)))
+    summed = [total, reduced(blocks)]
     base = 2 * c + zh
     q_slots = [half[:, at : at + 384] for at in (0, 384) for half in summed]
     kv_slots = [half[:, at : at + 64] for at in (768, 832) for half in summed]

time: 171 us -> 175 us (1.023)
  starting transfers between devices: 60 us -> 76.4 us
  waiting for transfers between devices: 77.4 us -> 66 us
    ppermute x24 -> x9, waiting for transfers between devices: 73.3 us -> 27.6 us  [swap(): return lax.ppermute(value, axis, [(i, i ^ d) for i in range(n)])]
    ppermute x2 -> x17, waiting for transfers between devices: 4.15 us -> 38.3 us  [move(): lax.ppermute(value, AXES, [(flat(*at), flat(*where(*at))) for at in every...]
    ppermute x2 -> x17, starting transfers between devices: 18.1 us -> 43.2 us  [move(): lax.ppermute(value, AXES, [(flat(*at), flat(*where(*at))) for at in every...]
    ppermute x24 -> x9, starting transfers between devices: 41.9 us -> 33.2 us  [swap(): return lax.ppermute(value, axis, [(i, i ^ d) for i in range(n)])]
  transfers between devices with their start and end apart: 27 -> 27, of which waited for: 14 -> 12; matrix products, arithmetic and copies ran while one was open for 3% -> 2% of each run, Pallas kernels for 2% -> 2%
where the time goes in v8:
time: 175 us; the launch traced here: 174 us
  starting transfers between devices  76.4 us (44%)
  waiting for transfers between devices  66 us (38%)
  between operations  14.6 us (8%)
  matrix products  8.59 us (5%)
  other arithmetic  4.17 us (2%)
  Pallas kernels  3.07 us (2%)
    ppermute x17, starting transfers between devices, move(): lax.ppermute(value, AXES, [(flat(*at), flat(*where(*at))) for at in every...  43.2 us
    ppermute x17, waiting for transfers between devices, move(): lax.ppermute(value, AXES, [(flat(*at), flat(*where(*at))) for at in every...  38.3 us
    ppermute x9, starting transfers between devices, swap(): return lax.ppermute(value, axis, [(i, i ^ d) for i in range(n)])  33.2 us
    ppermute x9, waiting for transfers between devices, swap(): return lax.ppermute(value, axis, [(i, i ^ d) for i in range(n)])  27.6 us
    dot_general x1, matrix products, body(): return jnp.dot(all_rows, wo, preferred_element_type=F32).astype(BF)  7.35 us
  transfers between devices with their start and end apart: 27, of which 12 were waited for; matrix products, arithmetic and copies ran while one was open for 2% of the time, Pallas kernels for 2%

profile of v8, /device:TPU:24, one launch (start us, length us, event | category | flops | bytes accessed | tf_op | source)
XLA Modules:
  0.0 173.9 jit_solution(353392944491251440)
XLA Ops:
  6.5 1.6 fusion.2
  8.4 2.0 %collective-permute-start.4 = (bf16[128,1024]{1,0:T(8,128)(2,1)S(1)}, bf16[128,1024]{1,0:T(8,128)(2,1)S(1)}, u32[]{:S(2)}, u32[]{:S(2)}) collective-permute-start(bf16[128,1024]{1,0:T(8,128)(2,1)S(1)} %pad_maximum_fusion.7), channel_id=1, source_target_pairs={{0,192},{1,193},{2,194},{3,195},{4,28},{5,29},{6,30},{7,31},{8,200... | collective-permute-start | bytes 786440 | tf_op jit(solution)/shard_map/ppermute | solution.py:43
  11.5 1.4 collective-permute-start.2
  12.9 6.5 %collective-permute-start = (bf16[896,128]{1,0:T(8,128)(2,1)S(1)}, bf16[896,128]{1,0:T(8,128)(2,1)S(1)}, u32[]{:S(2)}, u32[]{:S(2)}) collective-permute-start(bf16[896,128]{1,0:T(8,128)(2,1)S(1)} %shard_map.118), channel_id=1, source_target_pairs={{0,0},{1,32},{2,4},{3,36},{4,64},{5,96},{6,68},{7,100},{8,8},{9,40... | collective-permute-start | bytes 688136 | tf_op jit(solution)/shard_map/ppermute | solution.py:43
  19.4 3.4 %collective-permute-start.1 = (bf16[24,4096]{1,0:T(8,128)(2,1)S(1)}, bf16[24,4096]{1,0:T(8,128)(2,1)S(1)}, u32[]{:S(2)}, u32[]{:S(2)}) collective-permute-start(bf16[24,4096]{1,0:T(8,128)(2,1)S(1)} %copy-done.2), channel_id=1, source_target_pairs={{0,32},{32,0},{1,33},{33,1},{2,34},{34,2},{3,35},{35,3},{4,36},{36... | collective-permute-start | bytes 589832 | tf_op jit(solution)/shard_map/ppermute | solution.py:39
  22.9 7.8 %collective-permute-done.1 = bf16[24,4096]{1,0:T(8,128)(2,1)S(1)} collective-permute-done((bf16[24,4096]{1,0:T(8,128)(2,1)S(1)}, bf16[24,4096]{1,0:T(8,128)(2,1)S(1)}, u32[]{:S(2)}, u32[]{:S(2)}) %collective-permute-start.1) | collective-permute-done | bytes 196640 | tf_op jit(solution)/shard_map/ppermute | solution.py:39
  31.6 1.5 collective-permute-done.6
  33.1 1.6 collective-permute-start.7
  34.7 2.7 %collective-permute-start.8 = (bf16[2,896,128]{2,1,0:T(8,128)(2,1)S(1)}, bf16[2,896,128]{2,1,0:T(8,128)(2,1)S(1)}, u32[]{:S(2)}, u32[]{:S(2)}) collective-permute-start(bf16[2,896,128]{2,1,0:T(8,128)(2,1)S(1)} %pad_maximum_fusion.2.refs_0_), channel_id=1, source_target_pairs={{0,16},{1,17},{2,18},{3,19},{4,132},{5,133},{6,134},{7,135},{8,24}... | collective-permute-start | bytes 1376264 | tf_op jit(solution)/shard_map/ppermute | solution.py:43
  38.6 11.5 %collective-permute-start.5 = (bf16[896,128]{1,0:T(8,128)(2,1)S(1)}, bf16[896,128]{1,0:T(8,128)(2,1)S(1)}, u32[]{:S(2)}, u32[]{:S(2)}) collective-permute-start(bf16[896,128]{1,0:T(8,128)(2,1)S(1)} %shard_map.118), channel_id=1, source_target_pairs={{0,32},{1,0},{2,36},{3,4},{4,96},{5,64},{6,100},{7,68},{8,40},{9,8... | collective-permute-start | bytes 688136 | tf_op jit(solution)/shard_map/ppermute | solution.py:43
  50.2 10.0 %collective-permute-done.5 = bf16[896,128]{1,0:T(8,128)(2,1)S(1)} collective-permute-done((bf16[896,128]{1,0:T(8,128)(2,1)S(1)}, bf16[896,128]{1,0:T(8,128)(2,1)S(1)}, u32[]{:S(2)}, u32[]{:S(2)}) %collective-permute-start.5) | collective-permute-done | bytes 229408 | tf_op jit(solution)/shard_map/ppermute | solution.py:43
  60.2 3.5 %collective-permute-start.13 = (bf16[896,128]{1,0:T(8,128)(2,1)S(1)}, bf16[896,128]{1,0:T(8,128)(2,1)S(1)}, u32[]{:S(2)}, u32[]{:S(2)}) collective-permute-start(bf16[896,128]{1,0:T(8,128)(2,1)S(1)} %collective-permute-done.5), channel_id=1, source_target_pairs={{0,4},{4,0},{1,5},{5,1},{2,6},{6,2},{3,7},{7,3},{8,12},{12,8},{9,1... | collective-permute-start | bytes 688136 | tf_op jit(solution)/shard_map/ppermute | solution.py:39
  63.7 1.5 shard_map.119
  67.7 2.4 %collective-permute-start.12 = (bf16[128,896]{1,0:T(8,128)(2,1)S(1)}, bf16[128,896]{1,0:T(8,128)(2,1)S(1)}, u32[]{:S(2)}, u32[]{:S(2)}) collective-permute-start(bf16[128,896]{1,0:T(8,128)(2,1)S(1)} %get-tuple-element.78), channel_id=1, source_target_pairs={{0,192},{1,193},{2,194},{3,195},{4,28},{5,29},{6,30},{7,31},{8,200... | collective-permute-start | bytes 688136 | tf_op jit(solution)/shard_map/ppermute | solution.py:43
  70.1 1.3 collective-permute-start.14
  71.4 3.0 %collective-permute-start.15 = (bf16[2,896,128]{2,1,0:T(8,128)(2,1)S(1)}, bf16[2,896,128]{2,1,0:T(8,128)(2,1)S(1)}, u32[]{:S(2)}, u32[]{:S(2)}) collective-permute-start(bf16[2,896,128]{2,1,0:T(8,128)(2,1)S(1)} %pad_maximum_fusion.3.refs_0_), channel_id=1, source_target_pairs={{0,16},{1,17},{2,18},{3,19},{4,132},{5,133},{6,134},{7,135},{8,24}... | collective-permute-start | bytes 1376264 | tf_op jit(solution)/shard_map/ppermute | solution.py:43
  74.4 2.2 %collective-permute-start.16 = (bf16[2,896,128]{2,1,0:T(8,128)(2,1)S(1)}, bf16[2,896,128]{2,1,0:T(8,128)(2,1)S(1)}, u32[]{:S(2)}, u32[]{:S(2)}) collective-permute-start(bf16[2,896,128]{2,1,0:T(8,128)(2,1)S(1)} %pad_maximum_fusion.3.refs_0_), channel_id=1, source_target_pairs={{0,24},{1,25},{2,26},{3,27},{4,196},{5,197},{6,198},{7,199},{8,16}... | collective-permute-start | bytes 1376264 | tf_op jit(solution)/shard_map/ppermute | solution.py:43
  76.6 2.2 %collective-permute-done.11 = bf16[128,896]{1,0:T(8,128)(2,1)S(1)} collective-permute-done((bf16[128,896]{1,0:T(8,128)(2,1)S(1)}, bf16[128,896]{1,0:T(8,128)(2,1)S(1)}, u32[]{:S(2)}, u32[]{:S(2)}) %collective-permute-start.11) | collective-permute-done | bytes 229408 | tf_op jit(solution)/shard_map/ppermute | solution.py:43
  79.0 6.9 %collective-permute-done.15.refs_2_ = bf16[2,896,128]{2,1,0:T(8,128)(2,1)S(1)} collective-permute-done((bf16[2,896,128]{2,1,0:T(8,128)(2,1)S(1)}, bf16[2,896,128]{2,1,0:T(8,128)(2,1)S(1)}, u32[]{:S(2)}, u32[]{:S(2)}) %collective-permute-start.15) | collective-permute-done | bytes 458784 | tf_op jit(solution)/shard_map/ppermute | solution.py:43
  85.9 3.1 %collective-permute-done.16.refs_3_ = bf16[2,896,128]{2,1,0:T(8,128)(2,1)S(1)} collective-permute-done((bf16[2,896,128]{2,1,0:T(8,128)(2,1)S(1)}, bf16[2,896,128]{2,1,0:T(8,128)(2,1)S(1)}, u32[]{:S(2)}, u32[]{:S(2)}) %collective-permute-start.16) | collective-permute-done | bytes 458784 | tf_op jit(solution)/shard_map/ppermute | solution.py:43
  89.0 1.5 shard_map.120
  90.9 4.3 %collective-permute-start.18 = (bf16[128,896]{1,0:T(8,128)(2,1)S(1)}, bf16[128,896]{1,0:T(8,128)(2,1)S(1)}, u32[]{:S(2)}, u32[]{:S(2)}) collective-permute-start(bf16[128,896]{1,0:T(8,128)(2,1)S(1)} %get-tuple-element.76), channel_id=1, source_target_pairs={{0,128},{1,129},{2,130},{3,131},{4,20},{5,21},{6,22},{7,23},{8,136... | collective-permute-start | bytes 688136 | tf_op jit(solution)/shard_map/ppermute | solution.py:43
  95.4 6.2 %collective-permute-done.17 = bf16[128,896]{1,0:T(8,128)(2,1)S(1)} collective-permute-done((bf16[128,896]{1,0:T(8,128)(2,1)S(1)}, bf16[128,896]{1,0:T(8,128)(2,1)S(1)}, u32[]{:S(2)}, u32[]{:S(2)}) %collective-permute-start.17) | collective-permute-done | bytes 229408 | tf_op jit(solution)/shard_map/ppermute | solution.py:43
  101.6 9.8 %collective-permute-done.18 = bf16[128,896]{1,0:T(8,128)(2,1)S(1)} collective-permute-done((bf16[128,896]{1,0:T(8,128)(2,1)S(1)}, bf16[128,896]{1,0:T(8,128)(2,1)S(1)}, u32[]{:S(2)}, u32[]{:S(2)}) %collective-permute-start.18) | collective-permute-done | bytes 229408 | tf_op jit(solution)/shard_map/ppermute | solution.py:43
  112.1 18.0 %collective-permute-start.20 = (bf16[32,2688]{1,0:T(8,128)(2,1)S(1)}, bf16[32,2688]{1,0:T(8,128)(2,1)S(1)}, u32[]{:S(2)}, u32[]{:S(2)}) collective-permute-start(bf16[32,2688]{1,0:T(8,128)(2,1)S(1)} %get-tuple-element.116), channel_id=1, source_target_pairs={{0,1},{1,0},{2,3},{3,2},{4,5},{5,4},{6,7},{7,6},{8,9},{9,8},{10,11... | collective-permute-start | bytes 516104 | tf_op jit(solution)/shard_map/ppermute | solution.py:39
  130.1 2.5 %collective-permute-start.22 = (bf16[32,2688]{1,0:T(8,128)(2,1)S(1)}, bf16[32,2688]{1,0:T(8,128)(2,1)S(1)}, u32[]{:S(2)}, u32[]{:S(2)}) collective-permute-start(bf16[32,2688]{1,0:T(8,128)(2,1)S(1)} %get-tuple-element.118), channel_id=1, source_target_pairs={{0,3},{1,2},{2,1},{3,0},{4,7},{5,6},{6,5},{7,4},{8,11},{9,10},{10,... | collective-permute-start | bytes 516104 | tf_op jit(solution)/shard_map/ppermute | solution.py:39
  132.7 2.3 %collective-permute-done.20 = bf16[32,2688]{1,0:T(8,128)(2,1)S(1)} collective-permute-done((bf16[32,2688]{1,0:T(8,128)(2,1)S(1)}, bf16[32,2688]{1,0:T(8,128)(2,1)S(1)}, u32[]{:S(2)}, u32[]{:S(2)}) %collective-permute-start.20) | collective-permute-done | bytes 172064 | tf_op jit(solution)/shard_map/ppermute | solution.py:39
  135.0 8.9 %collective-permute-done.21 = bf16[32,2688]{1,0:T(8,128)(2,1)S(1)} collective-permute-done((bf16[32,2688]{1,0:T(8,128)(2,1)S(1)}, bf16[32,2688]{1,0:T(8,128)(2,1)S(1)}, u32[]{:S(2)}, u32[]{:S(2)}) %collective-permute-start.21) | collective-permute-done | bytes 172064 | tf_op jit(solution)/shard_map/ppermute | solution.py:39
  146.6 1.4 collective-permute-start.23
  148.1 4.2 %collective-permute-start.24 = (bf16[32,1536]{1,0:T(8,128)(2,1)S(1)}, bf16[32,1536]{1,0:T(8,128)(2,1)S(1)}, u32[]{:S(2)}, u32[]{:S(2)}) collective-permute-start(bf16[32,1536]{1,0:T(8,128)(2,1)S(1)} %pad_maximum_fusion.9), channel_id=1, source_target_pairs={{0,2},{1,3},{2,0},{3,1},{4,6},{5,7},{6,4},{7,5},{8,10},{9,11},{10,... | collective-permute-start | bytes 294920 | tf_op jit(solution)/shard_map/ppermute | solution.py:39
  153.2 6.3 %collective-permute-done.24 = bf16[32,1536]{1,0:T(8,128)(2,1)S(1)} collective-permute-done((bf16[32,1536]{1,0:T(8,128)(2,1)S(1)}, bf16[32,1536]{1,0:T(8,128)(2,1)S(1)}, u32[]{:S(2)}, u32[]{:S(2)}) %collective-permute-start.24) | collective-permute-done | bytes 98336 | tf_op jit(solution)/shard_map/ppermute | solution.py:39
  159.7 7.4 %convolution_convert_fusion = bf16[128,4096]{1,0:T(8,128)(2,1)} fusion(bf16[1536,4096]{1,0:T(8,128)(2,1)} %all-gather.2.cloned.1.call-done, bf16[32,1536]{1,0:T(8,128)(2,1)S(1)} %broadcast_select_fusion.8, bf16[32,1536]{1,0:T(8,128)(2,1)S(1)} %get-tuple-element.82, bf16[32,1536]{1,0:T(8,128)(2,1)S(1)} %get-tuple-element.81, ...), kind=kOutput, calls=%fused_computation.1 | convolution fusion | flops 1612709888 | bytes 14024704 | tf_op jit(solution)/shard_map/dot_general | solution.py:241
  (103 shorter events, 10.3 us)
Async XLA Ops:
  6.5 153.1 %all-gather.2.cloned.1.call-start = ((), (), s32[]{:S(2)}) async-start(), calls=%async_computation | async-start | bytes 12976128 | tf_op jit(solution)/shard_map/all_gather | solution.py:188
  8.2 4.7 %copy-start = (bf16[256,384]{1,0:T(8,128)(2,1)S(1)}, bf16[256,384]{1,0:T(8,128)(2,1)}, u32[]{:S(2)}) copy-start(bf16[256,384]{1,0:T(8,128)(2,1)} %q_ref.1) | copy-start | bytes 589828
  8.2 4.7 %copy-start.1 = (bf16[256,64]{0,1:T(8,128)(2,1)S(1)}, bf16[256,64]{0,1:T(8,128)(2,1)}, u32[]{:S(2)}) copy-start(bf16[256,64]{0,1:T(8,128)(2,1)} %param.15) | copy-start | bytes 98308
  8.2 11.2 %copy-start.2 = (bf16[24,4096]{1,0:T(8,128)(2,1)S(1)}, bf16[24,4096]{1,0:T(8,128)(2,1)}, u32[]{:S(2)}) copy-start(bf16[24,4096]{1,0:T(8,128)(2,1)} %param.16) | copy-start | bytes 589828
  8.4 22.3 %collective-permute-start.4 = (bf16[128,1024]{1,0:T(8,128)(2,1)S(1)}, bf16[128,1024]{1,0:T(8,128)(2,1)S(1)}, u32[]{:S(2)}, u32[]{:S(2)}) collective-permute-start(bf16[128,1024]{1,0:T(8,128)(2,1)S(1)} %pad_maximum_fusion.7), channel_id=1, source_target_pairs={{0,192},{1,193},{2,194},{3,195},{4,28},{5,29},{6,30},{7,31},{8,200... | collective-permute-start | bytes 786440 | tf_op jit(solution)/shard_map/ppermute | solution.py:43
  10.5 20.2 %collective-permute-start.3 = (bf16[128,1024]{1,0:T(8,128)(2,1)S(1)}, bf16[128,1024]{1,0:T(8,128)(2,1)S(1)}, u32[]{:S(2)}, u32[]{:S(2)}) collective-permute-start(bf16[128,1024]{1,0:T(8,128)(2,1)S(1)} %pad_maximum_fusion.6), channel_id=1, source_target_pairs={{0,128},{1,129},{2,130},{3,131},{4,20},{5,21},{6,22},{7,23},{8,136... | collective-permute-start | bytes 786440 | tf_op jit(solution)/shard_map/ppermute | solution.py:43
  11.5 19.2 %collective-permute-start.2 = (bf16[128,1024]{1,0:T(8,128)(2,1)S(1)}, bf16[128,1024]{1,0:T(8,128)(2,1)S(1)}, u32[]{:S(2)}, u32[]{:S(2)}) collective-permute-start(bf16[128,1024]{1,0:T(8,128)(2,1)S(1)} %pad_maximum_fusion.5), channel_id=1, source_target_pairs={{0,64},{1,65},{2,66},{3,67},{4,12},{5,13},{6,14},{7,15},{8,72},{9,... | collective-permute-start | bytes 786440 | tf_op jit(solution)/shard_map/ppermute | solution.py:43
  12.9 17.8 %collective-permute-start = (bf16[896,128]{1,0:T(8,128)(2,1)S(1)}, bf16[896,128]{1,0:T(8,128)(2,1)S(1)}, u32[]{:S(2)}, u32[]{:S(2)}) collective-permute-start(bf16[896,128]{1,0:T(8,128)(2,1)S(1)} %shard_map.118), channel_id=1, source_target_pairs={{0,0},{1,32},{2,4},{3,36},{4,64},{5,96},{6,68},{7,100},{8,8},{9,40... | collective-permute-start | bytes 688136 | tf_op jit(solution)/shard_map/ppermute | solution.py:43
  19.4 11.3 %collective-permute-start.1 = (bf16[24,4096]{1,0:T(8,128)(2,1)S(1)}, bf16[24,4096]{1,0:T(8,128)(2,1)S(1)}, u32[]{:S(2)}, u32[]{:S(2)}) collective-permute-start(bf16[24,4096]{1,0:T(8,128)(2,1)S(1)} %copy-done.2), channel_id=1, source_target_pairs={{0,32},{32,0},{1,33},{33,1},{2,34},{34,2},{3,35},{35,3},{4,36},{36... | collective-permute-start | bytes 589832 | tf_op jit(solution)/shard_map/ppermute | solution.py:39
  31.5 1.6 collective-permute-start.6
  33.1 27.0 %collective-permute-start.7 = (bf16[2,896,128]{2,1,0:T(8,128)(2,1)S(1)}, bf16[2,896,128]{2,1,0:T(8,128)(2,1)S(1)}, u32[]{:S(2)}, u32[]{:S(2)}) collective-permute-start(bf16[2,896,128]{2,1,0:T(8,128)(2,1)S(1)} %pad_maximum_fusion.2.refs_0_), channel_id=1, source_target_pairs={{0,8},{1,9},{2,10},{3,11},{4,68},{5,69},{6,70},{7,71},{8,0},{9,1},... | collective-permute-start | bytes 1376264 | tf_op jit(solution)/shard_map/ppermute | solution.py:43
  34.7 25.5 %collective-permute-start.8 = (bf16[2,896,128]{2,1,0:T(8,128)(2,1)S(1)}, bf16[2,896,128]{2,1,0:T(8,128)(2,1)S(1)}, u32[]{:S(2)}, u32[]{:S(2)}) collective-permute-start(bf16[2,896,128]{2,1,0:T(8,128)(2,1)S(1)} %pad_maximum_fusion.2.refs_0_), channel_id=1, source_target_pairs={{0,16},{1,17},{2,18},{3,19},{4,132},{5,133},{6,134},{7,135},{8,24}... | collective-permute-start | bytes 1376264 | tf_op jit(solution)/shard_map/ppermute | solution.py:43
  37.5 22.7 %collective-permute-start.9 = (bf16[2,896,128]{2,1,0:T(8,128)(2,1)S(1)}, bf16[2,896,128]{2,1,0:T(8,128)(2,1)S(1)}, u32[]{:S(2)}, u32[]{:S(2)}) collective-permute-start(bf16[2,896,128]{2,1,0:T(8,128)(2,1)S(1)} %pad_maximum_fusion.2.refs_0_), channel_id=1, source_target_pairs={{0,24},{1,25},{2,26},{3,27},{4,196},{5,197},{6,198},{7,199},{8,16}... | collective-permute-start | bytes 1376264 | tf_op jit(solution)/shard_map/ppermute | solution.py:43
  38.6 21.6 %collective-permute-start.5 = (bf16[896,128]{1,0:T(8,128)(2,1)S(1)}, bf16[896,128]{1,0:T(8,128)(2,1)S(1)}, u32[]{:S(2)}, u32[]{:S(2)}) collective-permute-start(bf16[896,128]{1,0:T(8,128)(2,1)S(1)} %shard_map.118), channel_id=1, source_target_pairs={{0,32},{1,0},{2,36},{3,4},{4,96},{5,64},{6,100},{7,68},{8,40},{9,8... | collective-permute-start | bytes 688136 | tf_op jit(solution)/shard_map/ppermute | solution.py:43
  50.2 26.4 %copy-start.3 = (f32[128,128]{1,0:T(8,128)S(1)}, f32[128,128]{1,0:T(8,128)}, u32[]{:S(2)}) copy-start(f32[128,128]{1,0:T(8,128)} %constant.76.clone) | copy-start | bytes 196612
  50.2 26.4 %copy-start.4 = (f32[128,128]{1,0:T(8,128)S(1)}, f32[128,128]{1,0:T(8,128)}, u32[]{:S(2)}) copy-start(f32[128,128]{1,0:T(8,128)} %constant.77.clone) | copy-start | bytes 196612
  60.2 9.9 %collective-permute-start.13 = (bf16[896,128]{1,0:T(8,128)(2,1)S(1)}, bf16[896,128]{1,0:T(8,128)(2,1)S(1)}, u32[]{:S(2)}, u32[]{:S(2)}) collective-permute-start(bf16[896,128]{1,0:T(8,128)(2,1)S(1)} %collective-permute-done.5), channel_id=1, source_target_pairs={{0,4},{4,0},{1,5},{5,1},{2,6},{6,2},{3,7},{7,3},{8,12},{12,8},{9,1... | collective-permute-start | bytes 688136 | tf_op jit(solution)/shard_map/ppermute | solution.py:39
  65.3 9.2 %collective-permute-start.10 = (bf16[128,896]{1,0:T(8,128)(2,1)S(1)}, bf16[128,896]{1,0:T(8,128)(2,1)S(1)}, u32[]{:S(2)}, u32[]{:S(2)}) collective-permute-start(bf16[128,896]{1,0:T(8,128)(2,1)S(1)} %get-tuple-element.77), channel_id=1, source_target_pairs={{0,64},{1,65},{2,66},{3,67},{4,12},{5,13},{6,14},{7,15},{8,72},{9,... | collective-permute-start | bytes 688136 | tf_op jit(solution)/shard_map/ppermute | solution.py:43
  66.5 12.4 %collective-permute-start.11 = (bf16[128,896]{1,0:T(8,128)(2,1)S(1)}, bf16[128,896]{1,0:T(8,128)(2,1)S(1)}, u32[]{:S(2)}, u32[]{:S(2)}) collective-permute-start(bf16[128,896]{1,0:T(8,128)(2,1)S(1)} %get-tuple-element.79), channel_id=1, source_target_pairs={{0,128},{1,129},{2,130},{3,131},{4,20},{5,21},{6,22},{7,23},{8,136... | collective-permute-start | bytes 688136 | tf_op jit(solution)/shard_map/ppermute | solution.py:43
  67.7 11.2 %collective-permute-start.12 = (bf16[128,896]{1,0:T(8,128)(2,1)S(1)}, bf16[128,896]{1,0:T(8,128)(2,1)S(1)}, u32[]{:S(2)}, u32[]{:S(2)}) collective-permute-start(bf16[128,896]{1,0:T(8,128)(2,1)S(1)} %get-tuple-element.78), channel_id=1, source_target_pairs={{0,192},{1,193},{2,194},{3,195},{4,28},{5,29},{6,30},{7,31},{8,200... | collective-permute-start | bytes 688136 | tf_op jit(solution)/shard_map/ppermute | solution.py:43
  70.1 8.8 %collective-permute-start.14 = (bf16[2,896,128]{2,1,0:T(8,128)(2,1)S(1)}, bf16[2,896,128]{2,1,0:T(8,128)(2,1)S(1)}, u32[]{:S(2)}, u32[]{:S(2)}) collective-permute-start(bf16[2,896,128]{2,1,0:T(8,128)(2,1)S(1)} %pad_maximum_fusion.3.refs_0_), channel_id=1, source_target_pairs={{0,8},{1,9},{2,10},{3,11},{4,68},{5,69},{6,70},{7,71},{8,0},{9,1},... | collective-permute-start | bytes 1376264 | tf_op jit(solution)/shard_map/ppermute | solution.py:43
  71.4 14.5 %collective-permute-start.15 = (bf16[2,896,128]{2,1,0:T(8,128)(2,1)S(1)}, bf16[2,896,128]{2,1,0:T(8,128)(2,1)S(1)}, u32[]{:S(2)}, u32[]{:S(2)}) collective-permute-start(bf16[2,896,128]{2,1,0:T(8,128)(2,1)S(1)} %pad_maximum_fusion.3.refs_0_), channel_id=1, source_target_pairs={{0,16},{1,17},{2,18},{3,19},{4,132},{5,133},{6,134},{7,135},{8,24}... | collective-permute-start | bytes 1376264 | tf_op jit(solution)/shard_map/ppermute | solution.py:43
  74.4 14.6 %collective-permute-start.16 = (bf16[2,896,128]{2,1,0:T(8,128)(2,1)S(1)}, bf16[2,896,128]{2,1,0:T(8,128)(2,1)S(1)}, u32[]{:S(2)}, u32[]{:S(2)}) collective-permute-start(bf16[2,896,128]{2,1,0:T(8,128)(2,1)S(1)} %pad_maximum_fusion.3.refs_0_), channel_id=1, source_target_pairs={{0,24},{1,25},{2,26},{3,27},{4,196},{5,197},{6,198},{7,199},{8,16}... | collective-permute-start | bytes 1376264 | tf_op jit(solution)/shard_map/ppermute | solution.py:43
  90.6 11.0 %collective-permute-start.17 = (bf16[128,896]{1,0:T(8,128)(2,1)S(1)}, bf16[128,896]{1,0:T(8,128)(2,1)S(1)}, u32[]{:S(2)}, u32[]{:S(2)}) collective-permute-start(bf16[128,896]{1,0:T(8,128)(2,1)S(1)} %get-tuple-element.74), channel_id=1, source_target_pairs={{0,64},{1,65},{2,66},{3,67},{4,12},{5,13},{6,14},{7,15},{8,72},{9,... | collective-permute-start | bytes 688136 | tf_op jit(solution)/shard_map/ppermute | solution.py:43
  90.9 20.6 %collective-permute-start.18 = (bf16[128,896]{1,0:T(8,128)(2,1)S(1)}, bf16[128,896]{1,0:T(8,128)(2,1)S(1)}, u32[]{:S(2)}, u32[]{:S(2)}) collective-permute-start(bf16[128,896]{1,0:T(8,128)(2,1)S(1)} %get-tuple-element.76), channel_id=1, source_target_pairs={{0,128},{1,129},{2,130},{3,131},{4,20},{5,21},{6,22},{7,23},{8,136... | collective-permute-start | bytes 688136 | tf_op jit(solution)/shard_map/ppermute | solution.py:43
  95.2 16.3 %collective-permute-start.19 = (bf16[128,896]{1,0:T(8,128)(2,1)S(1)}, bf16[128,896]{1,0:T(8,128)(2,1)S(1)}, u32[]{:S(2)}, u32[]{:S(2)}) collective-permute-start(bf16[128,896]{1,0:T(8,128)(2,1)S(1)} %get-tuple-element.75), channel_id=1, source_target_pairs={{0,192},{1,193},{2,194},{3,195},{4,28},{5,29},{6,30},{7,31},{8,200... | collective-permute-start | bytes 688136 | tf_op jit(solution)/shard_map/ppermute | solution.py:43
  112.1 22.9 %collective-permute-start.20 = (bf16[32,2688]{1,0:T(8,128)(2,1)S(1)}, bf16[32,2688]{1,0:T(8,128)(2,1)S(1)}, u32[]{:S(2)}, u32[]{:S(2)}) collective-permute-start(bf16[32,2688]{1,0:T(8,128)(2,1)S(1)} %get-tuple-element.116), channel_id=1, source_target_pairs={{0,1},{1,0},{2,3},{3,2},{4,5},{5,4},{6,7},{7,6},{8,9},{9,8},{10,11... | collective-permute-start | bytes 516104 | tf_op jit(solution)/shard_map/ppermute | solution.py:39
  130.1 13.7 %collective-permute-start.21 = (bf16[32,2688]{1,0:T(8,128)(2,1)S(1)}, bf16[32,2688]{1,0:T(8,128)(2,1)S(1)}, u32[]{:S(2)}, u32[]{:S(2)}) collective-permute-start(bf16[32,2688]{1,0:T(8,128)(2,1)S(1)} %get-tuple-element.117), channel_id=1, source_target_pairs={{0,2},{1,3},{2,0},{3,1},{4,6},{5,7},{6,4},{7,5},{8,10},{9,11},{10,... | collective-permute-start | bytes 516104 | tf_op jit(solution)/shard_map/ppermute | solution.py:39
  130.1 13.7 %collective-permute-start.22 = (bf16[32,2688]{1,0:T(8,128)(2,1)S(1)}, bf16[32,2688]{1,0:T(8,128)(2,1)S(1)}, u32[]{:S(2)}, u32[]{:S(2)}) collective-permute-start(bf16[32,2688]{1,0:T(8,128)(2,1)S(1)} %get-tuple-element.118), channel_id=1, source_target_pairs={{0,3},{1,2},{2,1},{3,0},{4,7},{5,6},{6,5},{7,4},{8,11},{9,10},{10,... | collective-permute-start | bytes 516104 | tf_op jit(solution)/shard_map/ppermute | solution.py:39
  146.6 6.5 %collective-permute-start.23 = (bf16[32,1536]{1,0:T(8,128)(2,1)S(1)}, bf16[32,1536]{1,0:T(8,128)(2,1)S(1)}, u32[]{:S(2)}, u32[]{:S(2)}) collective-permute-start(bf16[32,1536]{1,0:T(8,128)(2,1)S(1)} %pad_maximum_fusion.9), channel_id=1, source_target_pairs={{0,3},{1,2},{2,1},{3,0},{4,7},{5,6},{6,5},{7,4},{8,11},{9,10},{10,... | collective-permute-start | bytes 294920 | tf_op jit(solution)/shard_map/ppermute | solution.py:39
  148.1 11.4 %collective-permute-start.24 = (bf16[32,1536]{1,0:T(8,128)(2,1)S(1)}, bf16[32,1536]{1,0:T(8,128)(2,1)S(1)}, u32[]{:S(2)}, u32[]{:S(2)}) collective-permute-start(bf16[32,1536]{1,0:T(8,128)(2,1)S(1)} %pad_maximum_fusion.9), channel_id=1, source_target_pairs={{0,2},{1,3},{2,0},{3,1},{4,6},{5,7},{6,4},{7,5},{8,10},{9,11},{10,... | collective-permute-start | bytes 294920 | tf_op jit(solution)/shard_map/ppermute | solution.py:39
  152.3 7.2 %collective-permute-start.25 = (bf16[32,1536]{1,0:T(8,128)(2,1)S(1)}, bf16[32,1536]{1,0:T(8,128)(2,1)S(1)}, u32[]{:S(2)}, u32[]{:S(2)}) collective-permute-start(bf16[32,1536]{1,0:T(8,128)(2,1)S(1)} %pad_maximum_fusion.9), channel_id=1, source_target_pairs={{0,1},{1,0},{2,3},{3,2},{4,5},{5,4},{6,7},{7,6},{8,9},{9,8},{10,11... | collective-permute-start | bytes 294920 | tf_op jit(solution)/shard_map/ppermute | solution.py:39
  (2 other events, 3.1 us)
Sparse Core Ops, SparseCore 0:
  31.6 90.1 all-gather.1

commit v9 on v8

--- a/solution.py
+++ b/solution.py
@@ -180,15 +180,14 @@
         return jnp.concatenate(picked, axis=1)
 
     ring = [along(features(e), e, "y", "x") for e in (1, 2, 3)]
-    first, packed, wo_other, *ring = lax.optimization_barrier((first, packed, wo_other, *ring))
     second = move(packed, lambda y, zh, x, c, t: ((2 * zh + c) ^ y, 1 - (t & 1), x, t >> 1, y))
+    first, second, wo_other, *ring = lax.optimization_barrier((first, second, wo_other, *ring))
     inputs = jnp.concatenate([features(0)] + ring, axis=0)
 
     wo_piece = jnp.concatenate([out_weight, wo_other], axis=0)
     wo = lax.all_gather(wo_piece, ("y", "x", "core"), axis=0, tiled=True)
 
-    def gathered(block):
-        pair = jnp.stack([block, swap(block, "core", 1)])
+    def gathered(pair):
         return [pair] + [along(pair, d, "x", "y") for d in (1, 2, 3)]
 
     def reduced(blocks):
@@ -197,32 +196,45 @@
             total = total + along(sent[e - 1], e, "y", "x").astype(F32)
         return total
 
-    second, *blocks = lax.optimization_barrier((second, *gathered(first)))
-    total, *blocks = lax.optimization_barrier((reduced(blocks), *gathered(second)))
-    summed = [total, reduced(blocks)]
-    base = 2 * c + zh
-    q_slots = [half[:, at : at + 384] for at in (0, 384) for half in summed]
-    kv_slots = [half[:, at : at + 64] for at in (768, 832) for half in summed]
-    q_sum = jnp.concatenate(by_index(q_slots, base), axis=1)
-    kv_sum = jnp.concatenate(by_index(kv_slots, base), axis=1)
-
-    kv_short = kv_sum.astype(BF)
+    def over_zl(total, note):
+        kv = total[:, 768:]
+        kv_short = kv.astype(BF)
+        shared = [kv_short[32 * r : 32 * r + 32] for r in range(4)] + note
+
+        def rows_for(d):
+            return lax.dynamic_slice(total, ((t ^ d) * 32, 0), (32, 768))
+
+        q, extra = rows_for(0), 0.0
+        for d in (1, 2, 3):
+            came = swap(jnp.concatenate([rows_for(d).astype(BF)] + shared, axis=1), "zl", d).astype(F32)
+            q = q + came[:, :768]
+            kv = kv + jnp.concatenate([came[:, 768 + 128 * r : 896 + 128 * r] for r in range(4)], axis=0)
+            if note:
+                extra = extra + ((came[2, 1280:] + came[1, 1280:]) + came[0, 1280:])
+        return (q, kv, extra) if note else (q, kv)
+
     high = lax.reduce_precision(squares, 8, 7)
     middle = lax.reduce_precision(squares - high, 8, 7)
     low = squares - high - middle
     note = jnp.pad(jnp.stack([high, middle, low]), ((0, 29), (0, 0))).astype(BF)
-    shared = jnp.concatenate([kv_short[32 * r : 32 * r + 32] for r in range(4)] + [note], axis=1)
-
-    def rows_for(d):
-        return lax.dynamic_slice(q_sum, ((t ^ d) * 32, 0), (32, 1536))
-
-    q_raw, kv_raw, total = rows_for(0), kv_sum, squares
-    for d in (1, 2, 3):
-        came = swap(jnp.concatenate([rows_for(d).astype(BF), shared], axis=1), "zl", d).astype(F32)
-        q_raw = q_raw + came[:, :1536]
-        kv_raw = kv_raw + jnp.concatenate([came[:, 1536 + 256 * r : 1792 + 256 * r] for r in range(4)], axis=0)
-        total = total + ((came[2, 2560:] + came[1, 2560:]) + came[0, 2560:])
-    scales = lax.rsqrt(total / D + 1e-05)
+
+    others = swap(jnp.stack([first, second]), "core", 1)
+    near_pair, far_pair = jnp.stack([first, others[0]]), jnp.stack([second, others[1]])
+    far_pair, *blocks = lax.optimization_barrier((far_pair, *gathered(near_pair)))
+    total, *blocks = lax.optimization_barrier((reduced(blocks), *gathered(far_pair)))
+    far_total, *near_sums = lax.optimization_barrier((reduced(blocks), *over_zl(total, [note])))
+    far_sums = over_zl(far_total, [])
+    scales = lax.rsqrt((squares + near_sums[2]) / D + 1e-05)
+
+    base = 2 * c + zh
+
+    def ordered(near, far, width):
+        return jnp.concatenate(
+            by_index([half[:, at : at + width] for at in (0, width) for half in (near, far)], base), axis=1
+        )
+
+    q_raw = ordered(near_sums[0], far_sums[0], 384)
+    kv_raw = ordered(near_sums[1], far_sums[1], 64)
 
     limit = lengths[0]
     kv = (kv_raw * scales[:, None]).astype(BF)

time: 175 us -> 170 us (0.971)
  starting transfers between devices: 76.4 us -> 59.5 us
  waiting for transfers between devices: 66 us -> 78.7 us
    ppermute x17, waiting for transfers between devices: 38.3 us -> 67.9 us  [move(): lax.ppermute(value, AXES, [(flat(*at), flat(*where(*at))) for at in every...]
    ppermute x9 -> x11, waiting for transfers between devices: 27.6 us -> 10.8 us  [swap(): return lax.ppermute(value, axis, [(i, i ^ d) for i in range(n)])]
    ppermute x9 -> x11, starting transfers between devices: 33.2 us -> 19.1 us  [swap(): return lax.ppermute(value, axis, [(i, i ^ d) for i in range(n)])]
    ppermute x17, starting transfers between devices: 43.2 us -> 40.4 us  [move(): lax.ppermute(value, AXES, [(flat(*at), flat(*where(*at))) for at in every...]
  transfers between devices with their start and end apart: 27 -> 29, of which waited for: 12 -> 17; matrix products, arithmetic and copies ran while one was open for 2% -> 2% of each run, Pallas kernels for 2% -> 2%
where the time goes in v9:
time: 170 us
  waiting for transfers between devices  78.7 us (46%)
  starting transfers between devices  59.5 us (35%)
  between operations  14.7 us (9%)
  matrix products  8.6 us (5%)
  other arithmetic  4.17 us (2%)
  Pallas kernels  3.07 us (2%)
    ppermute x17, waiting for transfers between devices, move(): lax.ppermute(value, AXES, [(flat(*at), flat(*where(*at))) for at in every...  67.9 us
    ppermute x17, starting transfers between devices, move(): lax.ppermute(value, AXES, [(flat(*at), flat(*where(*at))) for at in every...  40.4 us
    ppermute x11, starting transfers between devices, swap(): return lax.ppermute(value, axis, [(i, i ^ d) for i in range(n)])  19.1 us
    ppermute x11, waiting for transfers between devices, swap(): return lax.ppermute(value, axis, [(i, i ^ d) for i in range(n)])  10.8 us
    dot_general x1, matrix products, body(): return jnp.dot(all_rows, wo, preferred_element_type=F32).astype(BF)  7.35 us
  transfers between devices with their start and end apart: 29, of which 17 were waited for; matrix products, arithmetic and copies ran while one was open for 2% of the time, Pallas kernels for 2%

profile of v9, /device:TPU:24, one launch (start us, length us, event | category | flops | bytes accessed | tf_op | source)
XLA Modules:
  0.0 170.1 jit_solution(10293657875694536725)
XLA Ops:
  6.5 1.7 fusion.2
  8.5 2.0 %collective-permute-start.5 = (bf16[128,1024]{1,0:T(8,128)(2,1)S(1)}, bf16[128,1024]{1,0:T(8,128)(2,1)S(1)}, u32[]{:S(2)}, u32[]{:S(2)}) collective-permute-start(bf16[128,1024]{1,0:T(8,128)(2,1)S(1)} %pad_maximum_fusion.7), channel_id=1, source_target_pairs={{0,192},{1,193},{2,194},{3,195},{4,28},{5,29},{6,30},{7,31},{8,200... | collective-permute-start | bytes 786440 | tf_op jit(solution)/shard_map/ppermute | solution.py:43
  10.5 5.5 %collective-permute-start.2 = (bf16[24,4096]{1,0:T(8,128)(2,1)S(1)}, bf16[24,4096]{1,0:T(8,128)(2,1)S(1)}, u32[]{:S(2)}, u32[]{:S(2)}) collective-permute-start(bf16[24,4096]{1,0:T(8,128)(2,1)S(1)} %copy-done.2), channel_id=1, source_target_pairs={{0,32},{32,0},{1,33},{33,1},{2,34},{34,2},{3,35},{35,3},{4,36},{36... | collective-permute-start | bytes 589832 | tf_op jit(solution)/shard_map/ppermute | solution.py:39
  16.0 2.7 %collective-permute-start.4 = (bf16[128,1024]{1,0:T(8,128)(2,1)S(1)}, bf16[128,1024]{1,0:T(8,128)(2,1)S(1)}, u32[]{:S(2)}, u32[]{:S(2)}) collective-permute-start(bf16[128,1024]{1,0:T(8,128)(2,1)S(1)} %pad_maximum_fusion.6), channel_id=1, source_target_pairs={{0,128},{1,129},{2,130},{3,131},{4,20},{5,21},{6,22},{7,23},{8,136... | collective-permute-start | bytes 786440 | tf_op jit(solution)/shard_map/ppermute | solution.py:43
  18.7 1.4 collective-permute-start.3
  20.1 3.8 %collective-permute-start = (bf16[896,128]{1,0:T(8,128)(2,1)S(1)}, bf16[896,128]{1,0:T(8,128)(2,1)S(1)}, u32[]{:S(2)}, u32[]{:S(2)}) collective-permute-start(bf16[896,128]{1,0:T(8,128)(2,1)S(1)} %shard_map.118), channel_id=1, source_target_pairs={{0,0},{1,32},{2,4},{3,36},{4,64},{5,96},{6,68},{7,100},{8,8},{9,40... | collective-permute-start | bytes 688136 | tf_op jit(solution)/shard_map/ppermute | solution.py:43
  24.0 7.0 %collective-permute-start.1 = (bf16[896,128]{1,0:T(8,128)(2,1)S(1)}, bf16[896,128]{1,0:T(8,128)(2,1)S(1)}, u32[]{:S(2)}, u32[]{:S(2)}) collective-permute-start(bf16[896,128]{1,0:T(8,128)(2,1)S(1)} %shard_map.118), channel_id=1, source_target_pairs={{0,32},{1,0},{2,36},{3,4},{4,96},{5,64},{6,100},{7,68},{8,40},{9,8... | collective-permute-start | bytes 688136 | tf_op jit(solution)/shard_map/ppermute | solution.py:43
  31.0 5.1 %collective-permute-done = bf16[896,128]{1,0:T(8,128)(2,1)S(1)} collective-permute-done((bf16[896,128]{1,0:T(8,128)(2,1)S(1)}, bf16[896,128]{1,0:T(8,128)(2,1)S(1)}, u32[]{:S(2)}, u32[]{:S(2)}) %collective-permute-start) | collective-permute-done | bytes 229408 | tf_op jit(solution)/shard_map/ppermute | solution.py:43
  36.1 10.6 %collective-permute-done.1 = bf16[896,128]{1,0:T(8,128)(2,1)S(1)} collective-permute-done((bf16[896,128]{1,0:T(8,128)(2,1)S(1)}, bf16[896,128]{1,0:T(8,128)(2,1)S(1)}, u32[]{:S(2)}, u32[]{:S(2)}) %collective-permute-start.1) | collective-permute-done | bytes 229408 | tf_op jit(solution)/shard_map/ppermute | solution.py:43
  49.5 1.4 collective-permute-start.7
  51.0 2.7 %collective-permute-start.8 = (bf16[2,896,128]{2,1,0:T(8,128)(2,1)S(1)}, bf16[2,896,128]{2,1,0:T(8,128)(2,1)S(1)}, u32[]{:S(2)}, u32[]{:S(2)}) collective-permute-start(bf16[2,896,128]{2,1,0:T(8,128)(2,1)S(1)} %pad_maximum_fusion.1.refs_0_), channel_id=1, source_target_pairs={{0,16},{1,17},{2,18},{3,19},{4,132},{5,133},{6,134},{7,135},{8,24}... | collective-permute-start | bytes 1376264 | tf_op jit(solution)/shard_map/ppermute | solution.py:43
  54.6 3.5 %collective-permute-done.7.refs_1_ = bf16[2,896,128]{2,1,0:T(8,128)(2,1)S(1)} collective-permute-done((bf16[2,896,128]{2,1,0:T(8,128)(2,1)S(1)}, bf16[2,896,128]{2,1,0:T(8,128)(2,1)S(1)}, u32[]{:S(2)}, u32[]{:S(2)}) %collective-permute-start.7) | collective-permute-done | bytes 458784 | tf_op jit(solution)/shard_map/ppermute | solution.py:43
  58.1 10.2 %collective-permute-done.8.refs_2_ = bf16[2,896,128]{2,1,0:T(8,128)(2,1)S(1)} collective-permute-done((bf16[2,896,128]{2,1,0:T(8,128)(2,1)S(1)}, bf16[2,896,128]{2,1,0:T(8,128)(2,1)S(1)}, u32[]{:S(2)}, u32[]{:S(2)}) %collective-permute-start.8) | collective-permute-done | bytes 458784 | tf_op jit(solution)/shard_map/ppermute | solution.py:43
  68.4 6.0 %collective-permute-done.9.refs_3_ = bf16[2,896,128]{2,1,0:T(8,128)(2,1)S(1)} collective-permute-done((bf16[2,896,128]{2,1,0:T(8,128)(2,1)S(1)}, bf16[2,896,128]{2,1,0:T(8,128)(2,1)S(1)}, u32[]{:S(2)}, u32[]{:S(2)}) %collective-permute-start.9) | collective-permute-done | bytes 458784 | tf_op jit(solution)/shard_map/ppermute | solution.py:43
  74.3 1.5 shard_map.119
  76.2 4.7 %collective-permute-start.12 = (bf16[128,896]{1,0:T(8,128)(2,1)S(1)}, bf16[128,896]{1,0:T(8,128)(2,1)S(1)}, u32[]{:S(2)}, u32[]{:S(2)}) collective-permute-start(bf16[128,896]{1,0:T(8,128)(2,1)S(1)} %get-tuple-element.75), channel_id=1, source_target_pairs={{0,192},{1,193},{2,194},{3,195},{4,28},{5,29},{6,30},{7,31},{8,200... | collective-permute-start | bytes 688136 | tf_op jit(solution)/shard_map/ppermute | solution.py:43
  80.8 2.8 %collective-permute-start.14 = (bf16[2,896,128]{2,1,0:T(8,128)(2,1)S(1)}, bf16[2,896,128]{2,1,0:T(8,128)(2,1)S(1)}, u32[]{:S(2)}, u32[]{:S(2)}) collective-permute-start(bf16[2,896,128]{2,1,0:T(8,128)(2,1)S(1)} %pad_maximum_fusion.3.refs_0_), channel_id=1, source_target_pairs={{0,16},{1,17},{2,18},{3,19},{4,132},{5,133},{6,134},{7,135},{8,24}... | collective-permute-start | bytes 1376264 | tf_op jit(solution)/shard_map/ppermute | solution.py:43
  85.8 3.0 %collective-permute-done.11 = bf16[128,896]{1,0:T(8,128)(2,1)S(1)} collective-permute-done((bf16[128,896]{1,0:T(8,128)(2,1)S(1)}, bf16[128,896]{1,0:T(8,128)(2,1)S(1)}, u32[]{:S(2)}, u32[]{:S(2)}) %collective-permute-start.11) | collective-permute-done | bytes 229408 | tf_op jit(solution)/shard_map/ppermute | solution.py:43
  88.8 5.7 %collective-permute-done.12 = bf16[128,896]{1,0:T(8,128)(2,1)S(1)} collective-permute-done((bf16[128,896]{1,0:T(8,128)(2,1)S(1)}, bf16[128,896]{1,0:T(8,128)(2,1)S(1)}, u32[]{:S(2)}, u32[]{:S(2)}) %collective-permute-start.12) | collective-permute-done | bytes 229408 | tf_op jit(solution)/shard_map/ppermute | solution.py:43
  94.7 13.2 %collective-permute-done.14.refs_2_ = bf16[2,896,128]{2,1,0:T(8,128)(2,1)S(1)} collective-permute-done((bf16[2,896,128]{2,1,0:T(8,128)(2,1)S(1)}, bf16[2,896,128]{2,1,0:T(8,128)(2,1)S(1)}, u32[]{:S(2)}, u32[]{:S(2)}) %collective-permute-start.14) | collective-permute-done | bytes 458784 | tf_op jit(solution)/shard_map/ppermute | solution.py:43
  110.2 3.2 %collective-permute-start.21 = (bf16[32,1408]{1,0:T(8,128)(2,1)S(1)}, bf16[32,1408]{1,0:T(8,128)(2,1)S(1)}, u32[]{:S(2)}, u32[]{:S(2)}) collective-permute-start(bf16[32,1408]{1,0:T(8,128)(2,1)S(1)} %get-tuple-element.148), channel_id=1, source_target_pairs={{0,3},{1,2},{2,1},{3,0},{4,7},{5,6},{6,5},{7,4},{8,11},{9,10},{10,... | collective-permute-start | bytes 270344 | tf_op jit(solution)/shard_map/ppermute | solution.py:39
  113.3 1.5 shard_map.120
  115.2 9.6 %collective-permute-start.17 = (bf16[128,896]{1,0:T(8,128)(2,1)S(1)}, bf16[128,896]{1,0:T(8,128)(2,1)S(1)}, u32[]{:S(2)}, u32[]{:S(2)}) collective-permute-start(bf16[128,896]{1,0:T(8,128)(2,1)S(1)} %get-tuple-element.73), channel_id=1, source_target_pairs={{0,128},{1,129},{2,130},{3,131},{4,20},{5,21},{6,22},{7,23},{8,136... | collective-permute-start | bytes 688136 | tf_op jit(solution)/shard_map/ppermute | solution.py:43
  125.0 6.3 %collective-permute-done.17 = bf16[128,896]{1,0:T(8,128)(2,1)S(1)} collective-permute-done((bf16[128,896]{1,0:T(8,128)(2,1)S(1)}, bf16[128,896]{1,0:T(8,128)(2,1)S(1)}, u32[]{:S(2)}, u32[]{:S(2)}) %collective-permute-start.17) | collective-permute-done | bytes 229408 | tf_op jit(solution)/shard_map/ppermute | solution.py:43
  131.4 2.4 %collective-permute-done.18 = bf16[128,896]{1,0:T(8,128)(2,1)S(1)} collective-permute-done((bf16[128,896]{1,0:T(8,128)(2,1)S(1)}, bf16[128,896]{1,0:T(8,128)(2,1)S(1)}, u32[]{:S(2)}, u32[]{:S(2)}) %collective-permute-start.18) | collective-permute-done | bytes 229408 | tf_op jit(solution)/shard_map/ppermute | solution.py:43
  134.0 1.5 collective-permute-start.24
  136.6 1.9 %collective-permute-start.22 = (bf16[32,1280]{1,0:T(8,128)(2,1)S(1)}, bf16[32,1280]{1,0:T(8,128)(2,1)S(1)}, u32[]{:S(2)}, u32[]{:S(2)}) collective-permute-start(bf16[32,1280]{1,0:T(8,128)(2,1)S(1)} %get-tuple-element.136), channel_id=1, source_target_pairs={{0,1},{1,0},{2,3},{3,2},{4,5},{5,4},{6,7},{7,6},{8,9},{9,8},{10,11... | collective-permute-start | bytes 245768 | tf_op jit(solution)/shard_map/ppermute | solution.py:39
  138.5 1.8 %collective-permute-done.24 = bf16[32,1280]{1,0:T(8,128)(2,1)S(1)} collective-permute-done((bf16[32,1280]{1,0:T(8,128)(2,1)S(1)}, bf16[32,1280]{1,0:T(8,128)(2,1)S(1)}, u32[]{:S(2)}, u32[]{:S(2)}) %collective-permute-start.24) | collective-permute-done | bytes 81952 | tf_op jit(solution)/shard_map/ppermute | solution.py:39
  140.4 4.6 %collective-permute-done.23 = bf16[32,1280]{1,0:T(8,128)(2,1)S(1)} collective-permute-done((bf16[32,1280]{1,0:T(8,128)(2,1)S(1)}, bf16[32,1280]{1,0:T(8,128)(2,1)S(1)}, u32[]{:S(2)}, u32[]{:S(2)}) %collective-permute-start.23) | collective-permute-done | bytes 81952 | tf_op jit(solution)/shard_map/ppermute | solution.py:39
  148.1 4.3 %collective-permute-start.27 = (bf16[32,1536]{1,0:T(8,128)(2,1)S(1)}, bf16[32,1536]{1,0:T(8,128)(2,1)S(1)}, u32[]{:S(2)}, u32[]{:S(2)}) collective-permute-start(bf16[32,1536]{1,0:T(8,128)(2,1)S(1)} %pad_maximum_fusion.8), channel_id=1, source_target_pairs={{0,1},{1,0},{2,3},{3,2},{4,5},{5,4},{6,7},{7,6},{8,9},{9,8},{10,11... | collective-permute-start | bytes 294920 | tf_op jit(solution)/shard_map/ppermute | solution.py:39
  152.4 2.2 %collective-permute-done.25 = bf16[32,1536]{1,0:T(8,128)(2,1)S(1)} collective-permute-done((bf16[32,1536]{1,0:T(8,128)(2,1)S(1)}, bf16[32,1536]{1,0:T(8,128)(2,1)S(1)}, u32[]{:S(2)}, u32[]{:S(2)}) %collective-permute-start.25) | collective-permute-done | bytes 98336 | tf_op jit(solution)/shard_map/ppermute | solution.py:39
  155.9 7.4 %convolution_convert_fusion = bf16[128,4096]{1,0:T(8,128)(2,1)} fusion(bf16[1536,4096]{1,0:T(8,128)(2,1)} %all-gather.2.cloned.1.call-done, bf16[32,1536]{1,0:T(8,128)(2,1)S(1)} %broadcast_select_fusion.4, bf16[32,1536]{1,0:T(8,128)(2,1)S(1)} %get-tuple-element.87, bf16[32,1536]{1,0:T(8,128)(2,1)S(1)} %get-tuple-element.86, ...), kind=kOutput, calls=%fused_computation.1 | convolution fusion | flops 1612709888 | bytes 14024704 | tf_op jit(solution)/shard_map/dot_general | solution.py:253
  (133 shorter events, 14.2 us)
Async XLA Ops:
  6.5 149.4 %all-gather.2.cloned.1.call-start = ((), (), s32[]{:S(2)}) async-start(), calls=%async_computation | async-start | bytes 12976128 | tf_op jit(solution)/shard_map/all_gather | solution.py:188
  8.2 11.9 %copy-start = (bf16[256,384]{1,0:T(8,128)(2,1)S(1)}, bf16[256,384]{1,0:T(8,128)(2,1)}, u32[]{:S(2)}) copy-start(bf16[256,384]{1,0:T(8,128)(2,1)} %q_ref.1) | copy-start | bytes 589828
  8.5 38.2 %collective-permute-start.5 = (bf16[128,1024]{1,0:T(8,128)(2,1)S(1)}, bf16[128,1024]{1,0:T(8,128)(2,1)S(1)}, u32[]{:S(2)}, u32[]{:S(2)}) collective-permute-start(bf16[128,1024]{1,0:T(8,128)(2,1)S(1)} %pad_maximum_fusion.7), channel_id=1, source_target_pairs={{0,192},{1,193},{2,194},{3,195},{4,28},{5,29},{6,30},{7,31},{8,200... | collective-permute-start | bytes 786440 | tf_op jit(solution)/shard_map/ppermute | solution.py:43
  10.5 13.4 %collective-permute-start.2 = (bf16[24,4096]{1,0:T(8,128)(2,1)S(1)}, bf16[24,4096]{1,0:T(8,128)(2,1)S(1)}, u32[]{:S(2)}, u32[]{:S(2)}) collective-permute-start(bf16[24,4096]{1,0:T(8,128)(2,1)S(1)} %copy-done.2), channel_id=1, source_target_pairs={{0,32},{32,0},{1,33},{33,1},{2,34},{34,2},{3,35},{35,3},{4,36},{36... | collective-permute-start | bytes 589832 | tf_op jit(solution)/shard_map/ppermute | solution.py:39
  16.0 30.7 %collective-permute-start.4 = (bf16[128,1024]{1,0:T(8,128)(2,1)S(1)}, bf16[128,1024]{1,0:T(8,128)(2,1)S(1)}, u32[]{:S(2)}, u32[]{:S(2)}) collective-permute-start(bf16[128,1024]{1,0:T(8,128)(2,1)S(1)} %pad_maximum_fusion.6), channel_id=1, source_target_pairs={{0,128},{1,129},{2,130},{3,131},{4,20},{5,21},{6,22},{7,23},{8,136... | collective-permute-start | bytes 786440 | tf_op jit(solution)/shard_map/ppermute | solution.py:43
  18.7 28.0 %collective-permute-start.3 = (bf16[128,1024]{1,0:T(8,128)(2,1)S(1)}, bf16[128,1024]{1,0:T(8,128)(2,1)S(1)}, u32[]{:S(2)}, u32[]{:S(2)}) collective-permute-start(bf16[128,1024]{1,0:T(8,128)(2,1)S(1)} %pad_maximum_fusion.5), channel_id=1, source_target_pairs={{0,64},{1,65},{2,66},{3,67},{4,12},{5,13},{6,14},{7,15},{8,72},{9,... | collective-permute-start | bytes 786440 | tf_op jit(solution)/shard_map/ppermute | solution.py:43
  20.1 16.0 %collective-permute-start = (bf16[896,128]{1,0:T(8,128)(2,1)S(1)}, bf16[896,128]{1,0:T(8,128)(2,1)S(1)}, u32[]{:S(2)}, u32[]{:S(2)}) collective-permute-start(bf16[896,128]{1,0:T(8,128)(2,1)S(1)} %shard_map.118), channel_id=1, source_target_pairs={{0,0},{1,32},{2,4},{3,36},{4,64},{5,96},{6,68},{7,100},{8,8},{9,40... | collective-permute-start | bytes 688136 | tf_op jit(solution)/shard_map/ppermute | solution.py:43
  24.0 22.7 %collective-permute-start.1 = (bf16[896,128]{1,0:T(8,128)(2,1)S(1)}, bf16[896,128]{1,0:T(8,128)(2,1)S(1)}, u32[]{:S(2)}, u32[]{:S(2)}) collective-permute-start(bf16[896,128]{1,0:T(8,128)(2,1)S(1)} %shard_map.118), channel_id=1, source_target_pairs={{0,32},{1,0},{2,36},{3,4},{4,96},{5,64},{6,100},{7,68},{8,40},{9,8... | collective-permute-start | bytes 688136 | tf_op jit(solution)/shard_map/ppermute | solution.py:43
  47.6 1.9 %collective-permute-start.6 = (bf16[2,896,128]{2,1,0:T(8,128)(2,1)S(1)}, bf16[2,896,128]{2,1,0:T(8,128)(2,1)S(1)}, u32[]{:S(2)}, u32[]{:S(2)}) collective-permute-start(bf16[2,896,128]{2,1,0:T(8,128)(2,1)S(1)} %pad_maximum_fusion.2), channel_id=1, source_target_pairs={{0,4},{4,0},{1,5},{5,1},{2,6},{6,2},{3,7},{7,3},{8,12},{12,8},{9,1... | collective-permute-start | bytes 1376264 | tf_op jit(solution)/shard_map/ppermute | solution.py:39
  49.5 8.6 %collective-permute-start.7 = (bf16[2,896,128]{2,1,0:T(8,128)(2,1)S(1)}, bf16[2,896,128]{2,1,0:T(8,128)(2,1)S(1)}, u32[]{:S(2)}, u32[]{:S(2)}) collective-permute-start(bf16[2,896,128]{2,1,0:T(8,128)(2,1)S(1)} %pad_maximum_fusion.1.refs_0_), channel_id=1, source_target_pairs={{0,8},{1,9},{2,10},{3,11},{4,68},{5,69},{6,70},{7,71},{8,0},{9,1},... | collective-permute-start | bytes 1376264 | tf_op jit(solution)/shard_map/ppermute | solution.py:43
  51.0 17.4 %collective-permute-start.8 = (bf16[2,896,128]{2,1,0:T(8,128)(2,1)S(1)}, bf16[2,896,128]{2,1,0:T(8,128)(2,1)S(1)}, u32[]{:S(2)}, u32[]{:S(2)}) collective-permute-start(bf16[2,896,128]{2,1,0:T(8,128)(2,1)S(1)} %pad_maximum_fusion.1.refs_0_), channel_id=1, source_target_pairs={{0,16},{1,17},{2,18},{3,19},{4,132},{5,133},{6,134},{7,135},{8,24}... | collective-permute-start | bytes 1376264 | tf_op jit(solution)/shard_map/ppermute | solution.py:43
  53.7 20.6 %collective-permute-start.9 = (bf16[2,896,128]{2,1,0:T(8,128)(2,1)S(1)}, bf16[2,896,128]{2,1,0:T(8,128)(2,1)S(1)}, u32[]{:S(2)}, u32[]{:S(2)}) collective-permute-start(bf16[2,896,128]{2,1,0:T(8,128)(2,1)S(1)} %pad_maximum_fusion.1.refs_0_), channel_id=1, source_target_pairs={{0,24},{1,25},{2,26},{3,27},{4,196},{5,197},{6,198},{7,199},{8,16}... | collective-permute-start | bytes 1376264 | tf_op jit(solution)/shard_map/ppermute | solution.py:43
  54.6 21.5 %copy-start.3 = (f32[128,128]{1,0:T(8,128)S(1)}, f32[128,128]{1,0:T(8,128)}, u32[]{:S(2)}) copy-start(f32[128,128]{1,0:T(8,128)} %constant.76.clone) | copy-start | bytes 196612
  54.6 21.5 %copy-start.4 = (f32[128,128]{1,0:T(8,128)S(1)}, f32[128,128]{1,0:T(8,128)}, u32[]{:S(2)}) copy-start(f32[128,128]{1,0:T(8,128)} %constant.77.clone) | copy-start | bytes 196612
  75.9 8.6 %collective-permute-start.10 = (bf16[128,896]{1,0:T(8,128)(2,1)S(1)}, bf16[128,896]{1,0:T(8,128)(2,1)S(1)}, u32[]{:S(2)}, u32[]{:S(2)}) collective-permute-start(bf16[128,896]{1,0:T(8,128)(2,1)S(1)} %get-tuple-element.74), channel_id=1, source_target_pairs={{0,64},{1,65},{2,66},{3,67},{4,12},{5,13},{6,14},{7,15},{8,72},{9,... | collective-permute-start | bytes 688136 | tf_op jit(solution)/shard_map/ppermute | solution.py:43
  76.1 12.8 %collective-permute-start.11 = (bf16[128,896]{1,0:T(8,128)(2,1)S(1)}, bf16[128,896]{1,0:T(8,128)(2,1)S(1)}, u32[]{:S(2)}, u32[]{:S(2)}) collective-permute-start(bf16[128,896]{1,0:T(8,128)(2,1)S(1)} %get-tuple-element.76), channel_id=1, source_target_pairs={{0,128},{1,129},{2,130},{3,131},{4,20},{5,21},{6,22},{7,23},{8,136... | collective-permute-start | bytes 688136 | tf_op jit(solution)/shard_map/ppermute | solution.py:43
  76.2 18.4 %collective-permute-start.12 = (bf16[128,896]{1,0:T(8,128)(2,1)S(1)}, bf16[128,896]{1,0:T(8,128)(2,1)S(1)}, u32[]{:S(2)}, u32[]{:S(2)}) collective-permute-start(bf16[128,896]{1,0:T(8,128)(2,1)S(1)} %get-tuple-element.75), channel_id=1, source_target_pairs={{0,192},{1,193},{2,194},{3,195},{4,28},{5,29},{6,30},{7,31},{8,200... | collective-permute-start | bytes 688136 | tf_op jit(solution)/shard_map/ppermute | solution.py:43
  80.8 13.8 %collective-permute-start.13 = (bf16[2,896,128]{2,1,0:T(8,128)(2,1)S(1)}, bf16[2,896,128]{2,1,0:T(8,128)(2,1)S(1)}, u32[]{:S(2)}, u32[]{:S(2)}) collective-permute-start(bf16[2,896,128]{2,1,0:T(8,128)(2,1)S(1)} %pad_maximum_fusion.3.refs_0_), channel_id=1, source_target_pairs={{0,8},{1,9},{2,10},{3,11},{4,68},{5,69},{6,70},{7,71},{8,0},{9,1},... | collective-permute-start | bytes 1376264 | tf_op jit(solution)/shard_map/ppermute | solution.py:43
  80.8 27.1 %collective-permute-start.14 = (bf16[2,896,128]{2,1,0:T(8,128)(2,1)S(1)}, bf16[2,896,128]{2,1,0:T(8,128)(2,1)S(1)}, u32[]{:S(2)}, u32[]{:S(2)}) collective-permute-start(bf16[2,896,128]{2,1,0:T(8,128)(2,1)S(1)} %pad_maximum_fusion.3.refs_0_), channel_id=1, source_target_pairs={{0,16},{1,17},{2,18},{3,19},{4,132},{5,133},{6,134},{7,135},{8,24}... | collective-permute-start | bytes 1376264 | tf_op jit(solution)/shard_map/ppermute | solution.py:43
  84.5 24.2 %collective-permute-start.15 = (bf16[2,896,128]{2,1,0:T(8,128)(2,1)S(1)}, bf16[2,896,128]{2,1,0:T(8,128)(2,1)S(1)}, u32[]{:S(2)}, u32[]{:S(2)}) collective-permute-start(bf16[2,896,128]{2,1,0:T(8,128)(2,1)S(1)} %pad_maximum_fusion.3.refs_0_), channel_id=1, source_target_pairs={{0,24},{1,25},{2,26},{3,27},{4,196},{5,197},{6,198},{7,199},{8,16}... | collective-permute-start | bytes 1376264 | tf_op jit(solution)/shard_map/ppermute | solution.py:43
  108.9 15.9 %collective-permute-start.19 = (bf16[32,1408]{1,0:T(8,128)(2,1)S(1)}, bf16[32,1408]{1,0:T(8,128)(2,1)S(1)}, u32[]{:S(2)}, u32[]{:S(2)}) collective-permute-start(bf16[32,1408]{1,0:T(8,128)(2,1)S(1)} %get-tuple-element.146), channel_id=1, source_target_pairs={{0,1},{1,0},{2,3},{3,2},{4,5},{5,4},{6,7},{7,6},{8,9},{9,8},{10,11... | collective-permute-start | bytes 270344 | tf_op jit(solution)/shard_map/ppermute | solution.py:39
  110.2 14.7 %collective-permute-start.20 = (bf16[32,1408]{1,0:T(8,128)(2,1)S(1)}, bf16[32,1408]{1,0:T(8,128)(2,1)S(1)}, u32[]{:S(2)}, u32[]{:S(2)}) collective-permute-start(bf16[32,1408]{1,0:T(8,128)(2,1)S(1)} %get-tuple-element.147), channel_id=1, source_target_pairs={{0,2},{1,3},{2,0},{3,1},{4,6},{5,7},{6,4},{7,5},{8,10},{9,11},{10,... | collective-permute-start | bytes 270344 | tf_op jit(solution)/shard_map/ppermute | solution.py:39
  110.2 14.7 %collective-permute-start.21 = (bf16[32,1408]{1,0:T(8,128)(2,1)S(1)}, bf16[32,1408]{1,0:T(8,128)(2,1)S(1)}, u32[]{:S(2)}, u32[]{:S(2)}) collective-permute-start(bf16[32,1408]{1,0:T(8,128)(2,1)S(1)} %get-tuple-element.148), channel_id=1, source_target_pairs={{0,3},{1,2},{2,1},{3,0},{4,7},{5,6},{6,5},{7,4},{8,11},{9,10},{10,... | collective-permute-start | bytes 270344 | tf_op jit(solution)/shard_map/ppermute | solution.py:39
  114.9 10.1 %collective-permute-start.16 = (bf16[128,896]{1,0:T(8,128)(2,1)S(1)}, bf16[128,896]{1,0:T(8,128)(2,1)S(1)}, u32[]{:S(2)}, u32[]{:S(2)}) collective-permute-start(bf16[128,896]{1,0:T(8,128)(2,1)S(1)} %get-tuple-element.71), channel_id=1, source_target_pairs={{0,64},{1,65},{2,66},{3,67},{4,12},{5,13},{6,14},{7,15},{8,72},{9,... | collective-permute-start | bytes 688136 | tf_op jit(solution)/shard_map/ppermute | solution.py:43
  115.2 16.2 %collective-permute-start.17 = (bf16[128,896]{1,0:T(8,128)(2,1)S(1)}, bf16[128,896]{1,0:T(8,128)(2,1)S(1)}, u32[]{:S(2)}, u32[]{:S(2)}) collective-permute-start(bf16[128,896]{1,0:T(8,128)(2,1)S(1)} %get-tuple-element.73), channel_id=1, source_target_pairs={{0,128},{1,129},{2,130},{3,131},{4,20},{5,21},{6,22},{7,23},{8,136... | collective-permute-start | bytes 688136 | tf_op jit(solution)/shard_map/ppermute | solution.py:43
  124.8 8.9 %collective-permute-start.18 = (bf16[128,896]{1,0:T(8,128)(2,1)S(1)}, bf16[128,896]{1,0:T(8,128)(2,1)S(1)}, u32[]{:S(2)}, u32[]{:S(2)}) collective-permute-start(bf16[128,896]{1,0:T(8,128)(2,1)S(1)} %get-tuple-element.72), channel_id=1, source_target_pairs={{0,192},{1,193},{2,194},{3,195},{4,28},{5,29},{6,30},{7,31},{8,200... | collective-permute-start | bytes 688136 | tf_op jit(solution)/shard_map/ppermute | solution.py:43
  134.0 6.4 %collective-permute-start.24 = (bf16[32,1280]{1,0:T(8,128)(2,1)S(1)}, bf16[32,1280]{1,0:T(8,128)(2,1)S(1)}, u32[]{:S(2)}, u32[]{:S(2)}) collective-permute-start(bf16[32,1280]{1,0:T(8,128)(2,1)S(1)} %constant_dynamic-update-slice_fusion.28), channel_id=1, source_target_pairs={{0,3},{1,2},{2,1},{3,0},{4,7},{5,6},{6,5},{7,4},{8,11},{9,10},{10,... | collective-permute-start | bytes 245768 | tf_op jit(solution)/shard_map/ppermute | solution.py:39
  135.4 9.5 %collective-permute-start.23 = (bf16[32,1280]{1,0:T(8,128)(2,1)S(1)}, bf16[32,1280]{1,0:T(8,128)(2,1)S(1)}, u32[]{:S(2)}, u32[]{:S(2)}) collective-permute-start(bf16[32,1280]{1,0:T(8,128)(2,1)S(1)} %get-tuple-element.139), channel_id=1, source_target_pairs={{0,2},{1,3},{2,0},{3,1},{4,6},{5,7},{6,4},{7,5},{8,10},{9,11},{10,... | collective-permute-start | bytes 245768 | tf_op jit(solution)/shard_map/ppermute | solution.py:39
  136.6 8.4 %collective-permute-start.22 = (bf16[32,1280]{1,0:T(8,128)(2,1)S(1)}, bf16[32,1280]{1,0:T(8,128)(2,1)S(1)}, u32[]{:S(2)}, u32[]{:S(2)}) collective-permute-start(bf16[32,1280]{1,0:T(8,128)(2,1)S(1)} %get-tuple-element.136), channel_id=1, source_target_pairs={{0,1},{1,0},{2,3},{3,2},{4,5},{5,4},{6,7},{7,6},{8,9},{9,8},{10,11... | collective-permute-start | bytes 245768 | tf_op jit(solution)/shard_map/ppermute | solution.py:39
  147.9 6.7 %collective-permute-start.25 = (bf16[32,1536]{1,0:T(8,128)(2,1)S(1)}, bf16[32,1536]{1,0:T(8,128)(2,1)S(1)}, u32[]{:S(2)}, u32[]{:S(2)}) collective-permute-start(bf16[32,1536]{1,0:T(8,128)(2,1)S(1)} %pad_maximum_fusion.8), channel_id=1, source_target_pairs={{0,3},{1,2},{2,1},{3,0},{4,7},{5,6},{6,5},{7,4},{8,11},{9,10},{10,... | collective-permute-start | bytes 294920 | tf_op jit(solution)/shard_map/ppermute | solution.py:39
  148.0 7.7 %collective-permute-start.26 = (bf16[32,1536]{1,0:T(8,128)(2,1)S(1)}, bf16[32,1536]{1,0:T(8,128)(2,1)S(1)}, u32[]{:S(2)}, u32[]{:S(2)}) collective-permute-start(bf16[32,1536]{1,0:T(8,128)(2,1)S(1)} %pad_maximum_fusion.8), channel_id=1, source_target_pairs={{0,2},{1,3},{2,0},{3,1},{4,6},{5,7},{6,4},{7,5},{8,10},{9,11},{10,... | collective-permute-start | bytes 294920 | tf_op jit(solution)/shard_map/ppermute | solution.py:39
  148.1 7.6 %collective-permute-start.27 = (bf16[32,1536]{1,0:T(8,128)(2,1)S(1)}, bf16[32,1536]{1,0:T(8,128)(2,1)S(1)}, u32[]{:S(2)}, u32[]{:S(2)}) collective-permute-start(bf16[32,1536]{1,0:T(8,128)(2,1)S(1)} %pad_maximum_fusion.8), channel_id=1, source_target_pairs={{0,1},{1,0},{2,3},{3,2},{4,5},{5,4},{6,7},{7,6},{8,9},{9,8},{10,11... | collective-permute-start | bytes 294920 | tf_op jit(solution)/shard_map/ppermute | solution.py:39
  (4 other events, 18.9 us)
Sparse Core Ops, SparseCore 0:
  47.6 82.1 all-gather.1

commit v10 on v9

--- a/solution.py
+++ b/solution.py
@@ -62,15 +62,6 @@
 
 
 COSINE, SINE = tables()
-
-
-def order_of(zh):
-    order = np.arange(384).reshape(2, 8, 24)
-    order = np.stack([order[zh], order[1 - zh]], axis=1).reshape(384)
-    return np.eye(384, dtype=np.float32)[:, order].astype(jnp.bfloat16)
-
-
-ORDER = (order_of(0), order_of(1))
 
 
 def rotate(values, cosine, sine):
@@ -148,6 +139,36 @@
     )(inputs, *blocks)
 
 
+def mix_kernel(core_ref, mine_ref, other_ref, *refs):
+    near, far, (kept_ref, sent_ref) = refs[:4], refs[4:8], refs[8:]
+
+    def run(rows_of):
+        for at in range(0, 2048, 512):
+            parts = [part for d in range(4) for half in (near, far) for part in rows_of(half, d, slice(at, at + 512))]
+            weight = jnp.concatenate(parts, axis=0)
+            kept_ref[:, at : at + 512] = jnp.dot(mine_ref[...], weight, preferred_element_type=F32).astype(BF)
+            sent_ref[:, at : at + 512] = jnp.dot(other_ref[...], weight, preferred_element_type=F32).astype(BF)
+
+    @pl.when(core_ref[0] == 0)
+    def _():
+        run(lambda half, d, columns: [half[d][:, columns]])
+
+    @pl.when(core_ref[0] == 1)
+    def _():
+        run(lambda half, d, columns: [half[e][48 * d : 48 * d + 48, columns] for e in range(4)])
+
+
+def mix(core, mine, other, near, far):
+    return pl.pallas_call(
+        mix_kernel,
+        out_shape=(jax.ShapeDtypeStruct((ROWS, 2048), BF),) * 2,
+        in_specs=[pl.BlockSpec(memory_space=pltpu.SMEM)] + [whole(0)] * 10,
+        out_specs=(whole(0),) * 2,
+        compiler_params=pltpu.CompilerParams(vmem_limit_bytes=48 * 2**20),
+        cost_estimate=pl.CostEstimate(flops=2 * 256 * 1536 * 2048, bytes_accessed=9000000, transcendentals=0),
+    )(core.reshape(1), mine, other, *near, *far)
+
+
 def attend(query, keys, values, limit, first):
     scores = jnp.einsum("qhd,kd->hqk", query, keys, preferred_element_type=F32) * HD ** (-0.5)
     keys_at = jnp.arange(ROWS, dtype=jnp.int32)
@@ -165,7 +186,15 @@
 
     packed = pack(query_weight, kv_weight.T)
     first = move(packed, lambda y, zh, x, c, t: ((2 * zh + c) ^ y, t & 1, x, t >> 1, y))
-    wo_other = swap(out_weight, "zh", 1)
+    wo_here = lax.dynamic_slice(out_weight, (0, c * 2048), (24, 2048))
+    wo_there = swap(lax.dynamic_slice(out_weight, (0, (1 - c) * 2048), (24, 2048)), "core", 1)
+    wo_pair = jnp.concatenate([pick(c == 1, wo_here, wo_there), pick(c == 1, wo_there, wo_here)], axis=0)
+
+    def first_ring(piece):
+        return jnp.concatenate([piece] + [along(piece, d, "x", "y") for d in (1, 2, 3)], axis=0)
+
+    wo_near = first_ring(wo_pair)
+    wo_near = [wo_near] + [along(wo_near, e, "y", "x") for e in (1, 2, 3)]
 
     widened = tokens.astype(F32)
     squares = jnp.sum(widened * widened, axis=1)
@@ -181,11 +210,9 @@
 
     ring = [along(features(e), e, "y", "x") for e in (1, 2, 3)]
     second = move(packed, lambda y, zh, x, c, t: ((2 * zh + c) ^ y, 1 - (t & 1), x, t >> 1, y))
-    first, second, wo_other, *ring = lax.optimization_barrier((first, second, wo_other, *ring))
+    first, second, wo_pair, *rest = lax.optimization_barrier((first, second, wo_pair, *ring, *wo_near))
+    ring, wo_near = rest[:3], rest[3:]
     inputs = jnp.concatenate([features(0)] + ring, axis=0)
-
-    wo_piece = jnp.concatenate([out_weight, wo_other], axis=0)
-    wo = lax.all_gather(wo_piece, ("y", "x", "core"), axis=0, tiled=True)
 
     def gathered(pair):
         return [pair] + [along(pair, d, "x", "y") for d in (1, 2, 3)]
@@ -220,10 +247,12 @@
 
     others = swap(jnp.stack([first, second]), "core", 1)
     near_pair, far_pair = jnp.stack([first, others[0]]), jnp.stack([second, others[1]])
-    far_pair, *blocks = lax.optimization_barrier((far_pair, *gathered(near_pair)))
+    far_pair, wo_far, *blocks = lax.optimization_barrier((far_pair, swap(wo_pair, "zh", 1), *gathered(near_pair)))
     total, *blocks = lax.optimization_barrier((reduced(blocks), *gathered(far_pair)))
-    far_total, *near_sums = lax.optimization_barrier((reduced(blocks), *over_zl(total, [note])))
-    far_sums = over_zl(far_total, [])
+    far_total, wo_far, *near_sums = lax.optimization_barrier(
+        (reduced(blocks), first_ring(wo_far), *over_zl(total, [note]))
+    )
+    wo_first, *far_sums = lax.optimization_barrier((along(wo_far, 1, "y", "x"), *over_zl(far_total, [])))
     scales = lax.rsqrt((squares + near_sums[2]) / D + 1e-05)
 
     base = 2 * c + zh
@@ -244,13 +273,20 @@
     scale_here = lax.dynamic_slice(scales, (t * 32,), (32,))
     query = rotate((q_raw * scale_here[:, None]).reshape(32, 12, HD), *mine_rows).astype(BF)
     attended = attend(query, keys, values, limit, t * 32).reshape(32, 1536)
-    stacked = jnp.concatenate([attended[:, 384 * d : 384 * d + 384] for d in range(4)], axis=0)
-    stacked = jnp.dot(stacked, pick(zh == 1, ORDER[0], ORDER[1]), preferred_element_type=F32).astype(BF)
+    stacked = jnp.concatenate(by_index([attended[:, 384 * d : 384 * d + 384] for d in range(4)], y), axis=0)
+    at = jnp.arange(384, dtype=jnp.int32)
+    source = (((at // 192) ^ zh) * 4 + ((at // 48) % 4 ^ x)) * 48 + at % 48
+    order = (at[:, None] == source[None, :]).astype(BF)
+    stacked = jnp.dot(stacked, order, preferred_element_type=F32).astype(BF)
     attended = jnp.concatenate([stacked[32 * d : 32 * d + 32] for d in range(4)], axis=1)
 
     got = [attended] + [swap(attended, "zl", d) for d in (1, 2, 3)]
-    all_rows = jnp.concatenate(by_index(got, t), axis=0)
-    return jnp.dot(all_rows, wo, preferred_element_type=F32).astype(BF)
+    wo_rest = [along(wo_far, e, "y", "x") for e in (2, 3)]
+    *got, wo_second, wo_third = lax.optimization_barrier((*got, *wo_rest))
+    mine = jnp.concatenate(by_index(got, t), axis=0)
+    kept, sent = mix(c, mine, swap(mine, "core", 1), wo_near, [wo_far, wo_first, wo_second, wo_third])
+    came = swap(sent, "core", 1)
+    return jnp.concatenate([pick(c == 1, kept, came), pick(c == 1, came, kept)], axis=1)
 
 
 def solution(mesh):

time: 170 us -> 188 us (1.11); the launches traced: 170 us -> 185 us
  starting transfers between devices: 59.5 us -> 81.2 us
  waiting for transfers between devices: 78.7 us -> 62.4 us
  between operations: 14.7 us -> 1.54 us
  local copies, waits for them, and re-layouts: 1.32 us -> 13.8 us
  other arithmetic: 4.17 us -> 15.8 us
  matrix products: 8.6 us -> 1.3 us
  Pallas kernels: 3.07 us -> 8.81 us
    ppermute x17 -> x29, waiting for transfers between devices: 67.9 us -> 41.2 us  [move(): lax.ppermute(value, AXES, [(flat(*at), flat(*where(*at))) for at in every...]
    ppermute x17 -> x29, starting transfers between devices: 40.4 us -> 56 us  [move(): lax.ppermute(value, AXES, [(flat(*at), flat(*where(*at))) for at in every...]
    ppermute x11 -> x14, waiting for transfers between devices: 10.8 us -> 21.2 us  [swap(): return lax.ppermute(value, axis, [(i, i ^ d) for i in range(n)])]
    dot_general x2 -> x1, matrix products: 7.57 us -> 0.27 us  [body(): stacked = jnp.dot(stacked, order, preferred_element_type=F32).astype(BF)]
    ppermute x11 -> x14, starting transfers between devices: 19.1 us -> 25.3 us  [swap(): return lax.ppermute(value, axis, [(i, i ^ d) for i in range(n)])]
    unnamed x31 -> x75, local copies, waits for them, and re-layouts: 0.24 us -> 6.18 us
    pallas_call x0 -> x1, Pallas kernels: none -> 3.42 us  [mix(): pl.pallas_call(mix_kernel, out_shape=(jax.ShapeDtypeStruct((ROWS, 2048),...]
    another operation x1, other arithmetic: 0.05 us -> 2.42 us  [body(): others = swap(jnp.stack([first, second]), 'core', 1)]
  transfers between devices with their start and end apart: 29 -> 43, of which waited for: 17 -> 21; matrix products, arithmetic and copies ran while one was open for 2% -> 9% of each run, Pallas kernels for 2% -> 1%
where the time goes in v10:
time: 188 us; the launch traced here: 185 us
  starting transfers between devices  81.2 us (43%)
  waiting for transfers between devices  62.4 us (33%)
  other arithmetic  15.8 us (8%)
  local copies, waits for them, and re-layouts  13.8 us (7%)
  Pallas kernels  8.81 us (5%)
    ppermute x29, starting transfers between devices, move(): lax.ppermute(value, AXES, [(flat(*at), flat(*where(*at))) for at in every...  56 us
    ppermute x29, waiting for transfers between devices, move(): lax.ppermute(value, AXES, [(flat(*at), flat(*where(*at))) for at in every...  41.2 us
    ppermute x14, starting transfers between devices, swap(): return lax.ppermute(value, axis, [(i, i ^ d) for i in range(n)])  25.3 us
    ppermute x14, waiting for transfers between devices, swap(): return lax.ppermute(value, axis, [(i, i ^ d) for i in range(n)])  21.2 us
    unnamed x75, local copies, waits for them, and re-layouts  6.18 us
    pallas_call x2, Pallas kernels, project(): pl.pallas_call(project_kernel, out_shape=(jax.ShapeDtypeStruct((3, ROWS,...  5.35 us
  transfers between devices with their start and end apart: 43, of which 21 were waited for; matrix products, arithmetic and copies ran while one was open for 9% of the time, Pallas kernels for 1%

profile of v10, /device:TPU:24, one launch (start us, length us, event | category | flops | bytes accessed | tf_op | source)
XLA Modules:
  0.0 184.9 jit_solution(2857849628008850895)
XLA Ops:
  2.7 6.7 %collective-permute-start = (bf16[896,128]{1,0:T(8,128)(2,1)S(1)}, bf16[896,128]{1,0:T(8,128)(2,1)}, u32[]{:S(2)}, u32[]{:S(2)}) collective-permute-start(bf16[896,128]{1,0:T(8,128)(2,1)S(1)} %shard_map.100), channel_id=1, source_target_pairs={{0,0},{1,32},{2,4},{3,36},{4,64},{5,96},{6,68},{7,100},{8,8},{9,40... | collective-permute-start | bytes 688136 | tf_op jit(solution)/shard_map/ppermute | solution.py:43
  13.9 2.7 %collective-permute-start.7 = (bf16[48,2048]{1,0:T(8,128)(2,1)S(1)}, bf16[48,2048]{1,0:T(8,128)(2,1)S(1)}, u32[]{:S(2)}, u32[]{:S(2)}) collective-permute-start(bf16[48,2048]{1,0:T(8,128)(2,1)S(1)} %pad_maximum_fusion.10), channel_id=1, source_target_pairs={{0,16},{1,17},{2,18},{3,19},{4,132},{5,133},{6,134},{7,135},{8,24}... | collective-permute-start | bytes 589832 | tf_op jit(solution)/shard_map/ppermute | solution.py:43
  17.1 3.9 %collective-permute-done.7 = bf16[48,2048]{1,0:T(8,128)(2,1)S(1)} collective-permute-done((bf16[48,2048]{1,0:T(8,128)(2,1)S(1)}, bf16[48,2048]{1,0:T(8,128)(2,1)S(1)}, u32[]{:S(2)}, u32[]{:S(2)}) %collective-permute-start.7) | collective-permute-done | bytes 196640 | tf_op jit(solution)/shard_map/ppermute | solution.py:43
  21.1 2.4 %collective-permute-done.8 = bf16[48,2048]{1,0:T(8,128)(2,1)S(1)} collective-permute-done((bf16[48,2048]{1,0:T(8,128)(2,1)S(1)}, bf16[48,2048]{1,0:T(8,128)(2,1)S(1)}, u32[]{:S(2)}, u32[]{:S(2)}) %collective-permute-start.8) | collective-permute-done | bytes 196640 | tf_op jit(solution)/shard_map/ppermute | solution.py:43
  23.7 4.6 %collective-permute-start.11 = (bf16[192,2048]{1,0:T(8,128)(2,1)S(1)}, bf16[192,2048]{1,0:T(8,128)(2,1)S(1)}, u32[]{:S(2)}, u32[]{:S(2)}) collective-permute-start(bf16[192,2048]{1,0:T(8,128)(2,1)S(1)} %constant_dynamic-update-slice_fusion.refs_0_), channel_id=1, source_target_pairs={{0,192},{1,193},{2,194},{3,195},{4,28},{5,29},{6,30},{7,31},{8,200... | collective-permute-start | bytes 2359304 | tf_op jit(solution)/shard_map/ppermute | solution.py:43
  30.5 4.8 %collective-permute-start.1 = (bf16[896,128]{1,0:T(8,128)(2,1)S(1)}, bf16[896,128]{1,0:T(8,128)(2,1)S(1)}, u32[]{:S(2)}, u32[]{:S(2)}) collective-permute-start(bf16[896,128]{1,0:T(8,128)(2,1)S(1)} %shard_map.100), channel_id=1, source_target_pairs={{0,32},{1,0},{2,36},{3,4},{4,96},{5,64},{6,100},{7,68},{8,40},{9,8... | collective-permute-start | bytes 688136 | tf_op jit(solution)/shard_map/ppermute | solution.py:43
  36.7 9.0 %collective-permute-done.1 = bf16[896,128]{1,0:T(8,128)(2,1)S(1)} collective-permute-done((bf16[896,128]{1,0:T(8,128)(2,1)S(1)}, bf16[896,128]{1,0:T(8,128)(2,1)S(1)}, u32[]{:S(2)}, u32[]{:S(2)}) %collective-permute-start.1) | collective-permute-done | bytes 229408 | tf_op jit(solution)/shard_map/ppermute | solution.py:43
  46.4 2.5 %collective-permute-start.4 = (bf16[128,1024]{1,0:T(8,128)(2,1)}, bf16[128,1024]{1,0:T(8,128)(2,1)}, u32[]{:S(2)}, u32[]{:S(2)}) collective-permute-start(bf16[128,1024]{1,0:T(8,128)(2,1)} %pad_maximum_fusion.8), channel_id=1, source_target_pairs={{0,128},{1,129},{2,130},{3,131},{4,20},{5,21},{6,22},{7,23},{8,136... | collective-permute-start | bytes 786440 | tf_op jit(solution)/shard_map/ppermute | solution.py:43
  49.5 4.5 %collective-permute-start.5 = (bf16[128,1024]{1,0:T(8,128)(2,1)}, bf16[128,1024]{1,0:T(8,128)(2,1)}, u32[]{:S(2)}, u32[]{:S(2)}) collective-permute-start(bf16[128,1024]{1,0:T(8,128)(2,1)} %pad_maximum_fusion.9), channel_id=1, source_target_pairs={{0,192},{1,193},{2,194},{3,195},{4,28},{5,29},{6,30},{7,31},{8,200... | collective-permute-start | bytes 786440 | tf_op jit(solution)/shard_map/ppermute | solution.py:43
  54.6 4.1 %collective-permute-done.5 = bf16[128,1024]{1,0:T(8,128)(2,1)} collective-permute-done((bf16[128,1024]{1,0:T(8,128)(2,1)}, bf16[128,1024]{1,0:T(8,128)(2,1)}, u32[]{:S(2)}, u32[]{:S(2)}) %collective-permute-start.5) | collective-permute-done | bytes 262176 | tf_op jit(solution)/shard_map/ppermute | solution.py:43
  58.7 2.4 %pad_maximum_fusion.4 = bf16[2,896,128]{2,1,0:T(8,128)(2,1)} fusion(bf16[1,896,128]{2,1,0:T(8,128)(2,1)} %bitcast.4, bf16[1,896,128]{2,1,0:T(8,128)(2,1)} %bitcast.47), kind=kLoop, calls=%fused_computation.21 | loop fusion | flops 229376 | bytes 917504 | tf_op jit(solution)/shard_map/stack | solution.py:248
  67.1 3.0 %collective-permute-start.15 = (bf16[2,896,128]{2,1,0:T(8,128)(2,1)}, bf16[2,896,128]{2,1,0:T(8,128)(2,1)S(1)}, u32[]{:S(2)}, u32[]{:S(2)}) collective-permute-start(bf16[2,896,128]{2,1,0:T(8,128)(2,1)} %pad_maximum_fusion.3.refs_0_), channel_id=1, source_target_pairs={{0,16},{1,17},{2,18},{3,19},{4,132},{5,133},{6,134},{7,135},{8,24}... | collective-permute-start | bytes 1376264 | tf_op jit(solution)/shard_map/ppermute | solution.py:43
  73.5 10.9 %collective-permute-start.13 = (bf16[48,2048]{1,0:T(8,128)(2,1)}, bf16[48,2048]{1,0:T(8,128)(2,1)S(1)}, u32[]{:S(2)}, u32[]{:S(2)}) collective-permute-start(bf16[48,2048]{1,0:T(8,128)(2,1)} %copy-done.19), channel_id=1, source_target_pairs={{0,32},{32,0},{1,33},{33,1},{2,34},{34,2},{3,35},{35,3},{4,36},{36... | collective-permute-start | bytes 589832 | tf_op jit(solution)/shard_map/ppermute | solution.py:39
  86.5 3.2 %collective-permute-done.13 = bf16[48,2048]{1,0:T(8,128)(2,1)S(1)} collective-permute-done((bf16[48,2048]{1,0:T(8,128)(2,1)}, bf16[48,2048]{1,0:T(8,128)(2,1)S(1)}, u32[]{:S(2)}, u32[]{:S(2)}) %collective-permute-start.13) | collective-permute-done | bytes 196640 | tf_op jit(solution)/shard_map/ppermute | solution.py:39
  90.4 2.8 %shard_map.101 = (bf16[3,128,896]{2,1,0:T(8,128)(2,1)S(1)}, f32[128,896]{1,0:T(8,128)S(1)}) custom-call(bf16[512,1024]{1,0:T(8,128)(2,1)S(1)} %pad_maximum_fusion.x_ref, bf16[2,896,128]{2,1,0:T(8,128)(2,1)} %pad_maximum_fusion.3.refs_0_, bf16[2,896,128]{2,1,0:T(8,128)(2,1)} %collective-permute-done.14.refs_1_, ...), custom_call_target="tpu_custom_call" | custom-call | flops 939524096 | bytes 4000000 | tf_op jit(solution)/shard_map/pallas_call | solution.py:132
  94.1 2.7 %collective-permute-start.19 = (bf16[128,896]{1,0:T(8,128)(2,1)S(1)}, bf16[128,896]{1,0:T(8,128)(2,1)S(1)}, u32[]{:S(2)}, u32[]{:S(2)}) collective-permute-start(bf16[128,896]{1,0:T(8,128)(2,1)S(1)} %get-tuple-element.115), channel_id=1, source_target_pairs={{0,192},{1,193},{2,194},{3,195},{4,28},{5,29},{6,30},{7,31},{8,200... | collective-permute-start | bytes 688136 | tf_op jit(solution)/shard_map/ppermute | solution.py:43
  96.9 2.7 %collective-permute-start.28 = (bf16[48,2048]{1,0:T(8,128)(2,1)S(1)}, bf16[48,2048]{1,0:T(8,128)(2,1)S(1)}, u32[]{:S(2)}, u32[]{:S(2)}) collective-permute-start(bf16[48,2048]{1,0:T(8,128)(2,1)S(1)} %copy-done.18), channel_id=1, source_target_pairs={{0,24},{1,25},{2,26},{3,27},{4,196},{5,197},{6,198},{7,199},{8,16}... | collective-permute-start | bytes 589832 | tf_op jit(solution)/shard_map/ppermute | solution.py:43
  102.5 2.4 %collective-permute-done.28 = bf16[48,2048]{1,0:T(8,128)(2,1)S(1)} collective-permute-done((bf16[48,2048]{1,0:T(8,128)(2,1)S(1)}, bf16[48,2048]{1,0:T(8,128)(2,1)S(1)}, u32[]{:S(2)}, u32[]{:S(2)}) %collective-permute-start.28) | collective-permute-done | bytes 196640 | tf_op jit(solution)/shard_map/ppermute | solution.py:43
  104.9 3.5 %collective-permute-start.21 = (bf16[2,896,128]{2,1,0:T(8,128)(2,1)}, bf16[2,896,128]{2,1,0:T(8,128)(2,1)S(1)}, u32[]{:S(2)}, u32[]{:S(2)}) collective-permute-start(bf16[2,896,128]{2,1,0:T(8,128)(2,1)} %pad_maximum_fusion.5.refs_0_), channel_id=1, source_target_pairs={{0,16},{1,17},{2,18},{3,19},{4,132},{5,133},{6,134},{7,135},{8,24}... | collective-permute-start | bytes 1376264 | tf_op jit(solution)/shard_map/ppermute | solution.py:43
  112.6 5.9 %collective-permute-done.18 = bf16[128,896]{1,0:T(8,128)(2,1)S(1)} collective-permute-done((bf16[128,896]{1,0:T(8,128)(2,1)}, bf16[128,896]{1,0:T(8,128)(2,1)S(1)}, u32[]{:S(2)}, u32[]{:S(2)}) %collective-permute-start.18) | collective-permute-done | bytes 229408 | tf_op jit(solution)/shard_map/ppermute | solution.py:43
  119.9 3.8 %collective-permute-done.21.refs_2_ = bf16[2,896,128]{2,1,0:T(8,128)(2,1)S(1)} collective-permute-done((bf16[2,896,128]{2,1,0:T(8,128)(2,1)}, bf16[2,896,128]{2,1,0:T(8,128)(2,1)S(1)}, u32[]{:S(2)}, u32[]{:S(2)}) %collective-permute-start.21) | collective-permute-done | bytes 458784 | tf_op jit(solution)/shard_map/ppermute | solution.py:43
  127.5 2.9 %collective-permute-start.30 = (bf16[32,1408]{1,0:T(8,128)(2,1)S(1)}, bf16[32,1408]{1,0:T(8,128)(2,1)S(1)}, u32[]{:S(2)}, u32[]{:S(2)}) collective-permute-start(bf16[32,1408]{1,0:T(8,128)(2,1)S(1)} %get-tuple-element.188), channel_id=1, source_target_pairs={{0,2},{1,3},{2,0},{3,1},{4,6},{5,7},{6,4},{7,5},{8,10},{9,11},{10,... | collective-permute-start | bytes 270344 | tf_op jit(solution)/shard_map/ppermute | solution.py:39
  130.9 2.5 %shard_map.102 = (bf16[3,128,896]{2,1,0:T(8,128)(2,1)S(1)}, f32[128,896]{1,0:T(8,128)S(1)}) custom-call(bf16[512,1024]{1,0:T(8,128)(2,1)S(1)} %pad_maximum_fusion.x_ref, bf16[2,896,128]{2,1,0:T(8,128)(2,1)} %pad_maximum_fusion.5.refs_0_, bf16[2,896,128]{2,1,0:T(8,128)(2,1)S(1)} %collective-permute-done.20.refs_1_, ...), custom_call_target="tpu_custom_call" | custom-call | flops 939524096 | bytes 4000000 | tf_op jit(solution)/shard_map/pallas_call | solution.py:132
  135.2 2.5 %collective-permute-start.23 = (bf16[128,896]{1,0:T(8,128)(2,1)S(1)}, bf16[128,896]{1,0:T(8,128)(2,1)S(1)}, u32[]{:S(2)}, u32[]{:S(2)}) collective-permute-start(bf16[128,896]{1,0:T(8,128)(2,1)S(1)} %get-tuple-element.111), channel_id=1, source_target_pairs={{0,64},{1,65},{2,66},{3,67},{4,12},{5,13},{6,14},{7,15},{8,72},{9,... | collective-permute-start | bytes 688136 | tf_op jit(solution)/shard_map/ppermute | solution.py:43
  137.9 5.4 %collective-permute-done.25 = bf16[128,896]{1,0:T(8,128)(2,1)S(1)} collective-permute-done((bf16[128,896]{1,0:T(8,128)(2,1)S(1)}, bf16[128,896]{1,0:T(8,128)(2,1)S(1)}, u32[]{:S(2)}, u32[]{:S(2)}) %collective-permute-start.25) | collective-permute-done | bytes 229408 | tf_op jit(solution)/shard_map/ppermute | solution.py:43
  144.4 3.0 %collective-permute-start.39 = (bf16[192,2048]{1,0:T(8,128)(2,1)S(1)}, bf16[192,2048]{1,0:T(8,128)(2,1)}, u32[]{:S(2)}, u32[]{:S(2)}) collective-permute-start(bf16[192,2048]{1,0:T(8,128)(2,1)S(1)} %pad_maximum_fusion.2.refs_4_), channel_id=1, source_target_pairs={{0,128},{1,129},{2,130},{3,131},{4,20},{5,21},{6,22},{7,23},{8,136... | collective-permute-start | bytes 2359304 | tf_op jit(solution)/shard_map/ppermute | solution.py:43
  149.2 2.5 %collective-permute-start.35 = (bf16[32,1280]{1,0:T(8,128)(2,1)S(1)}, bf16[32,1280]{1,0:T(8,128)(2,1)S(1)}, u32[]{:S(2)}, u32[]{:S(2)}) collective-permute-start(bf16[32,1280]{1,0:T(8,128)(2,1)S(1)} %constant_dynamic-update-slice_fusion.33), channel_id=1, source_target_pairs={{0,3},{1,2},{2,1},{3,0},{4,7},{5,6},{6,5},{7,4},{8,11},{9,10},{10,... | collective-permute-start | bytes 245768 | tf_op jit(solution)/shard_map/ppermute | solution.py:39
  152.9 4.6 %collective-permute-done.33 = bf16[32,1280]{1,0:T(8,128)(2,1)S(1)} collective-permute-done((bf16[32,1280]{1,0:T(8,128)(2,1)S(1)}, bf16[32,1280]{1,0:T(8,128)(2,1)S(1)}, u32[]{:S(2)}, u32[]{:S(2)}) %collective-permute-start.33) | collective-permute-done | bytes 81952 | tf_op jit(solution)/shard_map/ppermute | solution.py:39
  157.9 5.0 %collective-permute-done.34 = bf16[32,1280]{1,0:T(8,128)(2,1)S(1)} collective-permute-done((bf16[32,1280]{1,0:T(8,128)(2,1)S(1)}, bf16[32,1280]{1,0:T(8,128)(2,1)S(1)}, u32[]{:S(2)}, u32[]{:S(2)}) %collective-permute-start.34) | collective-permute-done | bytes 81952 | tf_op jit(solution)/shard_map/ppermute | solution.py:39
  167.4 2.6 %collective-permute-start.37 = (bf16[32,1536]{1,0:T(8,128)(2,1)S(1)}, bf16[32,1536]{1,0:T(8,128)(2,1)S(1)}, u32[]{:S(2)}, u32[]{:S(2)}) collective-permute-start(bf16[32,1536]{1,0:T(8,128)(2,1)S(1)} %pad_maximum_fusion.11), channel_id=1, source_target_pairs={{0,2},{1,3},{2,0},{3,1},{4,6},{5,7},{6,4},{7,5},{8,10},{9,11},{10,... | collective-permute-start | bytes 294920 | tf_op jit(solution)/shard_map/ppermute | solution.py:39
  173.0 3.4 %collective-permute-done.38 = bf16[32,1536]{1,0:T(8,128)(2,1)S(1)} collective-permute-done((bf16[32,1536]{1,0:T(8,128)(2,1)S(1)}, bf16[32,1536]{1,0:T(8,128)(2,1)S(1)}, u32[]{:S(2)}, u32[]{:S(2)}) %collective-permute-start.38) | collective-permute-done | bytes 98336 | tf_op jit(solution)/shard_map/ppermute | solution.py:39
  178.3 3.4 %shard_map.103 = (bf16[128,2048]{1,0:T(8,128)(2,1)S(1)}, bf16[128,2048]{1,0:T(8,128)(2,1)S(1)}) custom-call(s32[1]{0:T(128)} %bitcast.core_ref, bf16[128,1536]{1,0:T(8,128)(2,1)S(1)} %pad_maximum_fusion.6.mine_ref, bf16[128,1536]{1,0:T(8,128)(2,1)S(1)} %collective-permute-done.41.other_ref, bf16[192,2048]{1,0:T(8,128)(2,1)S(1)} %constant_dynamic-update-slice_fusion.refs_0_, ...), custom_call_target="tpu_custom_call" | custom-call | flops 1610612736 | bytes 9000000 | tf_op jit(solution)/shard_map/pallas_call | solution.py:162
  (212 shorter events, 57.0 us)
Async XLA Ops:
  1.0 8.5 %collective-permute-start.2 = (bf16[24,2048]{1,0:T(8,128)(2,1)S(1)}, bf16[24,2048]{1,0:T(8,128)(2,1)S(1)}, u32[]{:S(2)}, u32[]{:S(2)}) collective-permute-start(bf16[24,2048]{1,0:T(8,128)(2,1)S(1)} %constant_dynamic-slice_fusion.14), channel_id=1, source_target_pairs={{0,4},{4,0},{1,5},{5,1},{2,6},{6,2},{3,7},{7,3},{8,12},{12,8},{9,1... | collective-permute-start | bytes 294920 | tf_op jit(solution)/shard_map/ppermute | solution.py:39
  2.7 27.7 %collective-permute-start = (bf16[896,128]{1,0:T(8,128)(2,1)S(1)}, bf16[896,128]{1,0:T(8,128)(2,1)}, u32[]{:S(2)}, u32[]{:S(2)}) collective-permute-start(bf16[896,128]{1,0:T(8,128)(2,1)S(1)} %shard_map.100), channel_id=1, source_target_pairs={{0,0},{1,32},{2,4},{3,36},{4,64},{5,96},{6,68},{7,100},{8,8},{9,40... | collective-permute-start | bytes 688136 | tf_op jit(solution)/shard_map/ppermute | solution.py:43
  23.5 35.2 %collective-permute-start.9 = (bf16[192,2048]{1,0:T(8,128)(2,1)S(1)}, bf16[192,2048]{1,0:T(8,128)(2,1)S(1)}, u32[]{:S(2)}, u32[]{:S(2)}) collective-permute-start(bf16[192,2048]{1,0:T(8,128)(2,1)S(1)} %constant_dynamic-update-slice_fusion.refs_0_), channel_id=1, source_target_pairs={{0,64},{1,65},{2,66},{3,67},{4,12},{5,13},{6,14},{7,15},{8,72},{9,... | collective-permute-start | bytes 2359304 | tf_op jit(solution)/shard_map/ppermute | solution.py:43
  23.6 35.1 %collective-permute-start.10 = (bf16[192,2048]{1,0:T(8,128)(2,1)S(1)}, bf16[192,2048]{1,0:T(8,128)(2,1)S(1)}, u32[]{:S(2)}, u32[]{:S(2)}) collective-permute-start(bf16[192,2048]{1,0:T(8,128)(2,1)S(1)} %constant_dynamic-update-slice_fusion.refs_0_), channel_id=1, source_target_pairs={{0,128},{1,129},{2,130},{3,131},{4,20},{5,21},{6,22},{7,23},{8,136... | collective-permute-start | bytes 2359304 | tf_op jit(solution)/shard_map/ppermute | solution.py:43
  23.7 35.0 %collective-permute-start.11 = (bf16[192,2048]{1,0:T(8,128)(2,1)S(1)}, bf16[192,2048]{1,0:T(8,128)(2,1)S(1)}, u32[]{:S(2)}, u32[]{:S(2)}) collective-permute-start(bf16[192,2048]{1,0:T(8,128)(2,1)S(1)} %constant_dynamic-update-slice_fusion.refs_0_), channel_id=1, source_target_pairs={{0,192},{1,193},{2,194},{3,195},{4,28},{5,29},{6,30},{7,31},{8,200... | collective-permute-start | bytes 2359304 | tf_op jit(solution)/shard_map/ppermute | solution.py:43
  30.4 18.5 %collective-permute-start.3 = (bf16[128,1024]{1,0:T(8,128)(2,1)S(1)}, bf16[128,1024]{1,0:T(8,128)(2,1)S(1)}, u32[]{:S(2)}, u32[]{:S(2)}) collective-permute-start(bf16[128,1024]{1,0:T(8,128)(2,1)S(1)} %pad_maximum_fusion.7), channel_id=1, source_target_pairs={{0,64},{1,65},{2,66},{3,67},{4,12},{5,13},{6,14},{7,15},{8,72},{9,... | collective-permute-start | bytes 786440 | tf_op jit(solution)/shard_map/ppermute | solution.py:43
  30.5 15.2 %collective-permute-start.1 = (bf16[896,128]{1,0:T(8,128)(2,1)S(1)}, bf16[896,128]{1,0:T(8,128)(2,1)S(1)}, u32[]{:S(2)}, u32[]{:S(2)}) collective-permute-start(bf16[896,128]{1,0:T(8,128)(2,1)S(1)} %shard_map.100), channel_id=1, source_target_pairs={{0,32},{1,0},{2,36},{3,4},{4,96},{5,64},{6,100},{7,68},{8,40},{9,8... | collective-permute-start | bytes 688136 | tf_op jit(solution)/shard_map/ppermute | solution.py:43
  46.4 8.2 %collective-permute-start.4 = (bf16[128,1024]{1,0:T(8,128)(2,1)}, bf16[128,1024]{1,0:T(8,128)(2,1)}, u32[]{:S(2)}, u32[]{:S(2)}) collective-permute-start(bf16[128,1024]{1,0:T(8,128)(2,1)} %pad_maximum_fusion.8), channel_id=1, source_target_pairs={{0,128},{1,129},{2,130},{3,131},{4,20},{5,21},{6,22},{7,23},{8,136... | collective-permute-start | bytes 786440 | tf_op jit(solution)/shard_map/ppermute | solution.py:43
  49.5 9.2 %collective-permute-start.5 = (bf16[128,1024]{1,0:T(8,128)(2,1)}, bf16[128,1024]{1,0:T(8,128)(2,1)}, u32[]{:S(2)}, u32[]{:S(2)}) collective-permute-start(bf16[128,1024]{1,0:T(8,128)(2,1)} %pad_maximum_fusion.9), channel_id=1, source_target_pairs={{0,192},{1,193},{2,194},{3,195},{4,28},{5,29},{6,30},{7,31},{8,200... | collective-permute-start | bytes 786440 | tf_op jit(solution)/shard_map/ppermute | solution.py:43
  66.8 22.9 %collective-permute-start.14 = (bf16[2,896,128]{2,1,0:T(8,128)(2,1)}, bf16[2,896,128]{2,1,0:T(8,128)(2,1)}, u32[]{:S(2)}, u32[]{:S(2)}) collective-permute-start(bf16[2,896,128]{2,1,0:T(8,128)(2,1)} %pad_maximum_fusion.3.refs_0_), channel_id=1, source_target_pairs={{0,8},{1,9},{2,10},{3,11},{4,68},{5,69},{6,70},{7,71},{8,0},{9,1},... | collective-permute-start | bytes 1376264 | tf_op jit(solution)/shard_map/ppermute | solution.py:43
  67.1 22.7 %collective-permute-start.15 = (bf16[2,896,128]{2,1,0:T(8,128)(2,1)}, bf16[2,896,128]{2,1,0:T(8,128)(2,1)S(1)}, u32[]{:S(2)}, u32[]{:S(2)}) collective-permute-start(bf16[2,896,128]{2,1,0:T(8,128)(2,1)} %pad_maximum_fusion.3.refs_0_), channel_id=1, source_target_pairs={{0,16},{1,17},{2,18},{3,19},{4,132},{5,133},{6,134},{7,135},{8,24}... | collective-permute-start | bytes 1376264 | tf_op jit(solution)/shard_map/ppermute | solution.py:43
  70.1 20.3 %collective-permute-start.16 = (bf16[2,896,128]{2,1,0:T(8,128)(2,1)}, bf16[2,896,128]{2,1,0:T(8,128)(2,1)}, u32[]{:S(2)}, u32[]{:S(2)}) collective-permute-start(bf16[2,896,128]{2,1,0:T(8,128)(2,1)} %pad_maximum_fusion.3.refs_0_), channel_id=1, source_target_pairs={{0,24},{1,25},{2,26},{3,27},{4,196},{5,197},{6,198},{7,199},{8,16}... | collective-permute-start | bytes 1376264 | tf_op jit(solution)/shard_map/ppermute | solution.py:43
  73.5 16.2 %collective-permute-start.13 = (bf16[48,2048]{1,0:T(8,128)(2,1)}, bf16[48,2048]{1,0:T(8,128)(2,1)S(1)}, u32[]{:S(2)}, u32[]{:S(2)}) collective-permute-start(bf16[48,2048]{1,0:T(8,128)(2,1)} %copy-done.19), channel_id=1, source_target_pairs={{0,32},{32,0},{1,33},{33,1},{2,34},{34,2},{3,35},{35,3},{4,36},{36... | collective-permute-start | bytes 589832 | tf_op jit(solution)/shard_map/ppermute | solution.py:39
  94.1 16.7 %collective-permute-start.19 = (bf16[128,896]{1,0:T(8,128)(2,1)S(1)}, bf16[128,896]{1,0:T(8,128)(2,1)S(1)}, u32[]{:S(2)}, u32[]{:S(2)}) collective-permute-start(bf16[128,896]{1,0:T(8,128)(2,1)S(1)} %get-tuple-element.115), channel_id=1, source_target_pairs={{0,192},{1,193},{2,194},{3,195},{4,28},{5,29},{6,30},{7,31},{8,200... | collective-permute-start | bytes 688136 | tf_op jit(solution)/shard_map/ppermute | solution.py:43
  96.9 8.0 %collective-permute-start.28 = (bf16[48,2048]{1,0:T(8,128)(2,1)S(1)}, bf16[48,2048]{1,0:T(8,128)(2,1)S(1)}, u32[]{:S(2)}, u32[]{:S(2)}) collective-permute-start(bf16[48,2048]{1,0:T(8,128)(2,1)S(1)} %copy-done.18), channel_id=1, source_target_pairs={{0,24},{1,25},{2,26},{3,27},{4,196},{5,197},{6,198},{7,199},{8,16}... | collective-permute-start | bytes 589832 | tf_op jit(solution)/shard_map/ppermute | solution.py:43
  99.5 8.8 %collective-permute-start.27 = (bf16[48,2048]{1,0:T(8,128)(2,1)S(1)}, bf16[48,2048]{1,0:T(8,128)(2,1)S(1)}, u32[]{:S(2)}, u32[]{:S(2)}) collective-permute-start(bf16[48,2048]{1,0:T(8,128)(2,1)S(1)} %copy-done.18), channel_id=1, source_target_pairs={{0,16},{1,17},{2,18},{3,19},{4,132},{5,133},{6,134},{7,135},{8,24}... | collective-permute-start | bytes 589832 | tf_op jit(solution)/shard_map/ppermute | solution.py:43
  100.3 8.2 %collective-permute-start.26 = (bf16[48,2048]{1,0:T(8,128)(2,1)S(1)}, bf16[48,2048]{1,0:T(8,128)(2,1)S(1)}, u32[]{:S(2)}, u32[]{:S(2)}) collective-permute-start(bf16[48,2048]{1,0:T(8,128)(2,1)S(1)} %copy-done.18), channel_id=1, source_target_pairs={{0,8},{1,9},{2,10},{3,11},{4,68},{5,69},{6,70},{7,71},{8,0},{9,1},... | collective-permute-start | bytes 589832 | tf_op jit(solution)/shard_map/ppermute | solution.py:43
  101.2 18.6 %collective-permute-start.20 = (bf16[2,896,128]{2,1,0:T(8,128)(2,1)}, bf16[2,896,128]{2,1,0:T(8,128)(2,1)S(1)}, u32[]{:S(2)}, u32[]{:S(2)}) collective-permute-start(bf16[2,896,128]{2,1,0:T(8,128)(2,1)} %pad_maximum_fusion.5.refs_0_), channel_id=1, source_target_pairs={{0,8},{1,9},{2,10},{3,11},{4,68},{5,69},{6,70},{7,71},{8,0},{9,1},... | collective-permute-start | bytes 1376264 | tf_op jit(solution)/shard_map/ppermute | solution.py:43
  104.9 18.8 %collective-permute-start.21 = (bf16[2,896,128]{2,1,0:T(8,128)(2,1)}, bf16[2,896,128]{2,1,0:T(8,128)(2,1)S(1)}, u32[]{:S(2)}, u32[]{:S(2)}) collective-permute-start(bf16[2,896,128]{2,1,0:T(8,128)(2,1)} %pad_maximum_fusion.5.refs_0_), channel_id=1, source_target_pairs={{0,16},{1,17},{2,18},{3,19},{4,132},{5,133},{6,134},{7,135},{8,24}... | collective-permute-start | bytes 1376264 | tf_op jit(solution)/shard_map/ppermute | solution.py:43
  108.3 16.8 %collective-permute-start.22 = (bf16[2,896,128]{2,1,0:T(8,128)(2,1)}, bf16[2,896,128]{2,1,0:T(8,128)(2,1)S(1)}, u32[]{:S(2)}, u32[]{:S(2)}) collective-permute-start(bf16[2,896,128]{2,1,0:T(8,128)(2,1)} %pad_maximum_fusion.5.refs_0_), channel_id=1, source_target_pairs={{0,24},{1,25},{2,26},{3,27},{4,196},{5,197},{6,198},{7,199},{8,16}... | collective-permute-start | bytes 1376264 | tf_op jit(solution)/shard_map/ppermute | solution.py:43
  108.5 9.9 %collective-permute-start.18 = (bf16[128,896]{1,0:T(8,128)(2,1)}, bf16[128,896]{1,0:T(8,128)(2,1)S(1)}, u32[]{:S(2)}, u32[]{:S(2)}) collective-permute-start(bf16[128,896]{1,0:T(8,128)(2,1)} %get-tuple-element.116), channel_id=1, source_target_pairs={{0,128},{1,129},{2,130},{3,131},{4,20},{5,21},{6,22},{7,23},{8,136... | collective-permute-start | bytes 688136 | tf_op jit(solution)/shard_map/ppermute | solution.py:43
  111.6 8.2 %collective-permute-start.17 = (bf16[128,896]{1,0:T(8,128)(2,1)}, bf16[128,896]{1,0:T(8,128)(2,1)S(1)}, u32[]{:S(2)}, u32[]{:S(2)}) collective-permute-start(bf16[128,896]{1,0:T(8,128)(2,1)} %get-tuple-element.114), channel_id=1, source_target_pairs={{0,64},{1,65},{2,66},{3,67},{4,12},{5,13},{6,14},{7,15},{8,72},{9,... | collective-permute-start | bytes 688136 | tf_op jit(solution)/shard_map/ppermute | solution.py:43
  125.3 9.9 %collective-permute-start.31 = (bf16[32,1408]{1,0:T(8,128)(2,1)S(1)}, bf16[32,1408]{1,0:T(8,128)(2,1)S(1)}, u32[]{:S(2)}, u32[]{:S(2)}) collective-permute-start(bf16[32,1408]{1,0:T(8,128)(2,1)S(1)} %get-tuple-element.189), channel_id=1, source_target_pairs={{0,3},{1,2},{2,1},{3,0},{4,7},{5,6},{6,5},{7,4},{8,11},{9,10},{10,... | collective-permute-start | bytes 270344 | tf_op jit(solution)/shard_map/ppermute | solution.py:39
  127.5 10.2 %collective-permute-start.30 = (bf16[32,1408]{1,0:T(8,128)(2,1)S(1)}, bf16[32,1408]{1,0:T(8,128)(2,1)S(1)}, u32[]{:S(2)}, u32[]{:S(2)}) collective-permute-start(bf16[32,1408]{1,0:T(8,128)(2,1)S(1)} %get-tuple-element.188), channel_id=1, source_target_pairs={{0,2},{1,3},{2,0},{3,1},{4,6},{5,7},{6,4},{7,5},{8,10},{9,11},{10,... | collective-permute-start | bytes 270344 | tf_op jit(solution)/shard_map/ppermute | solution.py:39
  130.4 7.3 %collective-permute-start.29 = (bf16[32,1408]{1,0:T(8,128)(2,1)S(1)}, bf16[32,1408]{1,0:T(8,128)(2,1)S(1)}, u32[]{:S(2)}, u32[]{:S(2)}) collective-permute-start(bf16[32,1408]{1,0:T(8,128)(2,1)S(1)} %get-tuple-element.187), channel_id=1, source_target_pairs={{0,1},{1,0},{2,3},{3,2},{4,5},{5,4},{6,7},{7,6},{8,9},{9,8},{10,11... | collective-permute-start | bytes 270344 | tf_op jit(solution)/shard_map/ppermute | solution.py:39
  133.5 9.8 %collective-permute-start.25 = (bf16[128,896]{1,0:T(8,128)(2,1)S(1)}, bf16[128,896]{1,0:T(8,128)(2,1)S(1)}, u32[]{:S(2)}, u32[]{:S(2)}) collective-permute-start(bf16[128,896]{1,0:T(8,128)(2,1)S(1)} %get-tuple-element.112), channel_id=1, source_target_pairs={{0,192},{1,193},{2,194},{3,195},{4,28},{5,29},{6,30},{7,31},{8,200... | collective-permute-start | bytes 688136 | tf_op jit(solution)/shard_map/ppermute | solution.py:43
  135.2 8.1 %collective-permute-start.24 = (bf16[128,896]{1,0:T(8,128)(2,1)S(1)}, bf16[128,896]{1,0:T(8,128)(2,1)S(1)}, u32[]{:S(2)}, u32[]{:S(2)}) collective-permute-start(bf16[128,896]{1,0:T(8,128)(2,1)S(1)} %get-tuple-element.113), channel_id=1, source_target_pairs={{0,128},{1,129},{2,130},{3,131},{4,20},{5,21},{6,22},{7,23},{8,136... | collective-permute-start | bytes 688136 | tf_op jit(solution)/shard_map/ppermute | solution.py:43
  135.2 9.0 %collective-permute-start.23 = (bf16[128,896]{1,0:T(8,128)(2,1)S(1)}, bf16[128,896]{1,0:T(8,128)(2,1)S(1)}, u32[]{:S(2)}, u32[]{:S(2)}) collective-permute-start(bf16[128,896]{1,0:T(8,128)(2,1)S(1)} %get-tuple-element.111), channel_id=1, source_target_pairs={{0,64},{1,65},{2,66},{3,67},{4,12},{5,13},{6,14},{7,15},{8,72},{9,... | collective-permute-start | bytes 688136 | tf_op jit(solution)/shard_map/ppermute | solution.py:43
  144.3 18.7 %collective-permute-start.32 = (bf16[192,2048]{1,0:T(8,128)(2,1)S(1)}, bf16[192,2048]{1,0:T(8,128)(2,1)S(1)}, u32[]{:S(2)}, u32[]{:S(2)}) collective-permute-start(bf16[192,2048]{1,0:T(8,128)(2,1)S(1)} %pad_maximum_fusion.2.refs_4_), channel_id=1, source_target_pairs={{0,64},{1,65},{2,66},{3,67},{4,12},{5,13},{6,14},{7,15},{8,72},{9,... | collective-permute-start | bytes 2359304 | tf_op jit(solution)/shard_map/ppermute | solution.py:43
  144.4 27.3 %collective-permute-start.39 = (bf16[192,2048]{1,0:T(8,128)(2,1)S(1)}, bf16[192,2048]{1,0:T(8,128)(2,1)}, u32[]{:S(2)}, u32[]{:S(2)}) collective-permute-start(bf16[192,2048]{1,0:T(8,128)(2,1)S(1)} %pad_maximum_fusion.2.refs_4_), channel_id=1, source_target_pairs={{0,128},{1,129},{2,130},{3,131},{4,20},{5,21},{6,22},{7,23},{8,136... | collective-permute-start | bytes 2359304 | tf_op jit(solution)/shard_map/ppermute | solution.py:43
  147.5 24.3 %collective-permute-start.40 = (bf16[192,2048]{1,0:T(8,128)(2,1)S(1)}, bf16[192,2048]{1,0:T(8,128)(2,1)}, u32[]{:S(2)}, u32[]{:S(2)}) collective-permute-start(bf16[192,2048]{1,0:T(8,128)(2,1)S(1)} %pad_maximum_fusion.2.refs_4_), channel_id=1, source_target_pairs={{0,192},{1,193},{2,194},{3,195},{4,28},{5,29},{6,30},{7,31},{8,200... | collective-permute-start | bytes 2359304 | tf_op jit(solution)/shard_map/ppermute | solution.py:43
  149.2 13.7 %collective-permute-start.35 = (bf16[32,1280]{1,0:T(8,128)(2,1)S(1)}, bf16[32,1280]{1,0:T(8,128)(2,1)S(1)}, u32[]{:S(2)}, u32[]{:S(2)}) collective-permute-start(bf16[32,1280]{1,0:T(8,128)(2,1)S(1)} %constant_dynamic-update-slice_fusion.33), channel_id=1, source_target_pairs={{0,3},{1,2},{2,1},{3,0},{4,7},{5,6},{6,5},{7,4},{8,11},{9,10},{10,... | collective-permute-start | bytes 245768 | tf_op jit(solution)/shard_map/ppermute | solution.py:39
  (39 other events, 183.6 us)

commit v11 on v9

--- a/solution.py
+++ b/solution.py
@@ -41,15 +41,6 @@
 
 def move(value, where):
     return lax.ppermute(value, AXES, [(flat(*at), flat(*where(*at))) for at in every()])
-
-
-def along(value, e, first, second):
-    def target(*at):
-        at = list(at)
-        at[AXES.index((first, second)[at[3]])] ^= e
-        return at
-
-    return move(value, target)
 
 
 def tables():
@@ -114,20 +105,19 @@
     )(query_weight, kv_turned)
 
 
-def project_kernel(x_ref, *refs):
-    blocks, (out_ref, own_ref) = refs[:4], refs[4:]
+def project_kernel(x_ref, here_ref, there_ref, out_ref, own_ref):
     inputs = x_ref[...]
-    for slot in (0, 1):
+    for slot, ref in enumerate((here_ref, there_ref)):
         heads = [
-            jnp.concatenate([ref[slot, 256 * h : 256 * h + 256, :] for ref in blocks], axis=0) for h in range(3)
+            jnp.concatenate([ref[d, 256 * h : 256 * h + 256, :] for d in range(4)], axis=0) for h in range(3)
         ]
         q = jnp.dot(inputs, jnp.concatenate(heads, axis=1), preferred_element_type=F32)
         own_ref[:, 384 * slot : 384 * slot + 384] = q[:ROWS]
         for e in (1, 2, 3):
             out_ref[e - 1, :, 384 * slot : 384 * slot + 384] = q[ROWS * e : ROWS * e + ROWS].astype(BF)
     kv_rows = [
-        jnp.concatenate([ref[slot, 768 + 64 * h : 832 + 64 * h, :] for ref in blocks for h in (0, 1)], axis=1)
-        for slot in (0, 1)
+        jnp.concatenate([ref[d, 768 + 64 * h : 832 + 64 * h, :] for d in range(4) for h in (0, 1)], axis=1)
+        for ref in (here_ref, there_ref)
     ]
     kv = lax.dot_general(
         inputs, jnp.concatenate(kv_rows, axis=0), (((1,), (1,)), ((), ())), preferred_element_type=F32
@@ -137,15 +127,15 @@
         out_ref[e - 1, :, 768:] = kv[ROWS * e : ROWS * e + ROWS].astype(BF)
 
 
-def project(inputs, blocks):
+def project(inputs, here, there):
     return pl.pallas_call(
         project_kernel,
         out_shape=(jax.ShapeDtypeStruct((3, ROWS, 896), BF), jax.ShapeDtypeStruct((ROWS, 896), F32)),
-        in_specs=[whole(0)] * 5,
+        in_specs=[whole(0)] * 3,
         out_specs=(whole(0),) * 2,
         compiler_params=pltpu.CompilerParams(vmem_limit_bytes=32 * 2**20),
         cost_estimate=pl.CostEstimate(flops=2 * 512 * 1024 * 896, bytes_accessed=4000000, transcendentals=0),
-    )(inputs, *blocks)
+    )(inputs, here, there)
 
 
 def attend(query, keys, values, limit, first):
@@ -165,6 +155,7 @@
 
     packed = pack(query_weight, kv_weight.T)
     first = move(packed, lambda y, zh, x, c, t: ((2 * zh + c) ^ y, t & 1, x, t >> 1, y))
+    second = move(packed, lambda y, zh, x, c, t: ((2 * zh + c) ^ y, 1 - (t & 1), x, t >> 1, y))
     wo_other = swap(out_weight, "zh", 1)
 
     widened = tokens.astype(F32)
@@ -172,28 +163,27 @@
     gained = (widened * norm_gain[None, :]).astype(BF)
 
     def features(e):
-        picked = []
-        for d in range(4):
-            s = y ^ t ^ jnp.where(c == 0, e, d)
-            at = x ^ jnp.where(c == 0, d, e)
-            picked.append(lax.dynamic_slice(gained, (0, (((s >> 1) * 4 + at) * 2 + (s & 1)) * 256), (ROWS, 256)))
+        s = y ^ e ^ t
+        picked = [
+            lax.dynamic_slice(gained, (0, (((s >> 1) * 4 + (x ^ d)) * 2 + (s & 1)) * 256), (ROWS, 256))
+            for d in range(4)
+        ]
         return jnp.concatenate(picked, axis=1)
 
-    ring = [along(features(e), e, "y", "x") for e in (1, 2, 3)]
-    second = move(packed, lambda y, zh, x, c, t: ((2 * zh + c) ^ y, 1 - (t & 1), x, t >> 1, y))
+    ring = [swap(features(e), "y", e) for e in (1, 2, 3)]
     first, second, wo_other, *ring = lax.optimization_barrier((first, second, wo_other, *ring))
     inputs = jnp.concatenate([features(0)] + ring, axis=0)
 
     wo_piece = jnp.concatenate([out_weight, wo_other], axis=0)
     wo = lax.all_gather(wo_piece, ("y", "x", "core"), axis=0, tiled=True)
 
-    def gathered(pair):
-        return [pair] + [along(pair, d, "x", "y") for d in (1, 2, 3)]
-
-    def reduced(blocks):
-        sent, total = project(inputs, blocks)
+    def gathered(block):
+        return jnp.stack([block] + [swap(block, "x", d) for d in (1, 2, 3)])
+
+    def reduced(here, there):
+        sent, total = project(inputs, here, there)
         for e in (1, 2, 3):
-            total = total + along(sent[e - 1], e, "y", "x").astype(F32)
+            total = total + swap(sent[e - 1], "y", e).astype(F32)
         return total
 
     def over_zl(total, note):
@@ -218,11 +208,11 @@
     low = squares - high - middle
     note = jnp.pad(jnp.stack([high, middle, low]), ((0, 29), (0, 0))).astype(BF)
 
-    others = swap(jnp.stack([first, second]), "core", 1)
-    near_pair, far_pair = jnp.stack([first, others[0]]), jnp.stack([second, others[1]])
-    far_pair, *blocks = lax.optimization_barrier((far_pair, *gathered(near_pair)))
-    total, *blocks = lax.optimization_barrier((reduced(blocks), *gathered(far_pair)))
-    far_total, *near_sums = lax.optimization_barrier((reduced(blocks), *over_zl(total, [note])))
+    second, here = lax.optimization_barrier((second, gathered(first)))
+    total = reduced(here, swap(here, "core", 1))
+    here = gathered(second)
+    total, there = lax.optimization_barrier((total, swap(here, "core", 1)))
+    far_total, *near_sums = lax.optimization_barrier((reduced(here, there), *over_zl(total, [note])))
     far_sums = over_zl(far_total, [])
     scales = lax.rsqrt((squares + near_sums[2]) / D + 1e-05)
 

time: 170 us -> 180 us (1.059); the launches traced: 170 us -> 178 us
  waiting for transfers between devices: 78.7 us -> 86.2 us
  starting transfers between devices: 59.5 us -> 56.4 us
  Pallas kernels: 3.07 us -> 5.47 us
    ppermute x11 -> x27, waiting for transfers between devices: 10.8 us -> 72.2 us  [swap(): return lax.ppermute(value, axis, [(i, i ^ d) for i in range(n)])]
    ppermute x17 -> x2, waiting for transfers between devices: 67.9 us -> 14 us  [move(): lax.ppermute(value, AXES, [(flat(*at), flat(*where(*at))) for at in every...]
    ppermute x17 -> x2, starting transfers between devices: 40.4 us -> 10.2 us  [move(): lax.ppermute(value, AXES, [(flat(*at), flat(*where(*at))) for at in every...]
    ppermute x11 -> x27, starting transfers between devices: 19.1 us -> 46.2 us  [swap(): return lax.ppermute(value, axis, [(i, i ^ d) for i in range(n)])]
    pallas_call x2, Pallas kernels: 3.03 us -> 5.43 us  [project(): pl.pallas_call(project_kernel, out_shape=(jax.ShapeDtypeStruct((3, ROWS,...]
  transfers between devices with their start and end apart: 29 -> 30, of which waited for: 17 -> 16; matrix products, arithmetic and copies ran while one was open for 2% -> 3% of each run, Pallas kernels for 2% -> 3%
where the time goes in v11:
time: 180 us; the launch traced here: 178 us
  waiting for transfers between devices  86.2 us (48%)
  starting transfers between devices  56.4 us (31%)
  between operations  14.8 us (8%)
  matrix products  8.6 us (5%)
  Pallas kernels  5.47 us (3%)
  other arithmetic  4.27 us (2%)
  local copies, waits for them, and re-layouts  2.07 us (1%)
    ppermute x27, waiting for transfers between devices, swap(): return lax.ppermute(value, axis, [(i, i ^ d) for i in range(n)])  72.2 us
    ppermute x27, starting transfers between devices, swap(): return lax.ppermute(value, axis, [(i, i ^ d) for i in range(n)])  46.2 us
    ppermute x2, waiting for transfers between devices, move(): lax.ppermute(value, AXES, [(flat(*at), flat(*where(*at))) for at in every...  14 us
    ppermute x2, starting transfers between devices, move(): lax.ppermute(value, AXES, [(flat(*at), flat(*where(*at))) for at in every...  10.2 us
    dot_general x1, matrix products, body(): return jnp.dot(all_rows, wo, preferred_element_type=F32).astype(BF)  7.35 us
    pallas_call x2, Pallas kernels, project(): pl.pallas_call(project_kernel, out_shape=(jax.ShapeDtypeStruct((3, ROWS,...  5.43 us
  transfers between devices with their start and end apart: 30, of which 16 were waited for; matrix products, arithmetic and copies ran while one was open for 3% of the time, Pallas kernels for 3%

profile of v11, /device:TPU:24, one launch (start us, length us, event | category | flops | bytes accessed | tf_op | source)
XLA Modules:
  0.0 177.8 jit_solution(14415611856669298091)
XLA Ops:
  8.5 2.0 %collective-permute-start.5 = (bf16[128,1024]{1,0:T(8,128)(2,1)S(1)}, bf16[128,1024]{1,0:T(8,128)(2,1)S(1)}, u32[]{:S(2)}, u32[]{:S(2)}) collective-permute-start(bf16[128,1024]{1,0:T(8,128)(2,1)S(1)} %pad_maximum_fusion.6), channel_id=1, source_target_pairs={{0,192},{64,128},{128,64},{192,0},{1,193},{65,129},{129,65},{193,1... | collective-permute-start | bytes 786440 | tf_op jit(solution)/shard_map/ppermute | solution.py:39
  10.5 5.5 %collective-permute-start.2 = (bf16[24,4096]{1,0:T(8,128)(2,1)S(1)}, bf16[24,4096]{1,0:T(8,128)(2,1)S(1)}, u32[]{:S(2)}, u32[]{:S(2)}) collective-permute-start(bf16[24,4096]{1,0:T(8,128)(2,1)S(1)} %copy-done.2), channel_id=1, source_target_pairs={{0,32},{32,0},{1,33},{33,1},{2,34},{34,2},{3,35},{35,3},{4,36},{36... | collective-permute-start | bytes 589832 | tf_op jit(solution)/shard_map/ppermute | solution.py:39
  16.0 2.7 %collective-permute-start.4 = (bf16[128,1024]{1,0:T(8,128)(2,1)S(1)}, bf16[128,1024]{1,0:T(8,128)(2,1)S(1)}, u32[]{:S(2)}, u32[]{:S(2)}) collective-permute-start(bf16[128,1024]{1,0:T(8,128)(2,1)S(1)} %pad_maximum_fusion.5), channel_id=1, source_target_pairs={{0,128},{64,192},{128,0},{192,64},{1,129},{65,193},{129,1},{193,65... | collective-permute-start | bytes 786440 | tf_op jit(solution)/shard_map/ppermute | solution.py:39
  20.1 3.8 %collective-permute-start = (bf16[896,128]{1,0:T(8,128)(2,1)S(1)}, bf16[896,128]{1,0:T(8,128)(2,1)S(1)}, u32[]{:S(2)}, u32[]{:S(2)}) collective-permute-start(bf16[896,128]{1,0:T(8,128)(2,1)S(1)} %shard_map.118), channel_id=1, source_target_pairs={{0,0},{1,32},{2,4},{3,36},{4,64},{5,96},{6,68},{7,100},{8,8},{9,40... | collective-permute-start | bytes 688136 | tf_op jit(solution)/shard_map/ppermute | solution.py:43
  24.0 6.3 %collective-permute-start.1 = (bf16[896,128]{1,0:T(8,128)(2,1)S(1)}, bf16[896,128]{1,0:T(8,128)(2,1)S(1)}, u32[]{:S(2)}, u32[]{:S(2)}) collective-permute-start(bf16[896,128]{1,0:T(8,128)(2,1)S(1)} %shard_map.118), channel_id=1, source_target_pairs={{0,32},{1,0},{2,36},{3,4},{4,96},{5,64},{6,100},{7,68},{8,40},{9,8... | collective-permute-start | bytes 688136 | tf_op jit(solution)/shard_map/ppermute | solution.py:43
  30.3 6.2 %collective-permute-done = bf16[896,128]{1,0:T(8,128)(2,1)S(1)} collective-permute-done((bf16[896,128]{1,0:T(8,128)(2,1)S(1)}, bf16[896,128]{1,0:T(8,128)(2,1)S(1)}, u32[]{:S(2)}, u32[]{:S(2)}) %collective-permute-start) | collective-permute-done | bytes 229408 | tf_op jit(solution)/shard_map/ppermute | solution.py:43
  36.6 7.8 %collective-permute-done.1 = bf16[896,128]{1,0:T(8,128)(2,1)S(1)} collective-permute-done((bf16[896,128]{1,0:T(8,128)(2,1)S(1)}, bf16[896,128]{1,0:T(8,128)(2,1)S(1)}, u32[]{:S(2)}, u32[]{:S(2)}) %collective-permute-start.1) | collective-permute-done | bytes 229408 | tf_op jit(solution)/shard_map/ppermute | solution.py:43
  46.8 2.7 %collective-permute-start.7 = (bf16[896,128]{1,0:T(8,128)(2,1)S(1)}, bf16[896,128]{1,0:T(8,128)(2,1)S(1)}, u32[]{:S(2)}, u32[]{:S(2)}) collective-permute-start(bf16[896,128]{1,0:T(8,128)(2,1)S(1)} %collective-permute-done), channel_id=1, source_target_pairs={{0,16},{8,24},{16,0},{24,8},{1,17},{9,25},{17,1},{25,9},{2,18},{10... | collective-permute-start | bytes 688136 | tf_op jit(solution)/shard_map/ppermute | solution.py:39
  50.0 3.8 %collective-permute-done.6 = bf16[896,128]{1,0:T(8,128)(2,1)S(1)} collective-permute-done((bf16[896,128]{1,0:T(8,128)(2,1)S(1)}, bf16[896,128]{1,0:T(8,128)(2,1)S(1)}, u32[]{:S(2)}, u32[]{:S(2)}) %collective-permute-start.6) | collective-permute-done | bytes 229408 | tf_op jit(solution)/shard_map/ppermute | solution.py:39
  53.7 6.4 %collective-permute-done.7 = bf16[896,128]{1,0:T(8,128)(2,1)S(1)} collective-permute-done((bf16[896,128]{1,0:T(8,128)(2,1)S(1)}, bf16[896,128]{1,0:T(8,128)(2,1)S(1)}, u32[]{:S(2)}, u32[]{:S(2)}) %collective-permute-start.7) | collective-permute-done | bytes 229408 | tf_op jit(solution)/shard_map/ppermute | solution.py:39
  60.1 2.6 %collective-permute-done.8 = bf16[896,128]{1,0:T(8,128)(2,1)S(1)} collective-permute-done((bf16[896,128]{1,0:T(8,128)(2,1)S(1)}, bf16[896,128]{1,0:T(8,128)(2,1)S(1)}, u32[]{:S(2)}, u32[]{:S(2)}) %collective-permute-start.8) | collective-permute-done | bytes 229408 | tf_op jit(solution)/shard_map/ppermute | solution.py:39
  63.7 1.9 %collective-permute-start.10 = (bf16[896,128]{1,0:T(8,128)(2,1)S(1)}, bf16[896,128]{1,0:T(8,128)(2,1)S(1)}, u32[]{:S(2)}, u32[]{:S(2)}) collective-permute-start(bf16[896,128]{1,0:T(8,128)(2,1)S(1)} %collective-permute-done.1), channel_id=1, source_target_pairs={{0,16},{8,24},{16,0},{24,8},{1,17},{9,25},{17,1},{25,9},{2,18},{10... | collective-permute-start | bytes 688136 | tf_op jit(solution)/shard_map/ppermute | solution.py:39
  65.7 2.8 %collective-permute-start.11 = (bf16[896,128]{1,0:T(8,128)(2,1)S(1)}, bf16[896,128]{1,0:T(8,128)(2,1)S(1)}, u32[]{:S(2)}, u32[]{:S(2)}) collective-permute-start(bf16[896,128]{1,0:T(8,128)(2,1)S(1)} %collective-permute-done.1), channel_id=1, source_target_pairs={{0,24},{8,16},{16,8},{24,0},{1,25},{9,17},{17,9},{25,1},{2,26},{10... | collective-permute-start | bytes 688136 | tf_op jit(solution)/shard_map/ppermute | solution.py:39
  68.5 7.4 %collective-permute-done.9 = bf16[896,128]{1,0:T(8,128)(2,1)S(1)} collective-permute-done((bf16[896,128]{1,0:T(8,128)(2,1)S(1)}, bf16[896,128]{1,0:T(8,128)(2,1)S(1)}, u32[]{:S(2)}, u32[]{:S(2)}) %collective-permute-start.9) | collective-permute-done | bytes 229408 | tf_op jit(solution)/shard_map/ppermute | solution.py:39
  75.9 5.7 %collective-permute-done.10 = bf16[896,128]{1,0:T(8,128)(2,1)S(1)} collective-permute-done((bf16[896,128]{1,0:T(8,128)(2,1)S(1)}, bf16[896,128]{1,0:T(8,128)(2,1)S(1)}, u32[]{:S(2)}, u32[]{:S(2)}) %collective-permute-start.10) | collective-permute-done | bytes 229408 | tf_op jit(solution)/shard_map/ppermute | solution.py:39
  82.5 2.7 %shard_map.119 = (bf16[3,128,896]{2,1,0:T(8,128)(2,1)S(1)}, f32[128,896]{1,0:T(8,128)S(1)}) custom-call(bf16[512,1024]{1,0:T(8,128)(2,1)S(1)} %pad_maximum_fusion.x_ref, bf16[4,896,128]{2,1,0:T(8,128)(2,1)S(1)} %pad_maximum_fusion.1.here_ref, bf16[4,896,128]{2,1,0:T(8,128)(2,1)} %collective-permute-done.12.there_ref), custom_call_target="tpu_custom_call" | custom-call | flops 939524096 | bytes 4000000 | tf_op jit(solution)/shard_map/pallas_call | solution.py:131
  86.8 6.0 %collective-permute-start.14 = (bf16[128,896]{1,0:T(8,128)(2,1)}, bf16[128,896]{1,0:T(8,128)(2,1)S(1)}, u32[]{:S(2)}, u32[]{:S(2)}) collective-permute-start(bf16[128,896]{1,0:T(8,128)(2,1)} %get-tuple-element.64), channel_id=1, source_target_pairs={{0,128},{64,192},{128,0},{192,64},{1,129},{65,193},{129,1},{193,65... | collective-permute-start | bytes 688136 | tf_op jit(solution)/shard_map/ppermute | solution.py:39
  92.9 2.0 %collective-permute-done.13 = bf16[128,896]{1,0:T(8,128)(2,1)S(1)} collective-permute-done((bf16[128,896]{1,0:T(8,128)(2,1)}, bf16[128,896]{1,0:T(8,128)(2,1)S(1)}, u32[]{:S(2)}, u32[]{:S(2)}) %collective-permute-start.13) | collective-permute-done | bytes 229408 | tf_op jit(solution)/shard_map/ppermute | solution.py:39
  94.9 18.5 %collective-permute-done.14 = bf16[128,896]{1,0:T(8,128)(2,1)S(1)} collective-permute-done((bf16[128,896]{1,0:T(8,128)(2,1)}, bf16[128,896]{1,0:T(8,128)(2,1)S(1)}, u32[]{:S(2)}, u32[]{:S(2)}) %collective-permute-start.14) | collective-permute-done | bytes 229408 | tf_op jit(solution)/shard_map/ppermute | solution.py:39
  115.0 3.2 %collective-permute-start.22 = (bf16[32,1408]{1,0:T(8,128)(2,1)S(1)}, bf16[32,1408]{1,0:T(8,128)(2,1)S(1)}, u32[]{:S(2)}, u32[]{:S(2)}) collective-permute-start(bf16[32,1408]{1,0:T(8,128)(2,1)S(1)} %get-tuple-element.134), channel_id=1, source_target_pairs={{0,3},{1,2},{2,1},{3,0},{4,7},{5,6},{6,5},{7,4},{8,11},{9,10},{10,... | collective-permute-start | bytes 270344 | tf_op jit(solution)/shard_map/ppermute | solution.py:39
  118.2 2.7 %shard_map.120 = (bf16[3,128,896]{2,1,0:T(8,128)(2,1)S(1)}, f32[128,896]{1,0:T(8,128)S(1)}) custom-call(bf16[512,1024]{1,0:T(8,128)(2,1)S(1)} %pad_maximum_fusion.x_ref, bf16[4,896,128]{2,1,0:T(8,128)(2,1)S(1)} %pad_maximum_fusion.2.here_ref, bf16[4,896,128]{2,1,0:T(8,128)(2,1)} %collective-permute-done.16.there_ref), custom_call_target="tpu_custom_call" | custom-call | flops 939524096 | bytes 4000000 | tf_op jit(solution)/shard_map/pallas_call | solution.py:131
  121.1 4.3 %collective-permute-start.18 = (bf16[128,896]{1,0:T(8,128)(2,1)S(1)}, bf16[128,896]{1,0:T(8,128)(2,1)S(1)}, u32[]{:S(2)}, u32[]{:S(2)}) collective-permute-start(bf16[128,896]{1,0:T(8,128)(2,1)S(1)} %get-tuple-element.61), channel_id=1, source_target_pairs={{0,128},{64,192},{128,0},{192,64},{1,129},{65,193},{129,1},{193,65... | collective-permute-start | bytes 688136 | tf_op jit(solution)/shard_map/ppermute | solution.py:39
  126.0 4.9 %collective-permute-done.17 = bf16[128,896]{1,0:T(8,128)(2,1)S(1)} collective-permute-done((bf16[128,896]{1,0:T(8,128)(2,1)S(1)}, bf16[128,896]{1,0:T(8,128)(2,1)S(1)}, u32[]{:S(2)}, u32[]{:S(2)}) %collective-permute-start.17) | collective-permute-done | bytes 229408 | tf_op jit(solution)/shard_map/ppermute | solution.py:39
  130.9 8.1 %collective-permute-done.18 = bf16[128,896]{1,0:T(8,128)(2,1)S(1)} collective-permute-done((bf16[128,896]{1,0:T(8,128)(2,1)S(1)}, bf16[128,896]{1,0:T(8,128)(2,1)S(1)}, u32[]{:S(2)}, u32[]{:S(2)}) %collective-permute-start.18) | collective-permute-done | bytes 229408 | tf_op jit(solution)/shard_map/ppermute | solution.py:39
  139.3 3.5 %collective-permute-start.25 = (bf16[32,1280]{1,0:T(8,128)(2,1)S(1)}, bf16[32,1280]{1,0:T(8,128)(2,1)S(1)}, u32[]{:S(2)}, u32[]{:S(2)}) collective-permute-start(bf16[32,1280]{1,0:T(8,128)(2,1)S(1)} %constant_dynamic-update-slice_fusion.28), channel_id=1, source_target_pairs={{0,3},{1,2},{2,1},{3,0},{4,7},{5,6},{6,5},{7,4},{8,11},{9,10},{10,... | collective-permute-start | bytes 245768 | tf_op jit(solution)/shard_map/ppermute | solution.py:39
  143.8 2.3 %collective-permute-done.25 = bf16[32,1280]{1,0:T(8,128)(2,1)S(1)} collective-permute-done((bf16[32,1280]{1,0:T(8,128)(2,1)S(1)}, bf16[32,1280]{1,0:T(8,128)(2,1)S(1)}, u32[]{:S(2)}, u32[]{:S(2)}) %collective-permute-start.25) | collective-permute-done | bytes 81952 | tf_op jit(solution)/shard_map/ppermute | solution.py:39
  146.1 3.4 %collective-permute-done.24 = bf16[32,1280]{1,0:T(8,128)(2,1)S(1)} collective-permute-done((bf16[32,1280]{1,0:T(8,128)(2,1)S(1)}, bf16[32,1280]{1,0:T(8,128)(2,1)S(1)}, u32[]{:S(2)}, u32[]{:S(2)}) %collective-permute-start.24) | collective-permute-done | bytes 81952 | tf_op jit(solution)/shard_map/ppermute | solution.py:39
  152.4 2.7 %collective-permute-start.26 = (bf16[32,1536]{1,0:T(8,128)(2,1)S(1)}, bf16[32,1536]{1,0:T(8,128)(2,1)S(1)}, u32[]{:S(2)}, u32[]{:S(2)}) collective-permute-start(bf16[32,1536]{1,0:T(8,128)(2,1)S(1)} %pad_maximum_fusion.7), channel_id=1, source_target_pairs={{0,3},{1,2},{2,1},{3,0},{4,7},{5,6},{6,5},{7,4},{8,11},{9,10},{10,... | collective-permute-start | bytes 294920 | tf_op jit(solution)/shard_map/ppermute | solution.py:39
  155.2 1.7 collective-permute-start.28
  156.9 3.1 %collective-permute-done.26 = bf16[32,1536]{1,0:T(8,128)(2,1)S(1)} collective-permute-done((bf16[32,1536]{1,0:T(8,128)(2,1)S(1)}, bf16[32,1536]{1,0:T(8,128)(2,1)S(1)}, u32[]{:S(2)}, u32[]{:S(2)}) %collective-permute-start.26) | collective-permute-done | bytes 98336 | tf_op jit(solution)/shard_map/ppermute | solution.py:39
  160.1 3.4 %collective-permute-done.27 = bf16[32,1536]{1,0:T(8,128)(2,1)S(1)} collective-permute-done((bf16[32,1536]{1,0:T(8,128)(2,1)S(1)}, bf16[32,1536]{1,0:T(8,128)(2,1)S(1)}, u32[]{:S(2)}, u32[]{:S(2)}) %collective-permute-start.27) | collective-permute-done | bytes 98336 | tf_op jit(solution)/shard_map/ppermute | solution.py:39
  163.6 7.4 %convolution_convert_fusion = bf16[128,4096]{1,0:T(8,128)(2,1)} fusion(bf16[1536,4096]{1,0:T(8,128)(2,1)} %all-gather.2.cloned.1.call-done, bf16[32,1536]{1,0:T(8,128)(2,1)S(1)} %broadcast_select_fusion.4, bf16[32,1536]{1,0:T(8,128)(2,1)S(1)} %get-tuple-element.73, bf16[32,1536]{1,0:T(8,128)(2,1)S(1)} %get-tuple-element.72, ...), kind=kOutput, calls=%fused_computation.1 | convolution fusion | flops 1612709888 | bytes 14024704 | tf_op jit(solution)/shard_map/dot_general | solution.py:243
  (133 shorter events, 15.5 us)
Async XLA Ops:
  6.5 157.1 %all-gather.2.cloned.1.call-start = ((), (), s32[]{:S(2)}) async-start(), calls=%async_computation | async-start | bytes 12976128 | tf_op jit(solution)/shard_map/all_gather | solution.py:178
  8.5 35.9 %collective-permute-start.5 = (bf16[128,1024]{1,0:T(8,128)(2,1)S(1)}, bf16[128,1024]{1,0:T(8,128)(2,1)S(1)}, u32[]{:S(2)}, u32[]{:S(2)}) collective-permute-start(bf16[128,1024]{1,0:T(8,128)(2,1)S(1)} %pad_maximum_fusion.6), channel_id=1, source_target_pairs={{0,192},{64,128},{128,64},{192,0},{1,193},{65,129},{129,65},{193,1... | collective-permute-start | bytes 786440 | tf_op jit(solution)/shard_map/ppermute | solution.py:39
  10.5 13.5 %collective-permute-start.2 = (bf16[24,4096]{1,0:T(8,128)(2,1)S(1)}, bf16[24,4096]{1,0:T(8,128)(2,1)S(1)}, u32[]{:S(2)}, u32[]{:S(2)}) collective-permute-start(bf16[24,4096]{1,0:T(8,128)(2,1)S(1)} %copy-done.2), channel_id=1, source_target_pairs={{0,32},{32,0},{1,33},{33,1},{2,34},{34,2},{3,35},{35,3},{4,36},{36... | collective-permute-start | bytes 589832 | tf_op jit(solution)/shard_map/ppermute | solution.py:39
  16.0 47.6 %copy-start.3 = (f32[128,128]{1,0:T(8,128)S(1)}, f32[128,128]{1,0:T(8,128)}, u32[]{:S(2)}) copy-start(f32[128,128]{1,0:T(8,128)} %constant.76.clone) | copy-start | bytes 196612
  16.0 47.6 %copy-start.4 = (f32[128,128]{1,0:T(8,128)S(1)}, f32[128,128]{1,0:T(8,128)}, u32[]{:S(2)}) copy-start(f32[128,128]{1,0:T(8,128)} %constant.77.clone) | copy-start | bytes 196612
  16.0 28.4 %collective-permute-start.4 = (bf16[128,1024]{1,0:T(8,128)(2,1)S(1)}, bf16[128,1024]{1,0:T(8,128)(2,1)S(1)}, u32[]{:S(2)}, u32[]{:S(2)}) collective-permute-start(bf16[128,1024]{1,0:T(8,128)(2,1)S(1)} %pad_maximum_fusion.5), channel_id=1, source_target_pairs={{0,128},{64,192},{128,0},{192,64},{1,129},{65,193},{129,1},{193,65... | collective-permute-start | bytes 786440 | tf_op jit(solution)/shard_map/ppermute | solution.py:39
  18.7 25.7 %collective-permute-start.3 = (bf16[128,1024]{1,0:T(8,128)(2,1)S(1)}, bf16[128,1024]{1,0:T(8,128)(2,1)S(1)}, u32[]{:S(2)}, u32[]{:S(2)}) collective-permute-start(bf16[128,1024]{1,0:T(8,128)(2,1)S(1)} %pad_maximum_fusion.4), channel_id=1, source_target_pairs={{0,64},{64,0},{128,192},{192,128},{1,65},{65,1},{129,193},{193,129... | collective-permute-start | bytes 786440 | tf_op jit(solution)/shard_map/ppermute | solution.py:39
  20.1 16.4 %collective-permute-start = (bf16[896,128]{1,0:T(8,128)(2,1)S(1)}, bf16[896,128]{1,0:T(8,128)(2,1)S(1)}, u32[]{:S(2)}, u32[]{:S(2)}) collective-permute-start(bf16[896,128]{1,0:T(8,128)(2,1)S(1)} %shard_map.118), channel_id=1, source_target_pairs={{0,0},{1,32},{2,4},{3,36},{4,64},{5,96},{6,68},{7,100},{8,8},{9,40... | collective-permute-start | bytes 688136 | tf_op jit(solution)/shard_map/ppermute | solution.py:43
  24.0 20.4 %collective-permute-start.1 = (bf16[896,128]{1,0:T(8,128)(2,1)S(1)}, bf16[896,128]{1,0:T(8,128)(2,1)S(1)}, u32[]{:S(2)}, u32[]{:S(2)}) collective-permute-start(bf16[896,128]{1,0:T(8,128)(2,1)S(1)} %shard_map.118), channel_id=1, source_target_pairs={{0,32},{1,0},{2,36},{3,4},{4,96},{5,64},{6,100},{7,68},{8,40},{9,8... | collective-permute-start | bytes 688136 | tf_op jit(solution)/shard_map/ppermute | solution.py:43
  45.2 8.5 %collective-permute-start.6 = (bf16[896,128]{1,0:T(8,128)(2,1)S(1)}, bf16[896,128]{1,0:T(8,128)(2,1)S(1)}, u32[]{:S(2)}, u32[]{:S(2)}) collective-permute-start(bf16[896,128]{1,0:T(8,128)(2,1)S(1)} %collective-permute-done), channel_id=1, source_target_pairs={{0,8},{8,0},{16,24},{24,16},{1,9},{9,1},{17,25},{25,17},{2,10},{10... | collective-permute-start | bytes 688136 | tf_op jit(solution)/shard_map/ppermute | solution.py:39
  46.8 13.4 %collective-permute-start.7 = (bf16[896,128]{1,0:T(8,128)(2,1)S(1)}, bf16[896,128]{1,0:T(8,128)(2,1)S(1)}, u32[]{:S(2)}, u32[]{:S(2)}) collective-permute-start(bf16[896,128]{1,0:T(8,128)(2,1)S(1)} %collective-permute-done), channel_id=1, source_target_pairs={{0,16},{8,24},{16,0},{24,8},{1,17},{9,25},{17,1},{25,9},{2,18},{10... | collective-permute-start | bytes 688136 | tf_op jit(solution)/shard_map/ppermute | solution.py:39
  49.5 13.2 %collective-permute-start.8 = (bf16[896,128]{1,0:T(8,128)(2,1)S(1)}, bf16[896,128]{1,0:T(8,128)(2,1)S(1)}, u32[]{:S(2)}, u32[]{:S(2)}) collective-permute-start(bf16[896,128]{1,0:T(8,128)(2,1)S(1)} %collective-permute-done), channel_id=1, source_target_pairs={{0,24},{8,16},{16,8},{24,0},{1,25},{9,17},{17,9},{25,1},{2,26},{10... | collective-permute-start | bytes 688136 | tf_op jit(solution)/shard_map/ppermute | solution.py:39
  62.8 19.7 %collective-permute-start.12 = (bf16[4,896,128]{2,1,0:T(8,128)(2,1)S(1)}, bf16[4,896,128]{2,1,0:T(8,128)(2,1)}, u32[]{:S(2)}, u32[]{:S(2)}) collective-permute-start(bf16[4,896,128]{2,1,0:T(8,128)(2,1)S(1)} %pad_maximum_fusion.1.here_ref), channel_id=1, source_target_pairs={{0,4},{4,0},{1,5},{5,1},{2,6},{6,2},{3,7},{7,3},{8,12},{12,8},{9,1... | collective-permute-start | bytes 2752520 | tf_op jit(solution)/shard_map/ppermute | solution.py:39
  63.6 12.2 %collective-permute-start.9 = (bf16[896,128]{1,0:T(8,128)(2,1)S(1)}, bf16[896,128]{1,0:T(8,128)(2,1)S(1)}, u32[]{:S(2)}, u32[]{:S(2)}) collective-permute-start(bf16[896,128]{1,0:T(8,128)(2,1)S(1)} %collective-permute-done.1), channel_id=1, source_target_pairs={{0,8},{8,0},{16,24},{24,16},{1,9},{9,1},{17,25},{25,17},{2,10},{10... | collective-permute-start | bytes 688136 | tf_op jit(solution)/shard_map/ppermute | solution.py:39
  63.7 17.9 %collective-permute-start.10 = (bf16[896,128]{1,0:T(8,128)(2,1)S(1)}, bf16[896,128]{1,0:T(8,128)(2,1)S(1)}, u32[]{:S(2)}, u32[]{:S(2)}) collective-permute-start(bf16[896,128]{1,0:T(8,128)(2,1)S(1)} %collective-permute-done.1), channel_id=1, source_target_pairs={{0,16},{8,24},{16,0},{24,8},{1,17},{9,25},{17,1},{25,9},{2,18},{10... | collective-permute-start | bytes 688136 | tf_op jit(solution)/shard_map/ppermute | solution.py:39
  65.7 16.6 %collective-permute-start.11 = (bf16[896,128]{1,0:T(8,128)(2,1)S(1)}, bf16[896,128]{1,0:T(8,128)(2,1)S(1)}, u32[]{:S(2)}, u32[]{:S(2)}) collective-permute-start(bf16[896,128]{1,0:T(8,128)(2,1)S(1)} %collective-permute-done.1), channel_id=1, source_target_pairs={{0,24},{8,16},{16,8},{24,0},{1,25},{9,17},{17,9},{25,1},{2,26},{10... | collective-permute-start | bytes 688136 | tf_op jit(solution)/shard_map/ppermute | solution.py:39
  82.4 31.1 %collective-permute-start.16 = (bf16[4,896,128]{2,1,0:T(8,128)(2,1)S(1)}, bf16[4,896,128]{2,1,0:T(8,128)(2,1)}, u32[]{:S(2)}, u32[]{:S(2)}) collective-permute-start(bf16[4,896,128]{2,1,0:T(8,128)(2,1)S(1)} %pad_maximum_fusion.2.here_ref), channel_id=1, source_target_pairs={{0,4},{4,0},{1,5},{5,1},{2,6},{6,2},{3,7},{7,3},{8,12},{12,8},{9,1... | collective-permute-start | bytes 2752520 | tf_op jit(solution)/shard_map/ppermute | solution.py:39
  86.0 8.9 %collective-permute-start.13 = (bf16[128,896]{1,0:T(8,128)(2,1)}, bf16[128,896]{1,0:T(8,128)(2,1)S(1)}, u32[]{:S(2)}, u32[]{:S(2)}) collective-permute-start(bf16[128,896]{1,0:T(8,128)(2,1)} %get-tuple-element.62), channel_id=1, source_target_pairs={{0,64},{64,0},{128,192},{192,128},{1,65},{65,1},{129,193},{193,129... | collective-permute-start | bytes 688136 | tf_op jit(solution)/shard_map/ppermute | solution.py:39
  86.8 26.6 %collective-permute-start.14 = (bf16[128,896]{1,0:T(8,128)(2,1)}, bf16[128,896]{1,0:T(8,128)(2,1)S(1)}, u32[]{:S(2)}, u32[]{:S(2)}) collective-permute-start(bf16[128,896]{1,0:T(8,128)(2,1)} %get-tuple-element.64), channel_id=1, source_target_pairs={{0,128},{64,192},{128,0},{192,64},{1,129},{65,193},{129,1},{193,65... | collective-permute-start | bytes 688136 | tf_op jit(solution)/shard_map/ppermute | solution.py:39
  92.8 20.6 %collective-permute-start.15 = (bf16[128,896]{1,0:T(8,128)(2,1)S(1)}, bf16[128,896]{1,0:T(8,128)(2,1)S(1)}, u32[]{:S(2)}, u32[]{:S(2)}) collective-permute-start(bf16[128,896]{1,0:T(8,128)(2,1)S(1)} %get-tuple-element.63), channel_id=1, source_target_pairs={{0,192},{64,128},{128,64},{192,0},{1,193},{65,129},{129,65},{193,1... | collective-permute-start | bytes 688136 | tf_op jit(solution)/shard_map/ppermute | solution.py:39
  113.7 11.7 %collective-permute-start.20 = (bf16[32,1408]{1,0:T(8,128)(2,1)S(1)}, bf16[32,1408]{1,0:T(8,128)(2,1)S(1)}, u32[]{:S(2)}, u32[]{:S(2)}) collective-permute-start(bf16[32,1408]{1,0:T(8,128)(2,1)S(1)} %get-tuple-element.132), channel_id=1, source_target_pairs={{0,1},{1,0},{2,3},{3,2},{4,5},{5,4},{6,7},{7,6},{8,9},{9,8},{10,11... | collective-permute-start | bytes 270344 | tf_op jit(solution)/shard_map/ppermute | solution.py:39
  113.8 12.0 %collective-permute-start.21 = (bf16[32,1408]{1,0:T(8,128)(2,1)S(1)}, bf16[32,1408]{1,0:T(8,128)(2,1)S(1)}, u32[]{:S(2)}, u32[]{:S(2)}) collective-permute-start(bf16[32,1408]{1,0:T(8,128)(2,1)S(1)} %get-tuple-element.133), channel_id=1, source_target_pairs={{0,2},{1,3},{2,0},{3,1},{4,6},{5,7},{6,4},{7,5},{8,10},{9,11},{10,... | collective-permute-start | bytes 270344 | tf_op jit(solution)/shard_map/ppermute | solution.py:39
  115.0 10.8 %collective-permute-start.22 = (bf16[32,1408]{1,0:T(8,128)(2,1)S(1)}, bf16[32,1408]{1,0:T(8,128)(2,1)S(1)}, u32[]{:S(2)}, u32[]{:S(2)}) collective-permute-start(bf16[32,1408]{1,0:T(8,128)(2,1)S(1)} %get-tuple-element.134), channel_id=1, source_target_pairs={{0,3},{1,2},{2,1},{3,0},{4,7},{5,6},{6,5},{7,4},{8,11},{9,10},{10,... | collective-permute-start | bytes 270344 | tf_op jit(solution)/shard_map/ppermute | solution.py:39
  121.0 9.9 %collective-permute-start.17 = (bf16[128,896]{1,0:T(8,128)(2,1)S(1)}, bf16[128,896]{1,0:T(8,128)(2,1)S(1)}, u32[]{:S(2)}, u32[]{:S(2)}) collective-permute-start(bf16[128,896]{1,0:T(8,128)(2,1)S(1)} %get-tuple-element.59), channel_id=1, source_target_pairs={{0,64},{64,0},{128,192},{192,128},{1,65},{65,1},{129,193},{193,129... | collective-permute-start | bytes 688136 | tf_op jit(solution)/shard_map/ppermute | solution.py:39
  121.1 17.9 %collective-permute-start.18 = (bf16[128,896]{1,0:T(8,128)(2,1)S(1)}, bf16[128,896]{1,0:T(8,128)(2,1)S(1)}, u32[]{:S(2)}, u32[]{:S(2)}) collective-permute-start(bf16[128,896]{1,0:T(8,128)(2,1)S(1)} %get-tuple-element.61), channel_id=1, source_target_pairs={{0,128},{64,192},{128,0},{192,64},{1,129},{65,193},{129,1},{193,65... | collective-permute-start | bytes 688136 | tf_op jit(solution)/shard_map/ppermute | solution.py:39
  125.4 13.6 %collective-permute-start.19 = (bf16[128,896]{1,0:T(8,128)(2,1)S(1)}, bf16[128,896]{1,0:T(8,128)(2,1)S(1)}, u32[]{:S(2)}, u32[]{:S(2)}) collective-permute-start(bf16[128,896]{1,0:T(8,128)(2,1)S(1)} %get-tuple-element.60), channel_id=1, source_target_pairs={{0,192},{64,128},{128,64},{192,0},{1,193},{65,129},{129,65},{193,1... | collective-permute-start | bytes 688136 | tf_op jit(solution)/shard_map/ppermute | solution.py:39
  139.3 6.9 %collective-permute-start.25 = (bf16[32,1280]{1,0:T(8,128)(2,1)S(1)}, bf16[32,1280]{1,0:T(8,128)(2,1)S(1)}, u32[]{:S(2)}, u32[]{:S(2)}) collective-permute-start(bf16[32,1280]{1,0:T(8,128)(2,1)S(1)} %constant_dynamic-update-slice_fusion.28), channel_id=1, source_target_pairs={{0,3},{1,2},{2,1},{3,0},{4,7},{5,6},{6,5},{7,4},{8,11},{9,10},{10,... | collective-permute-start | bytes 245768 | tf_op jit(solution)/shard_map/ppermute | solution.py:39
  142.7 6.8 %collective-permute-start.24 = (bf16[32,1280]{1,0:T(8,128)(2,1)S(1)}, bf16[32,1280]{1,0:T(8,128)(2,1)S(1)}, u32[]{:S(2)}, u32[]{:S(2)}) collective-permute-start(bf16[32,1280]{1,0:T(8,128)(2,1)S(1)} %get-tuple-element.125), channel_id=1, source_target_pairs={{0,2},{1,3},{2,0},{3,1},{4,6},{5,7},{6,4},{7,5},{8,10},{9,11},{10,... | collective-permute-start | bytes 245768 | tf_op jit(solution)/shard_map/ppermute | solution.py:39
  142.7 6.8 %collective-permute-start.23 = (bf16[32,1280]{1,0:T(8,128)(2,1)S(1)}, bf16[32,1280]{1,0:T(8,128)(2,1)S(1)}, u32[]{:S(2)}, u32[]{:S(2)}) collective-permute-start(bf16[32,1280]{1,0:T(8,128)(2,1)S(1)} %get-tuple-element.122), channel_id=1, source_target_pairs={{0,1},{1,0},{2,3},{3,2},{4,5},{5,4},{6,7},{7,6},{8,9},{9,8},{10,11... | collective-permute-start | bytes 245768 | tf_op jit(solution)/shard_map/ppermute | solution.py:39
  152.4 7.6 %collective-permute-start.26 = (bf16[32,1536]{1,0:T(8,128)(2,1)S(1)}, bf16[32,1536]{1,0:T(8,128)(2,1)S(1)}, u32[]{:S(2)}, u32[]{:S(2)}) collective-permute-start(bf16[32,1536]{1,0:T(8,128)(2,1)S(1)} %pad_maximum_fusion.7), channel_id=1, source_target_pairs={{0,3},{1,2},{2,1},{3,0},{4,7},{5,6},{6,5},{7,4},{8,11},{9,10},{10,... | collective-permute-start | bytes 294920 | tf_op jit(solution)/shard_map/ppermute | solution.py:39
  155.2 8.3 %collective-permute-start.27 = (bf16[32,1536]{1,0:T(8,128)(2,1)S(1)}, bf16[32,1536]{1,0:T(8,128)(2,1)S(1)}, u32[]{:S(2)}, u32[]{:S(2)}) collective-permute-start(bf16[32,1536]{1,0:T(8,128)(2,1)S(1)} %pad_maximum_fusion.7), channel_id=1, source_target_pairs={{0,2},{1,3},{2,0},{3,1},{4,6},{5,7},{6,4},{7,5},{8,10},{9,11},{10,... | collective-permute-start | bytes 294920 | tf_op jit(solution)/shard_map/ppermute | solution.py:39
  155.2 8.3 %collective-permute-start.28 = (bf16[32,1536]{1,0:T(8,128)(2,1)S(1)}, bf16[32,1536]{1,0:T(8,128)(2,1)S(1)}, u32[]{:S(2)}, u32[]{:S(2)}) collective-permute-start(bf16[32,1536]{1,0:T(8,128)(2,1)S(1)} %pad_maximum_fusion.7), channel_id=1, source_target_pairs={{0,1},{1,0},{2,3},{3,2},{4,5},{5,4},{6,7},{7,6},{8,9},{9,8},{10,11... | collective-permute-start | bytes 294920 | tf_op jit(solution)/shard_map/ppermute | solution.py:39
  (5 other events, 30.8 us)
Sparse Core Ops, SparseCore 0:
  45.3 90.3 all-gather.1

commit v12 on v8

--- a/solution.py
+++ b/solution.py
@@ -117,7 +117,7 @@
 def project_kernel(x_ref, *refs):
     blocks, (out_ref, own_ref) = refs[:4], refs[4:]
     inputs = x_ref[...]
-    for slot in (0, 1):
+    for slot in range(4):
         heads = [
             jnp.concatenate([ref[slot, 256 * h : 256 * h + 256, :] for ref in blocks], axis=0) for h in range(3)
         ]
@@ -127,24 +127,24 @@
             out_ref[e - 1, :, 384 * slot : 384 * slot + 384] = q[ROWS * e : ROWS * e + ROWS].astype(BF)
     kv_rows = [
         jnp.concatenate([ref[slot, 768 + 64 * h : 832 + 64 * h, :] for ref in blocks for h in (0, 1)], axis=1)
-        for slot in (0, 1)
+        for slot in range(4)
     ]
     kv = lax.dot_general(
         inputs, jnp.concatenate(kv_rows, axis=0), (((1,), (1,)), ((), ())), preferred_element_type=F32
     )
-    own_ref[:, 768:] = kv[:ROWS]
+    own_ref[:, 1536:] = kv[:ROWS]
     for e in (1, 2, 3):
-        out_ref[e - 1, :, 768:] = kv[ROWS * e : ROWS * e + ROWS].astype(BF)
+        out_ref[e - 1, :, 1536:] = kv[ROWS * e : ROWS * e + ROWS].astype(BF)
 
 
 def project(inputs, blocks):
     return pl.pallas_call(
         project_kernel,
-        out_shape=(jax.ShapeDtypeStruct((3, ROWS, 896), BF), jax.ShapeDtypeStruct((ROWS, 896), F32)),
+        out_shape=(jax.ShapeDtypeStruct((3, ROWS, 1792), BF), jax.ShapeDtypeStruct((ROWS, 1792), F32)),
         in_specs=[whole(0)] * 5,
         out_specs=(whole(0),) * 2,
         compiler_params=pltpu.CompilerParams(vmem_limit_bytes=32 * 2**20),
-        cost_estimate=pl.CostEstimate(flops=2 * 512 * 1024 * 896, bytes_accessed=4000000, transcendentals=0),
+        cost_estimate=pl.CostEstimate(flops=2 * 512 * 1024 * 1792, bytes_accessed=8000000, transcendentals=0),
     )(inputs, *blocks)
 
 
@@ -180,49 +180,41 @@
         return jnp.concatenate(picked, axis=1)
 
     ring = [along(features(e), e, "y", "x") for e in (1, 2, 3)]
-    first, packed, wo_other, *ring = lax.optimization_barrier((first, packed, wo_other, *ring))
     second = move(packed, lambda y, zh, x, c, t: ((2 * zh + c) ^ y, 1 - (t & 1), x, t >> 1, y))
+    first, second, wo_other, *ring = lax.optimization_barrier((first, second, wo_other, *ring))
     inputs = jnp.concatenate([features(0)] + ring, axis=0)
 
     wo_piece = jnp.concatenate([out_weight, wo_other], axis=0)
     wo = lax.all_gather(wo_piece, ("y", "x", "core"), axis=0, tiled=True)
 
-    def gathered(block):
-        pair = jnp.stack([block, swap(block, "core", 1)])
-        return [pair] + [along(pair, d, "x", "y") for d in (1, 2, 3)]
-
-    def reduced(blocks):
-        sent, total = project(inputs, blocks)
-        for e in (1, 2, 3):
-            total = total + along(sent[e - 1], e, "y", "x").astype(F32)
-        return total
-
-    second, *blocks = lax.optimization_barrier((second, *gathered(first)))
-    total, *blocks = lax.optimization_barrier((reduced(blocks), *gathered(second)))
-    summed = [total, reduced(blocks)]
-    base = 2 * c + zh
-    q_slots = [half[:, at : at + 384] for at in (0, 384) for half in summed]
-    kv_slots = [half[:, at : at + 64] for at in (768, 832) for half in summed]
-    q_sum = jnp.concatenate(by_index(q_slots, base), axis=1)
-    kv_sum = jnp.concatenate(by_index(kv_slots, base), axis=1)
-
-    kv_short = kv_sum.astype(BF)
+    pair = jnp.stack([first, second])
+    pair = jnp.concatenate([pair, swap(pair, "core", 1)], axis=0)
+    sent, total = project(inputs, [pair] + [along(pair, d, "x", "y") for d in (1, 2, 3)])
+    for e in (1, 2, 3):
+        total = total + along(sent[e - 1], e, "y", "x").astype(F32)
+
+    kv_raw = total[:, 1536:]
+    kv_short = kv_raw.astype(BF)
     high = lax.reduce_precision(squares, 8, 7)
     middle = lax.reduce_precision(squares - high, 8, 7)
     low = squares - high - middle
     note = jnp.pad(jnp.stack([high, middle, low]), ((0, 29), (0, 0))).astype(BF)
-    shared = jnp.concatenate([kv_short[32 * r : 32 * r + 32] for r in range(4)] + [note], axis=1)
+    shared = [kv_short[32 * r : 32 * r + 32] for r in range(4)] + [note]
 
     def rows_for(d):
-        return lax.dynamic_slice(q_sum, ((t ^ d) * 32, 0), (32, 1536))
-
-    q_raw, kv_raw, total = rows_for(0), kv_sum, squares
+        return lax.dynamic_slice(total, ((t ^ d) * 32, 0), (32, 1536))
+
+    q_raw = rows_for(0)
     for d in (1, 2, 3):
-        came = swap(jnp.concatenate([rows_for(d).astype(BF), shared], axis=1), "zl", d).astype(F32)
+        came = swap(jnp.concatenate([rows_for(d).astype(BF)] + shared, axis=1), "zl", d).astype(F32)
         q_raw = q_raw + came[:, :1536]
         kv_raw = kv_raw + jnp.concatenate([came[:, 1536 + 256 * r : 1792 + 256 * r] for r in range(4)], axis=0)
-        total = total + ((came[2, 2560:] + came[1, 2560:]) + came[0, 2560:])
-    scales = lax.rsqrt(total / D + 1e-05)
+        squares = squares + ((came[2, 2560:] + came[1, 2560:]) + came[0, 2560:])
+    scales = lax.rsqrt(squares / D + 1e-05)
+
+    base = 2 * c + zh
+    q_raw = jnp.concatenate(by_index([q_raw[:, 384 * d : 384 * d + 384] for d in range(4)], base), axis=1)
+    kv_raw = jnp.concatenate(by_index([kv_raw[:, 64 * d : 64 * d + 64] for d in range(4)], base), axis=1)
 
     limit = lengths[0]
     kv = (kv_raw * scales[:, None]).astype(BF)

time: 175 us -> 166 us (0.949)
  starting transfers between devices: 76.4 us -> 41.8 us
  waiting for transfers between devices: 66 us -> 87.1 us
  local copies, waits for them, and re-layouts: 1.09 us -> 3.99 us
    ppermute x17 -> x11, waiting for transfers between devices: 38.3 us -> 70.1 us  [move(): lax.ppermute(value, AXES, [(flat(*at), flat(*where(*at))) for at in every...]
    ppermute x9 -> x8, starting transfers between devices: 33.2 us -> 15.4 us  [swap(): return lax.ppermute(value, axis, [(i, i ^ d) for i in range(n)])]
    ppermute x17 -> x11, starting transfers between devices: 43.2 us -> 26.4 us  [move(): lax.ppermute(value, AXES, [(flat(*at), flat(*where(*at))) for at in every...]
    ppermute x9 -> x8, waiting for transfers between devices: 27.6 us -> 16.9 us  [swap(): return lax.ppermute(value, axis, [(i, i ^ d) for i in range(n)])]
    unnamed x24 -> x30, local copies, waits for them, and re-layouts: 0.13 us -> 2.23 us
    pallas_call x2 -> x1, Pallas kernels: 3.03 us -> 3.78 us  [project(): pl.pallas_call(project_kernel, out_shape=(jax.ShapeDtypeStruct((3, ROWS,...]
  transfers between devices with their start and end apart: 27 -> 20, of which waited for: 12 -> 12; matrix products, arithmetic and copies ran while one was open for 2% -> 3% of each run, Pallas kernels for 2% -> 2%
where the time goes in v12:
time: 166 us; the launch traced here: 165 us
  waiting for transfers between devices  87.1 us (52%)
  starting transfers between devices  41.8 us (25%)
  between operations  14.6 us (9%)
  matrix products  8.6 us (5%)
  other arithmetic  5.15 us (3%)
  local copies, waits for them, and re-layouts  3.99 us (2%)
  Pallas kernels  3.82 us (2%)
    ppermute x11, waiting for transfers between devices, move(): lax.ppermute(value, AXES, [(flat(*at), flat(*where(*at))) for at in every...  70.1 us
    ppermute x11, starting transfers between devices, move(): lax.ppermute(value, AXES, [(flat(*at), flat(*where(*at))) for at in every...  26.4 us
    ppermute x8, waiting for transfers between devices, swap(): return lax.ppermute(value, axis, [(i, i ^ d) for i in range(n)])  16.9 us
    ppermute x8, starting transfers between devices, swap(): return lax.ppermute(value, axis, [(i, i ^ d) for i in range(n)])  15.4 us
    dot_general x1, matrix products, body(): return jnp.dot(all_rows, wo, preferred_element_type=F32).astype(BF)  7.35 us
    pallas_call x1, Pallas kernels, project(): pl.pallas_call(project_kernel, out_shape=(jax.ShapeDtypeStruct((3, ROWS,...  3.78 us
  transfers between devices with their start and end apart: 20, of which 12 were waited for; matrix products, arithmetic and copies ran while one was open for 3% of the time, Pallas kernels for 2%

profile of v12, /device:TPU:24, one launch (start us, length us, event | category | flops | bytes accessed | tf_op | source)
XLA Modules:
  0.0 165.0 jit_solution(11424146791804523021)
XLA Ops:
  6.5 1.7 %fusion.2 = (f32[128]{0:T(128)S(1)}, bf16[128,4096]{1,0:T(8,128)(2,1)S(1)}) fusion(bf16[128,4096]{1,0:T(8,128)(2,1)} %param.12, f32[4096]{0:T(1024)} %param.13), kind=kLoop, calls=%fused_computation.5 | loop fusion | flops 2621312 | bytes 2114048 | tf_op jit(solution)/shard_map/reduce_sum | solution.py:171
  8.5 2.0 %collective-permute-start.5 = (bf16[128,1024]{1,0:T(8,128)(2,1)S(1)}, bf16[128,1024]{1,0:T(8,128)(2,1)S(1)}, u32[]{:S(2)}, u32[]{:S(2)}) collective-permute-start(bf16[128,1024]{1,0:T(8,128)(2,1)S(1)} %pad_maximum_fusion.6), channel_id=1, source_target_pairs={{0,192},{1,193},{2,194},{3,195},{4,28},{5,29},{6,30},{7,31},{8,200... | collective-permute-start | bytes 786440 | tf_op jit(solution)/shard_map/ppermute | solution.py:43
  10.5 5.5 %collective-permute-start.2 = (bf16[24,4096]{1,0:T(8,128)(2,1)S(1)}, bf16[24,4096]{1,0:T(8,128)(2,1)S(1)}, u32[]{:S(2)}, u32[]{:S(2)}) collective-permute-start(bf16[24,4096]{1,0:T(8,128)(2,1)S(1)} %copy-done.5), channel_id=1, source_target_pairs={{0,32},{32,0},{1,33},{33,1},{2,34},{34,2},{3,35},{35,3},{4,36},{36... | collective-permute-start | bytes 589832 | tf_op jit(solution)/shard_map/ppermute | solution.py:39
  16.0 2.7 %collective-permute-start.4 = (bf16[128,1024]{1,0:T(8,128)(2,1)S(1)}, bf16[128,1024]{1,0:T(8,128)(2,1)S(1)}, u32[]{:S(2)}, u32[]{:S(2)}) collective-permute-start(bf16[128,1024]{1,0:T(8,128)(2,1)S(1)} %pad_maximum_fusion.5), channel_id=1, source_target_pairs={{0,128},{1,129},{2,130},{3,131},{4,20},{5,21},{6,22},{7,23},{8,136... | collective-permute-start | bytes 786440 | tf_op jit(solution)/shard_map/ppermute | solution.py:43
  18.7 1.4 collective-permute-start.3
  20.1 3.8 %collective-permute-start = (bf16[896,128]{1,0:T(8,128)(2,1)S(1)}, bf16[896,128]{1,0:T(8,128)(2,1)S(1)}, u32[]{:S(2)}, u32[]{:S(2)}) collective-permute-start(bf16[896,128]{1,0:T(8,128)(2,1)S(1)} %shard_map.118), channel_id=1, source_target_pairs={{0,0},{1,32},{2,4},{3,36},{4,64},{5,96},{6,68},{7,100},{8,8},{9,40... | collective-permute-start | bytes 688136 | tf_op jit(solution)/shard_map/ppermute | solution.py:43
  24.0 7.0 %collective-permute-start.1 = (bf16[896,128]{1,0:T(8,128)(2,1)S(1)}, bf16[896,128]{1,0:T(8,128)(2,1)S(1)}, u32[]{:S(2)}, u32[]{:S(2)}) collective-permute-start(bf16[896,128]{1,0:T(8,128)(2,1)S(1)} %shard_map.118), channel_id=1, source_target_pairs={{0,32},{1,0},{2,36},{3,4},{4,96},{5,64},{6,100},{7,68},{8,40},{9,8... | collective-permute-start | bytes 688136 | tf_op jit(solution)/shard_map/ppermute | solution.py:43
  31.0 5.1 %collective-permute-done = bf16[896,128]{1,0:T(8,128)(2,1)S(1)} collective-permute-done((bf16[896,128]{1,0:T(8,128)(2,1)S(1)}, bf16[896,128]{1,0:T(8,128)(2,1)S(1)}, u32[]{:S(2)}, u32[]{:S(2)}) %collective-permute-start) | collective-permute-done | bytes 229408 | tf_op jit(solution)/shard_map/ppermute | solution.py:43
  36.1 10.6 %collective-permute-done.1 = bf16[896,128]{1,0:T(8,128)(2,1)S(1)} collective-permute-done((bf16[896,128]{1,0:T(8,128)(2,1)S(1)}, bf16[896,128]{1,0:T(8,128)(2,1)S(1)}, u32[]{:S(2)}, u32[]{:S(2)}) %collective-permute-start.1) | collective-permute-done | bytes 229408 | tf_op jit(solution)/shard_map/ppermute | solution.py:43
  46.7 0.8 pad_maximum_fusion.3
  47.8 1.7 %collective-permute-done.6 = bf16[2,896,128]{2,1,0:T(8,128)(2,1)S(1)} collective-permute-done((bf16[2,896,128]{2,1,0:T(8,128)(2,1)S(1)}, bf16[2,896,128]{2,1,0:T(8,128)(2,1)S(1)}, u32[]{:S(2)}, u32[]{:S(2)}) %collective-permute-start.6) | collective-permute-done | bytes 458784 | tf_op jit(solution)/shard_map/ppermute | solution.py:39
  49.6 1.4 collective-permute-start.7
  51.1 2.7 %collective-permute-start.8 = (bf16[4,896,128]{2,1,0:T(8,128)(2,1)S(1)}, bf16[4,896,128]{2,1,0:T(8,128)(2,1)S(1)}, u32[]{:S(2)}, u32[]{:S(2)}) collective-permute-start(bf16[4,896,128]{2,1,0:T(8,128)(2,1)S(1)} %pad_maximum_fusion.1.refs_0_), channel_id=1, source_target_pairs={{0,16},{1,17},{2,18},{3,19},{4,132},{5,133},{6,134},{7,135},{8,24}... | collective-permute-start | bytes 2752520 | tf_op jit(solution)/shard_map/ppermute | solution.py:43
  55.1 1.0 pad_maximum_fusion.x_ref
  56.1 9.9 %collective-permute-done.7.refs_1_ = bf16[4,896,128]{2,1,0:T(8,128)(2,1)S(1)} collective-permute-done((bf16[4,896,128]{2,1,0:T(8,128)(2,1)S(1)}, bf16[4,896,128]{2,1,0:T(8,128)(2,1)S(1)}, u32[]{:S(2)}, u32[]{:S(2)}) %collective-permute-start.7) | collective-permute-done | bytes 917536 | tf_op jit(solution)/shard_map/ppermute | solution.py:43
  66.0 15.4 %collective-permute-done.8.refs_2_ = bf16[4,896,128]{2,1,0:T(8,128)(2,1)S(1)} collective-permute-done((bf16[4,896,128]{2,1,0:T(8,128)(2,1)S(1)}, bf16[4,896,128]{2,1,0:T(8,128)(2,1)S(1)}, u32[]{:S(2)}, u32[]{:S(2)}) %collective-permute-start.8) | collective-permute-done | bytes 917536 | tf_op jit(solution)/shard_map/ppermute | solution.py:43
  81.4 0.9 copy-done.2
  82.3 2.4 %collective-permute-done.9.refs_3_ = bf16[4,896,128]{2,1,0:T(8,128)(2,1)} collective-permute-done((bf16[4,896,128]{2,1,0:T(8,128)(2,1)S(1)}, bf16[4,896,128]{2,1,0:T(8,128)(2,1)}, u32[]{:S(2)}, u32[]{:S(2)}) %collective-permute-start.9) | collective-permute-done | bytes 917536 | tf_op jit(solution)/shard_map/ppermute | solution.py:43
  84.7 1.2 copy-done.3
  85.8 3.8 %shard_map.119 = (bf16[3,128,1792]{2,1,0:T(8,128)(2,1)S(1)}, f32[128,1792]{1,0:T(8,128)S(1)}) custom-call(bf16[512,1024]{1,0:T(8,128)(2,1)S(1)} %pad_maximum_fusion.x_ref, bf16[4,896,128]{2,1,0:T(8,128)(2,1)S(1)} %pad_maximum_fusion.1.refs_0_, bf16[4,896,128]{2,1,0:T(8,128)(2,1)S(1)} %collective-permute-done.7.refs_1_, bf16[4,896,128]{2,1,0:T(8,128)(2,1)S(1)} %copy-done.3, ...), custom_call_target="tpu_custom_call" | custom-call | flops 1879048192 | bytes 8000000 | tf_op jit(solution)/shard_map/pallas_call | solution.py:141
  89.6 0.9 slice_bitcast_fusion.2
  90.5 0.9 collective-permute-start.10
  91.4 3.8 %collective-permute-start.12 = (bf16[128,1792]{1,0:T(8,128)(2,1)S(1)}, bf16[128,1792]{1,0:T(8,128)(2,1)S(1)}, u32[]{:S(2)}, u32[]{:S(2)}) collective-permute-start(bf16[128,1792]{1,0:T(8,128)(2,1)S(1)} %get-tuple-element.22), channel_id=1, source_target_pairs={{0,192},{1,193},{2,194},{3,195},{4,28},{5,29},{6,30},{7,31},{8,200... | collective-permute-start | bytes 1376264 | tf_op jit(solution)/shard_map/ppermute | solution.py:43
  95.3 13.6 %collective-permute-done.10 = bf16[128,1792]{1,0:T(8,128)(2,1)S(1)} collective-permute-done((bf16[128,1792]{1,0:T(8,128)(2,1)}, bf16[128,1792]{1,0:T(8,128)(2,1)S(1)}, u32[]{:S(2)}, u32[]{:S(2)}) %collective-permute-start.10) | collective-permute-done | bytes 458784 | tf_op jit(solution)/shard_map/ppermute | solution.py:43
  108.8 13.2 %collective-permute-done.11 = bf16[128,1792]{1,0:T(8,128)(2,1)S(1)} collective-permute-done((bf16[128,1792]{1,0:T(8,128)(2,1)S(1)}, bf16[128,1792]{1,0:T(8,128)(2,1)S(1)}, u32[]{:S(2)}, u32[]{:S(2)}) %collective-permute-start.11) | collective-permute-done | bytes 458784 | tf_op jit(solution)/shard_map/ppermute | solution.py:43
  122.5 5.1 %collective-permute-start.14 = (bf16[32,2688]{1,0:T(8,128)(2,1)S(1)}, bf16[32,2688]{1,0:T(8,128)(2,1)S(1)}, u32[]{:S(2)}, u32[]{:S(2)}) collective-permute-start(bf16[32,2688]{1,0:T(8,128)(2,1)S(1)} %get-tuple-element.90), channel_id=1, source_target_pairs={{0,2},{1,3},{2,0},{3,1},{4,6},{5,7},{6,4},{7,5},{8,10},{9,11},{10,... | collective-permute-start | bytes 516104 | tf_op jit(solution)/shard_map/ppermute | solution.py:39
  127.7 7.5 %collective-permute-done.13 = bf16[32,2688]{1,0:T(8,128)(2,1)S(1)} collective-permute-done((bf16[32,2688]{1,0:T(8,128)(2,1)S(1)}, bf16[32,2688]{1,0:T(8,128)(2,1)S(1)}, u32[]{:S(2)}, u32[]{:S(2)}) %collective-permute-start.13) | collective-permute-done | bytes 172064 | tf_op jit(solution)/shard_map/ppermute | solution.py:39
  135.2 4.2 %collective-permute-done.14 = bf16[32,2688]{1,0:T(8,128)(2,1)S(1)} collective-permute-done((bf16[32,2688]{1,0:T(8,128)(2,1)S(1)}, bf16[32,2688]{1,0:T(8,128)(2,1)S(1)}, u32[]{:S(2)}, u32[]{:S(2)}) %collective-permute-start.14) | collective-permute-done | bytes 172064 | tf_op jit(solution)/shard_map/ppermute | solution.py:39
  143.0 4.1 %collective-permute-start.18 = (bf16[32,1536]{1,0:T(8,128)(2,1)S(1)}, bf16[32,1536]{1,0:T(8,128)(2,1)S(1)}, u32[]{:S(2)}, u32[]{:S(2)}) collective-permute-start(bf16[32,1536]{1,0:T(8,128)(2,1)S(1)} %pad_maximum_fusion.7), channel_id=1, source_target_pairs={{0,1},{1,0},{2,3},{3,2},{4,5},{5,4},{6,7},{7,6},{8,9},{9,8},{10,11... | collective-permute-start | bytes 294920 | tf_op jit(solution)/shard_map/ppermute | solution.py:39
  147.1 2.2 %collective-permute-done.16 = bf16[32,1536]{1,0:T(8,128)(2,1)S(1)} collective-permute-done((bf16[32,1536]{1,0:T(8,128)(2,1)S(1)}, bf16[32,1536]{1,0:T(8,128)(2,1)S(1)}, u32[]{:S(2)}, u32[]{:S(2)}) %collective-permute-start.16) | collective-permute-done | bytes 98336 | tf_op jit(solution)/shard_map/ppermute | solution.py:39
  149.3 1.3 collective-permute-done.17
  150.8 7.4 %convolution_convert_fusion = bf16[128,4096]{1,0:T(8,128)(2,1)} fusion(bf16[1536,4096]{1,0:T(8,128)(2,1)} %all-gather.2.cloned.1.call-done, bf16[32,1536]{1,0:T(8,128)(2,1)S(1)} %broadcast_select_fusion.4, bf16[32,1536]{1,0:T(8,128)(2,1)S(1)} %get-tuple-element.47, bf16[32,1536]{1,0:T(8,128)(2,1)S(1)} %get-tuple-element.46, ...), kind=kOutput, calls=%fused_computation.1 | convolution fusion | flops 1612709888 | bytes 14024704 | tf_op jit(solution)/shard_map/dot_general | solution.py:233
  (96 shorter events, 5.3 us)
Async XLA Ops:
  6.5 144.2 %all-gather.2.cloned.1.call-start = ((), (), s32[]{:S(2)}) async-start(), calls=%async_computation | async-start | bytes 12976128 | tf_op jit(solution)/shard_map/all_gather | solution.py:188
  6.5 4.0 %copy-start.5 = (bf16[24,4096]{1,0:T(8,128)(2,1)S(1)}, bf16[24,4096]{1,0:T(8,128)(2,1)}, u32[]{:S(2)}) copy-start(bf16[24,4096]{1,0:T(8,128)(2,1)} %param.16) | copy-start | bytes 589828
  8.2 11.9 %copy-start = (bf16[256,384]{1,0:T(8,128)(2,1)S(1)}, bf16[256,384]{1,0:T(8,128)(2,1)}, u32[]{:S(2)}) copy-start(bf16[256,384]{1,0:T(8,128)(2,1)} %q_ref.1) | copy-start | bytes 589828
  8.2 11.9 %copy-start.1 = (bf16[256,64]{0,1:T(8,128)(2,1)S(1)}, bf16[256,64]{0,1:T(8,128)(2,1)}, u32[]{:S(2)}) copy-start(bf16[256,64]{0,1:T(8,128)(2,1)} %param.15) | copy-start | bytes 98308
  8.5 38.2 %collective-permute-start.5 = (bf16[128,1024]{1,0:T(8,128)(2,1)S(1)}, bf16[128,1024]{1,0:T(8,128)(2,1)S(1)}, u32[]{:S(2)}, u32[]{:S(2)}) collective-permute-start(bf16[128,1024]{1,0:T(8,128)(2,1)S(1)} %pad_maximum_fusion.6), channel_id=1, source_target_pairs={{0,192},{1,193},{2,194},{3,195},{4,28},{5,29},{6,30},{7,31},{8,200... | collective-permute-start | bytes 786440 | tf_op jit(solution)/shard_map/ppermute | solution.py:43
  10.5 13.4 %collective-permute-start.2 = (bf16[24,4096]{1,0:T(8,128)(2,1)S(1)}, bf16[24,4096]{1,0:T(8,128)(2,1)S(1)}, u32[]{:S(2)}, u32[]{:S(2)}) collective-permute-start(bf16[24,4096]{1,0:T(8,128)(2,1)S(1)} %copy-done.5), channel_id=1, source_target_pairs={{0,32},{32,0},{1,33},{33,1},{2,34},{34,2},{3,35},{35,3},{4,36},{36... | collective-permute-start | bytes 589832 | tf_op jit(solution)/shard_map/ppermute | solution.py:39
  16.0 30.7 %collective-permute-start.4 = (bf16[128,1024]{1,0:T(8,128)(2,1)S(1)}, bf16[128,1024]{1,0:T(8,128)(2,1)S(1)}, u32[]{:S(2)}, u32[]{:S(2)}) collective-permute-start(bf16[128,1024]{1,0:T(8,128)(2,1)S(1)} %pad_maximum_fusion.5), channel_id=1, source_target_pairs={{0,128},{1,129},{2,130},{3,131},{4,20},{5,21},{6,22},{7,23},{8,136... | collective-permute-start | bytes 786440 | tf_op jit(solution)/shard_map/ppermute | solution.py:43
  18.7 28.0 %collective-permute-start.3 = (bf16[128,1024]{1,0:T(8,128)(2,1)S(1)}, bf16[128,1024]{1,0:T(8,128)(2,1)S(1)}, u32[]{:S(2)}, u32[]{:S(2)}) collective-permute-start(bf16[128,1024]{1,0:T(8,128)(2,1)S(1)} %pad_maximum_fusion.4), channel_id=1, source_target_pairs={{0,64},{1,65},{2,66},{3,67},{4,12},{5,13},{6,14},{7,15},{8,72},{9,... | collective-permute-start | bytes 786440 | tf_op jit(solution)/shard_map/ppermute | solution.py:43
  20.1 16.0 %collective-permute-start = (bf16[896,128]{1,0:T(8,128)(2,1)S(1)}, bf16[896,128]{1,0:T(8,128)(2,1)S(1)}, u32[]{:S(2)}, u32[]{:S(2)}) collective-permute-start(bf16[896,128]{1,0:T(8,128)(2,1)S(1)} %shard_map.118), channel_id=1, source_target_pairs={{0,0},{1,32},{2,4},{3,36},{4,64},{5,96},{6,68},{7,100},{8,8},{9,40... | collective-permute-start | bytes 688136 | tf_op jit(solution)/shard_map/ppermute | solution.py:43
  24.0 22.7 %collective-permute-start.1 = (bf16[896,128]{1,0:T(8,128)(2,1)S(1)}, bf16[896,128]{1,0:T(8,128)(2,1)S(1)}, u32[]{:S(2)}, u32[]{:S(2)}) collective-permute-start(bf16[896,128]{1,0:T(8,128)(2,1)S(1)} %shard_map.118), channel_id=1, source_target_pairs={{0,32},{1,0},{2,36},{3,4},{4,96},{5,64},{6,100},{7,68},{8,40},{9,8... | collective-permute-start | bytes 688136 | tf_op jit(solution)/shard_map/ppermute | solution.py:43
  46.7 1.1 copy-start.4
  47.6 1.9 %collective-permute-start.6 = (bf16[2,896,128]{2,1,0:T(8,128)(2,1)S(1)}, bf16[2,896,128]{2,1,0:T(8,128)(2,1)S(1)}, u32[]{:S(2)}, u32[]{:S(2)}) collective-permute-start(bf16[2,896,128]{2,1,0:T(8,128)(2,1)S(1)} %pad_maximum_fusion.2), channel_id=1, source_target_pairs={{0,4},{4,0},{1,5},{5,1},{2,6},{6,2},{3,7},{7,3},{8,12},{12,8},{9,1... | collective-permute-start | bytes 1376264 | tf_op jit(solution)/shard_map/ppermute | solution.py:39
  49.6 16.4 %collective-permute-start.7 = (bf16[4,896,128]{2,1,0:T(8,128)(2,1)S(1)}, bf16[4,896,128]{2,1,0:T(8,128)(2,1)S(1)}, u32[]{:S(2)}, u32[]{:S(2)}) collective-permute-start(bf16[4,896,128]{2,1,0:T(8,128)(2,1)S(1)} %pad_maximum_fusion.1.refs_0_), channel_id=1, source_target_pairs={{0,8},{1,9},{2,10},{3,11},{4,68},{5,69},{6,70},{7,71},{8,0},{9,1},... | collective-permute-start | bytes 2752520 | tf_op jit(solution)/shard_map/ppermute | solution.py:43
  51.1 30.3 %collective-permute-start.8 = (bf16[4,896,128]{2,1,0:T(8,128)(2,1)S(1)}, bf16[4,896,128]{2,1,0:T(8,128)(2,1)S(1)}, u32[]{:S(2)}, u32[]{:S(2)}) collective-permute-start(bf16[4,896,128]{2,1,0:T(8,128)(2,1)S(1)} %pad_maximum_fusion.1.refs_0_), channel_id=1, source_target_pairs={{0,16},{1,17},{2,18},{3,19},{4,132},{5,133},{6,134},{7,135},{8,24}... | collective-permute-start | bytes 2752520 | tf_op jit(solution)/shard_map/ppermute | solution.py:43
  53.8 30.9 %collective-permute-start.9 = (bf16[4,896,128]{2,1,0:T(8,128)(2,1)S(1)}, bf16[4,896,128]{2,1,0:T(8,128)(2,1)}, u32[]{:S(2)}, u32[]{:S(2)}) collective-permute-start(bf16[4,896,128]{2,1,0:T(8,128)(2,1)S(1)} %pad_maximum_fusion.1.refs_0_), channel_id=1, source_target_pairs={{0,24},{1,25},{2,26},{3,27},{4,196},{5,197},{6,198},{7,199},{8,16}... | collective-permute-start | bytes 2752520 | tf_op jit(solution)/shard_map/ppermute | solution.py:43
  81.4 0.9 copy-start.2
  84.7 1.2 copy-start.3
  89.6 5.6 %copy-start.6 = (f32[128,128]{1,0:T(8,128)S(1)}, f32[128,128]{1,0:T(8,128)}, u32[]{:S(2)}) copy-start(f32[128,128]{1,0:T(8,128)} %constant.76.clone) | copy-start | bytes 196612
  89.6 5.6 %copy-start.7 = (f32[128,128]{1,0:T(8,128)S(1)}, f32[128,128]{1,0:T(8,128)}, u32[]{:S(2)}) copy-start(f32[128,128]{1,0:T(8,128)} %constant.77.clone) | copy-start | bytes 196612
  90.5 18.3 %collective-permute-start.10 = (bf16[128,1792]{1,0:T(8,128)(2,1)}, bf16[128,1792]{1,0:T(8,128)(2,1)S(1)}, u32[]{:S(2)}, u32[]{:S(2)}) collective-permute-start(bf16[128,1792]{1,0:T(8,128)(2,1)} %get-tuple-element.21), channel_id=1, source_target_pairs={{0,64},{1,65},{2,66},{3,67},{4,12},{5,13},{6,14},{7,15},{8,72},{9,... | collective-permute-start | bytes 1376264 | tf_op jit(solution)/shard_map/ppermute | solution.py:43
  91.4 30.6 %collective-permute-start.11 = (bf16[128,1792]{1,0:T(8,128)(2,1)S(1)}, bf16[128,1792]{1,0:T(8,128)(2,1)S(1)}, u32[]{:S(2)}, u32[]{:S(2)}) collective-permute-start(bf16[128,1792]{1,0:T(8,128)(2,1)S(1)} %get-tuple-element.23), channel_id=1, source_target_pairs={{0,128},{1,129},{2,130},{3,131},{4,20},{5,21},{6,22},{7,23},{8,136... | collective-permute-start | bytes 1376264 | tf_op jit(solution)/shard_map/ppermute | solution.py:43
  91.4 30.6 %collective-permute-start.12 = (bf16[128,1792]{1,0:T(8,128)(2,1)S(1)}, bf16[128,1792]{1,0:T(8,128)(2,1)S(1)}, u32[]{:S(2)}, u32[]{:S(2)}) collective-permute-start(bf16[128,1792]{1,0:T(8,128)(2,1)S(1)} %get-tuple-element.22), channel_id=1, source_target_pairs={{0,192},{1,193},{2,194},{3,195},{4,28},{5,29},{6,30},{7,31},{8,200... | collective-permute-start | bytes 1376264 | tf_op jit(solution)/shard_map/ppermute | solution.py:43
  122.4 17.1 %collective-permute-start.15 = (bf16[32,2688]{1,0:T(8,128)(2,1)S(1)}, bf16[32,2688]{1,0:T(8,128)(2,1)S(1)}, u32[]{:S(2)}, u32[]{:S(2)}) collective-permute-start(bf16[32,2688]{1,0:T(8,128)(2,1)S(1)} %get-tuple-element.91), channel_id=1, source_target_pairs={{0,3},{1,2},{2,1},{3,0},{4,7},{5,6},{6,5},{7,4},{8,11},{9,10},{10,... | collective-permute-start | bytes 516104 | tf_op jit(solution)/shard_map/ppermute | solution.py:39
  122.5 16.9 %collective-permute-start.14 = (bf16[32,2688]{1,0:T(8,128)(2,1)S(1)}, bf16[32,2688]{1,0:T(8,128)(2,1)S(1)}, u32[]{:S(2)}, u32[]{:S(2)}) collective-permute-start(bf16[32,2688]{1,0:T(8,128)(2,1)S(1)} %get-tuple-element.90), channel_id=1, source_target_pairs={{0,2},{1,3},{2,0},{3,1},{4,6},{5,7},{6,4},{7,5},{8,10},{9,11},{10,... | collective-permute-start | bytes 516104 | tf_op jit(solution)/shard_map/ppermute | solution.py:39
  127.7 7.5 %collective-permute-start.13 = (bf16[32,2688]{1,0:T(8,128)(2,1)S(1)}, bf16[32,2688]{1,0:T(8,128)(2,1)S(1)}, u32[]{:S(2)}, u32[]{:S(2)}) collective-permute-start(bf16[32,2688]{1,0:T(8,128)(2,1)S(1)} %get-tuple-element.89), channel_id=1, source_target_pairs={{0,1},{1,0},{2,3},{3,2},{4,5},{5,4},{6,7},{7,6},{8,9},{9,8},{10,11... | collective-permute-start | bytes 516104 | tf_op jit(solution)/shard_map/ppermute | solution.py:39
  140.8 1.5 copy-start.8
  140.8 1.5 copy-start.9
  142.6 6.7 %collective-permute-start.16 = (bf16[32,1536]{1,0:T(8,128)(2,1)S(1)}, bf16[32,1536]{1,0:T(8,128)(2,1)S(1)}, u32[]{:S(2)}, u32[]{:S(2)}) collective-permute-start(bf16[32,1536]{1,0:T(8,128)(2,1)S(1)} %pad_maximum_fusion.7), channel_id=1, source_target_pairs={{0,3},{1,2},{2,1},{3,0},{4,7},{5,6},{6,5},{7,4},{8,11},{9,10},{10,... | collective-permute-start | bytes 294920 | tf_op jit(solution)/shard_map/ppermute | solution.py:39
  143.0 7.6 %collective-permute-start.17 = (bf16[32,1536]{1,0:T(8,128)(2,1)S(1)}, bf16[32,1536]{1,0:T(8,128)(2,1)S(1)}, u32[]{:S(2)}, u32[]{:S(2)}) collective-permute-start(bf16[32,1536]{1,0:T(8,128)(2,1)S(1)} %pad_maximum_fusion.7), channel_id=1, source_target_pairs={{0,2},{1,3},{2,0},{3,1},{4,6},{5,7},{6,4},{7,5},{8,10},{9,11},{10,... | collective-permute-start | bytes 294920 | tf_op jit(solution)/shard_map/ppermute | solution.py:39
  143.0 7.6 %collective-permute-start.18 = (bf16[32,1536]{1,0:T(8,128)(2,1)S(1)}, bf16[32,1536]{1,0:T(8,128)(2,1)S(1)}, u32[]{:S(2)}, u32[]{:S(2)}) collective-permute-start(bf16[32,1536]{1,0:T(8,128)(2,1)S(1)} %pad_maximum_fusion.7), channel_id=1, source_target_pairs={{0,1},{1,0},{2,3},{3,2},{4,5},{5,4},{6,7},{7,6},{8,9},{9,8},{10,11... | collective-permute-start | bytes 294920 | tf_op jit(solution)/shard_map/ppermute | solution.py:39
Sparse Core Ops, SparseCore 0:
  47.7 83.6 all-gather.1

commit v13 on v12

--- a/solution.py
+++ b/solution.py
@@ -165,7 +165,6 @@
 
     packed = pack(query_weight, kv_weight.T)
     first = move(packed, lambda y, zh, x, c, t: ((2 * zh + c) ^ y, t & 1, x, t >> 1, y))
-    wo_other = swap(out_weight, "zh", 1)
 
     widened = tokens.astype(F32)
     squares = jnp.sum(widened * widened, axis=1)
@@ -181,10 +180,10 @@
 
     ring = [along(features(e), e, "y", "x") for e in (1, 2, 3)]
     second = move(packed, lambda y, zh, x, c, t: ((2 * zh + c) ^ y, 1 - (t & 1), x, t >> 1, y))
-    first, second, wo_other, *ring = lax.optimization_barrier((first, second, wo_other, *ring))
+    first, second, out_weight, *ring = lax.optimization_barrier((first, second, out_weight, *ring))
     inputs = jnp.concatenate([features(0)] + ring, axis=0)
 
-    wo_piece = jnp.concatenate([out_weight, wo_other], axis=0)
+    wo_piece = jnp.concatenate([out_weight, swap(out_weight, "zh", 1)], axis=0)
     wo = lax.all_gather(wo_piece, ("y", "x", "core"), axis=0, tiled=True)
 
     pair = jnp.stack([first, second])

time: 166 us -> 176 us (1.060)
  the two profiles are of different devices: /device:TPU:24 before, /device:TPU:32 now
where the time goes in v13:
time: 176 us; the launch traced here: 175 us
  waiting for transfers between devices  102 us (58%)
  starting transfers between devices  37.5 us (21%)
  between operations  14.6 us (8%)
  matrix products  8.6 us (5%)
  other arithmetic  5.06 us (3%)
  local copies, waits for them, and re-layouts  3.99 us (2%)
  Pallas kernels  3.82 us (2%)
    ppermute x11, waiting for transfers between devices, move(): lax.ppermute(value, AXES, [(flat(*at), flat(*where(*at))) for at in every...  75.2 us
    ppermute x11, starting transfers between devices, move(): lax.ppermute(value, AXES, [(flat(*at), flat(*where(*at))) for at in every...  28.4 us
    ppermute x8, waiting for transfers between devices, swap(): return lax.ppermute(value, axis, [(i, i ^ d) for i in range(n)])  26.5 us
    ppermute x8, starting transfers between devices, swap(): return lax.ppermute(value, axis, [(i, i ^ d) for i in range(n)])  9.03 us
    dot_general x1, matrix products, body(): return jnp.dot(all_rows, wo, preferred_element_type=F32).astype(BF)  7.35 us
    pallas_call x1, Pallas kernels, project(): pl.pallas_call(project_kernel, out_shape=(jax.ShapeDtypeStruct((3, ROWS,...  3.78 us
  transfers between devices with their start and end apart: 20, of which 14 were waited for; matrix products, arithmetic and copies ran while one was open for 3% of the time, Pallas kernels for 2%

profile of v13, /device:TPU:32, one launch (start us, length us, event | category | flops | bytes accessed | tf_op | source)
XLA Modules:
  0.0 175.3 jit_solution(5783859745296578164)
XLA Ops:
  6.5 1.6 fusion.2
  8.4 3.1 %collective-permute-start.4 = (bf16[128,1024]{1,0:T(8,128)(2,1)S(1)}, bf16[128,1024]{1,0:T(8,128)(2,1)S(1)}, u32[]{:S(2)}, u32[]{:S(2)}) collective-permute-start(bf16[128,1024]{1,0:T(8,128)(2,1)S(1)} %pad_maximum_fusion.6), channel_id=1, source_target_pairs={{0,192},{1,193},{2,194},{3,195},{4,28},{5,29},{6,30},{7,31},{8,200... | collective-permute-start | bytes 786440 | tf_op jit(solution)/shard_map/ppermute | solution.py:43
  12.9 7.7 %collective-permute-start = (bf16[896,128]{1,0:T(8,128)(2,1)S(1)}, bf16[896,128]{1,0:T(8,128)(2,1)S(1)}, u32[]{:S(2)}, u32[]{:S(2)}) collective-permute-start(bf16[896,128]{1,0:T(8,128)(2,1)S(1)} %shard_map.118), channel_id=1, source_target_pairs={{0,0},{1,32},{2,4},{3,36},{4,64},{5,96},{6,68},{7,100},{8,8},{9,40... | collective-permute-start | bytes 688136 | tf_op jit(solution)/shard_map/ppermute | solution.py:43
  20.6 1.9 %collective-permute-start.1 = (bf16[896,128]{1,0:T(8,128)(2,1)S(1)}, bf16[896,128]{1,0:T(8,128)(2,1)S(1)}, u32[]{:S(2)}, u32[]{:S(2)}) collective-permute-start(bf16[896,128]{1,0:T(8,128)(2,1)S(1)} %shard_map.118), channel_id=1, source_target_pairs={{0,32},{1,0},{2,36},{3,4},{4,96},{5,64},{6,100},{7,68},{8,40},{9,8... | collective-permute-start | bytes 688136 | tf_op jit(solution)/shard_map/ppermute | solution.py:43
  22.6 8.6 %collective-permute-done = bf16[896,128]{1,0:T(8,128)(2,1)S(1)} collective-permute-done((bf16[896,128]{1,0:T(8,128)(2,1)S(1)}, bf16[896,128]{1,0:T(8,128)(2,1)S(1)}, u32[]{:S(2)}, u32[]{:S(2)}) %collective-permute-start) | collective-permute-done | bytes 229408 | tf_op jit(solution)/shard_map/ppermute | solution.py:43
  31.1 8.5 %collective-permute-done.1 = bf16[896,128]{1,0:T(8,128)(2,1)S(1)} collective-permute-done((bf16[896,128]{1,0:T(8,128)(2,1)S(1)}, bf16[896,128]{1,0:T(8,128)(2,1)S(1)}, u32[]{:S(2)}, u32[]{:S(2)}) %collective-permute-start.1) | collective-permute-done | bytes 229408 | tf_op jit(solution)/shard_map/ppermute | solution.py:43
  40.0 9.5 %collective-permute-done.18 = bf16[24,4096]{1,0:T(8,128)(2,1)S(1)} collective-permute-done((bf16[24,4096]{1,0:T(8,128)(2,1)S(1)}, bf16[24,4096]{1,0:T(8,128)(2,1)S(1)}, u32[]{:S(2)}, u32[]{:S(2)}) %collective-permute-start.18) | collective-permute-done | bytes 196640 | tf_op jit(solution)/shard_map/ppermute | solution.py:39
  50.4 1.8 %collective-permute-done.5 = bf16[2,896,128]{2,1,0:T(8,128)(2,1)S(1)} collective-permute-done((bf16[2,896,128]{2,1,0:T(8,128)(2,1)S(1)}, bf16[2,896,128]{2,1,0:T(8,128)(2,1)S(1)}, u32[]{:S(2)}, u32[]{:S(2)}) %collective-permute-start.5) | collective-permute-done | bytes 458784 | tf_op jit(solution)/shard_map/ppermute | solution.py:39
  52.3 1.6 collective-permute-start.6
  53.9 2.7 %collective-permute-start.7 = (bf16[4,896,128]{2,1,0:T(8,128)(2,1)S(1)}, bf16[4,896,128]{2,1,0:T(8,128)(2,1)S(1)}, u32[]{:S(2)}, u32[]{:S(2)}) collective-permute-start(bf16[4,896,128]{2,1,0:T(8,128)(2,1)S(1)} %pad_maximum_fusion.1.refs_0_), channel_id=1, source_target_pairs={{0,16},{1,17},{2,18},{3,19},{4,132},{5,133},{6,134},{7,135},{8,24}... | collective-permute-start | bytes 2752520 | tf_op jit(solution)/shard_map/ppermute | solution.py:43
  57.8 1.0 pad_maximum_fusion.x_ref
  58.8 7.0 %collective-permute-done.6.refs_1_ = bf16[4,896,128]{2,1,0:T(8,128)(2,1)S(1)} collective-permute-done((bf16[4,896,128]{2,1,0:T(8,128)(2,1)S(1)}, bf16[4,896,128]{2,1,0:T(8,128)(2,1)S(1)}, u32[]{:S(2)}, u32[]{:S(2)}) %collective-permute-start.6) | collective-permute-done | bytes 917536 | tf_op jit(solution)/shard_map/ppermute | solution.py:43
  65.8 15.8 %collective-permute-done.7.refs_2_ = bf16[4,896,128]{2,1,0:T(8,128)(2,1)S(1)} collective-permute-done((bf16[4,896,128]{2,1,0:T(8,128)(2,1)S(1)}, bf16[4,896,128]{2,1,0:T(8,128)(2,1)S(1)}, u32[]{:S(2)}, u32[]{:S(2)}) %collective-permute-start.7) | collective-permute-done | bytes 917536 | tf_op jit(solution)/shard_map/ppermute | solution.py:43
  81.6 0.9 copy-done.2
  82.5 4.4 %collective-permute-done.8.refs_3_ = bf16[4,896,128]{2,1,0:T(8,128)(2,1)} collective-permute-done((bf16[4,896,128]{2,1,0:T(8,128)(2,1)S(1)}, bf16[4,896,128]{2,1,0:T(8,128)(2,1)}, u32[]{:S(2)}, u32[]{:S(2)}) %collective-permute-start.8) | collective-permute-done | bytes 917536 | tf_op jit(solution)/shard_map/ppermute | solution.py:43
  87.0 1.2 copy-done.3
  88.1 3.8 %shard_map.119 = (bf16[3,128,1792]{2,1,0:T(8,128)(2,1)S(1)}, f32[128,1792]{1,0:T(8,128)S(1)}) custom-call(bf16[512,1024]{1,0:T(8,128)(2,1)S(1)} %pad_maximum_fusion.x_ref, bf16[4,896,128]{2,1,0:T(8,128)(2,1)S(1)} %pad_maximum_fusion.1.refs_0_, bf16[4,896,128]{2,1,0:T(8,128)(2,1)S(1)} %collective-permute-done.6.refs_1_, bf16[4,896,128]{2,1,0:T(8,128)(2,1)S(1)} %copy-done.3, ...), custom_call_target="tpu_custom_call" | custom-call | flops 1879048192 | bytes 8000000 | tf_op jit(solution)/shard_map/pallas_call | solution.py:141
  91.9 0.9 slice_bitcast_fusion.2
  92.8 8.4 %collective-permute-start.10 = (bf16[128,1792]{1,0:T(8,128)(2,1)}, bf16[128,1792]{1,0:T(8,128)(2,1)S(1)}, u32[]{:S(2)}, u32[]{:S(2)}) collective-permute-start(bf16[128,1792]{1,0:T(8,128)(2,1)} %get-tuple-element.23), channel_id=1, source_target_pairs={{0,128},{1,129},{2,130},{3,131},{4,20},{5,21},{6,22},{7,23},{8,136... | collective-permute-start | bytes 1376264 | tf_op jit(solution)/shard_map/ppermute | solution.py:43
  101.6 0.9 collective-permute-start.9
  102.5 14.5 %collective-permute-done.10 = bf16[128,1792]{1,0:T(8,128)(2,1)S(1)} collective-permute-done((bf16[128,1792]{1,0:T(8,128)(2,1)}, bf16[128,1792]{1,0:T(8,128)(2,1)S(1)}, u32[]{:S(2)}, u32[]{:S(2)}) %collective-permute-start.10) | collective-permute-done | bytes 458784 | tf_op jit(solution)/shard_map/ppermute | solution.py:43
  117.0 5.6 %collective-permute-done.11 = bf16[128,1792]{1,0:T(8,128)(2,1)S(1)} collective-permute-done((bf16[128,1792]{1,0:T(8,128)(2,1)S(1)}, bf16[128,1792]{1,0:T(8,128)(2,1)S(1)}, u32[]{:S(2)}, u32[]{:S(2)}) %collective-permute-start.11) | collective-permute-done | bytes 458784 | tf_op jit(solution)/shard_map/ppermute | solution.py:43
  122.6 10.9 %collective-permute-done.9 = bf16[128,1792]{1,0:T(8,128)(2,1)S(1)} collective-permute-done((bf16[128,1792]{1,0:T(8,128)(2,1)S(1)}, bf16[128,1792]{1,0:T(8,128)(2,1)S(1)}, u32[]{:S(2)}, u32[]{:S(2)}) %collective-permute-start.9) | collective-permute-done | bytes 458784 | tf_op jit(solution)/shard_map/ppermute | solution.py:43
  133.8 1.5 collective-permute-start.14
  135.3 2.1 %collective-permute-start.12 = (bf16[32,2688]{1,0:T(8,128)(2,1)S(1)}, bf16[32,2688]{1,0:T(8,128)(2,1)S(1)}, u32[]{:S(2)}, u32[]{:S(2)}) collective-permute-start(bf16[32,2688]{1,0:T(8,128)(2,1)S(1)} %get-tuple-element.89), channel_id=1, source_target_pairs={{0,1},{1,0},{2,3},{3,2},{4,5},{5,4},{6,7},{7,6},{8,9},{9,8},{10,11... | collective-permute-start | bytes 516104 | tf_op jit(solution)/shard_map/ppermute | solution.py:39
  137.5 5.8 %collective-permute-done.12 = bf16[32,2688]{1,0:T(8,128)(2,1)S(1)} collective-permute-done((bf16[32,2688]{1,0:T(8,128)(2,1)S(1)}, bf16[32,2688]{1,0:T(8,128)(2,1)S(1)}, u32[]{:S(2)}, u32[]{:S(2)}) %collective-permute-start.12) | collective-permute-done | bytes 172064 | tf_op jit(solution)/shard_map/ppermute | solution.py:39
  143.4 4.7 %collective-permute-done.13 = bf16[32,2688]{1,0:T(8,128)(2,1)S(1)} collective-permute-done((bf16[32,2688]{1,0:T(8,128)(2,1)S(1)}, bf16[32,2688]{1,0:T(8,128)(2,1)S(1)}, u32[]{:S(2)}, u32[]{:S(2)}) %collective-permute-start.13) | collective-permute-done | bytes 172064 | tf_op jit(solution)/shard_map/ppermute | solution.py:39
  151.3 3.5 %collective-permute-start.16 = (bf16[32,1536]{1,0:T(8,128)(2,1)S(1)}, bf16[32,1536]{1,0:T(8,128)(2,1)S(1)}, u32[]{:S(2)}, u32[]{:S(2)}) collective-permute-start(bf16[32,1536]{1,0:T(8,128)(2,1)S(1)} %pad_maximum_fusion.7), channel_id=1, source_target_pairs={{0,2},{1,3},{2,0},{3,1},{4,6},{5,7},{6,4},{7,5},{8,10},{9,11},{10,... | collective-permute-start | bytes 294920 | tf_op jit(solution)/shard_map/ppermute | solution.py:39
  154.8 1.4 collective-permute-start.17
  156.2 2.2 %collective-permute-done.16 = bf16[32,1536]{1,0:T(8,128)(2,1)S(1)} collective-permute-done((bf16[32,1536]{1,0:T(8,128)(2,1)S(1)}, bf16[32,1536]{1,0:T(8,128)(2,1)S(1)}, u32[]{:S(2)}, u32[]{:S(2)}) %collective-permute-start.16) | collective-permute-done | bytes 98336 | tf_op jit(solution)/shard_map/ppermute | solution.py:39
  158.4 2.6 %collective-permute-done.17 = bf16[32,1536]{1,0:T(8,128)(2,1)S(1)} collective-permute-done((bf16[32,1536]{1,0:T(8,128)(2,1)S(1)}, bf16[32,1536]{1,0:T(8,128)(2,1)S(1)}, u32[]{:S(2)}, u32[]{:S(2)}) %collective-permute-start.17) | collective-permute-done | bytes 98336 | tf_op jit(solution)/shard_map/ppermute | solution.py:39
  161.1 7.4 %convolution_convert_fusion = bf16[128,4096]{1,0:T(8,128)(2,1)} fusion(bf16[1536,4096]{1,0:T(8,128)(2,1)} %all-gather.2.cloned.1.call-done, bf16[32,1536]{1,0:T(8,128)(2,1)S(1)} %broadcast_select_fusion.4, bf16[32,1536]{1,0:T(8,128)(2,1)S(1)} %get-tuple-element.47, bf16[32,1536]{1,0:T(8,128)(2,1)S(1)} %get-tuple-element.46, ...), kind=kOutput, calls=%fused_computation.1 | convolution fusion | flops 1612709888 | bytes 14024704 | tf_op jit(solution)/shard_map/dot_general | solution.py:232
  (96 shorter events, 7.5 us)
Async XLA Ops:
  6.5 154.6 %all-gather.2.cloned.1.call-start = ((), (), s32[]{:S(2)}) async-start(), calls=%async_computation | async-start | bytes 12976128 | tf_op jit(solution)/shard_map/all_gather | solution.py:187
  8.2 4.7 %copy-start = (bf16[256,384]{1,0:T(8,128)(2,1)S(1)}, bf16[256,384]{1,0:T(8,128)(2,1)}, u32[]{:S(2)}) copy-start(bf16[256,384]{1,0:T(8,128)(2,1)} %q_ref.1) | copy-start | bytes 589828
  8.2 4.7 %copy-start.1 = (bf16[256,64]{0,1:T(8,128)(2,1)S(1)}, bf16[256,64]{0,1:T(8,128)(2,1)}, u32[]{:S(2)}) copy-start(bf16[256,64]{0,1:T(8,128)(2,1)} %param.15) | copy-start | bytes 98308
  8.2 31.4 %copy-start.5 = (bf16[24,4096]{1,0:T(8,128)(2,1)S(1)}, bf16[24,4096]{1,0:T(8,128)(2,1)}, u32[]{:S(2)}) copy-start(bf16[24,4096]{1,0:T(8,128)(2,1)} %param.16) | copy-start | bytes 589828
  8.4 31.2 %collective-permute-start.4 = (bf16[128,1024]{1,0:T(8,128)(2,1)S(1)}, bf16[128,1024]{1,0:T(8,128)(2,1)S(1)}, u32[]{:S(2)}, u32[]{:S(2)}) collective-permute-start(bf16[128,1024]{1,0:T(8,128)(2,1)S(1)} %pad_maximum_fusion.6), channel_id=1, source_target_pairs={{0,192},{1,193},{2,194},{3,195},{4,28},{5,29},{6,30},{7,31},{8,200... | collective-permute-start | bytes 786440 | tf_op jit(solution)/shard_map/ppermute | solution.py:43
  11.6 28.0 %collective-permute-start.3 = (bf16[128,1024]{1,0:T(8,128)(2,1)S(1)}, bf16[128,1024]{1,0:T(8,128)(2,1)S(1)}, u32[]{:S(2)}, u32[]{:S(2)}) collective-permute-start(bf16[128,1024]{1,0:T(8,128)(2,1)S(1)} %pad_maximum_fusion.5), channel_id=1, source_target_pairs={{0,128},{1,129},{2,130},{3,131},{4,20},{5,21},{6,22},{7,23},{8,136... | collective-permute-start | bytes 786440 | tf_op jit(solution)/shard_map/ppermute | solution.py:43
  12.3 27.3 %collective-permute-start.2 = (bf16[128,1024]{1,0:T(8,128)(2,1)S(1)}, bf16[128,1024]{1,0:T(8,128)(2,1)S(1)}, u32[]{:S(2)}, u32[]{:S(2)}) collective-permute-start(bf16[128,1024]{1,0:T(8,128)(2,1)S(1)} %pad_maximum_fusion.4), channel_id=1, source_target_pairs={{0,64},{1,65},{2,66},{3,67},{4,12},{5,13},{6,14},{7,15},{8,72},{9,... | collective-permute-start | bytes 786440 | tf_op jit(solution)/shard_map/ppermute | solution.py:43
  12.9 18.2 %collective-permute-start = (bf16[896,128]{1,0:T(8,128)(2,1)S(1)}, bf16[896,128]{1,0:T(8,128)(2,1)S(1)}, u32[]{:S(2)}, u32[]{:S(2)}) collective-permute-start(bf16[896,128]{1,0:T(8,128)(2,1)S(1)} %shard_map.118), channel_id=1, source_target_pairs={{0,0},{1,32},{2,4},{3,36},{4,64},{5,96},{6,68},{7,100},{8,8},{9,40... | collective-permute-start | bytes 688136 | tf_op jit(solution)/shard_map/ppermute | solution.py:43
  20.6 18.9 %collective-permute-start.1 = (bf16[896,128]{1,0:T(8,128)(2,1)S(1)}, bf16[896,128]{1,0:T(8,128)(2,1)S(1)}, u32[]{:S(2)}, u32[]{:S(2)}) collective-permute-start(bf16[896,128]{1,0:T(8,128)(2,1)S(1)} %shard_map.118), channel_id=1, source_target_pairs={{0,32},{1,0},{2,36},{3,4},{4,96},{5,64},{6,100},{7,68},{8,40},{9,8... | collective-permute-start | bytes 688136 | tf_op jit(solution)/shard_map/ppermute | solution.py:43
  39.6 10.8 %copy-start.4 = (bf16[128,1024]{1,0:T(8,128)(2,1)}, bf16[128,1024]{1,0:T(8,128)(2,1)S(1)}, u32[]{:S(2)}) copy-start(bf16[128,1024]{1,0:T(8,128)(2,1)S(1)} %collective-permute-done.2) | copy-start | bytes 786436
  39.6 9.8 %collective-permute-start.18 = (bf16[24,4096]{1,0:T(8,128)(2,1)S(1)}, bf16[24,4096]{1,0:T(8,128)(2,1)S(1)}, u32[]{:S(2)}, u32[]{:S(2)}) collective-permute-start(bf16[24,4096]{1,0:T(8,128)(2,1)S(1)} %copy-done.5), channel_id=1, source_target_pairs={{0,32},{32,0},{1,33},{33,1},{2,34},{34,2},{3,35},{35,3},{4,36},{36... | collective-permute-start | bytes 589832 | tf_op jit(solution)/shard_map/ppermute | solution.py:39
  50.3 1.9 %collective-permute-start.5 = (bf16[2,896,128]{2,1,0:T(8,128)(2,1)S(1)}, bf16[2,896,128]{2,1,0:T(8,128)(2,1)S(1)}, u32[]{:S(2)}, u32[]{:S(2)}) collective-permute-start(bf16[2,896,128]{2,1,0:T(8,128)(2,1)S(1)} %pad_maximum_fusion.2), channel_id=1, source_target_pairs={{0,4},{4,0},{1,5},{5,1},{2,6},{6,2},{3,7},{7,3},{8,12},{12,8},{9,1... | collective-permute-start | bytes 1376264 | tf_op jit(solution)/shard_map/ppermute | solution.py:39
  52.3 13.5 %collective-permute-start.6 = (bf16[4,896,128]{2,1,0:T(8,128)(2,1)S(1)}, bf16[4,896,128]{2,1,0:T(8,128)(2,1)S(1)}, u32[]{:S(2)}, u32[]{:S(2)}) collective-permute-start(bf16[4,896,128]{2,1,0:T(8,128)(2,1)S(1)} %pad_maximum_fusion.1.refs_0_), channel_id=1, source_target_pairs={{0,8},{1,9},{2,10},{3,11},{4,68},{5,69},{6,70},{7,71},{8,0},{9,1},... | collective-permute-start | bytes 2752520 | tf_op jit(solution)/shard_map/ppermute | solution.py:43
  53.9 27.7 %collective-permute-start.7 = (bf16[4,896,128]{2,1,0:T(8,128)(2,1)S(1)}, bf16[4,896,128]{2,1,0:T(8,128)(2,1)S(1)}, u32[]{:S(2)}, u32[]{:S(2)}) collective-permute-start(bf16[4,896,128]{2,1,0:T(8,128)(2,1)S(1)} %pad_maximum_fusion.1.refs_0_), channel_id=1, source_target_pairs={{0,16},{1,17},{2,18},{3,19},{4,132},{5,133},{6,134},{7,135},{8,24}... | collective-permute-start | bytes 2752520 | tf_op jit(solution)/shard_map/ppermute | solution.py:43
  56.6 30.3 %collective-permute-start.8 = (bf16[4,896,128]{2,1,0:T(8,128)(2,1)S(1)}, bf16[4,896,128]{2,1,0:T(8,128)(2,1)}, u32[]{:S(2)}, u32[]{:S(2)}) collective-permute-start(bf16[4,896,128]{2,1,0:T(8,128)(2,1)S(1)} %pad_maximum_fusion.1.refs_0_), channel_id=1, source_target_pairs={{0,24},{1,25},{2,26},{3,27},{4,196},{5,197},{6,198},{7,199},{8,16}... | collective-permute-start | bytes 2752520 | tf_op jit(solution)/shard_map/ppermute | solution.py:43
  81.6 0.9 copy-start.2
  87.0 1.2 copy-start.3
  91.9 10.5 %copy-start.6 = (f32[128,128]{1,0:T(8,128)S(1)}, f32[128,128]{1,0:T(8,128)}, u32[]{:S(2)}) copy-start(f32[128,128]{1,0:T(8,128)} %constant.76.clone) | copy-start | bytes 196612
  91.9 10.5 %copy-start.7 = (f32[128,128]{1,0:T(8,128)S(1)}, f32[128,128]{1,0:T(8,128)}, u32[]{:S(2)}) copy-start(f32[128,128]{1,0:T(8,128)} %constant.77.clone) | copy-start | bytes 196612
  92.8 24.1 %collective-permute-start.10 = (bf16[128,1792]{1,0:T(8,128)(2,1)}, bf16[128,1792]{1,0:T(8,128)(2,1)S(1)}, u32[]{:S(2)}, u32[]{:S(2)}) collective-permute-start(bf16[128,1792]{1,0:T(8,128)(2,1)} %get-tuple-element.23), channel_id=1, source_target_pairs={{0,128},{1,129},{2,130},{3,131},{4,20},{5,21},{6,22},{7,23},{8,136... | collective-permute-start | bytes 1376264 | tf_op jit(solution)/shard_map/ppermute | solution.py:43
  101.2 21.4 %collective-permute-start.11 = (bf16[128,1792]{1,0:T(8,128)(2,1)S(1)}, bf16[128,1792]{1,0:T(8,128)(2,1)S(1)}, u32[]{:S(2)}, u32[]{:S(2)}) collective-permute-start(bf16[128,1792]{1,0:T(8,128)(2,1)S(1)} %get-tuple-element.22), channel_id=1, source_target_pairs={{0,192},{1,193},{2,194},{3,195},{4,28},{5,29},{6,30},{7,31},{8,200... | collective-permute-start | bytes 1376264 | tf_op jit(solution)/shard_map/ppermute | solution.py:43
  101.6 31.9 %collective-permute-start.9 = (bf16[128,1792]{1,0:T(8,128)(2,1)S(1)}, bf16[128,1792]{1,0:T(8,128)(2,1)S(1)}, u32[]{:S(2)}, u32[]{:S(2)}) collective-permute-start(bf16[128,1792]{1,0:T(8,128)(2,1)S(1)} %get-tuple-element.21), channel_id=1, source_target_pairs={{0,64},{1,65},{2,66},{3,67},{4,12},{5,13},{6,14},{7,15},{8,72},{9,... | collective-permute-start | bytes 1376264 | tf_op jit(solution)/shard_map/ppermute | solution.py:43
  133.8 14.2 %collective-permute-start.14 = (bf16[32,2688]{1,0:T(8,128)(2,1)S(1)}, bf16[32,2688]{1,0:T(8,128)(2,1)S(1)}, u32[]{:S(2)}, u32[]{:S(2)}) collective-permute-start(bf16[32,2688]{1,0:T(8,128)(2,1)S(1)} %get-tuple-element.91), channel_id=1, source_target_pairs={{0,3},{1,2},{2,1},{3,0},{4,7},{5,6},{6,5},{7,4},{8,11},{9,10},{10,... | collective-permute-start | bytes 516104 | tf_op jit(solution)/shard_map/ppermute | solution.py:39
  135.3 12.7 %collective-permute-start.13 = (bf16[32,2688]{1,0:T(8,128)(2,1)S(1)}, bf16[32,2688]{1,0:T(8,128)(2,1)S(1)}, u32[]{:S(2)}, u32[]{:S(2)}) collective-permute-start(bf16[32,2688]{1,0:T(8,128)(2,1)S(1)} %get-tuple-element.90), channel_id=1, source_target_pairs={{0,2},{1,3},{2,0},{3,1},{4,6},{5,7},{6,4},{7,5},{8,10},{9,11},{10,... | collective-permute-start | bytes 516104 | tf_op jit(solution)/shard_map/ppermute | solution.py:39
  135.3 8.0 %collective-permute-start.12 = (bf16[32,2688]{1,0:T(8,128)(2,1)S(1)}, bf16[32,2688]{1,0:T(8,128)(2,1)S(1)}, u32[]{:S(2)}, u32[]{:S(2)}) collective-permute-start(bf16[32,2688]{1,0:T(8,128)(2,1)S(1)} %get-tuple-element.89), channel_id=1, source_target_pairs={{0,1},{1,0},{2,3},{3,2},{4,5},{5,4},{6,7},{7,6},{8,9},{9,8},{10,11... | collective-permute-start | bytes 516104 | tf_op jit(solution)/shard_map/ppermute | solution.py:39
  149.4 1.5 copy-start.8
  149.4 1.5 copy-start.9
  151.2 5.0 %collective-permute-start.15 = (bf16[32,1536]{1,0:T(8,128)(2,1)S(1)}, bf16[32,1536]{1,0:T(8,128)(2,1)S(1)}, u32[]{:S(2)}, u32[]{:S(2)}) collective-permute-start(bf16[32,1536]{1,0:T(8,128)(2,1)S(1)} %pad_maximum_fusion.7), channel_id=1, source_target_pairs={{0,3},{1,2},{2,1},{3,0},{4,7},{5,6},{6,5},{7,4},{8,11},{9,10},{10,... | collective-permute-start | bytes 294920 | tf_op jit(solution)/shard_map/ppermute | solution.py:39
  151.3 7.1 %collective-permute-start.16 = (bf16[32,1536]{1,0:T(8,128)(2,1)S(1)}, bf16[32,1536]{1,0:T(8,128)(2,1)S(1)}, u32[]{:S(2)}, u32[]{:S(2)}) collective-permute-start(bf16[32,1536]{1,0:T(8,128)(2,1)S(1)} %pad_maximum_fusion.7), channel_id=1, source_target_pairs={{0,2},{1,3},{2,0},{3,1},{4,6},{5,7},{6,4},{7,5},{8,10},{9,11},{10,... | collective-permute-start | bytes 294920 | tf_op jit(solution)/shard_map/ppermute | solution.py:39
  154.8 6.1 %collective-permute-start.17 = (bf16[32,1536]{1,0:T(8,128)(2,1)S(1)}, bf16[32,1536]{1,0:T(8,128)(2,1)S(1)}, u32[]{:S(2)}, u32[]{:S(2)}) collective-permute-start(bf16[32,1536]{1,0:T(8,128)(2,1)S(1)} %pad_maximum_fusion.7), channel_id=1, source_target_pairs={{0,1},{1,0},{2,3},{3,2},{4,5},{5,4},{6,7},{7,6},{8,9},{9,8},{10,11... | collective-permute-start | bytes 294920 | tf_op jit(solution)/shard_map/ppermute | solution.py:39
Sparse Core Ops, SparseCore 0:
  50.4 90.4 all-gather.1

commit v14 on v13

--- a/solution.py
+++ b/solution.py
@@ -183,12 +183,15 @@
     first, second, out_weight, *ring = lax.optimization_barrier((first, second, out_weight, *ring))
     inputs = jnp.concatenate([features(0)] + ring, axis=0)
 
-    wo_piece = jnp.concatenate([out_weight, swap(out_weight, "zh", 1)], axis=0)
-    wo = lax.all_gather(wo_piece, ("y", "x", "core"), axis=0, tiled=True)
-
     pair = jnp.stack([first, second])
     pair = jnp.concatenate([pair, swap(pair, "core", 1)], axis=0)
-    sent, total = project(inputs, [pair] + [along(pair, d, "x", "y") for d in (1, 2, 3)])
+    blocks = [along(pair, d, "x", "y") for d in (1, 2, 3)]
+    wo_other, *blocks = lax.optimization_barrier((swap(out_weight, "zh", 1), *blocks))
+    sent, total = project(inputs, [pair] + blocks)
+
+    wo_piece = jnp.concatenate([out_weight, wo_other], axis=0)
+    wo = lax.all_gather(wo_piece, ("y", "x", "core"), axis=0, tiled=True)
+
     for e in (1, 2, 3):
         total = total + along(sent[e - 1], e, "y", "x").astype(F32)
 

time: 176 us -> 160 us (0.909)
  the two profiles are of different devices: /device:TPU:32 before, /device:TPU:24 now
where the time goes in v14:
time: 160 us; the launch traced here: 158 us
  waiting for transfers between devices  90 us (56%)
  starting transfers between devices  33.1 us (21%)
  between operations  14.7 us (9%)
  matrix products  8.6 us (5%)
  other arithmetic  5.07 us (3%)
  local copies, waits for them, and re-layouts  3.98 us (2%)
  Pallas kernels  2.65 us (2%)
    ppermute x11, waiting for transfers between devices, move(): lax.ppermute(value, AXES, [(flat(*at), flat(*where(*at))) for at in every...  48.8 us
    ppermute x8, waiting for transfers between devices, swap(): return lax.ppermute(value, axis, [(i, i ^ d) for i in range(n)])  28.1 us
    ppermute x11, starting transfers between devices, move(): lax.ppermute(value, AXES, [(flat(*at), flat(*where(*at))) for at in every...  23.5 us
    all_gather x1, waiting for transfers between devices, body(): wo = lax.all_gather(wo_piece, ('y', 'x', 'core'), axis=0, tiled=True)  13.1 us
    ppermute x8, starting transfers between devices, swap(): return lax.ppermute(value, axis, [(i, i ^ d) for i in range(n)])  9.62 us
    dot_general x1, matrix products, body(): return jnp.dot(all_rows, wo, preferred_element_type=F32).astype(BF)  7.35 us
  transfers between devices with their start and end apart: 20, of which 14 were waited for; matrix products, arithmetic and copies ran while one was open for 3% of the time, Pallas kernels for 2%

profile of v14, /device:TPU:24, one launch (start us, length us, event | category | flops | bytes accessed | tf_op | source)
XLA Modules:
  0.0 158.1 jit_solution(8121455509431122766)
XLA Ops:
  6.5 1.6 %fusion.2 = (f32[128]{0:T(128)S(1)}, bf16[128,4096]{1,0:T(8,128)(2,1)S(1)}) fusion(bf16[128,4096]{1,0:T(8,128)(2,1)} %param.12, f32[4096]{0:T(1024)} %param.13), kind=kLoop, calls=%fused_computation.5 | loop fusion | flops 2621312 | bytes 2114048 | tf_op jit(solution)/shard_map/reduce_sum | solution.py:170
  8.4 2.0 %collective-permute-start.4 = (bf16[128,1024]{1,0:T(8,128)(2,1)S(1)}, bf16[128,1024]{1,0:T(8,128)(2,1)S(1)}, u32[]{:S(2)}, u32[]{:S(2)}) collective-permute-start(bf16[128,1024]{1,0:T(8,128)(2,1)S(1)} %pad_maximum_fusion.6), channel_id=1, source_target_pairs={{0,192},{1,193},{2,194},{3,195},{4,28},{5,29},{6,30},{7,31},{8,200... | collective-permute-start | bytes 786440 | tf_op jit(solution)/shard_map/ppermute | solution.py:43
  10.5 0.9 collective-permute-start.3
  11.5 1.4 collective-permute-start.2
  12.9 6.5 %collective-permute-start = (bf16[896,128]{1,0:T(8,128)(2,1)S(1)}, bf16[896,128]{1,0:T(8,128)(2,1)S(1)}, u32[]{:S(2)}, u32[]{:S(2)}) collective-permute-start(bf16[896,128]{1,0:T(8,128)(2,1)S(1)} %shard_map.118), channel_id=1, source_target_pairs={{0,0},{1,32},{2,4},{3,36},{4,64},{5,96},{6,68},{7,100},{8,8},{9,40... | collective-permute-start | bytes 688136 | tf_op jit(solution)/shard_map/ppermute | solution.py:43
  19.4 3.2 %collective-permute-start.1 = (bf16[896,128]{1,0:T(8,128)(2,1)S(1)}, bf16[896,128]{1,0:T(8,128)(2,1)S(1)}, u32[]{:S(2)}, u32[]{:S(2)}) collective-permute-start(bf16[896,128]{1,0:T(8,128)(2,1)S(1)} %shard_map.118), channel_id=1, source_target_pairs={{0,32},{1,0},{2,36},{3,4},{4,96},{5,64},{6,100},{7,68},{8,40},{9,8... | collective-permute-start | bytes 688136 | tf_op jit(solution)/shard_map/ppermute | solution.py:43
  22.6 5.6 %collective-permute-done = bf16[896,128]{1,0:T(8,128)(2,1)S(1)} collective-permute-done((bf16[896,128]{1,0:T(8,128)(2,1)S(1)}, bf16[896,128]{1,0:T(8,128)(2,1)S(1)}, u32[]{:S(2)}, u32[]{:S(2)}) %collective-permute-start) | collective-permute-done | bytes 229408 | tf_op jit(solution)/shard_map/ppermute | solution.py:43
  28.1 13.8 %collective-permute-done.1 = bf16[896,128]{1,0:T(8,128)(2,1)S(1)} collective-permute-done((bf16[896,128]{1,0:T(8,128)(2,1)S(1)}, bf16[896,128]{1,0:T(8,128)(2,1)S(1)}, u32[]{:S(2)}, u32[]{:S(2)}) %collective-permute-start.1) | collective-permute-done | bytes 229408 | tf_op jit(solution)/shard_map/ppermute | solution.py:43
  42.1 1.8 %collective-permute-done.5 = bf16[2,896,128]{2,1,0:T(8,128)(2,1)S(1)} collective-permute-done((bf16[2,896,128]{2,1,0:T(8,128)(2,1)S(1)}, bf16[2,896,128]{2,1,0:T(8,128)(2,1)S(1)}, u32[]{:S(2)}, u32[]{:S(2)}) %collective-permute-start.5) | collective-permute-done | bytes 458784 | tf_op jit(solution)/shard_map/ppermute | solution.py:39
  44.0 1.6 collective-permute-start.7
  45.6 2.7 %collective-permute-start.8 = (bf16[4,896,128]{2,1,0:T(8,128)(2,1)S(1)}, bf16[4,896,128]{2,1,0:T(8,128)(2,1)S(1)}, u32[]{:S(2)}, u32[]{:S(2)}) collective-permute-start(bf16[4,896,128]{2,1,0:T(8,128)(2,1)S(1)} %pad_maximum_fusion.1.refs_0_), channel_id=1, source_target_pairs={{0,16},{1,17},{2,18},{3,19},{4,132},{5,133},{6,134},{7,135},{8,24}... | collective-permute-start | bytes 2752520 | tf_op jit(solution)/shard_map/ppermute | solution.py:43
  48.8 11.0 %collective-permute-done.6 = bf16[24,4096]{1,0:T(8,128)(2,1)S(1)} collective-permute-done((bf16[24,4096]{1,0:T(8,128)(2,1)S(1)}, bf16[24,4096]{1,0:T(8,128)(2,1)S(1)}, u32[]{:S(2)}, u32[]{:S(2)}) %collective-permute-start.6) | collective-permute-done | bytes 196640 | tf_op jit(solution)/shard_map/ppermute | solution.py:39
  59.7 9.8 %collective-permute-done.8.refs_2_ = bf16[4,896,128]{2,1,0:T(8,128)(2,1)S(1)} collective-permute-done((bf16[4,896,128]{2,1,0:T(8,128)(2,1)S(1)}, bf16[4,896,128]{2,1,0:T(8,128)(2,1)S(1)}, u32[]{:S(2)}, u32[]{:S(2)}) %collective-permute-start.8) | collective-permute-done | bytes 917536 | tf_op jit(solution)/shard_map/ppermute | solution.py:43
  69.6 3.1 %collective-permute-done.9.refs_3_ = bf16[4,896,128]{2,1,0:T(8,128)(2,1)S(1)} collective-permute-done((bf16[4,896,128]{2,1,0:T(8,128)(2,1)S(1)}, bf16[4,896,128]{2,1,0:T(8,128)(2,1)S(1)}, u32[]{:S(2)}, u32[]{:S(2)}) %collective-permute-start.9) | collective-permute-done | bytes 917536 | tf_op jit(solution)/shard_map/ppermute | solution.py:43
  72.7 0.9 copy-done.4
  75.2 1.0 pad_maximum_fusion.x_ref
  76.3 1.2 copy-done.3
  77.5 2.6 %shard_map.119 = (bf16[3,128,1792]{2,1,0:T(8,128)(2,1)S(1)}, f32[128,1792]{1,0:T(8,128)S(1)}) custom-call(bf16[512,1024]{1,0:T(8,128)(2,1)S(1)} %pad_maximum_fusion.x_ref, bf16[4,896,128]{2,1,0:T(8,128)(2,1)S(1)} %pad_maximum_fusion.1.refs_0_, bf16[4,896,128]{2,1,0:T(8,128)(2,1)S(1)} %collective-permute-done.7.refs_1_, bf16[4,896,128]{2,1,0:T(8,128)(2,1)S(1)} %copy-done.3, ...), custom_call_target="tpu_custom_call" | custom-call | flops 1879048192 | bytes 8000000 | tf_op jit(solution)/shard_map/pallas_call | solution.py:141
  80.1 0.9 slice_bitcast_fusion.2
  81.0 4.7 %collective-permute-start.12 = (bf16[128,1792]{1,0:T(8,128)(2,1)S(1)}, bf16[128,1792]{1,0:T(8,128)(2,1)S(1)}, u32[]{:S(2)}, u32[]{:S(2)}) collective-permute-start(bf16[128,1792]{1,0:T(8,128)(2,1)S(1)} %get-tuple-element.30), channel_id=1, source_target_pairs={{0,192},{1,193},{2,194},{3,195},{4,28},{5,29},{6,30},{7,31},{8,200... | collective-permute-start | bytes 1376264 | tf_op jit(solution)/shard_map/ppermute | solution.py:43
  85.7 6.0 %collective-permute-done.10 = bf16[128,1792]{1,0:T(8,128)(2,1)S(1)} collective-permute-done((bf16[128,1792]{1,0:T(8,128)(2,1)}, bf16[128,1792]{1,0:T(8,128)(2,1)S(1)}, u32[]{:S(2)}, u32[]{:S(2)}) %collective-permute-start.10) | collective-permute-done | bytes 458784 | tf_op jit(solution)/shard_map/ppermute | solution.py:43
  91.8 4.1 %collective-permute-done.11 = bf16[128,1792]{1,0:T(8,128)(2,1)S(1)} collective-permute-done((bf16[128,1792]{1,0:T(8,128)(2,1)S(1)}, bf16[128,1792]{1,0:T(8,128)(2,1)S(1)}, u32[]{:S(2)}, u32[]{:S(2)}) %collective-permute-start.11) | collective-permute-done | bytes 458784 | tf_op jit(solution)/shard_map/ppermute | solution.py:43
  95.8 6.4 %collective-permute-done.12 = bf16[128,1792]{1,0:T(8,128)(2,1)S(1)} collective-permute-done((bf16[128,1792]{1,0:T(8,128)(2,1)S(1)}, bf16[128,1792]{1,0:T(8,128)(2,1)S(1)}, u32[]{:S(2)}, u32[]{:S(2)}) %collective-permute-start.12) | collective-permute-done | bytes 458784 | tf_op jit(solution)/shard_map/ppermute | solution.py:43
  102.6 4.3 %collective-permute-start.15 = (bf16[32,2688]{1,0:T(8,128)(2,1)S(1)}, bf16[32,2688]{1,0:T(8,128)(2,1)S(1)}, u32[]{:S(2)}, u32[]{:S(2)}) collective-permute-start(bf16[32,2688]{1,0:T(8,128)(2,1)S(1)} %get-tuple-element.99), channel_id=1, source_target_pairs={{0,3},{1,2},{2,1},{3,0},{4,7},{5,6},{6,5},{7,4},{8,11},{9,10},{10,... | collective-permute-start | bytes 516104 | tf_op jit(solution)/shard_map/ppermute | solution.py:39
  107.7 5.9 %collective-permute-done.13 = bf16[32,2688]{1,0:T(8,128)(2,1)S(1)} collective-permute-done((bf16[32,2688]{1,0:T(8,128)(2,1)S(1)}, bf16[32,2688]{1,0:T(8,128)(2,1)S(1)}, u32[]{:S(2)}, u32[]{:S(2)}) %collective-permute-start.13) | collective-permute-done | bytes 172064 | tf_op jit(solution)/shard_map/ppermute | solution.py:39
  113.6 3.6 %collective-permute-done.14 = bf16[32,2688]{1,0:T(8,128)(2,1)S(1)} collective-permute-done((bf16[32,2688]{1,0:T(8,128)(2,1)S(1)}, bf16[32,2688]{1,0:T(8,128)(2,1)S(1)}, u32[]{:S(2)}, u32[]{:S(2)}) %collective-permute-start.14) | collective-permute-done | bytes 172064 | tf_op jit(solution)/shard_map/ppermute | solution.py:39
  120.4 2.7 %collective-permute-start.16 = (bf16[32,1536]{1,0:T(8,128)(2,1)S(1)}, bf16[32,1536]{1,0:T(8,128)(2,1)S(1)}, u32[]{:S(2)}, u32[]{:S(2)}) collective-permute-start(bf16[32,1536]{1,0:T(8,128)(2,1)S(1)} %pad_maximum_fusion.7), channel_id=1, source_target_pairs={{0,3},{1,2},{2,1},{3,0},{4,7},{5,6},{6,5},{7,4},{8,11},{9,10},{10,... | collective-permute-start | bytes 294920 | tf_op jit(solution)/shard_map/ppermute | solution.py:39
  123.1 1.7 %collective-permute-start.18 = (bf16[32,1536]{1,0:T(8,128)(2,1)S(1)}, bf16[32,1536]{1,0:T(8,128)(2,1)S(1)}, u32[]{:S(2)}, u32[]{:S(2)}) collective-permute-start(bf16[32,1536]{1,0:T(8,128)(2,1)S(1)} %pad_maximum_fusion.7), channel_id=1, source_target_pairs={{0,1},{1,0},{2,3},{3,2},{4,5},{5,4},{6,7},{7,6},{8,9},{9,8},{10,11... | collective-permute-start | bytes 294920 | tf_op jit(solution)/shard_map/ppermute | solution.py:39
  124.9 2.2 %collective-permute-done.16 = bf16[32,1536]{1,0:T(8,128)(2,1)S(1)} collective-permute-done((bf16[32,1536]{1,0:T(8,128)(2,1)S(1)}, bf16[32,1536]{1,0:T(8,128)(2,1)S(1)}, u32[]{:S(2)}, u32[]{:S(2)}) %collective-permute-start.16) | collective-permute-done | bytes 98336 | tf_op jit(solution)/shard_map/ppermute | solution.py:39
  127.0 3.6 %collective-permute-done.17 = bf16[32,1536]{1,0:T(8,128)(2,1)S(1)} collective-permute-done((bf16[32,1536]{1,0:T(8,128)(2,1)S(1)}, bf16[32,1536]{1,0:T(8,128)(2,1)S(1)}, u32[]{:S(2)}, u32[]{:S(2)}) %collective-permute-start.17) | collective-permute-done | bytes 98336 | tf_op jit(solution)/shard_map/ppermute | solution.py:39
  130.8 13.1 %all-gather.2.cloned.1.call-done = bf16[1536,4096]{1,0:T(8,128)(2,1)} async-done(((bf16[48,4096]{1,0:T(8,128)(2,1)}), bf16[1536,4096]{1,0:T(8,128)(2,1)}) %all-gather.2.cloned.1.call-update) | async-done | bytes 12582928 | tf_op jit(solution)/shard_map/all_gather | solution.py:193
  143.9 7.3 %convolution_convert_fusion = bf16[128,4096]{1,0:T(8,128)(2,1)} fusion(bf16[1536,4096]{1,0:T(8,128)(2,1)} %all-gather.2.cloned.1.call-done, bf16[32,1536]{1,0:T(8,128)(2,1)S(1)} %broadcast_select_fusion.4, bf16[32,1536]{1,0:T(8,128)(2,1)S(1)} %get-tuple-element.55, bf16[32,1536]{1,0:T(8,128)(2,1)S(1)} %get-tuple-element.54, ...), kind=kOutput, calls=%fused_computation.1 | convolution fusion | flops 1612709888 | bytes 14024704 | tf_op jit(solution)/shard_map/dot_general | solution.py:235
  (100 shorter events, 6.1 us)
Async XLA Ops:
  6.5 137.3 %all-gather.2.cloned.1.call-start = ((), (), s32[]{:S(2)}) async-start(), calls=%async_computation | async-start | bytes 12976128 | tf_op jit(solution)/shard_map/all_gather | solution.py:193
  8.2 4.7 %copy-start = (bf16[256,384]{1,0:T(8,128)(2,1)S(1)}, bf16[256,384]{1,0:T(8,128)(2,1)}, u32[]{:S(2)}) copy-start(bf16[256,384]{1,0:T(8,128)(2,1)} %q_ref.1) | copy-start | bytes 589828
  8.2 4.7 %copy-start.1 = (bf16[256,64]{0,1:T(8,128)(2,1)S(1)}, bf16[256,64]{0,1:T(8,128)(2,1)}, u32[]{:S(2)}) copy-start(bf16[256,64]{0,1:T(8,128)(2,1)} %param.15) | copy-start | bytes 98308
  8.4 33.5 %collective-permute-start.4 = (bf16[128,1024]{1,0:T(8,128)(2,1)S(1)}, bf16[128,1024]{1,0:T(8,128)(2,1)S(1)}, u32[]{:S(2)}, u32[]{:S(2)}) collective-permute-start(bf16[128,1024]{1,0:T(8,128)(2,1)S(1)} %pad_maximum_fusion.6), channel_id=1, source_target_pairs={{0,192},{1,193},{2,194},{3,195},{4,28},{5,29},{6,30},{7,31},{8,200... | collective-permute-start | bytes 786440 | tf_op jit(solution)/shard_map/ppermute | solution.py:43
  10.5 38.3 %copy-start.7 = (bf16[24,4096]{1,0:T(8,128)(2,1)S(1)}, bf16[24,4096]{1,0:T(8,128)(2,1)}, u32[]{:S(2)}) copy-start(bf16[24,4096]{1,0:T(8,128)(2,1)} %param.16) | copy-start | bytes 589828
  10.5 31.4 %collective-permute-start.3 = (bf16[128,1024]{1,0:T(8,128)(2,1)S(1)}, bf16[128,1024]{1,0:T(8,128)(2,1)S(1)}, u32[]{:S(2)}, u32[]{:S(2)}) collective-permute-start(bf16[128,1024]{1,0:T(8,128)(2,1)S(1)} %pad_maximum_fusion.5), channel_id=1, source_target_pairs={{0,128},{1,129},{2,130},{3,131},{4,20},{5,21},{6,22},{7,23},{8,136... | collective-permute-start | bytes 786440 | tf_op jit(solution)/shard_map/ppermute | solution.py:43
  11.5 30.5 %collective-permute-start.2 = (bf16[128,1024]{1,0:T(8,128)(2,1)S(1)}, bf16[128,1024]{1,0:T(8,128)(2,1)S(1)}, u32[]{:S(2)}, u32[]{:S(2)}) collective-permute-start(bf16[128,1024]{1,0:T(8,128)(2,1)S(1)} %pad_maximum_fusion.4), channel_id=1, source_target_pairs={{0,64},{1,65},{2,66},{3,67},{4,12},{5,13},{6,14},{7,15},{8,72},{9,... | collective-permute-start | bytes 786440 | tf_op jit(solution)/shard_map/ppermute | solution.py:43
  12.9 15.3 %collective-permute-start = (bf16[896,128]{1,0:T(8,128)(2,1)S(1)}, bf16[896,128]{1,0:T(8,128)(2,1)S(1)}, u32[]{:S(2)}, u32[]{:S(2)}) collective-permute-start(bf16[896,128]{1,0:T(8,128)(2,1)S(1)} %shard_map.118), channel_id=1, source_target_pairs={{0,0},{1,32},{2,4},{3,36},{4,64},{5,96},{6,68},{7,100},{8,8},{9,40... | collective-permute-start | bytes 688136 | tf_op jit(solution)/shard_map/ppermute | solution.py:43
  19.4 22.5 %collective-permute-start.1 = (bf16[896,128]{1,0:T(8,128)(2,1)S(1)}, bf16[896,128]{1,0:T(8,128)(2,1)S(1)}, u32[]{:S(2)}, u32[]{:S(2)}) collective-permute-start(bf16[896,128]{1,0:T(8,128)(2,1)S(1)} %shard_map.118), channel_id=1, source_target_pairs={{0,32},{1,0},{2,36},{3,4},{4,96},{5,64},{6,100},{7,68},{8,40},{9,8... | collective-permute-start | bytes 688136 | tf_op jit(solution)/shard_map/ppermute | solution.py:43
  41.9 30.8 %copy-start.6 = (bf16[128,1024]{1,0:T(8,128)(2,1)}, bf16[128,1024]{1,0:T(8,128)(2,1)S(1)}, u32[]{:S(2)}) copy-start(bf16[128,1024]{1,0:T(8,128)(2,1)S(1)} %collective-permute-done.2) | copy-start | bytes 786436
  42.0 1.9 %collective-permute-start.5 = (bf16[2,896,128]{2,1,0:T(8,128)(2,1)S(1)}, bf16[2,896,128]{2,1,0:T(8,128)(2,1)S(1)}, u32[]{:S(2)}, u32[]{:S(2)}) collective-permute-start(bf16[2,896,128]{2,1,0:T(8,128)(2,1)S(1)} %pad_maximum_fusion.2), channel_id=1, source_target_pairs={{0,4},{4,0},{1,5},{5,1},{2,6},{6,2},{3,7},{7,3},{8,12},{12,8},{9,1... | collective-permute-start | bytes 1376264 | tf_op jit(solution)/shard_map/ppermute | solution.py:39
  44.0 15.8 %collective-permute-start.7 = (bf16[4,896,128]{2,1,0:T(8,128)(2,1)S(1)}, bf16[4,896,128]{2,1,0:T(8,128)(2,1)S(1)}, u32[]{:S(2)}, u32[]{:S(2)}) collective-permute-start(bf16[4,896,128]{2,1,0:T(8,128)(2,1)S(1)} %pad_maximum_fusion.1.refs_0_), channel_id=1, source_target_pairs={{0,8},{1,9},{2,10},{3,11},{4,68},{5,69},{6,70},{7,71},{8,0},{9,1},... | collective-permute-start | bytes 2752520 | tf_op jit(solution)/shard_map/ppermute | solution.py:43
  45.6 24.0 %collective-permute-start.8 = (bf16[4,896,128]{2,1,0:T(8,128)(2,1)S(1)}, bf16[4,896,128]{2,1,0:T(8,128)(2,1)S(1)}, u32[]{:S(2)}, u32[]{:S(2)}) collective-permute-start(bf16[4,896,128]{2,1,0:T(8,128)(2,1)S(1)} %pad_maximum_fusion.1.refs_0_), channel_id=1, source_target_pairs={{0,16},{1,17},{2,18},{3,19},{4,132},{5,133},{6,134},{7,135},{8,24}... | collective-permute-start | bytes 2752520 | tf_op jit(solution)/shard_map/ppermute | solution.py:43
  48.3 24.4 %collective-permute-start.9 = (bf16[4,896,128]{2,1,0:T(8,128)(2,1)S(1)}, bf16[4,896,128]{2,1,0:T(8,128)(2,1)S(1)}, u32[]{:S(2)}, u32[]{:S(2)}) collective-permute-start(bf16[4,896,128]{2,1,0:T(8,128)(2,1)S(1)} %pad_maximum_fusion.1.refs_0_), channel_id=1, source_target_pairs={{0,24},{1,25},{2,26},{3,27},{4,196},{5,197},{6,198},{7,199},{8,16}... | collective-permute-start | bytes 2752520 | tf_op jit(solution)/shard_map/ppermute | solution.py:43
  48.8 11.0 %collective-permute-start.6 = (bf16[24,4096]{1,0:T(8,128)(2,1)S(1)}, bf16[24,4096]{1,0:T(8,128)(2,1)S(1)}, u32[]{:S(2)}, u32[]{:S(2)}) collective-permute-start(bf16[24,4096]{1,0:T(8,128)(2,1)S(1)} %copy-done.7), channel_id=1, source_target_pairs={{0,32},{32,0},{1,33},{33,1},{2,34},{34,2},{3,35},{35,3},{4,36},{36... | collective-permute-start | bytes 589832 | tf_op jit(solution)/shard_map/ppermute | solution.py:39
  69.6 5.6 %copy-start.2 = (bf16[4,896,128]{2,1,0:T(8,128)(2,1)}, bf16[4,896,128]{2,1,0:T(8,128)(2,1)S(1)}, u32[]{:S(2)}) copy-start(bf16[4,896,128]{2,1,0:T(8,128)(2,1)S(1)} %collective-permute-done.8.refs_2_) | copy-start | bytes 2752516
  72.7 0.9 copy-start.4
  74.5 1.8 %copy-start.5 = (bf16[4,896,128]{2,1,0:T(8,128)(2,1)S(1)}, bf16[4,896,128]{2,1,0:T(8,128)(2,1)}, u32[]{:S(2)}) copy-start(bf16[4,896,128]{2,1,0:T(8,128)(2,1)} %copy-done.4) | copy-start | bytes 2752516
  76.3 1.2 copy-start.3
  80.1 5.6 %copy-start.8 = (f32[128,128]{1,0:T(8,128)S(1)}, f32[128,128]{1,0:T(8,128)}, u32[]{:S(2)}) copy-start(f32[128,128]{1,0:T(8,128)} %constant.76.clone) | copy-start | bytes 196612
  80.1 5.6 %copy-start.9 = (f32[128,128]{1,0:T(8,128)S(1)}, f32[128,128]{1,0:T(8,128)}, u32[]{:S(2)}) copy-start(f32[128,128]{1,0:T(8,128)} %constant.77.clone) | copy-start | bytes 196612
  81.0 10.8 %collective-permute-start.10 = (bf16[128,1792]{1,0:T(8,128)(2,1)}, bf16[128,1792]{1,0:T(8,128)(2,1)S(1)}, u32[]{:S(2)}, u32[]{:S(2)}) collective-permute-start(bf16[128,1792]{1,0:T(8,128)(2,1)} %get-tuple-element.29), channel_id=1, source_target_pairs={{0,64},{1,65},{2,66},{3,67},{4,12},{5,13},{6,14},{7,15},{8,72},{9,... | collective-permute-start | bytes 1376264 | tf_op jit(solution)/shard_map/ppermute | solution.py:43
  81.0 14.9 %collective-permute-start.11 = (bf16[128,1792]{1,0:T(8,128)(2,1)S(1)}, bf16[128,1792]{1,0:T(8,128)(2,1)S(1)}, u32[]{:S(2)}, u32[]{:S(2)}) collective-permute-start(bf16[128,1792]{1,0:T(8,128)(2,1)S(1)} %get-tuple-element.31), channel_id=1, source_target_pairs={{0,128},{1,129},{2,130},{3,131},{4,20},{5,21},{6,22},{7,23},{8,136... | collective-permute-start | bytes 1376264 | tf_op jit(solution)/shard_map/ppermute | solution.py:43
  81.0 21.2 %collective-permute-start.12 = (bf16[128,1792]{1,0:T(8,128)(2,1)S(1)}, bf16[128,1792]{1,0:T(8,128)(2,1)S(1)}, u32[]{:S(2)}, u32[]{:S(2)}) collective-permute-start(bf16[128,1792]{1,0:T(8,128)(2,1)S(1)} %get-tuple-element.30), channel_id=1, source_target_pairs={{0,192},{1,193},{2,194},{3,195},{4,28},{5,29},{6,30},{7,31},{8,200... | collective-permute-start | bytes 1376264 | tf_op jit(solution)/shard_map/ppermute | solution.py:43
  102.6 14.7 %collective-permute-start.15 = (bf16[32,2688]{1,0:T(8,128)(2,1)S(1)}, bf16[32,2688]{1,0:T(8,128)(2,1)S(1)}, u32[]{:S(2)}, u32[]{:S(2)}) collective-permute-start(bf16[32,2688]{1,0:T(8,128)(2,1)S(1)} %get-tuple-element.99), channel_id=1, source_target_pairs={{0,3},{1,2},{2,1},{3,0},{4,7},{5,6},{6,5},{7,4},{8,11},{9,10},{10,... | collective-permute-start | bytes 516104 | tf_op jit(solution)/shard_map/ppermute | solution.py:39
  106.9 10.3 %collective-permute-start.14 = (bf16[32,2688]{1,0:T(8,128)(2,1)S(1)}, bf16[32,2688]{1,0:T(8,128)(2,1)S(1)}, u32[]{:S(2)}, u32[]{:S(2)}) collective-permute-start(bf16[32,2688]{1,0:T(8,128)(2,1)S(1)} %get-tuple-element.98), channel_id=1, source_target_pairs={{0,2},{1,3},{2,0},{3,1},{4,6},{5,7},{6,4},{7,5},{8,10},{9,11},{10,... | collective-permute-start | bytes 516104 | tf_op jit(solution)/shard_map/ppermute | solution.py:39
  107.0 6.7 %collective-permute-start.13 = (bf16[32,2688]{1,0:T(8,128)(2,1)S(1)}, bf16[32,2688]{1,0:T(8,128)(2,1)S(1)}, u32[]{:S(2)}, u32[]{:S(2)}) collective-permute-start(bf16[32,2688]{1,0:T(8,128)(2,1)S(1)} %get-tuple-element.97), channel_id=1, source_target_pairs={{0,1},{1,0},{2,3},{3,2},{4,5},{5,4},{6,7},{7,6},{8,9},{9,8},{10,11... | collective-permute-start | bytes 516104 | tf_op jit(solution)/shard_map/ppermute | solution.py:39
  118.6 1.5 copy-start.10
  118.6 1.5 copy-start.11
  120.4 6.6 %collective-permute-start.16 = (bf16[32,1536]{1,0:T(8,128)(2,1)S(1)}, bf16[32,1536]{1,0:T(8,128)(2,1)S(1)}, u32[]{:S(2)}, u32[]{:S(2)}) collective-permute-start(bf16[32,1536]{1,0:T(8,128)(2,1)S(1)} %pad_maximum_fusion.7), channel_id=1, source_target_pairs={{0,3},{1,2},{2,1},{3,0},{4,7},{5,6},{6,5},{7,4},{8,11},{9,10},{10,... | collective-permute-start | bytes 294920 | tf_op jit(solution)/shard_map/ppermute | solution.py:39
  123.1 7.5 %collective-permute-start.17 = (bf16[32,1536]{1,0:T(8,128)(2,1)S(1)}, bf16[32,1536]{1,0:T(8,128)(2,1)S(1)}, u32[]{:S(2)}, u32[]{:S(2)}) collective-permute-start(bf16[32,1536]{1,0:T(8,128)(2,1)S(1)} %pad_maximum_fusion.7), channel_id=1, source_target_pairs={{0,2},{1,3},{2,0},{3,1},{4,6},{5,7},{6,4},{7,5},{8,10},{9,11},{10,... | collective-permute-start | bytes 294920 | tf_op jit(solution)/shard_map/ppermute | solution.py:39
  123.1 7.5 %collective-permute-start.18 = (bf16[32,1536]{1,0:T(8,128)(2,1)S(1)}, bf16[32,1536]{1,0:T(8,128)(2,1)S(1)}, u32[]{:S(2)}, u32[]{:S(2)}) collective-permute-start(bf16[32,1536]{1,0:T(8,128)(2,1)S(1)} %pad_maximum_fusion.7), channel_id=1, source_target_pairs={{0,1},{1,0},{2,3},{3,2},{4,5},{5,4},{6,7},{7,6},{8,9},{9,8},{10,11... | collective-permute-start | bytes 294920 | tf_op jit(solution)/shard_map/ppermute | solution.py:39
Sparse Core Ops, SparseCore 0:
  74.6 69.2 all-gather.1

commit v15 on v14

--- a/solution.py
+++ b/solution.py
@@ -185,9 +185,9 @@
 
     pair = jnp.stack([first, second])
     pair = jnp.concatenate([pair, swap(pair, "core", 1)], axis=0)
-    blocks = [along(pair, d, "x", "y") for d in (1, 2, 3)]
-    wo_other, *blocks = lax.optimization_barrier((swap(out_weight, "zh", 1), *blocks))
-    sent, total = project(inputs, [pair] + blocks)
+    wo_other, pair, opposite = lax.optimization_barrier((swap(out_weight, "zh", 1), pair, along(pair, 2, "x", "y")))
+    blocks = [pair, along(pair, 1, "x", "y"), opposite, along(pair, 3, "x", "y")]
+    sent, total = project(inputs, blocks)
 
     wo_piece = jnp.concatenate([out_weight, wo_other], axis=0)
     wo = lax.all_gather(wo_piece, ("y", "x", "core"), axis=0, tiled=True)

time: 160 us -> 145 us (0.906)
  waiting for transfers between devices: 90 us -> 72.6 us
    all_gather x1, waiting for transfers between devices: 13.1 us -> 0.02 us  [body(): wo = lax.all_gather(wo_piece, ('y', 'x', 'core'), axis=0, tiled=True)]
    ppermute x11, waiting for transfers between devices: 48.8 us -> 42.6 us  [move(): lax.ppermute(value, AXES, [(flat(*at), flat(*where(*at))) for at in every...]
    ppermute x11, starting transfers between devices: 23.5 us -> 25.5 us  [move(): lax.ppermute(value, AXES, [(flat(*at), flat(*where(*at))) for at in every...]
    ppermute x8, waiting for transfers between devices: 28.1 us -> 30 us  [swap(): return lax.ppermute(value, axis, [(i, i ^ d) for i in range(n)])]
  transfers between devices with their start and end apart: 20 -> 20, of which waited for: 14 -> 14; matrix products, arithmetic and copies ran while one was open for 3% -> 4% of each run, Pallas kernels for 2% -> 3%
where the time goes in v15:
time: 145 us; the launch traced here: 143 us
  waiting for transfers between devices  72.6 us (50%)
  starting transfers between devices  34.6 us (24%)
  between operations  14.6 us (10%)
  matrix products  8.6 us (6%)
  other arithmetic  5.07 us (3%)
  local copies, waits for them, and re-layouts  3.99 us (3%)
  Pallas kernels  3.82 us (3%)
    ppermute x11, waiting for transfers between devices, move(): lax.ppermute(value, AXES, [(flat(*at), flat(*where(*at))) for at in every...  42.6 us
    ppermute x8, waiting for transfers between devices, swap(): return lax.ppermute(value, axis, [(i, i ^ d) for i in range(n)])  30 us
    ppermute x11, starting transfers between devices, move(): lax.ppermute(value, AXES, [(flat(*at), flat(*where(*at))) for at in every...  25.5 us
    ppermute x8, starting transfers between devices, swap(): return lax.ppermute(value, axis, [(i, i ^ d) for i in range(n)])  9.08 us
    dot_general x1, matrix products, body(): return jnp.dot(all_rows, wo, preferred_element_type=F32).astype(BF)  7.35 us
    pallas_call x1, Pallas kernels, project(): pl.pallas_call(project_kernel, out_shape=(jax.ShapeDtypeStruct((3, ROWS,...  3.78 us
  transfers between devices with their start and end apart: 20, of which 14 were waited for; matrix products, arithmetic and copies ran while one was open for 4% of the time, Pallas kernels for 3%

profile of v15, /device:TPU:24, one launch (start us, length us, event | category | flops | bytes accessed | tf_op | source)
XLA Modules:
  0.0 143.3 jit_solution(4049129567302046596)
XLA Ops:
  6.5 1.6 %fusion.2 = (f32[128]{0:T(128)S(1)}, bf16[128,4096]{1,0:T(8,128)(2,1)S(1)}) fusion(bf16[128,4096]{1,0:T(8,128)(2,1)} %param.12, f32[4096]{0:T(1024)} %param.13), kind=kLoop, calls=%fused_computation.5 | loop fusion | flops 2621312 | bytes 2114048 | tf_op jit(solution)/shard_map/reduce_sum | solution.py:170
  8.4 2.0 %collective-permute-start.4 = (bf16[128,1024]{1,0:T(8,128)(2,1)S(1)}, bf16[128,1024]{1,0:T(8,128)(2,1)S(1)}, u32[]{:S(2)}, u32[]{:S(2)}) collective-permute-start(bf16[128,1024]{1,0:T(8,128)(2,1)S(1)} %pad_maximum_fusion.6), channel_id=1, source_target_pairs={{0,192},{1,193},{2,194},{3,195},{4,28},{5,29},{6,30},{7,31},{8,200... | collective-permute-start | bytes 786440 | tf_op jit(solution)/shard_map/ppermute | solution.py:43
  10.5 0.9 collective-permute-start.3
  11.5 1.4 collective-permute-start.2
  12.9 6.5 %collective-permute-start = (bf16[896,128]{1,0:T(8,128)(2,1)S(1)}, bf16[896,128]{1,0:T(8,128)(2,1)S(1)}, u32[]{:S(2)}, u32[]{:S(2)}) collective-permute-start(bf16[896,128]{1,0:T(8,128)(2,1)S(1)} %shard_map.118), channel_id=1, source_target_pairs={{0,0},{1,32},{2,4},{3,36},{4,64},{5,96},{6,68},{7,100},{8,8},{9,40... | collective-permute-start | bytes 688136 | tf_op jit(solution)/shard_map/ppermute | solution.py:43
  19.4 3.2 %collective-permute-start.1 = (bf16[896,128]{1,0:T(8,128)(2,1)S(1)}, bf16[896,128]{1,0:T(8,128)(2,1)S(1)}, u32[]{:S(2)}, u32[]{:S(2)}) collective-permute-start(bf16[896,128]{1,0:T(8,128)(2,1)S(1)} %shard_map.118), channel_id=1, source_target_pairs={{0,32},{1,0},{2,36},{3,4},{4,96},{5,64},{6,100},{7,68},{8,40},{9,8... | collective-permute-start | bytes 688136 | tf_op jit(solution)/shard_map/ppermute | solution.py:43
  22.6 5.6 %collective-permute-done = bf16[896,128]{1,0:T(8,128)(2,1)S(1)} collective-permute-done((bf16[896,128]{1,0:T(8,128)(2,1)S(1)}, bf16[896,128]{1,0:T(8,128)(2,1)S(1)}, u32[]{:S(2)}, u32[]{:S(2)}) %collective-permute-start) | collective-permute-done | bytes 229408 | tf_op jit(solution)/shard_map/ppermute | solution.py:43
  28.1 13.8 %collective-permute-done.1 = bf16[896,128]{1,0:T(8,128)(2,1)S(1)} collective-permute-done((bf16[896,128]{1,0:T(8,128)(2,1)S(1)}, bf16[896,128]{1,0:T(8,128)(2,1)S(1)}, u32[]{:S(2)}, u32[]{:S(2)}) %collective-permute-start.1) | collective-permute-done | bytes 229408 | tf_op jit(solution)/shard_map/ppermute | solution.py:43
  42.1 1.8 %collective-permute-done.6 = bf16[2,896,128]{2,1,0:T(8,128)(2,1)S(1)} collective-permute-done((bf16[2,896,128]{2,1,0:T(8,128)(2,1)S(1)}, bf16[2,896,128]{2,1,0:T(8,128)(2,1)S(1)}, u32[]{:S(2)}, u32[]{:S(2)}) %collective-permute-start.6) | collective-permute-done | bytes 458784 | tf_op jit(solution)/shard_map/ppermute | solution.py:39
  44.0 3.1 %collective-permute-start.7 = (bf16[4,896,128]{2,1,0:T(8,128)(2,1)S(1)}, bf16[4,896,128]{2,1,0:T(8,128)(2,1)S(1)}, u32[]{:S(2)}, u32[]{:S(2)}) collective-permute-start(bf16[4,896,128]{2,1,0:T(8,128)(2,1)S(1)} %pad_maximum_fusion.1.refs_0_), channel_id=1, source_target_pairs={{0,16},{1,17},{2,18},{3,19},{4,132},{5,133},{6,134},{7,135},{8,24}... | collective-permute-start | bytes 2752520 | tf_op jit(solution)/shard_map/ppermute | solution.py:43
  47.1 10.3 %collective-permute-done.5 = bf16[24,4096]{1,0:T(8,128)(2,1)S(1)} collective-permute-done((bf16[24,4096]{1,0:T(8,128)(2,1)S(1)}, bf16[24,4096]{1,0:T(8,128)(2,1)S(1)}, u32[]{:S(2)}, u32[]{:S(2)}) %collective-permute-start.5) | collective-permute-done | bytes 196640 | tf_op jit(solution)/shard_map/ppermute | solution.py:39
  57.4 1.6 %collective-permute-done.7.refs_2_ = bf16[4,896,128]{2,1,0:T(8,128)(2,1)S(1)} collective-permute-done((bf16[4,896,128]{2,1,0:T(8,128)(2,1)S(1)}, bf16[4,896,128]{2,1,0:T(8,128)(2,1)S(1)}, u32[]{:S(2)}, u32[]{:S(2)}) %collective-permute-start.7) | collective-permute-done | bytes 917536 | tf_op jit(solution)/shard_map/ppermute | solution.py:43
  59.8 1.6 %collective-permute-start.8 = (bf16[4,896,128]{2,1,0:T(8,128)(2,1)S(1)}, bf16[4,896,128]{2,1,0:T(8,128)(2,1)S(1)}, u32[]{:S(2)}, u32[]{:S(2)}) collective-permute-start(bf16[4,896,128]{2,1,0:T(8,128)(2,1)S(1)} %pad_maximum_fusion.1.refs_0_), channel_id=1, source_target_pairs={{0,8},{1,9},{2,10},{3,11},{4,68},{5,69},{6,70},{7,71},{8,0},{9,1},... | collective-permute-start | bytes 2752520 | tf_op jit(solution)/shard_map/ppermute | solution.py:43
  61.4 2.1 %collective-permute-start.9 = (bf16[4,896,128]{2,1,0:T(8,128)(2,1)S(1)}, bf16[4,896,128]{2,1,0:T(8,128)(2,1)}, u32[]{:S(2)}, u32[]{:S(2)}) collective-permute-start(bf16[4,896,128]{2,1,0:T(8,128)(2,1)S(1)} %pad_maximum_fusion.1.refs_0_), channel_id=1, source_target_pairs={{0,24},{1,25},{2,26},{3,27},{4,196},{5,197},{6,198},{7,199},{8,16}... | collective-permute-start | bytes 2752520 | tf_op jit(solution)/shard_map/ppermute | solution.py:43
  64.1 1.0 pad_maximum_fusion.x_ref
  65.2 8.1 %collective-permute-done.8.refs_1_ = bf16[4,896,128]{2,1,0:T(8,128)(2,1)S(1)} collective-permute-done((bf16[4,896,128]{2,1,0:T(8,128)(2,1)S(1)}, bf16[4,896,128]{2,1,0:T(8,128)(2,1)S(1)}, u32[]{:S(2)}, u32[]{:S(2)}) %collective-permute-start.8) | collective-permute-done | bytes 917536 | tf_op jit(solution)/shard_map/ppermute | solution.py:43
  74.2 1.9 %collective-permute-done.9.refs_3_ = bf16[4,896,128]{2,1,0:T(8,128)(2,1)} collective-permute-done((bf16[4,896,128]{2,1,0:T(8,128)(2,1)S(1)}, bf16[4,896,128]{2,1,0:T(8,128)(2,1)}, u32[]{:S(2)}, u32[]{:S(2)}) %collective-permute-start.9) | collective-permute-done | bytes 917536 | tf_op jit(solution)/shard_map/ppermute | solution.py:43
  76.1 1.2 copy-done.3
  77.2 3.8 %shard_map.119 = (bf16[3,128,1792]{2,1,0:T(8,128)(2,1)S(1)}, f32[128,1792]{1,0:T(8,128)S(1)}) custom-call(bf16[512,1024]{1,0:T(8,128)(2,1)S(1)} %pad_maximum_fusion.x_ref, bf16[4,896,128]{2,1,0:T(8,128)(2,1)S(1)} %pad_maximum_fusion.1.refs_0_, bf16[4,896,128]{2,1,0:T(8,128)(2,1)S(1)} %copy-done.3, bf16[4,896,128]{2,1,0:T(8,128)(2,1)S(1)} %collective-permute-done.7.refs_2_, ...), custom_call_target="tpu_custom_call" | custom-call | flops 1879048192 | bytes 8000000 | tf_op jit(solution)/shard_map/pallas_call | solution.py:141
  81.9 1.9 %collective-permute-start.11 = (bf16[128,1792]{1,0:T(8,128)(2,1)S(1)}, bf16[128,1792]{1,0:T(8,128)(2,1)S(1)}, u32[]{:S(2)}, u32[]{:S(2)}) collective-permute-start(bf16[128,1792]{1,0:T(8,128)(2,1)S(1)} %get-tuple-element.29), channel_id=1, source_target_pairs={{0,128},{1,129},{2,130},{3,131},{4,20},{5,21},{6,22},{7,23},{8,136... | collective-permute-start | bytes 1376264 | tf_op jit(solution)/shard_map/ppermute | solution.py:43
  83.8 2.8 %collective-permute-start.12 = (bf16[128,1792]{1,0:T(8,128)(2,1)S(1)}, bf16[128,1792]{1,0:T(8,128)(2,1)S(1)}, u32[]{:S(2)}, u32[]{:S(2)}) collective-permute-start(bf16[128,1792]{1,0:T(8,128)(2,1)S(1)} %get-tuple-element.28), channel_id=1, source_target_pairs={{0,192},{1,193},{2,194},{3,195},{4,28},{5,29},{6,30},{7,31},{8,200... | collective-permute-start | bytes 1376264 | tf_op jit(solution)/shard_map/ppermute | solution.py:43
  86.7 3.9 %collective-permute-done.10 = bf16[128,1792]{1,0:T(8,128)(2,1)S(1)} collective-permute-done((bf16[128,1792]{1,0:T(8,128)(2,1)}, bf16[128,1792]{1,0:T(8,128)(2,1)S(1)}, u32[]{:S(2)}, u32[]{:S(2)}) %collective-permute-start.10) | collective-permute-done | bytes 458784 | tf_op jit(solution)/shard_map/ppermute | solution.py:43
  90.6 5.8 %collective-permute-done.11 = bf16[128,1792]{1,0:T(8,128)(2,1)S(1)} collective-permute-done((bf16[128,1792]{1,0:T(8,128)(2,1)S(1)}, bf16[128,1792]{1,0:T(8,128)(2,1)S(1)}, u32[]{:S(2)}, u32[]{:S(2)}) %collective-permute-start.11) | collective-permute-done | bytes 458784 | tf_op jit(solution)/shard_map/ppermute | solution.py:43
  96.4 2.1 %collective-permute-done.12 = bf16[128,1792]{1,0:T(8,128)(2,1)S(1)} collective-permute-done((bf16[128,1792]{1,0:T(8,128)(2,1)S(1)}, bf16[128,1792]{1,0:T(8,128)(2,1)S(1)}, u32[]{:S(2)}, u32[]{:S(2)}) %collective-permute-start.12) | collective-permute-done | bytes 458784 | tf_op jit(solution)/shard_map/ppermute | solution.py:43
  98.8 3.3 %collective-permute-start.15 = (bf16[32,2688]{1,0:T(8,128)(2,1)S(1)}, bf16[32,2688]{1,0:T(8,128)(2,1)S(1)}, u32[]{:S(2)}, u32[]{:S(2)}) collective-permute-start(bf16[32,2688]{1,0:T(8,128)(2,1)S(1)} %get-tuple-element.97), channel_id=1, source_target_pairs={{0,3},{1,2},{2,1},{3,0},{4,7},{5,6},{6,5},{7,4},{8,11},{9,10},{10,... | collective-permute-start | bytes 516104 | tf_op jit(solution)/shard_map/ppermute | solution.py:39
  103.4 8.7 %collective-permute-done.13 = bf16[32,2688]{1,0:T(8,128)(2,1)S(1)} collective-permute-done((bf16[32,2688]{1,0:T(8,128)(2,1)S(1)}, bf16[32,2688]{1,0:T(8,128)(2,1)S(1)}, u32[]{:S(2)}, u32[]{:S(2)}) %collective-permute-start.13) | collective-permute-done | bytes 172064 | tf_op jit(solution)/shard_map/ppermute | solution.py:39
  112.1 3.4 %collective-permute-done.14 = bf16[32,2688]{1,0:T(8,128)(2,1)S(1)} collective-permute-done((bf16[32,2688]{1,0:T(8,128)(2,1)S(1)}, bf16[32,2688]{1,0:T(8,128)(2,1)S(1)}, u32[]{:S(2)}, u32[]{:S(2)}) %collective-permute-start.14) | collective-permute-done | bytes 172064 | tf_op jit(solution)/shard_map/ppermute | solution.py:39
  118.6 2.7 %collective-permute-start.16 = (bf16[32,1536]{1,0:T(8,128)(2,1)S(1)}, bf16[32,1536]{1,0:T(8,128)(2,1)S(1)}, u32[]{:S(2)}, u32[]{:S(2)}) collective-permute-start(bf16[32,1536]{1,0:T(8,128)(2,1)S(1)} %pad_maximum_fusion.7), channel_id=1, source_target_pairs={{0,3},{1,2},{2,1},{3,0},{4,7},{5,6},{6,5},{7,4},{8,11},{9,10},{10,... | collective-permute-start | bytes 294920 | tf_op jit(solution)/shard_map/ppermute | solution.py:39
  121.3 1.7 %collective-permute-start.18 = (bf16[32,1536]{1,0:T(8,128)(2,1)S(1)}, bf16[32,1536]{1,0:T(8,128)(2,1)S(1)}, u32[]{:S(2)}, u32[]{:S(2)}) collective-permute-start(bf16[32,1536]{1,0:T(8,128)(2,1)S(1)} %pad_maximum_fusion.7), channel_id=1, source_target_pairs={{0,1},{1,0},{2,3},{3,2},{4,5},{5,4},{6,7},{7,6},{8,9},{9,8},{10,11... | collective-permute-start | bytes 294920 | tf_op jit(solution)/shard_map/ppermute | solution.py:39
  123.1 3.2 %collective-permute-done.16 = bf16[32,1536]{1,0:T(8,128)(2,1)S(1)} collective-permute-done((bf16[32,1536]{1,0:T(8,128)(2,1)S(1)}, bf16[32,1536]{1,0:T(8,128)(2,1)S(1)}, u32[]{:S(2)}, u32[]{:S(2)}) %collective-permute-start.16) | collective-permute-done | bytes 98336 | tf_op jit(solution)/shard_map/ppermute | solution.py:39
  126.3 2.6 %collective-permute-done.17 = bf16[32,1536]{1,0:T(8,128)(2,1)S(1)} collective-permute-done((bf16[32,1536]{1,0:T(8,128)(2,1)S(1)}, bf16[32,1536]{1,0:T(8,128)(2,1)S(1)}, u32[]{:S(2)}, u32[]{:S(2)}) %collective-permute-start.17) | collective-permute-done | bytes 98336 | tf_op jit(solution)/shard_map/ppermute | solution.py:39
  129.1 7.4 %convolution_convert_fusion = bf16[128,4096]{1,0:T(8,128)(2,1)} fusion(bf16[1536,4096]{1,0:T(8,128)(2,1)} %all-gather.2.cloned.1.call-done, bf16[32,1536]{1,0:T(8,128)(2,1)S(1)} %broadcast_select_fusion.4, bf16[32,1536]{1,0:T(8,128)(2,1)S(1)} %get-tuple-element.53, bf16[32,1536]{1,0:T(8,128)(2,1)S(1)} %get-tuple-element.52, ...), kind=kOutput, calls=%fused_computation.1 | convolution fusion | flops 1612709888 | bytes 14024704 | tf_op jit(solution)/shard_map/dot_general | solution.py:235
  (96 shorter events, 7.9 us)
Async XLA Ops:
  6.5 122.5 %all-gather.2.cloned.1.call-start = ((), (), s32[]{:S(2)}) async-start(), calls=%async_computation | async-start | bytes 12976128 | tf_op jit(solution)/shard_map/all_gather | solution.py:193
  8.2 4.7 %copy-start = (bf16[256,384]{1,0:T(8,128)(2,1)S(1)}, bf16[256,384]{1,0:T(8,128)(2,1)}, u32[]{:S(2)}) copy-start(bf16[256,384]{1,0:T(8,128)(2,1)} %q_ref.1) | copy-start | bytes 589828
  8.2 4.7 %copy-start.1 = (bf16[256,64]{0,1:T(8,128)(2,1)S(1)}, bf16[256,64]{0,1:T(8,128)(2,1)}, u32[]{:S(2)}) copy-start(bf16[256,64]{0,1:T(8,128)(2,1)} %param.15) | copy-start | bytes 98308
  8.4 33.5 %collective-permute-start.4 = (bf16[128,1024]{1,0:T(8,128)(2,1)S(1)}, bf16[128,1024]{1,0:T(8,128)(2,1)S(1)}, u32[]{:S(2)}, u32[]{:S(2)}) collective-permute-start(bf16[128,1024]{1,0:T(8,128)(2,1)S(1)} %pad_maximum_fusion.6), channel_id=1, source_target_pairs={{0,192},{1,193},{2,194},{3,195},{4,28},{5,29},{6,30},{7,31},{8,200... | collective-permute-start | bytes 786440 | tf_op jit(solution)/shard_map/ppermute | solution.py:43
  10.5 36.6 %copy-start.5 = (bf16[24,4096]{1,0:T(8,128)(2,1)S(1)}, bf16[24,4096]{1,0:T(8,128)(2,1)}, u32[]{:S(2)}) copy-start(bf16[24,4096]{1,0:T(8,128)(2,1)} %param.16) | copy-start | bytes 589828
  10.5 31.4 %collective-permute-start.3 = (bf16[128,1024]{1,0:T(8,128)(2,1)S(1)}, bf16[128,1024]{1,0:T(8,128)(2,1)S(1)}, u32[]{:S(2)}, u32[]{:S(2)}) collective-permute-start(bf16[128,1024]{1,0:T(8,128)(2,1)S(1)} %pad_maximum_fusion.5), channel_id=1, source_target_pairs={{0,128},{1,129},{2,130},{3,131},{4,20},{5,21},{6,22},{7,23},{8,136... | collective-permute-start | bytes 786440 | tf_op jit(solution)/shard_map/ppermute | solution.py:43
  11.5 30.5 %collective-permute-start.2 = (bf16[128,1024]{1,0:T(8,128)(2,1)S(1)}, bf16[128,1024]{1,0:T(8,128)(2,1)S(1)}, u32[]{:S(2)}, u32[]{:S(2)}) collective-permute-start(bf16[128,1024]{1,0:T(8,128)(2,1)S(1)} %pad_maximum_fusion.4), channel_id=1, source_target_pairs={{0,64},{1,65},{2,66},{3,67},{4,12},{5,13},{6,14},{7,15},{8,72},{9,... | collective-permute-start | bytes 786440 | tf_op jit(solution)/shard_map/ppermute | solution.py:43
  12.9 15.3 %collective-permute-start = (bf16[896,128]{1,0:T(8,128)(2,1)S(1)}, bf16[896,128]{1,0:T(8,128)(2,1)S(1)}, u32[]{:S(2)}, u32[]{:S(2)}) collective-permute-start(bf16[896,128]{1,0:T(8,128)(2,1)S(1)} %shard_map.118), channel_id=1, source_target_pairs={{0,0},{1,32},{2,4},{3,36},{4,64},{5,96},{6,68},{7,100},{8,8},{9,40... | collective-permute-start | bytes 688136 | tf_op jit(solution)/shard_map/ppermute | solution.py:43
  19.4 22.5 %collective-permute-start.1 = (bf16[896,128]{1,0:T(8,128)(2,1)S(1)}, bf16[896,128]{1,0:T(8,128)(2,1)S(1)}, u32[]{:S(2)}, u32[]{:S(2)}) collective-permute-start(bf16[896,128]{1,0:T(8,128)(2,1)S(1)} %shard_map.118), channel_id=1, source_target_pairs={{0,32},{1,0},{2,36},{3,4},{4,96},{5,64},{6,100},{7,68},{8,40},{9,8... | collective-permute-start | bytes 688136 | tf_op jit(solution)/shard_map/ppermute | solution.py:43
  41.9 17.1 %copy-start.4 = (bf16[128,1024]{1,0:T(8,128)(2,1)}, bf16[128,1024]{1,0:T(8,128)(2,1)S(1)}, u32[]{:S(2)}) copy-start(bf16[128,1024]{1,0:T(8,128)(2,1)S(1)} %collective-permute-done.2) | copy-start | bytes 786436
  42.0 1.9 %collective-permute-start.6 = (bf16[2,896,128]{2,1,0:T(8,128)(2,1)S(1)}, bf16[2,896,128]{2,1,0:T(8,128)(2,1)S(1)}, u32[]{:S(2)}, u32[]{:S(2)}) collective-permute-start(bf16[2,896,128]{2,1,0:T(8,128)(2,1)S(1)} %pad_maximum_fusion.2), channel_id=1, source_target_pairs={{0,4},{4,0},{1,5},{5,1},{2,6},{6,2},{3,7},{7,3},{8,12},{12,8},{9,1... | collective-permute-start | bytes 1376264 | tf_op jit(solution)/shard_map/ppermute | solution.py:39
  44.0 15.0 %collective-permute-start.7 = (bf16[4,896,128]{2,1,0:T(8,128)(2,1)S(1)}, bf16[4,896,128]{2,1,0:T(8,128)(2,1)S(1)}, u32[]{:S(2)}, u32[]{:S(2)}) collective-permute-start(bf16[4,896,128]{2,1,0:T(8,128)(2,1)S(1)} %pad_maximum_fusion.1.refs_0_), channel_id=1, source_target_pairs={{0,16},{1,17},{2,18},{3,19},{4,132},{5,133},{6,134},{7,135},{8,24}... | collective-permute-start | bytes 2752520 | tf_op jit(solution)/shard_map/ppermute | solution.py:43
  47.1 10.3 %collective-permute-start.5 = (bf16[24,4096]{1,0:T(8,128)(2,1)S(1)}, bf16[24,4096]{1,0:T(8,128)(2,1)S(1)}, u32[]{:S(2)}, u32[]{:S(2)}) collective-permute-start(bf16[24,4096]{1,0:T(8,128)(2,1)S(1)} %copy-done.5), channel_id=1, source_target_pairs={{0,32},{32,0},{1,33},{33,1},{2,34},{34,2},{3,35},{35,3},{4,36},{36... | collective-permute-start | bytes 589832 | tf_op jit(solution)/shard_map/ppermute | solution.py:39
  59.8 13.5 %collective-permute-start.8 = (bf16[4,896,128]{2,1,0:T(8,128)(2,1)S(1)}, bf16[4,896,128]{2,1,0:T(8,128)(2,1)S(1)}, u32[]{:S(2)}, u32[]{:S(2)}) collective-permute-start(bf16[4,896,128]{2,1,0:T(8,128)(2,1)S(1)} %pad_maximum_fusion.1.refs_0_), channel_id=1, source_target_pairs={{0,8},{1,9},{2,10},{3,11},{4,68},{5,69},{6,70},{7,71},{8,0},{9,1},... | collective-permute-start | bytes 2752520 | tf_op jit(solution)/shard_map/ppermute | solution.py:43
  61.4 14.7 %collective-permute-start.9 = (bf16[4,896,128]{2,1,0:T(8,128)(2,1)S(1)}, bf16[4,896,128]{2,1,0:T(8,128)(2,1)}, u32[]{:S(2)}, u32[]{:S(2)}) collective-permute-start(bf16[4,896,128]{2,1,0:T(8,128)(2,1)S(1)} %pad_maximum_fusion.1.refs_0_), channel_id=1, source_target_pairs={{0,24},{1,25},{2,26},{3,27},{4,196},{5,197},{6,198},{7,199},{8,16}... | collective-permute-start | bytes 2752520 | tf_op jit(solution)/shard_map/ppermute | solution.py:43
  73.3 0.9 copy-start.2
  76.1 1.2 copy-start.3
  81.0 5.6 %copy-start.6 = (f32[128,128]{1,0:T(8,128)S(1)}, f32[128,128]{1,0:T(8,128)}, u32[]{:S(2)}) copy-start(f32[128,128]{1,0:T(8,128)} %constant.76.clone) | copy-start | bytes 196612
  81.0 5.6 %copy-start.7 = (f32[128,128]{1,0:T(8,128)S(1)}, f32[128,128]{1,0:T(8,128)}, u32[]{:S(2)}) copy-start(f32[128,128]{1,0:T(8,128)} %constant.77.clone) | copy-start | bytes 196612
  81.9 8.7 %collective-permute-start.10 = (bf16[128,1792]{1,0:T(8,128)(2,1)}, bf16[128,1792]{1,0:T(8,128)(2,1)S(1)}, u32[]{:S(2)}, u32[]{:S(2)}) collective-permute-start(bf16[128,1792]{1,0:T(8,128)(2,1)} %get-tuple-element.27), channel_id=1, source_target_pairs={{0,64},{1,65},{2,66},{3,67},{4,12},{5,13},{6,14},{7,15},{8,72},{9,... | collective-permute-start | bytes 1376264 | tf_op jit(solution)/shard_map/ppermute | solution.py:43
  81.9 14.4 %collective-permute-start.11 = (bf16[128,1792]{1,0:T(8,128)(2,1)S(1)}, bf16[128,1792]{1,0:T(8,128)(2,1)S(1)}, u32[]{:S(2)}, u32[]{:S(2)}) collective-permute-start(bf16[128,1792]{1,0:T(8,128)(2,1)S(1)} %get-tuple-element.29), channel_id=1, source_target_pairs={{0,128},{1,129},{2,130},{3,131},{4,20},{5,21},{6,22},{7,23},{8,136... | collective-permute-start | bytes 1376264 | tf_op jit(solution)/shard_map/ppermute | solution.py:43
  83.8 14.6 %collective-permute-start.12 = (bf16[128,1792]{1,0:T(8,128)(2,1)S(1)}, bf16[128,1792]{1,0:T(8,128)(2,1)S(1)}, u32[]{:S(2)}, u32[]{:S(2)}) collective-permute-start(bf16[128,1792]{1,0:T(8,128)(2,1)S(1)} %get-tuple-element.28), channel_id=1, source_target_pairs={{0,192},{1,193},{2,194},{3,195},{4,28},{5,29},{6,30},{7,31},{8,200... | collective-permute-start | bytes 1376264 | tf_op jit(solution)/shard_map/ppermute | solution.py:43
  98.8 16.7 %collective-permute-start.15 = (bf16[32,2688]{1,0:T(8,128)(2,1)S(1)}, bf16[32,2688]{1,0:T(8,128)(2,1)S(1)}, u32[]{:S(2)}, u32[]{:S(2)}) collective-permute-start(bf16[32,2688]{1,0:T(8,128)(2,1)S(1)} %get-tuple-element.97), channel_id=1, source_target_pairs={{0,3},{1,2},{2,1},{3,0},{4,7},{5,6},{6,5},{7,4},{8,11},{9,10},{10,... | collective-permute-start | bytes 516104 | tf_op jit(solution)/shard_map/ppermute | solution.py:39
  102.1 13.3 %collective-permute-start.14 = (bf16[32,2688]{1,0:T(8,128)(2,1)S(1)}, bf16[32,2688]{1,0:T(8,128)(2,1)S(1)}, u32[]{:S(2)}, u32[]{:S(2)}) collective-permute-start(bf16[32,2688]{1,0:T(8,128)(2,1)S(1)} %get-tuple-element.96), channel_id=1, source_target_pairs={{0,2},{1,3},{2,0},{3,1},{4,6},{5,7},{6,4},{7,5},{8,10},{9,11},{10,... | collective-permute-start | bytes 516104 | tf_op jit(solution)/shard_map/ppermute | solution.py:39
  102.6 9.5 %collective-permute-start.13 = (bf16[32,2688]{1,0:T(8,128)(2,1)S(1)}, bf16[32,2688]{1,0:T(8,128)(2,1)S(1)}, u32[]{:S(2)}, u32[]{:S(2)}) collective-permute-start(bf16[32,2688]{1,0:T(8,128)(2,1)S(1)} %get-tuple-element.95), channel_id=1, source_target_pairs={{0,1},{1,0},{2,3},{3,2},{4,5},{5,4},{6,7},{7,6},{8,9},{9,8},{10,11... | collective-permute-start | bytes 516104 | tf_op jit(solution)/shard_map/ppermute | solution.py:39
  116.8 1.5 %copy-start.8 = (bf16[384,384]{1,0:T(8,128)(2,1)S(1)}, bf16[384,384]{1,0:T(8,128)(2,1)}, u32[]{:S(2)}) copy-start(bf16[384,384]{1,0:T(8,128)(2,1)} %constant.78.clone) | copy-start | bytes 884740
  116.8 1.5 %copy-start.9 = (bf16[384,384]{1,0:T(8,128)(2,1)S(1)}, bf16[384,384]{1,0:T(8,128)(2,1)}, u32[]{:S(2)}) copy-start(bf16[384,384]{1,0:T(8,128)(2,1)} %constant.79.clone) | copy-start | bytes 884740
  118.6 7.7 %collective-permute-start.16 = (bf16[32,1536]{1,0:T(8,128)(2,1)S(1)}, bf16[32,1536]{1,0:T(8,128)(2,1)S(1)}, u32[]{:S(2)}, u32[]{:S(2)}) collective-permute-start(bf16[32,1536]{1,0:T(8,128)(2,1)S(1)} %pad_maximum_fusion.7), channel_id=1, source_target_pairs={{0,3},{1,2},{2,1},{3,0},{4,7},{5,6},{6,5},{7,4},{8,11},{9,10},{10,... | collective-permute-start | bytes 294920 | tf_op jit(solution)/shard_map/ppermute | solution.py:39
  121.3 7.6 %collective-permute-start.17 = (bf16[32,1536]{1,0:T(8,128)(2,1)S(1)}, bf16[32,1536]{1,0:T(8,128)(2,1)S(1)}, u32[]{:S(2)}, u32[]{:S(2)}) collective-permute-start(bf16[32,1536]{1,0:T(8,128)(2,1)S(1)} %pad_maximum_fusion.7), channel_id=1, source_target_pairs={{0,2},{1,3},{2,0},{3,1},{4,6},{5,7},{6,4},{7,5},{8,10},{9,11},{10,... | collective-permute-start | bytes 294920 | tf_op jit(solution)/shard_map/ppermute | solution.py:39
  121.3 7.6 %collective-permute-start.18 = (bf16[32,1536]{1,0:T(8,128)(2,1)S(1)}, bf16[32,1536]{1,0:T(8,128)(2,1)S(1)}, u32[]{:S(2)}, u32[]{:S(2)}) collective-permute-start(bf16[32,1536]{1,0:T(8,128)(2,1)S(1)} %pad_maximum_fusion.7), channel_id=1, source_target_pairs={{0,1},{1,0},{2,3},{3,2},{4,5},{5,4},{6,7},{7,6},{8,9},{9,8},{10,11... | collective-permute-start | bytes 294920 | tf_op jit(solution)/shard_map/ppermute | solution.py:39
Sparse Core Ops, SparseCore 0:
  59.9 68.9 all-gather.1

commit v16 on v15

--- a/solution.py
+++ b/solution.py
@@ -178,15 +178,14 @@
             picked.append(lax.dynamic_slice(gained, (0, (((s >> 1) * 4 + at) * 2 + (s & 1)) * 256), (ROWS, 256)))
         return jnp.concatenate(picked, axis=1)
 
+    second = move(packed, lambda y, zh, x, c, t: ((2 * zh + c) ^ y, 1 - (t & 1), x, t >> 1, y))
+    first, second, gained, out_weight = lax.optimization_barrier((first, second, gained, out_weight))
     ring = [along(features(e), e, "y", "x") for e in (1, 2, 3)]
-    second = move(packed, lambda y, zh, x, c, t: ((2 * zh + c) ^ y, 1 - (t & 1), x, t >> 1, y))
-    first, second, out_weight, *ring = lax.optimization_barrier((first, second, out_weight, *ring))
-    inputs = jnp.concatenate([features(0)] + ring, axis=0)
-
     pair = jnp.stack([first, second])
     pair = jnp.concatenate([pair, swap(pair, "core", 1)], axis=0)
-    wo_other, pair, opposite = lax.optimization_barrier((swap(out_weight, "zh", 1), pair, along(pair, 2, "x", "y")))
-    blocks = [pair, along(pair, 1, "x", "y"), opposite, along(pair, 3, "x", "y")]
+    wo_other, pair, *ring = lax.optimization_barrier((swap(out_weight, "zh", 1), pair, *ring))
+    inputs = jnp.concatenate([features(0)] + ring, axis=0)
+    blocks = [pair] + [along(pair, d, "x", "y") for d in (1, 2, 3)]
     sent, total = project(inputs, blocks)
 
     wo_piece = jnp.concatenate([out_weight, wo_other], axis=0)

time: 145 us -> 168 us (1.16)
  waiting for transfers between devices: 72.6 us -> 89.9 us
  starting transfers between devices: 34.6 us -> 37.6 us
    ppermute x11, waiting for transfers between devices: 42.6 us -> 67.1 us  [move(): lax.ppermute(value, AXES, [(flat(*at), flat(*where(*at))) for at in every...]
    ppermute x8, waiting for transfers between devices: 30 us -> 22.8 us  [swap(): return lax.ppermute(value, axis, [(i, i ^ d) for i in range(n)])]
    ppermute x8, starting transfers between devices: 9.08 us -> 13.2 us  [swap(): return lax.ppermute(value, axis, [(i, i ^ d) for i in range(n)])]
    unnamed x30 -> x28, local copies, waits for them, and re-layouts: 2.23 us -> 3.9 us
  transfers between devices with their start and end apart: 20 -> 20, of which waited for: 14 -> 12; matrix products, arithmetic and copies ran while one was open for 4% -> 4% of each run, Pallas kernels for 3% -> 2%
where the time goes in v16:
time: 168 us; the launch traced here: 165 us
  waiting for transfers between devices  89.9 us (54%)
  starting transfers between devices  37.6 us (22%)
  between operations  14.8 us (9%)
  matrix products  8.61 us (5%)
  local copies, waits for them, and re-layouts  5.63 us (3%)
  other arithmetic  5.06 us (3%)
  Pallas kernels  3.82 us (2%)
    ppermute x11, waiting for transfers between devices, move(): lax.ppermute(value, AXES, [(flat(*at), flat(*where(*at))) for at in every...  67.1 us
    ppermute x11, starting transfers between devices, move(): lax.ppermute(value, AXES, [(flat(*at), flat(*where(*at))) for at in every...  24.4 us
    ppermute x8, waiting for transfers between devices, swap(): return lax.ppermute(value, axis, [(i, i ^ d) for i in range(n)])  22.8 us
    ppermute x8, starting transfers between devices, swap(): return lax.ppermute(value, axis, [(i, i ^ d) for i in range(n)])  13.2 us
    dot_general x1, matrix products, body(): return jnp.dot(all_rows, wo, preferred_element_type=F32).astype(BF)  7.35 us
    unnamed x28, local copies, waits for them, and re-layouts  3.9 us
    pallas_call x1, Pallas kernels, project(): pl.pallas_call(project_kernel, out_shape=(jax.ShapeDtypeStruct((3, ROWS,...  3.78 us
  transfers between devices with their start and end apart: 20, of which 12 were waited for; matrix products, arithmetic and copies ran while one was open for 4% of the time, Pallas kernels for 2%

profile of v16, /device:TPU:24, one launch (start us, length us, event | category | flops | bytes accessed | tf_op | source)
XLA Modules:
  0.0 165.4 jit_solution(10080017718583173381)
XLA Ops:
  6.5 0.9 copy-done
  8.3 6.5 %collective-permute-start = (bf16[896,128]{1,0:T(8,128)(2,1)S(1)}, bf16[896,128]{1,0:T(8,128)(2,1)S(1)}, u32[]{:S(2)}, u32[]{:S(2)}) collective-permute-start(bf16[896,128]{1,0:T(8,128)(2,1)S(1)} %shard_map.118), channel_id=1, source_target_pairs={{0,0},{1,32},{2,4},{3,36},{4,64},{5,96},{6,68},{7,100},{8,8},{9,40... | collective-permute-start | bytes 688136 | tf_op jit(solution)/shard_map/ppermute | solution.py:43
  14.8 3.8 %collective-permute-start.1 = (bf16[896,128]{1,0:T(8,128)(2,1)S(1)}, bf16[896,128]{1,0:T(8,128)(2,1)S(1)}, u32[]{:S(2)}, u32[]{:S(2)}) collective-permute-start(bf16[896,128]{1,0:T(8,128)(2,1)S(1)} %shard_map.118), channel_id=1, source_target_pairs={{0,32},{1,0},{2,36},{3,4},{4,96},{5,64},{6,100},{7,68},{8,40},{9,8... | collective-permute-start | bytes 688136 | tf_op jit(solution)/shard_map/ppermute | solution.py:43
  18.8 1.6 fusion.2
  20.5 3.1 %collective-permute-done = bf16[896,128]{1,0:T(8,128)(2,1)S(1)} collective-permute-done((bf16[896,128]{1,0:T(8,128)(2,1)S(1)}, bf16[896,128]{1,0:T(8,128)(2,1)S(1)}, u32[]{:S(2)}, u32[]{:S(2)}) %collective-permute-start) | collective-permute-done | bytes 229408 | tf_op jit(solution)/shard_map/ppermute | solution.py:43
  23.5 13.7 %collective-permute-done.1 = bf16[896,128]{1,0:T(8,128)(2,1)S(1)} collective-permute-done((bf16[896,128]{1,0:T(8,128)(2,1)S(1)}, bf16[896,128]{1,0:T(8,128)(2,1)S(1)}, u32[]{:S(2)}, u32[]{:S(2)}) %collective-permute-start.1) | collective-permute-done | bytes 229408 | tf_op jit(solution)/shard_map/ppermute | solution.py:43
  37.8 1.9 %collective-permute-start.5 = (bf16[128,1024]{1,0:T(8,128)(2,1)S(1)}, bf16[128,1024]{1,0:T(8,128)(2,1)S(1)}, u32[]{:S(2)}, u32[]{:S(2)}) collective-permute-start(bf16[128,1024]{1,0:T(8,128)(2,1)S(1)} %pad_maximum_fusion.5), channel_id=1, source_target_pairs={{0,128},{1,129},{2,130},{3,131},{4,20},{5,21},{6,22},{7,23},{8,136... | collective-permute-start | bytes 786440 | tf_op jit(solution)/shard_map/ppermute | solution.py:43
  39.8 2.3 %collective-permute-start.4 = (bf16[128,1024]{1,0:T(8,128)(2,1)S(1)}, bf16[128,1024]{1,0:T(8,128)(2,1)}, u32[]{:S(2)}, u32[]{:S(2)}) collective-permute-start(bf16[128,1024]{1,0:T(8,128)(2,1)S(1)} %pad_maximum_fusion.4), channel_id=1, source_target_pairs={{0,64},{1,65},{2,66},{3,67},{4,12},{5,13},{6,14},{7,15},{8,72},{9,... | collective-permute-start | bytes 786440 | tf_op jit(solution)/shard_map/ppermute | solution.py:43
  42.1 4.1 %collective-permute-start.2 = (bf16[24,4096]{1,0:T(8,128)(2,1)S(1)}, bf16[24,4096]{1,0:T(8,128)(2,1)S(1)}, u32[]{:S(2)}, u32[]{:S(2)}) collective-permute-start(bf16[24,4096]{1,0:T(8,128)(2,1)S(1)} %copy-done.4), channel_id=1, source_target_pairs={{0,32},{32,0},{1,33},{33,1},{2,34},{34,2},{3,35},{35,3},{4,36},{36... | collective-permute-start | bytes 589832 | tf_op jit(solution)/shard_map/ppermute | solution.py:39
  46.3 8.4 %collective-permute-done.2 = bf16[24,4096]{1,0:T(8,128)(2,1)S(1)} collective-permute-done((bf16[24,4096]{1,0:T(8,128)(2,1)S(1)}, bf16[24,4096]{1,0:T(8,128)(2,1)S(1)}, u32[]{:S(2)}, u32[]{:S(2)}) %collective-permute-start.2) | collective-permute-done | bytes 196640 | tf_op jit(solution)/shard_map/ppermute | solution.py:39
  55.5 1.6 collective-permute-start.7
  57.1 2.7 %collective-permute-start.8 = (bf16[4,896,128]{2,1,0:T(8,128)(2,1)S(1)}, bf16[4,896,128]{2,1,0:T(8,128)(2,1)S(1)}, u32[]{:S(2)}, u32[]{:S(2)}) collective-permute-start(bf16[4,896,128]{2,1,0:T(8,128)(2,1)S(1)} %pad_maximum_fusion.1.refs_0_), channel_id=1, source_target_pairs={{0,16},{1,17},{2,18},{3,19},{4,132},{5,133},{6,134},{7,135},{8,24}... | collective-permute-start | bytes 2752520 | tf_op jit(solution)/shard_map/ppermute | solution.py:43
  61.0 1.0 pad_maximum_fusion.x_ref
  62.0 7.0 %collective-permute-done.7.refs_1_ = bf16[4,896,128]{2,1,0:T(8,128)(2,1)S(1)} collective-permute-done((bf16[4,896,128]{2,1,0:T(8,128)(2,1)S(1)}, bf16[4,896,128]{2,1,0:T(8,128)(2,1)S(1)}, u32[]{:S(2)}, u32[]{:S(2)}) %collective-permute-start.7) | collective-permute-done | bytes 917536 | tf_op jit(solution)/shard_map/ppermute | solution.py:43
  69.0 15.9 %collective-permute-done.8.refs_2_ = bf16[4,896,128]{2,1,0:T(8,128)(2,1)S(1)} collective-permute-done((bf16[4,896,128]{2,1,0:T(8,128)(2,1)S(1)}, bf16[4,896,128]{2,1,0:T(8,128)(2,1)S(1)}, u32[]{:S(2)}, u32[]{:S(2)}) %collective-permute-start.8) | collective-permute-done | bytes 917536 | tf_op jit(solution)/shard_map/ppermute | solution.py:43
  84.9 0.9 copy-done.2
  85.8 4.6 %collective-permute-done.9.refs_3_ = bf16[4,896,128]{2,1,0:T(8,128)(2,1)} collective-permute-done((bf16[4,896,128]{2,1,0:T(8,128)(2,1)S(1)}, bf16[4,896,128]{2,1,0:T(8,128)(2,1)}, u32[]{:S(2)}, u32[]{:S(2)}) %collective-permute-start.9) | collective-permute-done | bytes 917536 | tf_op jit(solution)/shard_map/ppermute | solution.py:43
  90.5 1.2 copy-done.3
  91.7 3.8 %shard_map.119 = (bf16[3,128,1792]{2,1,0:T(8,128)(2,1)S(1)}, f32[128,1792]{1,0:T(8,128)S(1)}) custom-call(bf16[512,1024]{1,0:T(8,128)(2,1)S(1)} %pad_maximum_fusion.x_ref, bf16[4,896,128]{2,1,0:T(8,128)(2,1)S(1)} %pad_maximum_fusion.1.refs_0_, bf16[4,896,128]{2,1,0:T(8,128)(2,1)S(1)} %collective-permute-done.7.refs_1_, bf16[4,896,128]{2,1,0:T(8,128)(2,1)S(1)} %copy-done.3, ...), custom_call_target="tpu_custom_call" | custom-call | flops 1879048192 | bytes 8000000 | tf_op jit(solution)/shard_map/pallas_call | solution.py:141
  96.3 2.3 %collective-permute-start.10 = (bf16[128,1792]{1,0:T(8,128)(2,1)}, bf16[128,1792]{1,0:T(8,128)(2,1)S(1)}, u32[]{:S(2)}, u32[]{:S(2)}) collective-permute-start(bf16[128,1792]{1,0:T(8,128)(2,1)} %get-tuple-element.27), channel_id=1, source_target_pairs={{0,64},{1,65},{2,66},{3,67},{4,12},{5,13},{6,14},{7,15},{8,72},{9,... | collective-permute-start | bytes 1376264 | tf_op jit(solution)/shard_map/ppermute | solution.py:43
  98.6 2.7 %collective-permute-start.12 = (bf16[128,1792]{1,0:T(8,128)(2,1)S(1)}, bf16[128,1792]{1,0:T(8,128)(2,1)S(1)}, u32[]{:S(2)}, u32[]{:S(2)}) collective-permute-start(bf16[128,1792]{1,0:T(8,128)(2,1)S(1)} %get-tuple-element.28), channel_id=1, source_target_pairs={{0,192},{1,193},{2,194},{3,195},{4,28},{5,29},{6,30},{7,31},{8,200... | collective-permute-start | bytes 1376264 | tf_op jit(solution)/shard_map/ppermute | solution.py:43
  101.3 8.0 %collective-permute-done.10 = bf16[128,1792]{1,0:T(8,128)(2,1)S(1)} collective-permute-done((bf16[128,1792]{1,0:T(8,128)(2,1)}, bf16[128,1792]{1,0:T(8,128)(2,1)S(1)}, u32[]{:S(2)}, u32[]{:S(2)}) %collective-permute-start.10) | collective-permute-done | bytes 458784 | tf_op jit(solution)/shard_map/ppermute | solution.py:43
  109.4 14.6 %collective-permute-done.11 = bf16[128,1792]{1,0:T(8,128)(2,1)S(1)} collective-permute-done((bf16[128,1792]{1,0:T(8,128)(2,1)S(1)}, bf16[128,1792]{1,0:T(8,128)(2,1)S(1)}, u32[]{:S(2)}, u32[]{:S(2)}) %collective-permute-start.11) | collective-permute-done | bytes 458784 | tf_op jit(solution)/shard_map/ppermute | solution.py:43
  124.4 1.5 collective-permute-start.15
  126.4 2.5 %collective-permute-start.13 = (bf16[32,2688]{1,0:T(8,128)(2,1)S(1)}, bf16[32,2688]{1,0:T(8,128)(2,1)S(1)}, u32[]{:S(2)}, u32[]{:S(2)}) collective-permute-start(bf16[32,2688]{1,0:T(8,128)(2,1)S(1)} %get-tuple-element.95), channel_id=1, source_target_pairs={{0,1},{1,0},{2,3},{3,2},{4,5},{5,4},{6,7},{7,6},{8,9},{9,8},{10,11... | collective-permute-start | bytes 516104 | tf_op jit(solution)/shard_map/ppermute | solution.py:39
  129.0 6.6 %collective-permute-done.13 = bf16[32,2688]{1,0:T(8,128)(2,1)S(1)} collective-permute-done((bf16[32,2688]{1,0:T(8,128)(2,1)S(1)}, bf16[32,2688]{1,0:T(8,128)(2,1)S(1)}, u32[]{:S(2)}, u32[]{:S(2)}) %collective-permute-start.13) | collective-permute-done | bytes 172064 | tf_op jit(solution)/shard_map/ppermute | solution.py:39
  135.6 3.7 %collective-permute-done.14 = bf16[32,2688]{1,0:T(8,128)(2,1)S(1)} collective-permute-done((bf16[32,2688]{1,0:T(8,128)(2,1)S(1)}, bf16[32,2688]{1,0:T(8,128)(2,1)S(1)}, u32[]{:S(2)}, u32[]{:S(2)}) %collective-permute-start.14) | collective-permute-done | bytes 172064 | tf_op jit(solution)/shard_map/ppermute | solution.py:39
  142.4 2.8 %collective-permute-start.16 = (bf16[32,1536]{1,0:T(8,128)(2,1)S(1)}, bf16[32,1536]{1,0:T(8,128)(2,1)S(1)}, u32[]{:S(2)}, u32[]{:S(2)}) collective-permute-start(bf16[32,1536]{1,0:T(8,128)(2,1)S(1)} %pad_maximum_fusion.7), channel_id=1, source_target_pairs={{0,3},{1,2},{2,1},{3,0},{4,7},{5,6},{6,5},{7,4},{8,11},{9,10},{10,... | collective-permute-start | bytes 294920 | tf_op jit(solution)/shard_map/ppermute | solution.py:39
  145.2 1.7 %collective-permute-start.18 = (bf16[32,1536]{1,0:T(8,128)(2,1)S(1)}, bf16[32,1536]{1,0:T(8,128)(2,1)S(1)}, u32[]{:S(2)}, u32[]{:S(2)}) collective-permute-start(bf16[32,1536]{1,0:T(8,128)(2,1)S(1)} %pad_maximum_fusion.7), channel_id=1, source_target_pairs={{0,1},{1,0},{2,3},{3,2},{4,5},{5,4},{6,7},{7,6},{8,9},{9,8},{10,11... | collective-permute-start | bytes 294920 | tf_op jit(solution)/shard_map/ppermute | solution.py:39
  146.9 2.0 %collective-permute-done.16 = bf16[32,1536]{1,0:T(8,128)(2,1)S(1)} collective-permute-done((bf16[32,1536]{1,0:T(8,128)(2,1)S(1)}, bf16[32,1536]{1,0:T(8,128)(2,1)S(1)}, u32[]{:S(2)}, u32[]{:S(2)}) %collective-permute-start.16) | collective-permute-done | bytes 98336 | tf_op jit(solution)/shard_map/ppermute | solution.py:39
  148.9 2.1 %collective-permute-done.17 = bf16[32,1536]{1,0:T(8,128)(2,1)S(1)} collective-permute-done((bf16[32,1536]{1,0:T(8,128)(2,1)S(1)}, bf16[32,1536]{1,0:T(8,128)(2,1)S(1)}, u32[]{:S(2)}, u32[]{:S(2)}) %collective-permute-start.17) | collective-permute-done | bytes 98336 | tf_op jit(solution)/shard_map/ppermute | solution.py:39
  151.2 7.4 %convolution_convert_fusion = bf16[128,4096]{1,0:T(8,128)(2,1)} fusion(bf16[1536,4096]{1,0:T(8,128)(2,1)} %all-gather.2.cloned.1.call-done, bf16[32,1536]{1,0:T(8,128)(2,1)S(1)} %broadcast_select_fusion.4, bf16[32,1536]{1,0:T(8,128)(2,1)S(1)} %get-tuple-element.53, bf16[32,1536]{1,0:T(8,128)(2,1)S(1)} %get-tuple-element.52, ...), kind=kOutput, calls=%fused_computation.1 | convolution fusion | flops 1612709888 | bytes 14024704 | tf_op jit(solution)/shard_map/dot_general | solution.py:234
  (94 shorter events, 7.6 us)
Async XLA Ops:
  6.5 144.6 %all-gather.2.cloned.1.call-start = ((), (), s32[]{:S(2)}) async-start(), calls=%async_computation | async-start | bytes 12976128 | tf_op jit(solution)/shard_map/all_gather | solution.py:192
  6.5 0.9 copy-start
  7.5 0.8 copy-start.1
  8.3 15.3 %collective-permute-start = (bf16[896,128]{1,0:T(8,128)(2,1)S(1)}, bf16[896,128]{1,0:T(8,128)(2,1)S(1)}, u32[]{:S(2)}, u32[]{:S(2)}) collective-permute-start(bf16[896,128]{1,0:T(8,128)(2,1)S(1)} %shard_map.118), channel_id=1, source_target_pairs={{0,0},{1,32},{2,4},{3,36},{4,64},{5,96},{6,68},{7,100},{8,8},{9,40... | collective-permute-start | bytes 688136 | tf_op jit(solution)/shard_map/ppermute | solution.py:43
  14.8 22.5 %collective-permute-start.1 = (bf16[896,128]{1,0:T(8,128)(2,1)S(1)}, bf16[896,128]{1,0:T(8,128)(2,1)S(1)}, u32[]{:S(2)}, u32[]{:S(2)}) collective-permute-start(bf16[896,128]{1,0:T(8,128)(2,1)S(1)} %shard_map.118), channel_id=1, source_target_pairs={{0,32},{1,0},{2,36},{3,4},{4,96},{5,64},{6,100},{7,68},{8,40},{9,8... | collective-permute-start | bytes 688136 | tf_op jit(solution)/shard_map/ppermute | solution.py:43
  37.3 4.8 %copy-start.4 = (bf16[24,4096]{1,0:T(8,128)(2,1)S(1)}, bf16[24,4096]{1,0:T(8,128)(2,1)}, u32[]{:S(2)}) copy-start(bf16[24,4096]{1,0:T(8,128)(2,1)} %param.16) | copy-start | bytes 589828
  37.3 8.9 %collective-permute-start.3 = (bf16[2,896,128]{2,1,0:T(8,128)(2,1)S(1)}, bf16[2,896,128]{2,1,0:T(8,128)(2,1)S(1)}, u32[]{:S(2)}, u32[]{:S(2)}) collective-permute-start(bf16[2,896,128]{2,1,0:T(8,128)(2,1)S(1)} %pad_maximum_fusion.2), channel_id=1, source_target_pairs={{0,4},{4,0},{1,5},{5,1},{2,6},{6,2},{3,7},{7,3},{8,12},{12,8},{9,1... | collective-permute-start | bytes 1376264 | tf_op jit(solution)/shard_map/ppermute | solution.py:39
  37.7 17.0 %collective-permute-start.6 = (bf16[128,1024]{1,0:T(8,128)(2,1)S(1)}, bf16[128,1024]{1,0:T(8,128)(2,1)S(1)}, u32[]{:S(2)}, u32[]{:S(2)}) collective-permute-start(bf16[128,1024]{1,0:T(8,128)(2,1)S(1)} %pad_maximum_fusion.6), channel_id=1, source_target_pairs={{0,192},{1,193},{2,194},{3,195},{4,28},{5,29},{6,30},{7,31},{8,200... | collective-permute-start | bytes 786440 | tf_op jit(solution)/shard_map/ppermute | solution.py:43
  37.8 16.9 %collective-permute-start.5 = (bf16[128,1024]{1,0:T(8,128)(2,1)S(1)}, bf16[128,1024]{1,0:T(8,128)(2,1)S(1)}, u32[]{:S(2)}, u32[]{:S(2)}) collective-permute-start(bf16[128,1024]{1,0:T(8,128)(2,1)S(1)} %pad_maximum_fusion.5), channel_id=1, source_target_pairs={{0,128},{1,129},{2,130},{3,131},{4,20},{5,21},{6,22},{7,23},{8,136... | collective-permute-start | bytes 786440 | tf_op jit(solution)/shard_map/ppermute | solution.py:43
  39.8 14.9 %collective-permute-start.4 = (bf16[128,1024]{1,0:T(8,128)(2,1)S(1)}, bf16[128,1024]{1,0:T(8,128)(2,1)}, u32[]{:S(2)}, u32[]{:S(2)}) collective-permute-start(bf16[128,1024]{1,0:T(8,128)(2,1)S(1)} %pad_maximum_fusion.4), channel_id=1, source_target_pairs={{0,64},{1,65},{2,66},{3,67},{4,12},{5,13},{6,14},{7,15},{8,72},{9,... | collective-permute-start | bytes 786440 | tf_op jit(solution)/shard_map/ppermute | solution.py:43
  42.1 12.6 %collective-permute-start.2 = (bf16[24,4096]{1,0:T(8,128)(2,1)S(1)}, bf16[24,4096]{1,0:T(8,128)(2,1)S(1)}, u32[]{:S(2)}, u32[]{:S(2)}) collective-permute-start(bf16[24,4096]{1,0:T(8,128)(2,1)S(1)} %copy-done.4), channel_id=1, source_target_pairs={{0,32},{32,0},{1,33},{33,1},{2,34},{34,2},{3,35},{35,3},{4,36},{36... | collective-permute-start | bytes 589832 | tf_op jit(solution)/shard_map/ppermute | solution.py:39
  55.5 13.5 %collective-permute-start.7 = (bf16[4,896,128]{2,1,0:T(8,128)(2,1)S(1)}, bf16[4,896,128]{2,1,0:T(8,128)(2,1)S(1)}, u32[]{:S(2)}, u32[]{:S(2)}) collective-permute-start(bf16[4,896,128]{2,1,0:T(8,128)(2,1)S(1)} %pad_maximum_fusion.1.refs_0_), channel_id=1, source_target_pairs={{0,8},{1,9},{2,10},{3,11},{4,68},{5,69},{6,70},{7,71},{8,0},{9,1},... | collective-permute-start | bytes 2752520 | tf_op jit(solution)/shard_map/ppermute | solution.py:43
  57.1 27.8 %collective-permute-start.8 = (bf16[4,896,128]{2,1,0:T(8,128)(2,1)S(1)}, bf16[4,896,128]{2,1,0:T(8,128)(2,1)S(1)}, u32[]{:S(2)}, u32[]{:S(2)}) collective-permute-start(bf16[4,896,128]{2,1,0:T(8,128)(2,1)S(1)} %pad_maximum_fusion.1.refs_0_), channel_id=1, source_target_pairs={{0,16},{1,17},{2,18},{3,19},{4,132},{5,133},{6,134},{7,135},{8,24}... | collective-permute-start | bytes 2752520 | tf_op jit(solution)/shard_map/ppermute | solution.py:43
  59.8 30.7 %collective-permute-start.9 = (bf16[4,896,128]{2,1,0:T(8,128)(2,1)S(1)}, bf16[4,896,128]{2,1,0:T(8,128)(2,1)}, u32[]{:S(2)}, u32[]{:S(2)}) collective-permute-start(bf16[4,896,128]{2,1,0:T(8,128)(2,1)S(1)} %pad_maximum_fusion.1.refs_0_), channel_id=1, source_target_pairs={{0,24},{1,25},{2,26},{3,27},{4,196},{5,197},{6,198},{7,199},{8,16}... | collective-permute-start | bytes 2752520 | tf_op jit(solution)/shard_map/ppermute | solution.py:43
  84.9 0.9 copy-start.2
  90.5 1.2 copy-start.3
  95.5 5.8 %copy-start.5 = (f32[128,128]{1,0:T(8,128)S(1)}, f32[128,128]{1,0:T(8,128)}, u32[]{:S(2)}) copy-start(f32[128,128]{1,0:T(8,128)} %constant.76.clone) | copy-start | bytes 196612
  95.5 5.8 %copy-start.6 = (f32[128,128]{1,0:T(8,128)S(1)}, f32[128,128]{1,0:T(8,128)}, u32[]{:S(2)}) copy-start(f32[128,128]{1,0:T(8,128)} %constant.77.clone) | copy-start | bytes 196612
  96.3 13.1 %collective-permute-start.10 = (bf16[128,1792]{1,0:T(8,128)(2,1)}, bf16[128,1792]{1,0:T(8,128)(2,1)S(1)}, u32[]{:S(2)}, u32[]{:S(2)}) collective-permute-start(bf16[128,1792]{1,0:T(8,128)(2,1)} %get-tuple-element.27), channel_id=1, source_target_pairs={{0,64},{1,65},{2,66},{3,67},{4,12},{5,13},{6,14},{7,15},{8,72},{9,... | collective-permute-start | bytes 1376264 | tf_op jit(solution)/shard_map/ppermute | solution.py:43
  98.6 25.4 %collective-permute-start.11 = (bf16[128,1792]{1,0:T(8,128)(2,1)S(1)}, bf16[128,1792]{1,0:T(8,128)(2,1)S(1)}, u32[]{:S(2)}, u32[]{:S(2)}) collective-permute-start(bf16[128,1792]{1,0:T(8,128)(2,1)S(1)} %get-tuple-element.29), channel_id=1, source_target_pairs={{0,128},{1,129},{2,130},{3,131},{4,20},{5,21},{6,22},{7,23},{8,136... | collective-permute-start | bytes 1376264 | tf_op jit(solution)/shard_map/ppermute | solution.py:43
  98.6 25.4 %collective-permute-start.12 = (bf16[128,1792]{1,0:T(8,128)(2,1)S(1)}, bf16[128,1792]{1,0:T(8,128)(2,1)S(1)}, u32[]{:S(2)}, u32[]{:S(2)}) collective-permute-start(bf16[128,1792]{1,0:T(8,128)(2,1)S(1)} %get-tuple-element.28), channel_id=1, source_target_pairs={{0,192},{1,193},{2,194},{3,195},{4,28},{5,29},{6,30},{7,31},{8,200... | collective-permute-start | bytes 1376264 | tf_op jit(solution)/shard_map/ppermute | solution.py:43
  124.4 14.9 %collective-permute-start.15 = (bf16[32,2688]{1,0:T(8,128)(2,1)S(1)}, bf16[32,2688]{1,0:T(8,128)(2,1)S(1)}, u32[]{:S(2)}, u32[]{:S(2)}) collective-permute-start(bf16[32,2688]{1,0:T(8,128)(2,1)S(1)} %get-tuple-element.97), channel_id=1, source_target_pairs={{0,3},{1,2},{2,1},{3,0},{4,7},{5,6},{6,5},{7,4},{8,11},{9,10},{10,... | collective-permute-start | bytes 516104 | tf_op jit(solution)/shard_map/ppermute | solution.py:39
  125.9 13.4 %collective-permute-start.14 = (bf16[32,2688]{1,0:T(8,128)(2,1)S(1)}, bf16[32,2688]{1,0:T(8,128)(2,1)S(1)}, u32[]{:S(2)}, u32[]{:S(2)}) collective-permute-start(bf16[32,2688]{1,0:T(8,128)(2,1)S(1)} %get-tuple-element.96), channel_id=1, source_target_pairs={{0,2},{1,3},{2,0},{3,1},{4,6},{5,7},{6,4},{7,5},{8,10},{9,11},{10,... | collective-permute-start | bytes 516104 | tf_op jit(solution)/shard_map/ppermute | solution.py:39
  126.4 9.2 %collective-permute-start.13 = (bf16[32,2688]{1,0:T(8,128)(2,1)S(1)}, bf16[32,2688]{1,0:T(8,128)(2,1)S(1)}, u32[]{:S(2)}, u32[]{:S(2)}) collective-permute-start(bf16[32,2688]{1,0:T(8,128)(2,1)S(1)} %get-tuple-element.95), channel_id=1, source_target_pairs={{0,1},{1,0},{2,3},{3,2},{4,5},{5,4},{6,7},{7,6},{8,9},{9,8},{10,11... | collective-permute-start | bytes 516104 | tf_op jit(solution)/shard_map/ppermute | solution.py:39
  140.6 1.5 copy-start.7
  140.6 1.5 copy-start.8
  142.4 6.5 %collective-permute-start.16 = (bf16[32,1536]{1,0:T(8,128)(2,1)S(1)}, bf16[32,1536]{1,0:T(8,128)(2,1)S(1)}, u32[]{:S(2)}, u32[]{:S(2)}) collective-permute-start(bf16[32,1536]{1,0:T(8,128)(2,1)S(1)} %pad_maximum_fusion.7), channel_id=1, source_target_pairs={{0,3},{1,2},{2,1},{3,0},{4,7},{5,6},{6,5},{7,4},{8,11},{9,10},{10,... | collective-permute-start | bytes 294920 | tf_op jit(solution)/shard_map/ppermute | solution.py:39
  145.2 5.8 %collective-permute-start.17 = (bf16[32,1536]{1,0:T(8,128)(2,1)S(1)}, bf16[32,1536]{1,0:T(8,128)(2,1)S(1)}, u32[]{:S(2)}, u32[]{:S(2)}) collective-permute-start(bf16[32,1536]{1,0:T(8,128)(2,1)S(1)} %pad_maximum_fusion.7), channel_id=1, source_target_pairs={{0,2},{1,3},{2,0},{3,1},{4,6},{5,7},{6,4},{7,5},{8,10},{9,11},{10,... | collective-permute-start | bytes 294920 | tf_op jit(solution)/shard_map/ppermute | solution.py:39
  145.2 5.8 %collective-permute-start.18 = (bf16[32,1536]{1,0:T(8,128)(2,1)S(1)}, bf16[32,1536]{1,0:T(8,128)(2,1)S(1)}, u32[]{:S(2)}, u32[]{:S(2)}) collective-permute-start(bf16[32,1536]{1,0:T(8,128)(2,1)S(1)} %pad_maximum_fusion.7), channel_id=1, source_target_pairs={{0,1},{1,0},{2,3},{3,2},{4,5},{5,4},{6,7},{7,6},{8,9},{9,8},{10,11... | collective-permute-start | bytes 294920 | tf_op jit(solution)/shard_map/ppermute | solution.py:39
Sparse Core Ops, SparseCore 0:
  55.6 84.5 all-gather.1

commit v17 on v16

--- a/solution.py
+++ b/solution.py
@@ -183,9 +183,11 @@
     ring = [along(features(e), e, "y", "x") for e in (1, 2, 3)]
     pair = jnp.stack([first, second])
     pair = jnp.concatenate([pair, swap(pair, "core", 1)], axis=0)
-    wo_other, pair, *ring = lax.optimization_barrier((swap(out_weight, "zh", 1), pair, *ring))
+    wo_other, pair, opposite, *ring = lax.optimization_barrier(
+        (swap(out_weight, "zh", 1), pair, along(pair, 2, "x", "y"), *ring)
+    )
     inputs = jnp.concatenate([features(0)] + ring, axis=0)
-    blocks = [pair] + [along(pair, d, "x", "y") for d in (1, 2, 3)]
+    blocks = [pair, along(pair, 1, "x", "y"), opposite, along(pair, 3, "x", "y")]
     sent, total = project(inputs, blocks)
 
     wo_piece = jnp.concatenate([out_weight, wo_other], axis=0)

time: 168 us -> 147 us (0.88)
  waiting for transfers between devices: 89.9 us -> 67.1 us
  starting transfers between devices: 37.6 us -> 39.3 us
    ppermute x11, waiting for transfers between devices: 67.1 us -> 41.2 us  [move(): lax.ppermute(value, AXES, [(flat(*at), flat(*where(*at))) for at in every...]
    ppermute x8, waiting for transfers between devices: 22.8 us -> 25 us  [swap(): return lax.ppermute(value, axis, [(i, i ^ d) for i in range(n)])]
    ppermute x11, starting transfers between devices: 24.4 us -> 26.2 us  [move(): lax.ppermute(value, AXES, [(flat(*at), flat(*where(*at))) for at in every...]
    unnamed x28 -> x26, local copies, waits for them, and re-layouts: 3.9 us -> 3.89 us
  transfers between devices with their start and end apart: 20 -> 20, of which waited for: 12 -> 16; matrix products, arithmetic and copies ran while one was open for 4% -> 5% of each run, Pallas kernels for 2% -> 3%
where the time goes in v17:
time: 147 us; the launch traced here: 145 us
  waiting for transfers between devices  67.1 us (46%)
  starting transfers between devices  39.3 us (27%)
  between operations  14.5 us (10%)
  matrix products  8.6 us (6%)
  other arithmetic  6.06 us (4%)
  local copies, waits for them, and re-layouts  5.58 us (4%)
  Pallas kernels  3.82 us (3%)
    ppermute x11, waiting for transfers between devices, move(): lax.ppermute(value, AXES, [(flat(*at), flat(*where(*at))) for at in every...  41.2 us
    ppermute x11, starting transfers between devices, move(): lax.ppermute(value, AXES, [(flat(*at), flat(*where(*at))) for at in every...  26.2 us
    ppermute x8, waiting for transfers between devices, swap(): return lax.ppermute(value, axis, [(i, i ^ d) for i in range(n)])  25 us
    ppermute x8, starting transfers between devices, swap(): return lax.ppermute(value, axis, [(i, i ^ d) for i in range(n)])  13.2 us
    dot_general x1, matrix products, body(): return jnp.dot(all_rows, wo, preferred_element_type=F32).astype(BF)  7.35 us
    unnamed x26, local copies, waits for them, and re-layouts  3.89 us
    pallas_call x1, Pallas kernels, project(): pl.pallas_call(project_kernel, out_shape=(jax.ShapeDtypeStruct((3, ROWS,...  3.78 us
  transfers between devices with their start and end apart: 20, of which 16 were waited for; matrix products, arithmetic and copies ran while one was open for 5% of the time, Pallas kernels for 3%

profile of v17, /device:TPU:24, one launch (start us, length us, event | category | flops | bytes accessed | tf_op | source)
XLA Modules:
  0.0 145.1 jit_solution(2638956802941646909)
XLA Ops:
  8.3 6.5 %collective-permute-start = (bf16[896,128]{1,0:T(8,128)(2,1)S(1)}, bf16[896,128]{1,0:T(8,128)(2,1)S(1)}, u32[]{:S(2)}, u32[]{:S(2)}) collective-permute-start(bf16[896,128]{1,0:T(8,128)(2,1)S(1)} %shard_map.118), channel_id=1, source_target_pairs={{0,0},{1,32},{2,4},{3,36},{4,64},{5,96},{6,68},{7,100},{8,8},{9,40... | collective-permute-start | bytes 688136 | tf_op jit(solution)/shard_map/ppermute | solution.py:43
  14.8 3.8 %collective-permute-start.1 = (bf16[896,128]{1,0:T(8,128)(2,1)S(1)}, bf16[896,128]{1,0:T(8,128)(2,1)S(1)}, u32[]{:S(2)}, u32[]{:S(2)}) collective-permute-start(bf16[896,128]{1,0:T(8,128)(2,1)S(1)} %shard_map.118), channel_id=1, source_target_pairs={{0,32},{1,0},{2,36},{3,4},{4,96},{5,64},{6,100},{7,68},{8,40},{9,8... | collective-permute-start | bytes 688136 | tf_op jit(solution)/shard_map/ppermute | solution.py:43
  18.6 1.6 %fusion.2 = (f32[128]{0:T(128)S(1)}, bf16[128,4096]{1,0:T(8,128)(2,1)S(1)}) fusion(bf16[128,4096]{1,0:T(8,128)(2,1)} %param.12, f32[4096]{0:T(1024)} %param.13), kind=kLoop, calls=%fused_computation.5 | loop fusion | flops 2621312 | bytes 2114048 | tf_op jit(solution)/shard_map/reduce_sum | solution.py:170
  20.3 3.3 %collective-permute-done = bf16[896,128]{1,0:T(8,128)(2,1)S(1)} collective-permute-done((bf16[896,128]{1,0:T(8,128)(2,1)S(1)}, bf16[896,128]{1,0:T(8,128)(2,1)S(1)}, u32[]{:S(2)}, u32[]{:S(2)}) %collective-permute-start) | collective-permute-done | bytes 229408 | tf_op jit(solution)/shard_map/ppermute | solution.py:43
  23.5 13.7 %collective-permute-done.1 = bf16[896,128]{1,0:T(8,128)(2,1)S(1)} collective-permute-done((bf16[896,128]{1,0:T(8,128)(2,1)S(1)}, bf16[896,128]{1,0:T(8,128)(2,1)S(1)}, u32[]{:S(2)}, u32[]{:S(2)}) %collective-permute-start.1) | collective-permute-done | bytes 229408 | tf_op jit(solution)/shard_map/ppermute | solution.py:43
  37.4 1.8 %collective-permute-done.3 = bf16[2,896,128]{2,1,0:T(8,128)(2,1)S(1)} collective-permute-done((bf16[2,896,128]{2,1,0:T(8,128)(2,1)S(1)}, bf16[2,896,128]{2,1,0:T(8,128)(2,1)S(1)}, u32[]{:S(2)}, u32[]{:S(2)}) %collective-permute-start.3) | collective-permute-done | bytes 458784 | tf_op jit(solution)/shard_map/ppermute | solution.py:39
  39.3 3.1 %collective-permute-start.4 = (bf16[4,896,128]{2,1,0:T(8,128)(2,1)S(1)}, bf16[4,896,128]{2,1,0:T(8,128)(2,1)S(1)}, u32[]{:S(2)}, u32[]{:S(2)}) collective-permute-start(bf16[4,896,128]{2,1,0:T(8,128)(2,1)S(1)} %pad_maximum_fusion.1.refs_0_), channel_id=1, source_target_pairs={{0,16},{1,17},{2,18},{3,19},{4,132},{5,133},{6,134},{7,135},{8,24}... | collective-permute-start | bytes 2752520 | tf_op jit(solution)/shard_map/ppermute | solution.py:43
  42.7 1.7 %collective-permute-start.6 = (bf16[128,1024]{1,0:T(8,128)(2,1)S(1)}, bf16[128,1024]{1,0:T(8,128)(2,1)}, u32[]{:S(2)}, u32[]{:S(2)}) collective-permute-start(bf16[128,1024]{1,0:T(8,128)(2,1)S(1)} %pad_maximum_fusion.5), channel_id=1, source_target_pairs={{0,128},{1,129},{2,130},{3,131},{4,20},{5,21},{6,22},{7,23},{8,136... | collective-permute-start | bytes 786440 | tf_op jit(solution)/shard_map/ppermute | solution.py:43
  44.4 2.6 %collective-permute-start.5 = (bf16[128,1024]{1,0:T(8,128)(2,1)S(1)}, bf16[128,1024]{1,0:T(8,128)(2,1)}, u32[]{:S(2)}, u32[]{:S(2)}) collective-permute-start(bf16[128,1024]{1,0:T(8,128)(2,1)S(1)} %pad_maximum_fusion.4), channel_id=1, source_target_pairs={{0,64},{1,65},{2,66},{3,67},{4,12},{5,13},{6,14},{7,15},{8,72},{9,... | collective-permute-start | bytes 786440 | tf_op jit(solution)/shard_map/ppermute | solution.py:43
  47.0 4.1 %collective-permute-start.2 = (bf16[24,4096]{1,0:T(8,128)(2,1)}, bf16[24,4096]{1,0:T(8,128)(2,1)S(1)}, u32[]{:S(2)}, u32[]{:S(2)}) collective-permute-start(bf16[24,4096]{1,0:T(8,128)(2,1)} %param.16), channel_id=1, source_target_pairs={{0,32},{32,0},{1,33},{33,1},{2,34},{34,2},{3,35},{35,3},{4,36},{36... | collective-permute-start | bytes 589832 | tf_op jit(solution)/shard_map/ppermute | solution.py:39
  51.1 6.2 %collective-permute-done.2 = bf16[24,4096]{1,0:T(8,128)(2,1)S(1)} collective-permute-done((bf16[24,4096]{1,0:T(8,128)(2,1)}, bf16[24,4096]{1,0:T(8,128)(2,1)S(1)}, u32[]{:S(2)}, u32[]{:S(2)}) %collective-permute-start.2) | collective-permute-done | bytes 196640 | tf_op jit(solution)/shard_map/ppermute | solution.py:39
  57.3 1.8 %collective-permute-done.7 = bf16[128,1024]{1,0:T(8,128)(2,1)S(1)} collective-permute-done((bf16[128,1024]{1,0:T(8,128)(2,1)S(1)}, bf16[128,1024]{1,0:T(8,128)(2,1)S(1)}, u32[]{:S(2)}, u32[]{:S(2)}) %collective-permute-start.7) | collective-permute-done | bytes 262176 | tf_op jit(solution)/shard_map/ppermute | solution.py:43
  60.0 1.7 %pad_maximum_fusion.3 = bf16[48,4096]{1,0:T(8,128)(2,1)} fusion(bf16[24,4096]{1,0:T(8,128)(2,1)S(1)} %collective-permute-done.2, bf16[24,4096]{1,0:T(8,128)(2,1)} %param.16), kind=kLoop, calls=%fused_computation.29 | loop fusion | flops 786432 | bytes 786432 | tf_op jit(solution)/shard_map/concatenate | solution.py:193
  61.7 1.6 %collective-permute-start.8 = (bf16[4,896,128]{2,1,0:T(8,128)(2,1)S(1)}, bf16[4,896,128]{2,1,0:T(8,128)(2,1)S(1)}, u32[]{:S(2)}, u32[]{:S(2)}) collective-permute-start(bf16[4,896,128]{2,1,0:T(8,128)(2,1)S(1)} %pad_maximum_fusion.1.refs_0_), channel_id=1, source_target_pairs={{0,8},{1,9},{2,10},{3,11},{4,68},{5,69},{6,70},{7,71},{8,0},{9,1},... | collective-permute-start | bytes 2752520 | tf_op jit(solution)/shard_map/ppermute | solution.py:43
  63.3 2.1 %collective-permute-start.9 = (bf16[4,896,128]{2,1,0:T(8,128)(2,1)S(1)}, bf16[4,896,128]{2,1,0:T(8,128)(2,1)}, u32[]{:S(2)}, u32[]{:S(2)}) collective-permute-start(bf16[4,896,128]{2,1,0:T(8,128)(2,1)S(1)} %pad_maximum_fusion.1.refs_0_), channel_id=1, source_target_pairs={{0,24},{1,25},{2,26},{3,27},{4,196},{5,197},{6,198},{7,199},{8,16}... | collective-permute-start | bytes 2752520 | tf_op jit(solution)/shard_map/ppermute | solution.py:43
  67.1 8.0 %collective-permute-done.8.refs_1_ = bf16[4,896,128]{2,1,0:T(8,128)(2,1)S(1)} collective-permute-done((bf16[4,896,128]{2,1,0:T(8,128)(2,1)S(1)}, bf16[4,896,128]{2,1,0:T(8,128)(2,1)S(1)}, u32[]{:S(2)}, u32[]{:S(2)}) %collective-permute-start.8) | collective-permute-done | bytes 917536 | tf_op jit(solution)/shard_map/ppermute | solution.py:43
  76.1 1.9 %collective-permute-done.9.refs_3_ = bf16[4,896,128]{2,1,0:T(8,128)(2,1)} collective-permute-done((bf16[4,896,128]{2,1,0:T(8,128)(2,1)S(1)}, bf16[4,896,128]{2,1,0:T(8,128)(2,1)}, u32[]{:S(2)}, u32[]{:S(2)}) %collective-permute-start.9) | collective-permute-done | bytes 917536 | tf_op jit(solution)/shard_map/ppermute | solution.py:43
  79.1 3.8 %shard_map.119 = (bf16[3,128,1792]{2,1,0:T(8,128)(2,1)S(1)}, f32[128,1792]{1,0:T(8,128)S(1)}) custom-call(bf16[512,1024]{1,0:T(8,128)(2,1)S(1)} %pad_maximum_fusion.x_ref, bf16[4,896,128]{2,1,0:T(8,128)(2,1)S(1)} %pad_maximum_fusion.1.refs_0_, bf16[4,896,128]{2,1,0:T(8,128)(2,1)S(1)} %copy-done.3, bf16[4,896,128]{2,1,0:T(8,128)(2,1)S(1)} %collective-permute-done.4.refs_2_, ...), custom_call_target="tpu_custom_call" | custom-call | flops 1879048192 | bytes 8000000 | tf_op jit(solution)/shard_map/pallas_call | solution.py:141
  83.8 1.8 %collective-permute-start.11 = (bf16[128,1792]{1,0:T(8,128)(2,1)S(1)}, bf16[128,1792]{1,0:T(8,128)(2,1)S(1)}, u32[]{:S(2)}, u32[]{:S(2)}) collective-permute-start(bf16[128,1792]{1,0:T(8,128)(2,1)S(1)} %get-tuple-element.31), channel_id=1, source_target_pairs={{0,128},{1,129},{2,130},{3,131},{4,20},{5,21},{6,22},{7,23},{8,136... | collective-permute-start | bytes 1376264 | tf_op jit(solution)/shard_map/ppermute | solution.py:43
  85.6 2.9 %collective-permute-start.12 = (bf16[128,1792]{1,0:T(8,128)(2,1)S(1)}, bf16[128,1792]{1,0:T(8,128)(2,1)S(1)}, u32[]{:S(2)}, u32[]{:S(2)}) collective-permute-start(bf16[128,1792]{1,0:T(8,128)(2,1)S(1)} %get-tuple-element.30), channel_id=1, source_target_pairs={{0,192},{1,193},{2,194},{3,195},{4,28},{5,29},{6,30},{7,31},{8,200... | collective-permute-start | bytes 1376264 | tf_op jit(solution)/shard_map/ppermute | solution.py:43
  88.6 3.9 %collective-permute-done.10 = bf16[128,1792]{1,0:T(8,128)(2,1)S(1)} collective-permute-done((bf16[128,1792]{1,0:T(8,128)(2,1)}, bf16[128,1792]{1,0:T(8,128)(2,1)S(1)}, u32[]{:S(2)}, u32[]{:S(2)}) %collective-permute-start.10) | collective-permute-done | bytes 458784 | tf_op jit(solution)/shard_map/ppermute | solution.py:43
  92.5 5.8 %collective-permute-done.11 = bf16[128,1792]{1,0:T(8,128)(2,1)S(1)} collective-permute-done((bf16[128,1792]{1,0:T(8,128)(2,1)S(1)}, bf16[128,1792]{1,0:T(8,128)(2,1)S(1)}, u32[]{:S(2)}, u32[]{:S(2)}) %collective-permute-start.11) | collective-permute-done | bytes 458784 | tf_op jit(solution)/shard_map/ppermute | solution.py:43
  98.3 1.8 %collective-permute-done.12 = bf16[128,1792]{1,0:T(8,128)(2,1)S(1)} collective-permute-done((bf16[128,1792]{1,0:T(8,128)(2,1)S(1)}, bf16[128,1792]{1,0:T(8,128)(2,1)S(1)}, u32[]{:S(2)}, u32[]{:S(2)}) %collective-permute-start.12) | collective-permute-done | bytes 458784 | tf_op jit(solution)/shard_map/ppermute | solution.py:43
  100.6 2.4 %collective-permute-start.15 = (bf16[32,2688]{1,0:T(8,128)(2,1)S(1)}, bf16[32,2688]{1,0:T(8,128)(2,1)S(1)}, u32[]{:S(2)}, u32[]{:S(2)}) collective-permute-start(bf16[32,2688]{1,0:T(8,128)(2,1)S(1)} %get-tuple-element.99), channel_id=1, source_target_pairs={{0,3},{1,2},{2,1},{3,0},{4,7},{5,6},{6,5},{7,4},{8,11},{9,10},{10,... | collective-permute-start | bytes 516104 | tf_op jit(solution)/shard_map/ppermute | solution.py:39
  103.0 2.1 %collective-permute-start.13 = (bf16[32,2688]{1,0:T(8,128)(2,1)S(1)}, bf16[32,2688]{1,0:T(8,128)(2,1)S(1)}, u32[]{:S(2)}, u32[]{:S(2)}) collective-permute-start(bf16[32,2688]{1,0:T(8,128)(2,1)S(1)} %get-tuple-element.97), channel_id=1, source_target_pairs={{0,1},{1,0},{2,3},{3,2},{4,5},{5,4},{6,7},{7,6},{8,9},{9,8},{10,11... | collective-permute-start | bytes 516104 | tf_op jit(solution)/shard_map/ppermute | solution.py:39
  105.1 8.1 %collective-permute-done.13 = bf16[32,2688]{1,0:T(8,128)(2,1)S(1)} collective-permute-done((bf16[32,2688]{1,0:T(8,128)(2,1)S(1)}, bf16[32,2688]{1,0:T(8,128)(2,1)S(1)}, u32[]{:S(2)}, u32[]{:S(2)}) %collective-permute-start.13) | collective-permute-done | bytes 172064 | tf_op jit(solution)/shard_map/ppermute | solution.py:39
  113.3 3.5 %collective-permute-done.14 = bf16[32,2688]{1,0:T(8,128)(2,1)S(1)} collective-permute-done((bf16[32,2688]{1,0:T(8,128)(2,1)S(1)}, bf16[32,2688]{1,0:T(8,128)(2,1)S(1)}, u32[]{:S(2)}, u32[]{:S(2)}) %collective-permute-start.14) | collective-permute-done | bytes 172064 | tf_op jit(solution)/shard_map/ppermute | solution.py:39
  120.0 2.3 %collective-permute-start.16 = (bf16[32,1536]{1,0:T(8,128)(2,1)S(1)}, bf16[32,1536]{1,0:T(8,128)(2,1)S(1)}, u32[]{:S(2)}, u32[]{:S(2)}) collective-permute-start(bf16[32,1536]{1,0:T(8,128)(2,1)S(1)} %pad_maximum_fusion.7), channel_id=1, source_target_pairs={{0,3},{1,2},{2,1},{3,0},{4,7},{5,6},{6,5},{7,4},{8,11},{9,10},{10,... | collective-permute-start | bytes 294920 | tf_op jit(solution)/shard_map/ppermute | solution.py:39
  122.2 2.2 %collective-permute-start.18 = (bf16[32,1536]{1,0:T(8,128)(2,1)S(1)}, bf16[32,1536]{1,0:T(8,128)(2,1)S(1)}, u32[]{:S(2)}, u32[]{:S(2)}) collective-permute-start(bf16[32,1536]{1,0:T(8,128)(2,1)S(1)} %pad_maximum_fusion.7), channel_id=1, source_target_pairs={{0,1},{1,0},{2,3},{3,2},{4,5},{5,4},{6,7},{7,6},{8,9},{9,8},{10,11... | collective-permute-start | bytes 294920 | tf_op jit(solution)/shard_map/ppermute | solution.py:39
  124.4 3.0 %collective-permute-done.16 = bf16[32,1536]{1,0:T(8,128)(2,1)S(1)} collective-permute-done((bf16[32,1536]{1,0:T(8,128)(2,1)S(1)}, bf16[32,1536]{1,0:T(8,128)(2,1)S(1)}, u32[]{:S(2)}, u32[]{:S(2)}) %collective-permute-start.16) | collective-permute-done | bytes 98336 | tf_op jit(solution)/shard_map/ppermute | solution.py:39
  127.5 2.3 %collective-permute-done.17 = bf16[32,1536]{1,0:T(8,128)(2,1)S(1)} collective-permute-done((bf16[32,1536]{1,0:T(8,128)(2,1)S(1)}, bf16[32,1536]{1,0:T(8,128)(2,1)S(1)}, u32[]{:S(2)}, u32[]{:S(2)}) %collective-permute-start.17) | collective-permute-done | bytes 98336 | tf_op jit(solution)/shard_map/ppermute | solution.py:39
  130.9 7.3 %convolution_convert_fusion = bf16[128,4096]{1,0:T(8,128)(2,1)} fusion(bf16[1536,4096]{1,0:T(8,128)(2,1)} %all-gather.2.cloned.1.call-done, bf16[32,1536]{1,0:T(8,128)(2,1)S(1)} %broadcast_select_fusion.4, bf16[32,1536]{1,0:T(8,128)(2,1)S(1)} %get-tuple-element.55, bf16[32,1536]{1,0:T(8,128)(2,1)S(1)} %get-tuple-element.54, ...), kind=kOutput, calls=%fused_computation.1 | convolution fusion | flops 1612709888 | bytes 14024704 | tf_op jit(solution)/shard_map/dot_general | solution.py:236
  (92 shorter events, 11.7 us)
Async XLA Ops:
  6.5 124.4 %all-gather.2.cloned.1.call-start = ((), (), s32[]{:S(2)}) async-start(), calls=%async_computation | async-start | bytes 12976128 | tf_op jit(solution)/shard_map/all_gather | solution.py:194
  6.5 0.9 copy-start
  7.5 0.8 copy-start.1
  8.3 15.3 %collective-permute-start = (bf16[896,128]{1,0:T(8,128)(2,1)S(1)}, bf16[896,128]{1,0:T(8,128)(2,1)S(1)}, u32[]{:S(2)}, u32[]{:S(2)}) collective-permute-start(bf16[896,128]{1,0:T(8,128)(2,1)S(1)} %shard_map.118), channel_id=1, source_target_pairs={{0,0},{1,32},{2,4},{3,36},{4,64},{5,96},{6,68},{7,100},{8,8},{9,40... | collective-permute-start | bytes 688136 | tf_op jit(solution)/shard_map/ppermute | solution.py:43
  14.8 22.5 %collective-permute-start.1 = (bf16[896,128]{1,0:T(8,128)(2,1)S(1)}, bf16[896,128]{1,0:T(8,128)(2,1)S(1)}, u32[]{:S(2)}, u32[]{:S(2)}) collective-permute-start(bf16[896,128]{1,0:T(8,128)(2,1)S(1)} %shard_map.118), channel_id=1, source_target_pairs={{0,32},{1,0},{2,36},{3,4},{4,96},{5,64},{6,100},{7,68},{8,40},{9,8... | collective-permute-start | bytes 688136 | tf_op jit(solution)/shard_map/ppermute | solution.py:43
  37.3 1.9 %collective-permute-start.3 = (bf16[2,896,128]{2,1,0:T(8,128)(2,1)S(1)}, bf16[2,896,128]{2,1,0:T(8,128)(2,1)S(1)}, u32[]{:S(2)}, u32[]{:S(2)}) collective-permute-start(bf16[2,896,128]{2,1,0:T(8,128)(2,1)S(1)} %pad_maximum_fusion.2), channel_id=1, source_target_pairs={{0,4},{4,0},{1,5},{5,1},{2,6},{6,2},{3,7},{7,3},{8,12},{12,8},{9,1... | collective-permute-start | bytes 1376264 | tf_op jit(solution)/shard_map/ppermute | solution.py:39
  39.3 20.6 %collective-permute-start.4 = (bf16[4,896,128]{2,1,0:T(8,128)(2,1)S(1)}, bf16[4,896,128]{2,1,0:T(8,128)(2,1)S(1)}, u32[]{:S(2)}, u32[]{:S(2)}) collective-permute-start(bf16[4,896,128]{2,1,0:T(8,128)(2,1)S(1)} %pad_maximum_fusion.1.refs_0_), channel_id=1, source_target_pairs={{0,16},{1,17},{2,18},{3,19},{4,132},{5,133},{6,134},{7,135},{8,24}... | collective-permute-start | bytes 2752520 | tf_op jit(solution)/shard_map/ppermute | solution.py:43
  42.6 16.5 %collective-permute-start.7 = (bf16[128,1024]{1,0:T(8,128)(2,1)S(1)}, bf16[128,1024]{1,0:T(8,128)(2,1)S(1)}, u32[]{:S(2)}, u32[]{:S(2)}) collective-permute-start(bf16[128,1024]{1,0:T(8,128)(2,1)S(1)} %pad_maximum_fusion.6), channel_id=1, source_target_pairs={{0,192},{1,193},{2,194},{3,195},{4,28},{5,29},{6,30},{7,31},{8,200... | collective-permute-start | bytes 786440 | tf_op jit(solution)/shard_map/ppermute | solution.py:43
  42.7 16.4 %collective-permute-start.6 = (bf16[128,1024]{1,0:T(8,128)(2,1)S(1)}, bf16[128,1024]{1,0:T(8,128)(2,1)}, u32[]{:S(2)}, u32[]{:S(2)}) collective-permute-start(bf16[128,1024]{1,0:T(8,128)(2,1)S(1)} %pad_maximum_fusion.5), channel_id=1, source_target_pairs={{0,128},{1,129},{2,130},{3,131},{4,20},{5,21},{6,22},{7,23},{8,136... | collective-permute-start | bytes 786440 | tf_op jit(solution)/shard_map/ppermute | solution.py:43
  44.4 14.7 %collective-permute-start.5 = (bf16[128,1024]{1,0:T(8,128)(2,1)S(1)}, bf16[128,1024]{1,0:T(8,128)(2,1)}, u32[]{:S(2)}, u32[]{:S(2)}) collective-permute-start(bf16[128,1024]{1,0:T(8,128)(2,1)S(1)} %pad_maximum_fusion.4), channel_id=1, source_target_pairs={{0,64},{1,65},{2,66},{3,67},{4,12},{5,13},{6,14},{7,15},{8,72},{9,... | collective-permute-start | bytes 786440 | tf_op jit(solution)/shard_map/ppermute | solution.py:43
  47.0 10.3 %collective-permute-start.2 = (bf16[24,4096]{1,0:T(8,128)(2,1)}, bf16[24,4096]{1,0:T(8,128)(2,1)S(1)}, u32[]{:S(2)}, u32[]{:S(2)}) collective-permute-start(bf16[24,4096]{1,0:T(8,128)(2,1)} %param.16), channel_id=1, source_target_pairs={{0,32},{32,0},{1,33},{33,1},{2,34},{34,2},{3,35},{35,3},{4,36},{36... | collective-permute-start | bytes 589832 | tf_op jit(solution)/shard_map/ppermute | solution.py:39
  61.7 13.5 %collective-permute-start.8 = (bf16[4,896,128]{2,1,0:T(8,128)(2,1)S(1)}, bf16[4,896,128]{2,1,0:T(8,128)(2,1)S(1)}, u32[]{:S(2)}, u32[]{:S(2)}) collective-permute-start(bf16[4,896,128]{2,1,0:T(8,128)(2,1)S(1)} %pad_maximum_fusion.1.refs_0_), channel_id=1, source_target_pairs={{0,8},{1,9},{2,10},{3,11},{4,68},{5,69},{6,70},{7,71},{8,0},{9,1},... | collective-permute-start | bytes 2752520 | tf_op jit(solution)/shard_map/ppermute | solution.py:43
  63.3 14.7 %collective-permute-start.9 = (bf16[4,896,128]{2,1,0:T(8,128)(2,1)S(1)}, bf16[4,896,128]{2,1,0:T(8,128)(2,1)}, u32[]{:S(2)}, u32[]{:S(2)}) collective-permute-start(bf16[4,896,128]{2,1,0:T(8,128)(2,1)S(1)} %pad_maximum_fusion.1.refs_0_), channel_id=1, source_target_pairs={{0,24},{1,25},{2,26},{3,27},{4,196},{5,197},{6,198},{7,199},{8,16}... | collective-permute-start | bytes 2752520 | tf_op jit(solution)/shard_map/ppermute | solution.py:43
  75.2 0.9 copy-start.2
  78.0 1.2 copy-start.3
  82.9 5.6 %copy-start.4 = (f32[128,128]{1,0:T(8,128)S(1)}, f32[128,128]{1,0:T(8,128)}, u32[]{:S(2)}) copy-start(f32[128,128]{1,0:T(8,128)} %constant.76.clone) | copy-start | bytes 196612
  83.0 5.6 %copy-start.5 = (f32[128,128]{1,0:T(8,128)S(1)}, f32[128,128]{1,0:T(8,128)}, u32[]{:S(2)}) copy-start(f32[128,128]{1,0:T(8,128)} %constant.77.clone) | copy-start | bytes 196612
  83.8 8.7 %collective-permute-start.10 = (bf16[128,1792]{1,0:T(8,128)(2,1)}, bf16[128,1792]{1,0:T(8,128)(2,1)S(1)}, u32[]{:S(2)}, u32[]{:S(2)}) collective-permute-start(bf16[128,1792]{1,0:T(8,128)(2,1)} %get-tuple-element.29), channel_id=1, source_target_pairs={{0,64},{1,65},{2,66},{3,67},{4,12},{5,13},{6,14},{7,15},{8,72},{9,... | collective-permute-start | bytes 1376264 | tf_op jit(solution)/shard_map/ppermute | solution.py:43
  83.8 14.5 %collective-permute-start.11 = (bf16[128,1792]{1,0:T(8,128)(2,1)S(1)}, bf16[128,1792]{1,0:T(8,128)(2,1)S(1)}, u32[]{:S(2)}, u32[]{:S(2)}) collective-permute-start(bf16[128,1792]{1,0:T(8,128)(2,1)S(1)} %get-tuple-element.31), channel_id=1, source_target_pairs={{0,128},{1,129},{2,130},{3,131},{4,20},{5,21},{6,22},{7,23},{8,136... | collective-permute-start | bytes 1376264 | tf_op jit(solution)/shard_map/ppermute | solution.py:43
  85.6 14.6 %collective-permute-start.12 = (bf16[128,1792]{1,0:T(8,128)(2,1)S(1)}, bf16[128,1792]{1,0:T(8,128)(2,1)S(1)}, u32[]{:S(2)}, u32[]{:S(2)}) collective-permute-start(bf16[128,1792]{1,0:T(8,128)(2,1)S(1)} %get-tuple-element.30), channel_id=1, source_target_pairs={{0,192},{1,193},{2,194},{3,195},{4,28},{5,29},{6,30},{7,31},{8,200... | collective-permute-start | bytes 1376264 | tf_op jit(solution)/shard_map/ppermute | solution.py:43
  100.6 16.3 %collective-permute-start.15 = (bf16[32,2688]{1,0:T(8,128)(2,1)S(1)}, bf16[32,2688]{1,0:T(8,128)(2,1)S(1)}, u32[]{:S(2)}, u32[]{:S(2)}) collective-permute-start(bf16[32,2688]{1,0:T(8,128)(2,1)S(1)} %get-tuple-element.99), channel_id=1, source_target_pairs={{0,3},{1,2},{2,1},{3,0},{4,7},{5,6},{6,5},{7,4},{8,11},{9,10},{10,... | collective-permute-start | bytes 516104 | tf_op jit(solution)/shard_map/ppermute | solution.py:39
  103.0 13.9 %collective-permute-start.14 = (bf16[32,2688]{1,0:T(8,128)(2,1)S(1)}, bf16[32,2688]{1,0:T(8,128)(2,1)S(1)}, u32[]{:S(2)}, u32[]{:S(2)}) collective-permute-start(bf16[32,2688]{1,0:T(8,128)(2,1)S(1)} %get-tuple-element.98), channel_id=1, source_target_pairs={{0,2},{1,3},{2,0},{3,1},{4,6},{5,7},{6,4},{7,5},{8,10},{9,11},{10,... | collective-permute-start | bytes 516104 | tf_op jit(solution)/shard_map/ppermute | solution.py:39
  103.0 10.3 %collective-permute-start.13 = (bf16[32,2688]{1,0:T(8,128)(2,1)S(1)}, bf16[32,2688]{1,0:T(8,128)(2,1)S(1)}, u32[]{:S(2)}, u32[]{:S(2)}) collective-permute-start(bf16[32,2688]{1,0:T(8,128)(2,1)S(1)} %get-tuple-element.97), channel_id=1, source_target_pairs={{0,1},{1,0},{2,3},{3,2},{4,5},{5,4},{6,7},{7,6},{8,9},{9,8},{10,11... | collective-permute-start | bytes 516104 | tf_op jit(solution)/shard_map/ppermute | solution.py:39
  118.1 1.5 %copy-start.6 = (bf16[384,384]{1,0:T(8,128)(2,1)S(1)}, bf16[384,384]{1,0:T(8,128)(2,1)}, u32[]{:S(2)}) copy-start(bf16[384,384]{1,0:T(8,128)(2,1)} %constant.78.clone) | copy-start | bytes 884740
  118.1 1.5 %copy-start.7 = (bf16[384,384]{1,0:T(8,128)(2,1)S(1)}, bf16[384,384]{1,0:T(8,128)(2,1)}, u32[]{:S(2)}) copy-start(bf16[384,384]{1,0:T(8,128)(2,1)} %constant.79.clone) | copy-start | bytes 884740
  120.0 7.5 %collective-permute-start.16 = (bf16[32,1536]{1,0:T(8,128)(2,1)S(1)}, bf16[32,1536]{1,0:T(8,128)(2,1)S(1)}, u32[]{:S(2)}, u32[]{:S(2)}) collective-permute-start(bf16[32,1536]{1,0:T(8,128)(2,1)S(1)} %pad_maximum_fusion.7), channel_id=1, source_target_pairs={{0,3},{1,2},{2,1},{3,0},{4,7},{5,6},{6,5},{7,4},{8,11},{9,10},{10,... | collective-permute-start | bytes 294920 | tf_op jit(solution)/shard_map/ppermute | solution.py:39
  122.2 7.6 %collective-permute-start.17 = (bf16[32,1536]{1,0:T(8,128)(2,1)S(1)}, bf16[32,1536]{1,0:T(8,128)(2,1)S(1)}, u32[]{:S(2)}, u32[]{:S(2)}) collective-permute-start(bf16[32,1536]{1,0:T(8,128)(2,1)S(1)} %pad_maximum_fusion.7), channel_id=1, source_target_pairs={{0,2},{1,3},{2,0},{3,1},{4,6},{5,7},{6,4},{7,5},{8,10},{9,11},{10,... | collective-permute-start | bytes 294920 | tf_op jit(solution)/shard_map/ppermute | solution.py:39
  122.2 7.6 %collective-permute-start.18 = (bf16[32,1536]{1,0:T(8,128)(2,1)S(1)}, bf16[32,1536]{1,0:T(8,128)(2,1)S(1)}, u32[]{:S(2)}, u32[]{:S(2)}) collective-permute-start(bf16[32,1536]{1,0:T(8,128)(2,1)S(1)} %pad_maximum_fusion.7), channel_id=1, source_target_pairs={{0,1},{1,0},{2,3},{3,2},{4,5},{5,4},{6,7},{7,6},{8,9},{9,8},{10,11... | collective-permute-start | bytes 294920 | tf_op jit(solution)/shard_map/ppermute | solution.py:39
Sparse Core Ops, SparseCore 0:
  61.8 69.0 all-gather.1

commit v18 on v15

--- a/solution.py
+++ b/solution.py
@@ -178,9 +178,10 @@
             picked.append(lax.dynamic_slice(gained, (0, (((s >> 1) * 4 + at) * 2 + (s & 1)) * 256), (ROWS, 256)))
         return jnp.concatenate(picked, axis=1)
 
-    ring = [along(features(e), e, "y", "x") for e in (1, 2, 3)]
+    ring = [along(features(e)[:, at : at + 512], e, "y", "x") for e in (1, 2, 3) for at in (0, 512)]
     second = move(packed, lambda y, zh, x, c, t: ((2 * zh + c) ^ y, 1 - (t & 1), x, t >> 1, y))
     first, second, out_weight, *ring = lax.optimization_barrier((first, second, out_weight, *ring))
+    ring = [jnp.concatenate(ring[at : at + 2], axis=1) for at in (0, 2, 4)]
     inputs = jnp.concatenate([features(0)] + ring, axis=0)
 
     pair = jnp.stack([first, second])

time: 145 us -> 148 us (1.021)
  waiting for transfers between devices: 72.6 us -> 60.9 us
  starting transfers between devices: 34.6 us -> 45.1 us
  local copies, waits for them, and re-layouts: 3.99 us -> 7.23 us
    ppermute x11 -> x14, waiting for transfers between devices: 42.6 us -> 35.8 us  [move(): lax.ppermute(value, AXES, [(flat(*at), flat(*where(*at))) for at in every...]
    ppermute x11 -> x14, starting transfers between devices: 25.5 us -> 31 us  [move(): lax.ppermute(value, AXES, [(flat(*at), flat(*where(*at))) for at in every...]
    ppermute x8, starting transfers between devices: 9.08 us -> 14.1 us  [swap(): return lax.ppermute(value, axis, [(i, i ^ d) for i in range(n)])]
    ppermute x8, waiting for transfers between devices: 30 us -> 25 us  [swap(): return lax.ppermute(value, axis, [(i, i ^ d) for i in range(n)])]
    unnamed x30, local copies, waits for them, and re-layouts: 2.23 us -> 4.76 us
  transfers between devices with their start and end apart: 20 -> 23, of which waited for: 14 -> 16; matrix products, arithmetic and copies ran while one was open for 4% -> 6% of each run, Pallas kernels for 3% -> 3%
where the time goes in v18:
time: 148 us; the launch traced here: 146 us
  waiting for transfers between devices  60.9 us (41%)
  starting transfers between devices  45.1 us (30%)
  between operations  14.8 us (10%)
  matrix products  8.59 us (6%)
  local copies, waits for them, and re-layouts  7.23 us (5%)
  other arithmetic  5.26 us (4%)
  Pallas kernels  3.82 us (3%)
    ppermute x14, waiting for transfers between devices, move(): lax.ppermute(value, AXES, [(flat(*at), flat(*where(*at))) for at in every...  35.8 us
    ppermute x14, starting transfers between devices, move(): lax.ppermute(value, AXES, [(flat(*at), flat(*where(*at))) for at in every...  31 us
    ppermute x8, waiting for transfers between devices, swap(): return lax.ppermute(value, axis, [(i, i ^ d) for i in range(n)])  25 us
    ppermute x8, starting transfers between devices, swap(): return lax.ppermute(value, axis, [(i, i ^ d) for i in range(n)])  14.1 us
    dot_general x1, matrix products, body(): return jnp.dot(all_rows, wo, preferred_element_type=F32).astype(BF)  7.35 us
    unnamed x30, local copies, waits for them, and re-layouts  4.76 us
    pallas_call x1, Pallas kernels, project(): pl.pallas_call(project_kernel, out_shape=(jax.ShapeDtypeStruct((3, ROWS,...  3.78 us
  transfers between devices with their start and end apart: 23, of which 16 were waited for; matrix products, arithmetic and copies ran while one was open for 6% of the time, Pallas kernels for 3%

profile of v18, /device:TPU:24, one launch (start us, length us, event | category | flops | bytes accessed | tf_op | source)
XLA Modules:
  0.0 145.7 jit_solution(14092554945345965551)
XLA Ops:
  8.3 6.5 %collective-permute-start = (bf16[896,128]{1,0:T(8,128)(2,1)S(1)}, bf16[896,128]{1,0:T(8,128)(2,1)S(1)}, u32[]{:S(2)}, u32[]{:S(2)}) collective-permute-start(bf16[896,128]{1,0:T(8,128)(2,1)S(1)} %shard_map.118), channel_id=1, source_target_pairs={{0,0},{1,32},{2,4},{3,36},{4,64},{5,96},{6,68},{7,100},{8,8},{9,40... | collective-permute-start | bytes 688136 | tf_op jit(solution)/shard_map/ppermute | solution.py:43
  14.8 3.8 %collective-permute-start.1 = (bf16[896,128]{1,0:T(8,128)(2,1)S(1)}, bf16[896,128]{1,0:T(8,128)(2,1)S(1)}, u32[]{:S(2)}, u32[]{:S(2)}) collective-permute-start(bf16[896,128]{1,0:T(8,128)(2,1)S(1)} %shard_map.118), channel_id=1, source_target_pairs={{0,32},{1,0},{2,36},{3,4},{4,96},{5,64},{6,100},{7,68},{8,40},{9,8... | collective-permute-start | bytes 688136 | tf_op jit(solution)/shard_map/ppermute | solution.py:43
  18.8 1.6 %fusion.2 = (f32[128]{0:T(128)S(1)}, bf16[128,4096]{1,0:T(8,128)(2,1)S(1)}) fusion(bf16[128,4096]{1,0:T(8,128)(2,1)} %param.12, f32[4096]{0:T(1024)} %param.13), kind=kLoop, calls=%fused_computation.5 | loop fusion | flops 2621312 | bytes 2114048 | tf_op jit(solution)/shard_map/reduce_sum | solution.py:170
  20.7 2.3 %collective-permute-start.7 = (bf16[128,512]{1,0:T(8,128)(2,1)S(1)}, bf16[128,512]{1,0:T(8,128)(2,1)S(1)}, u32[]{:S(2)}, u32[]{:S(2)}) collective-permute-start(bf16[128,512]{1,0:T(8,128)(2,1)S(1)} %pad_maximum_fusion.8), channel_id=1, source_target_pairs={{0,192},{1,193},{2,194},{3,195},{4,28},{5,29},{6,30},{7,31},{8,200... | collective-permute-start | bytes 393224 | tf_op jit(solution)/shard_map/ppermute | solution.py:43
  24.1 2.6 %collective-permute-start.5 = (bf16[128,512]{1,0:T(8,128)(2,1)S(1)}, bf16[128,512]{1,0:T(8,128)(2,1)}, u32[]{:S(2)}, u32[]{:S(2)}) collective-permute-start(bf16[128,512]{1,0:T(8,128)(2,1)S(1)} %pad_maximum_fusion.6), channel_id=1, source_target_pairs={{0,128},{1,129},{2,130},{3,131},{4,20},{5,21},{6,22},{7,23},{8,136... | collective-permute-start | bytes 393224 | tf_op jit(solution)/shard_map/ppermute | solution.py:43
  26.8 1.6 %collective-permute-done.7 = bf16[128,512]{1,0:T(8,128)(2,1)S(1)} collective-permute-done((bf16[128,512]{1,0:T(8,128)(2,1)S(1)}, bf16[128,512]{1,0:T(8,128)(2,1)S(1)}, u32[]{:S(2)}, u32[]{:S(2)}) %collective-permute-start.7) | collective-permute-done | bytes 131104 | tf_op jit(solution)/shard_map/ppermute | solution.py:43
  29.5 7.0 %collective-permute-done.6 = bf16[128,512]{1,0:T(8,128)(2,1)S(1)} collective-permute-done((bf16[128,512]{1,0:T(8,128)(2,1)S(1)}, bf16[128,512]{1,0:T(8,128)(2,1)S(1)}, u32[]{:S(2)}, u32[]{:S(2)}) %collective-permute-start.6) | collective-permute-done | bytes 131104 | tf_op jit(solution)/shard_map/ppermute | solution.py:43
  36.5 2.0 %collective-permute-start.2 = (bf16[128,512]{1,0:T(8,128)(2,1)S(1)}, bf16[128,512]{1,0:T(8,128)(2,1)S(1)}, u32[]{:S(2)}, u32[]{:S(2)}) collective-permute-start(bf16[128,512]{1,0:T(8,128)(2,1)S(1)} %pad_maximum_fusion.3), channel_id=1, source_target_pairs={{0,64},{1,65},{2,66},{3,67},{4,12},{5,13},{6,14},{7,15},{8,72},{9,... | collective-permute-start | bytes 393224 | tf_op jit(solution)/shard_map/ppermute | solution.py:43
  38.5 3.0 %collective-permute-done.3 = bf16[128,512]{1,0:T(8,128)(2,1)} collective-permute-done((bf16[128,512]{1,0:T(8,128)(2,1)S(1)}, bf16[128,512]{1,0:T(8,128)(2,1)}, u32[]{:S(2)}, u32[]{:S(2)}) %collective-permute-start.3) | collective-permute-done | bytes 131104 | tf_op jit(solution)/shard_map/ppermute | solution.py:43
  41.6 1.3 collective-permute-done.2
  43.7 1.8 %collective-permute-done.9 = bf16[2,896,128]{2,1,0:T(8,128)(2,1)S(1)} collective-permute-done((bf16[2,896,128]{2,1,0:T(8,128)(2,1)S(1)}, bf16[2,896,128]{2,1,0:T(8,128)(2,1)S(1)}, u32[]{:S(2)}, u32[]{:S(2)}) %collective-permute-start.9) | collective-permute-done | bytes 458784 | tf_op jit(solution)/shard_map/ppermute | solution.py:39
  45.6 3.1 %collective-permute-start.10 = (bf16[4,896,128]{2,1,0:T(8,128)(2,1)S(1)}, bf16[4,896,128]{2,1,0:T(8,128)(2,1)S(1)}, u32[]{:S(2)}, u32[]{:S(2)}) collective-permute-start(bf16[4,896,128]{2,1,0:T(8,128)(2,1)S(1)} %pad_maximum_fusion.refs_0_), channel_id=1, source_target_pairs={{0,16},{1,17},{2,18},{3,19},{4,132},{5,133},{6,134},{7,135},{8,24}... | collective-permute-start | bytes 2752520 | tf_op jit(solution)/shard_map/ppermute | solution.py:43
  48.7 4.9 %collective-permute-start.8 = (bf16[24,4096]{1,0:T(8,128)(2,1)S(1)}, bf16[24,4096]{1,0:T(8,128)(2,1)S(1)}, u32[]{:S(2)}, u32[]{:S(2)}) collective-permute-start(bf16[24,4096]{1,0:T(8,128)(2,1)S(1)} %copy-done.4), channel_id=1, source_target_pairs={{0,32},{32,0},{1,33},{33,1},{2,34},{34,2},{3,35},{35,3},{4,36},{36... | collective-permute-start | bytes 589832 | tf_op jit(solution)/shard_map/ppermute | solution.py:39
  53.6 6.5 %collective-permute-done.8 = bf16[24,4096]{1,0:T(8,128)(2,1)S(1)} collective-permute-done((bf16[24,4096]{1,0:T(8,128)(2,1)S(1)}, bf16[24,4096]{1,0:T(8,128)(2,1)S(1)}, u32[]{:S(2)}, u32[]{:S(2)}) %collective-permute-start.8) | collective-permute-done | bytes 196640 | tf_op jit(solution)/shard_map/ppermute | solution.py:39
  61.3 1.6 %collective-permute-start.11 = (bf16[4,896,128]{2,1,0:T(8,128)(2,1)S(1)}, bf16[4,896,128]{2,1,0:T(8,128)(2,1)S(1)}, u32[]{:S(2)}, u32[]{:S(2)}) collective-permute-start(bf16[4,896,128]{2,1,0:T(8,128)(2,1)S(1)} %pad_maximum_fusion.refs_0_), channel_id=1, source_target_pairs={{0,8},{1,9},{2,10},{3,11},{4,68},{5,69},{6,70},{7,71},{8,0},{9,1},... | collective-permute-start | bytes 2752520 | tf_op jit(solution)/shard_map/ppermute | solution.py:43
  62.9 2.1 %collective-permute-start.12 = (bf16[4,896,128]{2,1,0:T(8,128)(2,1)S(1)}, bf16[4,896,128]{2,1,0:T(8,128)(2,1)}, u32[]{:S(2)}, u32[]{:S(2)}) collective-permute-start(bf16[4,896,128]{2,1,0:T(8,128)(2,1)S(1)} %pad_maximum_fusion.refs_0_), channel_id=1, source_target_pairs={{0,24},{1,25},{2,26},{3,27},{4,196},{5,197},{6,198},{7,199},{8,16}... | collective-permute-start | bytes 2752520 | tf_op jit(solution)/shard_map/ppermute | solution.py:43
  66.9 7.9 %collective-permute-done.11.refs_1_ = bf16[4,896,128]{2,1,0:T(8,128)(2,1)S(1)} collective-permute-done((bf16[4,896,128]{2,1,0:T(8,128)(2,1)S(1)}, bf16[4,896,128]{2,1,0:T(8,128)(2,1)S(1)}, u32[]{:S(2)}, u32[]{:S(2)}) %collective-permute-start.11) | collective-permute-done | bytes 917536 | tf_op jit(solution)/shard_map/ppermute | solution.py:43
  75.8 1.9 %collective-permute-done.12.refs_3_ = bf16[4,896,128]{2,1,0:T(8,128)(2,1)} collective-permute-done((bf16[4,896,128]{2,1,0:T(8,128)(2,1)S(1)}, bf16[4,896,128]{2,1,0:T(8,128)(2,1)}, u32[]{:S(2)}, u32[]{:S(2)}) %collective-permute-start.12) | collective-permute-done | bytes 917536 | tf_op jit(solution)/shard_map/ppermute | solution.py:43
  78.8 3.8 %shard_map.119 = (bf16[3,128,1792]{2,1,0:T(8,128)(2,1)S(1)}, f32[128,1792]{1,0:T(8,128)S(1)}) custom-call(bf16[512,1024]{1,0:T(8,128)(2,1)S(1)} %maximum_maximum_fusion.x_ref, bf16[4,896,128]{2,1,0:T(8,128)(2,1)S(1)} %pad_maximum_fusion.refs_0_, bf16[4,896,128]{2,1,0:T(8,128)(2,1)S(1)} %copy-done.3, ...), custom_call_target="tpu_custom_call" | custom-call | flops 1879048192 | bytes 8000000 | tf_op jit(solution)/shard_map/pallas_call | solution.py:141
  84.1 2.9 %collective-permute-start.14 = (bf16[128,1792]{1,0:T(8,128)(2,1)S(1)}, bf16[128,1792]{1,0:T(8,128)(2,1)S(1)}, u32[]{:S(2)}, u32[]{:S(2)}) collective-permute-start(bf16[128,1792]{1,0:T(8,128)(2,1)S(1)} %get-tuple-element.35), channel_id=1, source_target_pairs={{0,128},{1,129},{2,130},{3,131},{4,20},{5,21},{6,22},{7,23},{8,136... | collective-permute-start | bytes 1376264 | tf_op jit(solution)/shard_map/ppermute | solution.py:43
  88.9 3.8 %collective-permute-done.13 = bf16[128,1792]{1,0:T(8,128)(2,1)S(1)} collective-permute-done((bf16[128,1792]{1,0:T(8,128)(2,1)}, bf16[128,1792]{1,0:T(8,128)(2,1)S(1)}, u32[]{:S(2)}, u32[]{:S(2)}) %collective-permute-start.13) | collective-permute-done | bytes 458784 | tf_op jit(solution)/shard_map/ppermute | solution.py:43
  92.7 6.5 %collective-permute-done.14 = bf16[128,1792]{1,0:T(8,128)(2,1)S(1)} collective-permute-done((bf16[128,1792]{1,0:T(8,128)(2,1)S(1)}, bf16[128,1792]{1,0:T(8,128)(2,1)S(1)}, u32[]{:S(2)}, u32[]{:S(2)}) %collective-permute-start.14) | collective-permute-done | bytes 458784 | tf_op jit(solution)/shard_map/ppermute | solution.py:43
  99.2 2.4 %collective-permute-done.15 = bf16[128,1792]{1,0:T(8,128)(2,1)S(1)} collective-permute-done((bf16[128,1792]{1,0:T(8,128)(2,1)S(1)}, bf16[128,1792]{1,0:T(8,128)(2,1)S(1)}, u32[]{:S(2)}, u32[]{:S(2)}) %collective-permute-start.15) | collective-permute-done | bytes 458784 | tf_op jit(solution)/shard_map/ppermute | solution.py:43
  102.0 1.9 %collective-permute-start.18 = (bf16[32,2688]{1,0:T(8,128)(2,1)S(1)}, bf16[32,2688]{1,0:T(8,128)(2,1)S(1)}, u32[]{:S(2)}, u32[]{:S(2)}) collective-permute-start(bf16[32,2688]{1,0:T(8,128)(2,1)S(1)} %get-tuple-element.103), channel_id=1, source_target_pairs={{0,3},{1,2},{2,1},{3,0},{4,7},{5,6},{6,5},{7,4},{8,11},{9,10},{10,... | collective-permute-start | bytes 516104 | tf_op jit(solution)/shard_map/ppermute | solution.py:39
  104.7 1.9 %collective-permute-start.16 = (bf16[32,2688]{1,0:T(8,128)(2,1)S(1)}, bf16[32,2688]{1,0:T(8,128)(2,1)S(1)}, u32[]{:S(2)}, u32[]{:S(2)}) collective-permute-start(bf16[32,2688]{1,0:T(8,128)(2,1)S(1)} %get-tuple-element.101), channel_id=1, source_target_pairs={{0,1},{1,0},{2,3},{3,2},{4,5},{5,4},{6,7},{7,6},{8,9},{9,8},{10,11... | collective-permute-start | bytes 516104 | tf_op jit(solution)/shard_map/ppermute | solution.py:39
  106.7 6.9 %collective-permute-done.16 = bf16[32,2688]{1,0:T(8,128)(2,1)S(1)} collective-permute-done((bf16[32,2688]{1,0:T(8,128)(2,1)S(1)}, bf16[32,2688]{1,0:T(8,128)(2,1)S(1)}, u32[]{:S(2)}, u32[]{:S(2)}) %collective-permute-start.16) | collective-permute-done | bytes 172064 | tf_op jit(solution)/shard_map/ppermute | solution.py:39
  113.7 4.1 %collective-permute-done.17 = bf16[32,2688]{1,0:T(8,128)(2,1)S(1)} collective-permute-done((bf16[32,2688]{1,0:T(8,128)(2,1)S(1)}, bf16[32,2688]{1,0:T(8,128)(2,1)S(1)}, u32[]{:S(2)}, u32[]{:S(2)}) %collective-permute-start.17) | collective-permute-done | bytes 172064 | tf_op jit(solution)/shard_map/ppermute | solution.py:39
  121.2 2.6 %collective-permute-start.19 = (bf16[32,1536]{1,0:T(8,128)(2,1)S(1)}, bf16[32,1536]{1,0:T(8,128)(2,1)S(1)}, u32[]{:S(2)}, u32[]{:S(2)}) collective-permute-start(bf16[32,1536]{1,0:T(8,128)(2,1)S(1)} %pad_maximum_fusion.9), channel_id=1, source_target_pairs={{0,3},{1,2},{2,1},{3,0},{4,7},{5,6},{6,5},{7,4},{8,11},{9,10},{10,... | collective-permute-start | bytes 294920 | tf_op jit(solution)/shard_map/ppermute | solution.py:39
  123.7 1.9 %collective-permute-start.21 = (bf16[32,1536]{1,0:T(8,128)(2,1)S(1)}, bf16[32,1536]{1,0:T(8,128)(2,1)S(1)}, u32[]{:S(2)}, u32[]{:S(2)}) collective-permute-start(bf16[32,1536]{1,0:T(8,128)(2,1)S(1)} %pad_maximum_fusion.9), channel_id=1, source_target_pairs={{0,1},{1,0},{2,3},{3,2},{4,5},{5,4},{6,7},{7,6},{8,9},{9,8},{10,11... | collective-permute-start | bytes 294920 | tf_op jit(solution)/shard_map/ppermute | solution.py:39
  125.6 3.0 %collective-permute-done.19 = bf16[32,1536]{1,0:T(8,128)(2,1)S(1)} collective-permute-done((bf16[32,1536]{1,0:T(8,128)(2,1)S(1)}, bf16[32,1536]{1,0:T(8,128)(2,1)S(1)}, u32[]{:S(2)}, u32[]{:S(2)}) %collective-permute-start.19) | collective-permute-done | bytes 98336 | tf_op jit(solution)/shard_map/ppermute | solution.py:39
  128.7 2.6 %collective-permute-done.20 = bf16[32,1536]{1,0:T(8,128)(2,1)S(1)} collective-permute-done((bf16[32,1536]{1,0:T(8,128)(2,1)S(1)}, bf16[32,1536]{1,0:T(8,128)(2,1)S(1)}, u32[]{:S(2)}, u32[]{:S(2)}) %collective-permute-start.20) | collective-permute-done | bytes 98336 | tf_op jit(solution)/shard_map/ppermute | solution.py:39
  131.5 7.4 %convolution_convert_fusion = bf16[128,4096]{1,0:T(8,128)(2,1)} fusion(bf16[1536,4096]{1,0:T(8,128)(2,1)} %all-gather.2.cloned.1.call-done, bf16[32,1536]{1,0:T(8,128)(2,1)S(1)} %broadcast_select_fusion.4, bf16[32,1536]{1,0:T(8,128)(2,1)S(1)} %get-tuple-element.59, bf16[32,1536]{1,0:T(8,128)(2,1)S(1)} %get-tuple-element.58, ...), kind=kOutput, calls=%fused_computation.1 | convolution fusion | flops 1612709888 | bytes 14024704 | tf_op jit(solution)/shard_map/dot_general | solution.py:236
  (105 shorter events, 17.7 us)
Async XLA Ops:
  6.5 124.9 %all-gather.2.cloned.1.call-start = ((), (), s32[]{:S(2)}) async-start(), calls=%async_computation | async-start | bytes 12976128 | tf_op jit(solution)/shard_map/all_gather | solution.py:194
  6.5 0.9 copy-start
  7.5 0.8 copy-start.1
  8.3 34.6 %collective-permute-start = (bf16[896,128]{1,0:T(8,128)(2,1)S(1)}, bf16[896,128]{1,0:T(8,128)(2,1)S(1)}, u32[]{:S(2)}, u32[]{:S(2)}) collective-permute-start(bf16[896,128]{1,0:T(8,128)(2,1)S(1)} %shard_map.118), channel_id=1, source_target_pairs={{0,0},{1,32},{2,4},{3,36},{4,64},{5,96},{6,68},{7,100},{8,8},{9,40... | collective-permute-start | bytes 688136 | tf_op jit(solution)/shard_map/ppermute | solution.py:43
  14.8 28.1 %collective-permute-start.1 = (bf16[896,128]{1,0:T(8,128)(2,1)S(1)}, bf16[896,128]{1,0:T(8,128)(2,1)S(1)}, u32[]{:S(2)}, u32[]{:S(2)}) collective-permute-start(bf16[896,128]{1,0:T(8,128)(2,1)S(1)} %shard_map.118), channel_id=1, source_target_pairs={{0,32},{1,0},{2,36},{3,4},{4,96},{5,64},{6,100},{7,68},{8,40},{9,8... | collective-permute-start | bytes 688136 | tf_op jit(solution)/shard_map/ppermute | solution.py:43
  20.7 28.0 %copy-start.4 = (bf16[24,4096]{1,0:T(8,128)(2,1)S(1)}, bf16[24,4096]{1,0:T(8,128)(2,1)}, u32[]{:S(2)}) copy-start(bf16[24,4096]{1,0:T(8,128)(2,1)} %param.16) | copy-start | bytes 589828
  20.7 7.7 %collective-permute-start.7 = (bf16[128,512]{1,0:T(8,128)(2,1)S(1)}, bf16[128,512]{1,0:T(8,128)(2,1)S(1)}, u32[]{:S(2)}, u32[]{:S(2)}) collective-permute-start(bf16[128,512]{1,0:T(8,128)(2,1)S(1)} %pad_maximum_fusion.8), channel_id=1, source_target_pairs={{0,192},{1,193},{2,194},{3,195},{4,28},{5,29},{6,30},{7,31},{8,200... | collective-permute-start | bytes 393224 | tf_op jit(solution)/shard_map/ppermute | solution.py:43
  23.1 13.4 %collective-permute-start.6 = (bf16[128,512]{1,0:T(8,128)(2,1)S(1)}, bf16[128,512]{1,0:T(8,128)(2,1)S(1)}, u32[]{:S(2)}, u32[]{:S(2)}) collective-permute-start(bf16[128,512]{1,0:T(8,128)(2,1)S(1)} %pad_maximum_fusion.7), channel_id=1, source_target_pairs={{0,192},{1,193},{2,194},{3,195},{4,28},{5,29},{6,30},{7,31},{8,200... | collective-permute-start | bytes 393224 | tf_op jit(solution)/shard_map/ppermute | solution.py:43
  24.1 12.4 %collective-permute-start.5 = (bf16[128,512]{1,0:T(8,128)(2,1)S(1)}, bf16[128,512]{1,0:T(8,128)(2,1)}, u32[]{:S(2)}, u32[]{:S(2)}) collective-permute-start(bf16[128,512]{1,0:T(8,128)(2,1)S(1)} %pad_maximum_fusion.6), channel_id=1, source_target_pairs={{0,128},{1,129},{2,130},{3,131},{4,20},{5,21},{6,22},{7,23},{8,136... | collective-permute-start | bytes 393224 | tf_op jit(solution)/shard_map/ppermute | solution.py:43
  28.4 10.2 %collective-permute-start.4 = (bf16[128,512]{1,0:T(8,128)(2,1)S(1)}, bf16[128,512]{1,0:T(8,128)(2,1)}, u32[]{:S(2)}, u32[]{:S(2)}) collective-permute-start(bf16[128,512]{1,0:T(8,128)(2,1)S(1)} %pad_maximum_fusion.5), channel_id=1, source_target_pairs={{0,128},{1,129},{2,130},{3,131},{4,20},{5,21},{6,22},{7,23},{8,136... | collective-permute-start | bytes 393224 | tf_op jit(solution)/shard_map/ppermute | solution.py:43
  36.5 5.1 %collective-permute-start.3 = (bf16[128,512]{1,0:T(8,128)(2,1)S(1)}, bf16[128,512]{1,0:T(8,128)(2,1)}, u32[]{:S(2)}, u32[]{:S(2)}) collective-permute-start(bf16[128,512]{1,0:T(8,128)(2,1)S(1)} %pad_maximum_fusion.4), channel_id=1, source_target_pairs={{0,64},{1,65},{2,66},{3,67},{4,12},{5,13},{6,14},{7,15},{8,72},{9,... | collective-permute-start | bytes 393224 | tf_op jit(solution)/shard_map/ppermute | solution.py:43
  36.5 6.4 %collective-permute-start.2 = (bf16[128,512]{1,0:T(8,128)(2,1)S(1)}, bf16[128,512]{1,0:T(8,128)(2,1)S(1)}, u32[]{:S(2)}, u32[]{:S(2)}) collective-permute-start(bf16[128,512]{1,0:T(8,128)(2,1)S(1)} %pad_maximum_fusion.3), channel_id=1, source_target_pairs={{0,64},{1,65},{2,66},{3,67},{4,12},{5,13},{6,14},{7,15},{8,72},{9,... | collective-permute-start | bytes 393224 | tf_op jit(solution)/shard_map/ppermute | solution.py:43
  43.6 1.9 %collective-permute-start.9 = (bf16[2,896,128]{2,1,0:T(8,128)(2,1)S(1)}, bf16[2,896,128]{2,1,0:T(8,128)(2,1)S(1)}, u32[]{:S(2)}, u32[]{:S(2)}) collective-permute-start(bf16[2,896,128]{2,1,0:T(8,128)(2,1)S(1)} %pad_maximum_fusion.1), channel_id=1, source_target_pairs={{0,4},{4,0},{1,5},{5,1},{2,6},{6,2},{3,7},{7,3},{8,12},{12,8},{9,1... | collective-permute-start | bytes 1376264 | tf_op jit(solution)/shard_map/ppermute | solution.py:39
  45.6 15.0 %collective-permute-start.10 = (bf16[4,896,128]{2,1,0:T(8,128)(2,1)S(1)}, bf16[4,896,128]{2,1,0:T(8,128)(2,1)S(1)}, u32[]{:S(2)}, u32[]{:S(2)}) collective-permute-start(bf16[4,896,128]{2,1,0:T(8,128)(2,1)S(1)} %pad_maximum_fusion.refs_0_), channel_id=1, source_target_pairs={{0,16},{1,17},{2,18},{3,19},{4,132},{5,133},{6,134},{7,135},{8,24}... | collective-permute-start | bytes 2752520 | tf_op jit(solution)/shard_map/ppermute | solution.py:43
  48.7 11.4 %collective-permute-start.8 = (bf16[24,4096]{1,0:T(8,128)(2,1)S(1)}, bf16[24,4096]{1,0:T(8,128)(2,1)S(1)}, u32[]{:S(2)}, u32[]{:S(2)}) collective-permute-start(bf16[24,4096]{1,0:T(8,128)(2,1)S(1)} %copy-done.4), channel_id=1, source_target_pairs={{0,32},{32,0},{1,33},{33,1},{2,34},{34,2},{3,35},{35,3},{4,36},{36... | collective-permute-start | bytes 589832 | tf_op jit(solution)/shard_map/ppermute | solution.py:39
  61.3 13.5 %collective-permute-start.11 = (bf16[4,896,128]{2,1,0:T(8,128)(2,1)S(1)}, bf16[4,896,128]{2,1,0:T(8,128)(2,1)S(1)}, u32[]{:S(2)}, u32[]{:S(2)}) collective-permute-start(bf16[4,896,128]{2,1,0:T(8,128)(2,1)S(1)} %pad_maximum_fusion.refs_0_), channel_id=1, source_target_pairs={{0,8},{1,9},{2,10},{3,11},{4,68},{5,69},{6,70},{7,71},{8,0},{9,1},... | collective-permute-start | bytes 2752520 | tf_op jit(solution)/shard_map/ppermute | solution.py:43
  62.9 14.7 %collective-permute-start.12 = (bf16[4,896,128]{2,1,0:T(8,128)(2,1)S(1)}, bf16[4,896,128]{2,1,0:T(8,128)(2,1)}, u32[]{:S(2)}, u32[]{:S(2)}) collective-permute-start(bf16[4,896,128]{2,1,0:T(8,128)(2,1)S(1)} %pad_maximum_fusion.refs_0_), channel_id=1, source_target_pairs={{0,24},{1,25},{2,26},{3,27},{4,196},{5,197},{6,198},{7,199},{8,16}... | collective-permute-start | bytes 2752520 | tf_op jit(solution)/shard_map/ppermute | solution.py:43
  74.8 0.9 copy-start.2
  77.6 1.2 copy-start.3
  82.6 5.6 %copy-start.6 = (f32[128,128]{1,0:T(8,128)S(1)}, f32[128,128]{1,0:T(8,128)}, u32[]{:S(2)}) copy-start(f32[128,128]{1,0:T(8,128)} %constant.76.clone) | copy-start | bytes 196612
  83.5 9.3 %collective-permute-start.13 = (bf16[128,1792]{1,0:T(8,128)(2,1)}, bf16[128,1792]{1,0:T(8,128)(2,1)S(1)}, u32[]{:S(2)}, u32[]{:S(2)}) collective-permute-start(bf16[128,1792]{1,0:T(8,128)(2,1)} %get-tuple-element.33), channel_id=1, source_target_pairs={{0,64},{1,65},{2,66},{3,67},{4,12},{5,13},{6,14},{7,15},{8,72},{9,... | collective-permute-start | bytes 1376264 | tf_op jit(solution)/shard_map/ppermute | solution.py:43
  84.1 15.1 %collective-permute-start.14 = (bf16[128,1792]{1,0:T(8,128)(2,1)S(1)}, bf16[128,1792]{1,0:T(8,128)(2,1)S(1)}, u32[]{:S(2)}, u32[]{:S(2)}) collective-permute-start(bf16[128,1792]{1,0:T(8,128)(2,1)S(1)} %get-tuple-element.35), channel_id=1, source_target_pairs={{0,128},{1,129},{2,130},{3,131},{4,20},{5,21},{6,22},{7,23},{8,136... | collective-permute-start | bytes 1376264 | tf_op jit(solution)/shard_map/ppermute | solution.py:43
  87.0 14.6 %collective-permute-start.15 = (bf16[128,1792]{1,0:T(8,128)(2,1)S(1)}, bf16[128,1792]{1,0:T(8,128)(2,1)S(1)}, u32[]{:S(2)}, u32[]{:S(2)}) collective-permute-start(bf16[128,1792]{1,0:T(8,128)(2,1)S(1)} %get-tuple-element.34), channel_id=1, source_target_pairs={{0,192},{1,193},{2,194},{3,195},{4,28},{5,29},{6,30},{7,31},{8,200... | collective-permute-start | bytes 1376264 | tf_op jit(solution)/shard_map/ppermute | solution.py:43
  102.0 15.9 %collective-permute-start.18 = (bf16[32,2688]{1,0:T(8,128)(2,1)S(1)}, bf16[32,2688]{1,0:T(8,128)(2,1)S(1)}, u32[]{:S(2)}, u32[]{:S(2)}) collective-permute-start(bf16[32,2688]{1,0:T(8,128)(2,1)S(1)} %get-tuple-element.103), channel_id=1, source_target_pairs={{0,3},{1,2},{2,1},{3,0},{4,7},{5,6},{6,5},{7,4},{8,11},{9,10},{10,... | collective-permute-start | bytes 516104 | tf_op jit(solution)/shard_map/ppermute | solution.py:39
  103.8 14.0 %collective-permute-start.17 = (bf16[32,2688]{1,0:T(8,128)(2,1)S(1)}, bf16[32,2688]{1,0:T(8,128)(2,1)S(1)}, u32[]{:S(2)}, u32[]{:S(2)}) collective-permute-start(bf16[32,2688]{1,0:T(8,128)(2,1)S(1)} %get-tuple-element.102), channel_id=1, source_target_pairs={{0,2},{1,3},{2,0},{3,1},{4,6},{5,7},{6,4},{7,5},{8,10},{9,11},{10,... | collective-permute-start | bytes 516104 | tf_op jit(solution)/shard_map/ppermute | solution.py:39
  104.7 8.9 %collective-permute-start.16 = (bf16[32,2688]{1,0:T(8,128)(2,1)S(1)}, bf16[32,2688]{1,0:T(8,128)(2,1)S(1)}, u32[]{:S(2)}, u32[]{:S(2)}) collective-permute-start(bf16[32,2688]{1,0:T(8,128)(2,1)S(1)} %get-tuple-element.101), channel_id=1, source_target_pairs={{0,1},{1,0},{2,3},{3,2},{4,5},{5,4},{6,7},{7,6},{8,9},{9,8},{10,11... | collective-permute-start | bytes 516104 | tf_op jit(solution)/shard_map/ppermute | solution.py:39
  118.7 0.9 copy-start.7
  119.1 1.8 %copy-start.8 = (bf16[384,384]{1,0:T(8,128)(2,1)S(1)}, bf16[384,384]{1,0:T(8,128)(2,1)}, u32[]{:S(2)}) copy-start(bf16[384,384]{1,0:T(8,128)(2,1)} %constant.78.clone) | copy-start | bytes 884740
  119.1 1.8 %copy-start.9 = (bf16[384,384]{1,0:T(8,128)(2,1)S(1)}, bf16[384,384]{1,0:T(8,128)(2,1)}, u32[]{:S(2)}) copy-start(bf16[384,384]{1,0:T(8,128)(2,1)} %constant.79.clone) | copy-start | bytes 884740
  121.2 7.5 %collective-permute-start.19 = (bf16[32,1536]{1,0:T(8,128)(2,1)S(1)}, bf16[32,1536]{1,0:T(8,128)(2,1)S(1)}, u32[]{:S(2)}, u32[]{:S(2)}) collective-permute-start(bf16[32,1536]{1,0:T(8,128)(2,1)S(1)} %pad_maximum_fusion.9), channel_id=1, source_target_pairs={{0,3},{1,2},{2,1},{3,0},{4,7},{5,6},{6,5},{7,4},{8,11},{9,10},{10,... | collective-permute-start | bytes 294920 | tf_op jit(solution)/shard_map/ppermute | solution.py:39
  123.7 7.6 %collective-permute-start.20 = (bf16[32,1536]{1,0:T(8,128)(2,1)S(1)}, bf16[32,1536]{1,0:T(8,128)(2,1)S(1)}, u32[]{:S(2)}, u32[]{:S(2)}) collective-permute-start(bf16[32,1536]{1,0:T(8,128)(2,1)S(1)} %pad_maximum_fusion.9), channel_id=1, source_target_pairs={{0,2},{1,3},{2,0},{3,1},{4,6},{5,7},{6,4},{7,5},{8,10},{9,11},{10,... | collective-permute-start | bytes 294920 | tf_op jit(solution)/shard_map/ppermute | solution.py:39
  123.7 7.6 %collective-permute-start.21 = (bf16[32,1536]{1,0:T(8,128)(2,1)S(1)}, bf16[32,1536]{1,0:T(8,128)(2,1)S(1)}, u32[]{:S(2)}, u32[]{:S(2)}) collective-permute-start(bf16[32,1536]{1,0:T(8,128)(2,1)S(1)} %pad_maximum_fusion.9), channel_id=1, source_target_pairs={{0,1},{1,0},{2,3},{3,2},{4,5},{5,4},{6,7},{7,6},{8,9},{9,8},{10,11... | collective-permute-start | bytes 294920 | tf_op jit(solution)/shard_map/ppermute | solution.py:39
  (1 other events, 0.7 us)
Sparse Core Ops, SparseCore 0:
  61.5 69.9 all-gather.1

commit v19 on v17

--- a/solution.py
+++ b/solution.py
@@ -180,12 +180,13 @@
 
     second = move(packed, lambda y, zh, x, c, t: ((2 * zh + c) ^ y, 1 - (t & 1), x, t >> 1, y))
     first, second, gained, out_weight = lax.optimization_barrier((first, second, gained, out_weight))
-    ring = [along(features(e), e, "y", "x") for e in (1, 2, 3)]
+    ring = [along(features(e)[:, at : at + 512], e, "y", "x") for e in (1, 2, 3) for at in (0, 512)]
     pair = jnp.stack([first, second])
     pair = jnp.concatenate([pair, swap(pair, "core", 1)], axis=0)
     wo_other, pair, opposite, *ring = lax.optimization_barrier(
         (swap(out_weight, "zh", 1), pair, along(pair, 2, "x", "y"), *ring)
     )
+    ring = [jnp.concatenate(ring[at : at + 2], axis=1) for at in (0, 2, 4)]
     inputs = jnp.concatenate([features(0)] + ring, axis=0)
     blocks = [pair, along(pair, 1, "x", "y"), opposite, along(pair, 3, "x", "y")]
     sent, total = project(inputs, blocks)

time: 147 us -> 156 us (1.061)
  the two profiles are of different devices: /device:TPU:24 before, /device:TPU:28 now
where the time goes in v19:
time: 156 us; the launch traced here: 155 us
  waiting for transfers between devices  76 us (49%)
  starting transfers between devices  41.5 us (27%)
  between operations  14.8 us (9%)
  matrix products  8.6 us (6%)
  local copies, waits for them, and re-layouts  5.65 us (4%)
  other arithmetic  5.15 us (3%)
  Pallas kernels  3.85 us (2%)
    ppermute x14, waiting for transfers between devices, move(): lax.ppermute(value, AXES, [(flat(*at), flat(*where(*at))) for at in every...  61.5 us
    ppermute x14, starting transfers between devices, move(): lax.ppermute(value, AXES, [(flat(*at), flat(*where(*at))) for at in every...  27.4 us
    ppermute x8, waiting for transfers between devices, swap(): return lax.ppermute(value, axis, [(i, i ^ d) for i in range(n)])  14.4 us
    ppermute x8, starting transfers between devices, swap(): return lax.ppermute(value, axis, [(i, i ^ d) for i in range(n)])  14.1 us
    dot_general x1, matrix products, body(): return jnp.dot(all_rows, wo, preferred_element_type=F32).astype(BF)  7.35 us
    unnamed x32, local copies, waits for them, and re-layouts  3.96 us
    pallas_call x1, Pallas kernels, project(): pl.pallas_call(project_kernel, out_shape=(jax.ShapeDtypeStruct((3, ROWS,...  3.81 us
  transfers between devices with their start and end apart: 23, of which 16 were waited for; matrix products, arithmetic and copies ran while one was open for 5% of the time, Pallas kernels for 2%

profile of v19, /device:TPU:28, one launch (start us, length us, event | category | flops | bytes accessed | tf_op | source)
XLA Modules:
  0.0 155.5 jit_solution(6310277129343273464)
XLA Ops:
  6.5 0.9 copy-done
  8.3 6.5 %collective-permute-start = (bf16[896,128]{1,0:T(8,128)(2,1)S(1)}, bf16[896,128]{1,0:T(8,128)(2,1)S(1)}, u32[]{:S(2)}, u32[]{:S(2)}) collective-permute-start(bf16[896,128]{1,0:T(8,128)(2,1)S(1)} %shard_map.118), channel_id=1, source_target_pairs={{0,0},{1,32},{2,4},{3,36},{4,64},{5,96},{6,68},{7,100},{8,8},{9,40... | collective-permute-start | bytes 688136 | tf_op jit(solution)/shard_map/ppermute | solution.py:43
  14.8 3.8 %collective-permute-start.1 = (bf16[896,128]{1,0:T(8,128)(2,1)S(1)}, bf16[896,128]{1,0:T(8,128)(2,1)S(1)}, u32[]{:S(2)}, u32[]{:S(2)}) collective-permute-start(bf16[896,128]{1,0:T(8,128)(2,1)S(1)} %shard_map.118), channel_id=1, source_target_pairs={{0,32},{1,0},{2,36},{3,4},{4,96},{5,64},{6,100},{7,68},{8,40},{9,8... | collective-permute-start | bytes 688136 | tf_op jit(solution)/shard_map/ppermute | solution.py:43
  18.6 1.6 %fusion.2 = (f32[128]{0:T(128)S(1)}, bf16[128,4096]{1,0:T(8,128)(2,1)S(1)}) fusion(bf16[128,4096]{1,0:T(8,128)(2,1)} %param.12, f32[4096]{0:T(1024)} %param.13), kind=kLoop, calls=%fused_computation.5 | loop fusion | flops 2621312 | bytes 2114048 | tf_op jit(solution)/shard_map/reduce_sum | solution.py:170
  20.3 3.3 %collective-permute-done = bf16[896,128]{1,0:T(8,128)(2,1)S(1)} collective-permute-done((bf16[896,128]{1,0:T(8,128)(2,1)S(1)}, bf16[896,128]{1,0:T(8,128)(2,1)S(1)}, u32[]{:S(2)}, u32[]{:S(2)}) %collective-permute-start) | collective-permute-done | bytes 229408 | tf_op jit(solution)/shard_map/ppermute | solution.py:43
  23.5 13.7 %collective-permute-done.1 = bf16[896,128]{1,0:T(8,128)(2,1)S(1)} collective-permute-done((bf16[896,128]{1,0:T(8,128)(2,1)S(1)}, bf16[896,128]{1,0:T(8,128)(2,1)S(1)}, u32[]{:S(2)}, u32[]{:S(2)}) %collective-permute-start.1) | collective-permute-done | bytes 229408 | tf_op jit(solution)/shard_map/ppermute | solution.py:43
  37.6 1.6 %collective-permute-done.3 = bf16[2,896,128]{2,1,0:T(8,128)(2,1)S(1)} collective-permute-done((bf16[2,896,128]{2,1,0:T(8,128)(2,1)S(1)}, bf16[2,896,128]{2,1,0:T(8,128)(2,1)S(1)}, u32[]{:S(2)}, u32[]{:S(2)}) %collective-permute-start.3) | collective-permute-done | bytes 458784 | tf_op jit(solution)/shard_map/ppermute | solution.py:39
  40.2 3.3 %collective-permute-start.9 = (bf16[128,512]{1,0:T(8,128)(2,1)S(1)}, bf16[128,512]{1,0:T(8,128)(2,1)S(1)}, u32[]{:S(2)}, u32[]{:S(2)}) collective-permute-start(bf16[128,512]{1,0:T(8,128)(2,1)S(1)} %pad_maximum_fusion.7), channel_id=1, source_target_pairs={{0,192},{1,193},{2,194},{3,195},{4,28},{5,29},{6,30},{7,31},{8,200... | collective-permute-start | bytes 393224 | tf_op jit(solution)/shard_map/ppermute | solution.py:43
  43.6 4.9 %collective-permute-start.2 = (bf16[24,4096]{1,0:T(8,128)(2,1)S(1)}, bf16[24,4096]{1,0:T(8,128)(2,1)S(1)}, u32[]{:S(2)}, u32[]{:S(2)}) collective-permute-start(bf16[24,4096]{1,0:T(8,128)(2,1)S(1)} %copy-done.4), channel_id=1, source_target_pairs={{0,32},{32,0},{1,33},{33,1},{2,34},{34,2},{3,35},{35,3},{4,36},{36... | collective-permute-start | bytes 589832 | tf_op jit(solution)/shard_map/ppermute | solution.py:39
  48.5 7.8 %collective-permute-done.10 = bf16[128,512]{1,0:T(8,128)(2,1)S(1)} collective-permute-done((bf16[128,512]{1,0:T(8,128)(2,1)S(1)}, bf16[128,512]{1,0:T(8,128)(2,1)S(1)}, u32[]{:S(2)}, u32[]{:S(2)}) %collective-permute-start.10) | collective-permute-done | bytes 131104 | tf_op jit(solution)/shard_map/ppermute | solution.py:43
  56.3 1.4 collective-permute-done.9
  57.7 2.0 %collective-permute-start.5 = (bf16[128,512]{1,0:T(8,128)(2,1)S(1)}, bf16[128,512]{1,0:T(8,128)(2,1)S(1)}, u32[]{:S(2)}, u32[]{:S(2)}) collective-permute-start(bf16[128,512]{1,0:T(8,128)(2,1)S(1)} %pad_maximum_fusion.3), channel_id=1, source_target_pairs={{0,64},{1,65},{2,66},{3,67},{4,12},{5,13},{6,14},{7,15},{8,72},{9,... | collective-permute-start | bytes 393224 | tf_op jit(solution)/shard_map/ppermute | solution.py:43
  59.7 3.0 %collective-permute-done.7 = bf16[128,512]{1,0:T(8,128)(2,1)S(1)} collective-permute-done((bf16[128,512]{1,0:T(8,128)(2,1)S(1)}, bf16[128,512]{1,0:T(8,128)(2,1)S(1)}, u32[]{:S(2)}, u32[]{:S(2)}) %collective-permute-start.7) | collective-permute-done | bytes 131104 | tf_op jit(solution)/shard_map/ppermute | solution.py:43
  62.7 1.3 collective-permute-done.5
  64.9 1.3 collective-permute-start.11
  66.8 1.1 maximum_maximum_fusion.x_ref
  67.9 10.4 %collective-permute-done.11.refs_1_ = bf16[4,896,128]{2,1,0:T(8,128)(2,1)S(1)} collective-permute-done((bf16[4,896,128]{2,1,0:T(8,128)(2,1)S(1)}, bf16[4,896,128]{2,1,0:T(8,128)(2,1)S(1)}, u32[]{:S(2)}, u32[]{:S(2)}) %collective-permute-start.11) | collective-permute-done | bytes 917536 | tf_op jit(solution)/shard_map/ppermute | solution.py:43
  78.4 0.9 copy-done.2
  79.7 1.2 copy-done.3
  80.9 3.8 %shard_map.119 = (bf16[3,128,1792]{2,1,0:T(8,128)(2,1)S(1)}, f32[128,1792]{1,0:T(8,128)S(1)}) custom-call(bf16[512,1024]{1,0:T(8,128)(2,1)S(1)} %maximum_maximum_fusion.x_ref, bf16[4,896,128]{2,1,0:T(8,128)(2,1)S(1)} %pad_maximum_fusion.refs_0_, bf16[4,896,128]{2,1,0:T(8,128)(2,1)S(1)} %copy-done.3, bf16[4,896,128]{2,1,0:T(8,128)(2,1)S(1)} %collective-permute-done.4.refs_2_, ...), custom_call_target="tpu_custom_call" | custom-call | flops 1879048192 | bytes 8000000 | tf_op jit(solution)/shard_map/pallas_call | solution.py:141
  84.7 0.9 slice_bitcast_fusion.2
  86.3 9.0 %collective-permute-start.14 = (bf16[128,1792]{1,0:T(8,128)(2,1)S(1)}, bf16[128,1792]{1,0:T(8,128)(2,1)S(1)}, u32[]{:S(2)}, u32[]{:S(2)}) collective-permute-start(bf16[128,1792]{1,0:T(8,128)(2,1)S(1)} %get-tuple-element.37), channel_id=1, source_target_pairs={{0,128},{1,129},{2,130},{3,131},{4,20},{5,21},{6,22},{7,23},{8,136... | collective-permute-start | bytes 1376264 | tf_op jit(solution)/shard_map/ppermute | solution.py:43
  95.6 11.3 %collective-permute-done.14 = bf16[128,1792]{1,0:T(8,128)(2,1)S(1)} collective-permute-done((bf16[128,1792]{1,0:T(8,128)(2,1)S(1)}, bf16[128,1792]{1,0:T(8,128)(2,1)S(1)}, u32[]{:S(2)}, u32[]{:S(2)}) %collective-permute-start.14) | collective-permute-done | bytes 458784 | tf_op jit(solution)/shard_map/ppermute | solution.py:43
  106.9 8.6 %collective-permute-done.15 = bf16[128,1792]{1,0:T(8,128)(2,1)S(1)} collective-permute-done((bf16[128,1792]{1,0:T(8,128)(2,1)S(1)}, bf16[128,1792]{1,0:T(8,128)(2,1)S(1)}, u32[]{:S(2)}, u32[]{:S(2)}) %collective-permute-start.15) | collective-permute-done | bytes 458784 | tf_op jit(solution)/shard_map/ppermute | solution.py:43
  116.3 4.3 %collective-permute-start.16 = (bf16[32,2688]{1,0:T(8,128)(2,1)S(1)}, bf16[32,2688]{1,0:T(8,128)(2,1)S(1)}, u32[]{:S(2)}, u32[]{:S(2)}) collective-permute-start(bf16[32,2688]{1,0:T(8,128)(2,1)S(1)} %get-tuple-element.103), channel_id=1, source_target_pairs={{0,1},{1,0},{2,3},{3,2},{4,5},{5,4},{6,7},{7,6},{8,9},{9,8},{10,11... | collective-permute-start | bytes 516104 | tf_op jit(solution)/shard_map/ppermute | solution.py:39
  120.7 7.1 %collective-permute-done.16 = bf16[32,2688]{1,0:T(8,128)(2,1)S(1)} collective-permute-done((bf16[32,2688]{1,0:T(8,128)(2,1)S(1)}, bf16[32,2688]{1,0:T(8,128)(2,1)S(1)}, u32[]{:S(2)}, u32[]{:S(2)}) %collective-permute-start.16) | collective-permute-done | bytes 172064 | tf_op jit(solution)/shard_map/ppermute | solution.py:39
  127.8 1.6 %collective-permute-done.17 = bf16[32,2688]{1,0:T(8,128)(2,1)S(1)} collective-permute-done((bf16[32,2688]{1,0:T(8,128)(2,1)S(1)}, bf16[32,2688]{1,0:T(8,128)(2,1)S(1)}, u32[]{:S(2)}, u32[]{:S(2)}) %collective-permute-start.17) | collective-permute-done | bytes 172064 | tf_op jit(solution)/shard_map/ppermute | solution.py:39
  132.6 0.9 collective-permute-start.19
  133.6 3.5 %collective-permute-start.21 = (bf16[32,1536]{1,0:T(8,128)(2,1)S(1)}, bf16[32,1536]{1,0:T(8,128)(2,1)S(1)}, u32[]{:S(2)}, u32[]{:S(2)}) collective-permute-start(bf16[32,1536]{1,0:T(8,128)(2,1)S(1)} %pad_maximum_fusion.9), channel_id=1, source_target_pairs={{0,1},{1,0},{2,3},{3,2},{4,5},{5,4},{6,7},{7,6},{8,9},{9,8},{10,11... | collective-permute-start | bytes 294920 | tf_op jit(solution)/shard_map/ppermute | solution.py:39
  137.1 2.2 %collective-permute-done.19 = bf16[32,1536]{1,0:T(8,128)(2,1)S(1)} collective-permute-done((bf16[32,1536]{1,0:T(8,128)(2,1)S(1)}, bf16[32,1536]{1,0:T(8,128)(2,1)S(1)}, u32[]{:S(2)}, u32[]{:S(2)}) %collective-permute-start.19) | collective-permute-done | bytes 98336 | tf_op jit(solution)/shard_map/ppermute | solution.py:39
  139.3 1.8 %collective-permute-done.20 = bf16[32,1536]{1,0:T(8,128)(2,1)S(1)} collective-permute-done((bf16[32,1536]{1,0:T(8,128)(2,1)S(1)}, bf16[32,1536]{1,0:T(8,128)(2,1)S(1)}, u32[]{:S(2)}, u32[]{:S(2)}) %collective-permute-start.20) | collective-permute-done | bytes 98336 | tf_op jit(solution)/shard_map/ppermute | solution.py:39
  141.3 7.4 %convolution_convert_fusion = bf16[128,4096]{1,0:T(8,128)(2,1)} fusion(bf16[1536,4096]{1,0:T(8,128)(2,1)} %all-gather.2.cloned.1.call-done, bf16[32,1536]{1,0:T(8,128)(2,1)S(1)} %broadcast_select_fusion.4, bf16[32,1536]{1,0:T(8,128)(2,1)S(1)} %get-tuple-element.61, bf16[32,1536]{1,0:T(8,128)(2,1)S(1)} %get-tuple-element.60, ...), kind=kOutput, calls=%fused_computation.1 | convolution fusion | flops 1612709888 | bytes 14024704 | tf_op jit(solution)/shard_map/dot_general | solution.py:237
  (107 shorter events, 8.2 us)
Async XLA Ops:
  6.5 134.8 %all-gather.2.cloned.1.call-start = ((), (), s32[]{:S(2)}) async-start(), calls=%async_computation | async-start | bytes 12976128 | tf_op jit(solution)/shard_map/all_gather | solution.py:195
  6.5 0.9 copy-start
  8.3 15.3 %collective-permute-start = (bf16[896,128]{1,0:T(8,128)(2,1)S(1)}, bf16[896,128]{1,0:T(8,128)(2,1)S(1)}, u32[]{:S(2)}, u32[]{:S(2)}) collective-permute-start(bf16[896,128]{1,0:T(8,128)(2,1)S(1)} %shard_map.118), channel_id=1, source_target_pairs={{0,0},{1,32},{2,4},{3,36},{4,64},{5,96},{6,68},{7,100},{8,8},{9,40... | collective-permute-start | bytes 688136 | tf_op jit(solution)/shard_map/ppermute | solution.py:43
  14.8 22.5 %collective-permute-start.1 = (bf16[896,128]{1,0:T(8,128)(2,1)S(1)}, bf16[896,128]{1,0:T(8,128)(2,1)S(1)}, u32[]{:S(2)}, u32[]{:S(2)}) collective-permute-start(bf16[896,128]{1,0:T(8,128)(2,1)S(1)} %shard_map.118), channel_id=1, source_target_pairs={{0,32},{1,0},{2,36},{3,4},{4,96},{5,64},{6,100},{7,68},{8,40},{9,8... | collective-permute-start | bytes 688136 | tf_op jit(solution)/shard_map/ppermute | solution.py:43
  37.3 1.9 %collective-permute-start.3 = (bf16[2,896,128]{2,1,0:T(8,128)(2,1)S(1)}, bf16[2,896,128]{2,1,0:T(8,128)(2,1)S(1)}, u32[]{:S(2)}, u32[]{:S(2)}) collective-permute-start(bf16[2,896,128]{2,1,0:T(8,128)(2,1)S(1)} %pad_maximum_fusion.1), channel_id=1, source_target_pairs={{0,4},{4,0},{1,5},{5,1},{2,6},{6,2},{3,7},{7,3},{8,12},{12,8},{9,1... | collective-permute-start | bytes 1376264 | tf_op jit(solution)/shard_map/ppermute | solution.py:39
  37.6 6.0 %copy-start.4 = (bf16[24,4096]{1,0:T(8,128)(2,1)S(1)}, bf16[24,4096]{1,0:T(8,128)(2,1)}, u32[]{:S(2)}) copy-start(bf16[24,4096]{1,0:T(8,128)(2,1)} %param.16) | copy-start | bytes 589828
  39.3 24.7 %collective-permute-start.4 = (bf16[4,896,128]{2,1,0:T(8,128)(2,1)S(1)}, bf16[4,896,128]{2,1,0:T(8,128)(2,1)S(1)}, u32[]{:S(2)}, u32[]{:S(2)}) collective-permute-start(bf16[4,896,128]{2,1,0:T(8,128)(2,1)S(1)} %pad_maximum_fusion.refs_0_), channel_id=1, source_target_pairs={{0,16},{1,17},{2,18},{3,19},{4,132},{5,133},{6,134},{7,135},{8,24}... | collective-permute-start | bytes 2752520 | tf_op jit(solution)/shard_map/ppermute | solution.py:43
  40.1 16.2 %collective-permute-start.10 = (bf16[128,512]{1,0:T(8,128)(2,1)S(1)}, bf16[128,512]{1,0:T(8,128)(2,1)S(1)}, u32[]{:S(2)}, u32[]{:S(2)}) collective-permute-start(bf16[128,512]{1,0:T(8,128)(2,1)S(1)} %pad_maximum_fusion.8), channel_id=1, source_target_pairs={{0,192},{1,193},{2,194},{3,195},{4,28},{5,29},{6,30},{7,31},{8,200... | collective-permute-start | bytes 393224 | tf_op jit(solution)/shard_map/ppermute | solution.py:43
  40.2 17.5 %collective-permute-start.9 = (bf16[128,512]{1,0:T(8,128)(2,1)S(1)}, bf16[128,512]{1,0:T(8,128)(2,1)S(1)}, u32[]{:S(2)}, u32[]{:S(2)}) collective-permute-start(bf16[128,512]{1,0:T(8,128)(2,1)S(1)} %pad_maximum_fusion.7), channel_id=1, source_target_pairs={{0,192},{1,193},{2,194},{3,195},{4,28},{5,29},{6,30},{7,31},{8,200... | collective-permute-start | bytes 393224 | tf_op jit(solution)/shard_map/ppermute | solution.py:43
  43.5 14.2 %collective-permute-start.8 = (bf16[128,512]{1,0:T(8,128)(2,1)S(1)}, bf16[128,512]{1,0:T(8,128)(2,1)S(1)}, u32[]{:S(2)}, u32[]{:S(2)}) collective-permute-start(bf16[128,512]{1,0:T(8,128)(2,1)S(1)} %pad_maximum_fusion.6), channel_id=1, source_target_pairs={{0,128},{1,129},{2,130},{3,131},{4,20},{5,21},{6,22},{7,23},{8,136... | collective-permute-start | bytes 393224 | tf_op jit(solution)/shard_map/ppermute | solution.py:43
  43.6 20.4 %collective-permute-start.2 = (bf16[24,4096]{1,0:T(8,128)(2,1)S(1)}, bf16[24,4096]{1,0:T(8,128)(2,1)S(1)}, u32[]{:S(2)}, u32[]{:S(2)}) collective-permute-start(bf16[24,4096]{1,0:T(8,128)(2,1)S(1)} %copy-done.4), channel_id=1, source_target_pairs={{0,32},{32,0},{1,33},{33,1},{2,34},{34,2},{3,35},{35,3},{4,36},{36... | collective-permute-start | bytes 589832 | tf_op jit(solution)/shard_map/ppermute | solution.py:39
  56.3 6.5 %collective-permute-start.7 = (bf16[128,512]{1,0:T(8,128)(2,1)S(1)}, bf16[128,512]{1,0:T(8,128)(2,1)S(1)}, u32[]{:S(2)}, u32[]{:S(2)}) collective-permute-start(bf16[128,512]{1,0:T(8,128)(2,1)S(1)} %pad_maximum_fusion.5), channel_id=1, source_target_pairs={{0,128},{1,129},{2,130},{3,131},{4,20},{5,21},{6,22},{7,23},{8,136... | collective-permute-start | bytes 393224 | tf_op jit(solution)/shard_map/ppermute | solution.py:43
  57.7 5.1 %collective-permute-start.6 = (bf16[128,512]{1,0:T(8,128)(2,1)S(1)}, bf16[128,512]{1,0:T(8,128)(2,1)S(1)}, u32[]{:S(2)}, u32[]{:S(2)}) collective-permute-start(bf16[128,512]{1,0:T(8,128)(2,1)S(1)} %pad_maximum_fusion.4), channel_id=1, source_target_pairs={{0,64},{1,65},{2,66},{3,67},{4,12},{5,13},{6,14},{7,15},{8,72},{9,... | collective-permute-start | bytes 393224 | tf_op jit(solution)/shard_map/ppermute | solution.py:43
  57.7 6.4 %collective-permute-start.5 = (bf16[128,512]{1,0:T(8,128)(2,1)S(1)}, bf16[128,512]{1,0:T(8,128)(2,1)S(1)}, u32[]{:S(2)}, u32[]{:S(2)}) collective-permute-start(bf16[128,512]{1,0:T(8,128)(2,1)S(1)} %pad_maximum_fusion.3), channel_id=1, source_target_pairs={{0,64},{1,65},{2,66},{3,67},{4,12},{5,13},{6,14},{7,15},{8,72},{9,... | collective-permute-start | bytes 393224 | tf_op jit(solution)/shard_map/ppermute | solution.py:43
  62.7 2.1 %copy-start.5 = (bf16[128,512]{1,0:T(8,128)(2,1)}, bf16[128,512]{1,0:T(8,128)(2,1)S(1)}, u32[]{:S(2)}) copy-start(bf16[128,512]{1,0:T(8,128)(2,1)S(1)} %collective-permute-done.6) | copy-start | bytes 393220
  64.9 13.5 %collective-permute-start.11 = (bf16[4,896,128]{2,1,0:T(8,128)(2,1)S(1)}, bf16[4,896,128]{2,1,0:T(8,128)(2,1)S(1)}, u32[]{:S(2)}, u32[]{:S(2)}) collective-permute-start(bf16[4,896,128]{2,1,0:T(8,128)(2,1)S(1)} %pad_maximum_fusion.refs_0_), channel_id=1, source_target_pairs={{0,8},{1,9},{2,10},{3,11},{4,68},{5,69},{6,70},{7,71},{8,0},{9,1},... | collective-permute-start | bytes 2752520 | tf_op jit(solution)/shard_map/ppermute | solution.py:43
  66.2 13.5 %collective-permute-start.12 = (bf16[4,896,128]{2,1,0:T(8,128)(2,1)S(1)}, bf16[4,896,128]{2,1,0:T(8,128)(2,1)}, u32[]{:S(2)}, u32[]{:S(2)}) collective-permute-start(bf16[4,896,128]{2,1,0:T(8,128)(2,1)S(1)} %pad_maximum_fusion.refs_0_), channel_id=1, source_target_pairs={{0,24},{1,25},{2,26},{3,27},{4,196},{5,197},{6,198},{7,199},{8,16}... | collective-permute-start | bytes 2752520 | tf_op jit(solution)/shard_map/ppermute | solution.py:43
  78.3 0.9 copy-start.2
  79.7 1.2 copy-start.3
  84.7 10.6 %copy-start.7 = (f32[128,128]{1,0:T(8,128)S(1)}, f32[128,128]{1,0:T(8,128)}, u32[]{:S(2)}) copy-start(f32[128,128]{1,0:T(8,128)} %constant.76.clone) | copy-start | bytes 196612
  84.7 10.6 %copy-start.8 = (f32[128,128]{1,0:T(8,128)S(1)}, f32[128,128]{1,0:T(8,128)}, u32[]{:S(2)}) copy-start(f32[128,128]{1,0:T(8,128)} %constant.77.clone) | copy-start | bytes 196612
  85.6 10.0 %collective-permute-start.13 = (bf16[128,1792]{1,0:T(8,128)(2,1)}, bf16[128,1792]{1,0:T(8,128)(2,1)S(1)}, u32[]{:S(2)}, u32[]{:S(2)}) collective-permute-start(bf16[128,1792]{1,0:T(8,128)(2,1)} %get-tuple-element.35), channel_id=1, source_target_pairs={{0,64},{1,65},{2,66},{3,67},{4,12},{5,13},{6,14},{7,15},{8,72},{9,... | collective-permute-start | bytes 1376264 | tf_op jit(solution)/shard_map/ppermute | solution.py:43
  86.3 20.6 %collective-permute-start.14 = (bf16[128,1792]{1,0:T(8,128)(2,1)S(1)}, bf16[128,1792]{1,0:T(8,128)(2,1)S(1)}, u32[]{:S(2)}, u32[]{:S(2)}) collective-permute-start(bf16[128,1792]{1,0:T(8,128)(2,1)S(1)} %get-tuple-element.37), channel_id=1, source_target_pairs={{0,128},{1,129},{2,130},{3,131},{4,20},{5,21},{6,22},{7,23},{8,136... | collective-permute-start | bytes 1376264 | tf_op jit(solution)/shard_map/ppermute | solution.py:43
  95.2 20.3 %collective-permute-start.15 = (bf16[128,1792]{1,0:T(8,128)(2,1)S(1)}, bf16[128,1792]{1,0:T(8,128)(2,1)S(1)}, u32[]{:S(2)}, u32[]{:S(2)}) collective-permute-start(bf16[128,1792]{1,0:T(8,128)(2,1)S(1)} %get-tuple-element.36), channel_id=1, source_target_pairs={{0,192},{1,193},{2,194},{3,195},{4,28},{5,29},{6,30},{7,31},{8,200... | collective-permute-start | bytes 1376264 | tf_op jit(solution)/shard_map/ppermute | solution.py:43
  115.9 13.6 %collective-permute-start.18 = (bf16[32,2688]{1,0:T(8,128)(2,1)S(1)}, bf16[32,2688]{1,0:T(8,128)(2,1)S(1)}, u32[]{:S(2)}, u32[]{:S(2)}) collective-permute-start(bf16[32,2688]{1,0:T(8,128)(2,1)S(1)} %get-tuple-element.105), channel_id=1, source_target_pairs={{0,3},{1,2},{2,1},{3,0},{4,7},{5,6},{6,5},{7,4},{8,11},{9,10},{10,... | collective-permute-start | bytes 516104 | tf_op jit(solution)/shard_map/ppermute | solution.py:39
  116.2 13.2 %collective-permute-start.17 = (bf16[32,2688]{1,0:T(8,128)(2,1)S(1)}, bf16[32,2688]{1,0:T(8,128)(2,1)S(1)}, u32[]{:S(2)}, u32[]{:S(2)}) collective-permute-start(bf16[32,2688]{1,0:T(8,128)(2,1)S(1)} %get-tuple-element.104), channel_id=1, source_target_pairs={{0,2},{1,3},{2,0},{3,1},{4,6},{5,7},{6,4},{7,5},{8,10},{9,11},{10,... | collective-permute-start | bytes 516104 | tf_op jit(solution)/shard_map/ppermute | solution.py:39
  116.3 11.5 %collective-permute-start.16 = (bf16[32,2688]{1,0:T(8,128)(2,1)S(1)}, bf16[32,2688]{1,0:T(8,128)(2,1)S(1)}, u32[]{:S(2)}, u32[]{:S(2)}) collective-permute-start(bf16[32,2688]{1,0:T(8,128)(2,1)S(1)} %get-tuple-element.103), channel_id=1, source_target_pairs={{0,1},{1,0},{2,3},{3,2},{4,5},{5,4},{6,7},{7,6},{8,9},{9,8},{10,11... | collective-permute-start | bytes 516104 | tf_op jit(solution)/shard_map/ppermute | solution.py:39
  130.8 1.5 copy-start.9
  130.8 1.5 copy-start.10
  132.6 6.7 %collective-permute-start.19 = (bf16[32,1536]{1,0:T(8,128)(2,1)S(1)}, bf16[32,1536]{1,0:T(8,128)(2,1)S(1)}, u32[]{:S(2)}, u32[]{:S(2)}) collective-permute-start(bf16[32,1536]{1,0:T(8,128)(2,1)S(1)} %pad_maximum_fusion.9), channel_id=1, source_target_pairs={{0,3},{1,2},{2,1},{3,0},{4,7},{5,6},{6,5},{7,4},{8,11},{9,10},{10,... | collective-permute-start | bytes 294920 | tf_op jit(solution)/shard_map/ppermute | solution.py:39
  133.5 7.6 %collective-permute-start.20 = (bf16[32,1536]{1,0:T(8,128)(2,1)S(1)}, bf16[32,1536]{1,0:T(8,128)(2,1)S(1)}, u32[]{:S(2)}, u32[]{:S(2)}) collective-permute-start(bf16[32,1536]{1,0:T(8,128)(2,1)S(1)} %pad_maximum_fusion.9), channel_id=1, source_target_pairs={{0,2},{1,3},{2,0},{3,1},{4,6},{5,7},{6,4},{7,5},{8,10},{9,11},{10,... | collective-permute-start | bytes 294920 | tf_op jit(solution)/shard_map/ppermute | solution.py:39
  133.6 7.5 %collective-permute-start.21 = (bf16[32,1536]{1,0:T(8,128)(2,1)S(1)}, bf16[32,1536]{1,0:T(8,128)(2,1)S(1)}, u32[]{:S(2)}, u32[]{:S(2)}) collective-permute-start(bf16[32,1536]{1,0:T(8,128)(2,1)S(1)} %pad_maximum_fusion.9), channel_id=1, source_target_pairs={{0,1},{1,0},{2,3},{3,2},{4,5},{5,4},{6,7},{7,6},{8,9},{9,8},{10,11... | collective-permute-start | bytes 294920 | tf_op jit(solution)/shard_map/ppermute | solution.py:39
  (2 other events, 1.6 us)
Sparse Core Ops, SparseCore 0:
  65.0 72.0 all-gather.1
